TPU v7x, 512 devices: a whole 4x8x8 slice. The times are simulated.
512 devices in a mesh: lat: 8 (over z_lo, x), lon: 64 (over z_hi, y, core).
Axes of the slice: x: 4, y: 8, z: 8 (z_hi: 4, z_lo: 2; z = z_hi * 2 + z_lo), core: 2. Of those that a mesh axis runs over, the one named last changes fastest.
Arguments:
- innovations: float32 [8, 64, 16, 512], P('lat', 'lon'), may hold values from -6 to 6
- obs_error: float32 [8, 64, 512], P('lat', 'lon'), may hold values from 0.3 to 1.2
- where_frac: bfloat16 [8, 64, 3, 512], P('lat', 'lon'), may hold values from 0 to 1
- spread: bfloat16 [8, 64, 512], P('lat', 'lon'), may hold values from 2 to 4
- obs_type: int32 [8, 64, 512], P('lat', 'lon'), may hold values from 0 to 2
Outputs:
- solution: float32 [8, 64, 16, 512], P('lat', 'lon')
- residual: float32 [8, 64, 16, 512], P('lat', 'lon')
All inputs are finite; a program needn't handle non-finite values.
Results may differ from a plain program's by a relative error of at most 0.0098.
Values may be sent and summed in bfloat16 or wider, within the bound.
No kernel may reach another device: no remote copies, remote signals or barrier semaphores. Data moves between devices by JAX's collectives and lax.ppermute only.
A program may use at most 64 MiB of HBM per device.

v0:
```python
import math

import jax
import jax.numpy as jnp
from jax import lax
from jax.sharding import PartitionSpec as P

ITERS = 3


LAT_LIMIT = 80.0 * math.pi / 180.0
HORIZ_SQ = 0.05 * 0.05
VERT_SQ = 0.3 * 0.3
TAPER_STEP = 0.45


def extended(block, sides, width):
    for axis, dim in sides:
        count = lax.axis_size(axis)
        forward = [(i, i + 1) for i in range(count - 1)]
        forward.append((count - 1, 0))
        backward = [(target, source) for source, target in forward]
        low = lax.ppermute(
            lax.slice_in_dim(block, block.shape[dim] - width, None, axis=dim), axis, forward
        )
        high = lax.ppermute(lax.slice_in_dim(block, 0, width, axis=dim), axis, backward)
        block = jnp.concatenate([low, block, high], axis=dim)
    return block


def passed_along(value, axis, steps):
    count = lax.axis_size(axis)
    initial, last = (max(0, -steps), min(count, count - steps))
    return lax.ppermute(value, axis, [(source, source + steps) for source in range(initial, last)])


def features(obs_info, band_at, sector_at, bands, sectors):
    values = obs_info.astype(jnp.float32)
    latitude = (band_at.astype(jnp.float32) + values[0]) * (2.0 * LAT_LIMIT / bands) - LAT_LIMIT
    longitude = (sector_at.astype(jnp.float32) + values[1]) * (2.0 * math.pi / sectors)
    cos_lat = jnp.cos(latitude)
    return (
        cos_lat * jnp.cos(longitude),
        cos_lat * jnp.sin(longitude),
        jnp.sin(latitude),
        values[2],
        values[3],
        values[4],
    )


def tile_rows(own_feat, far_feat, weight):
    inner = (
        own_feat[0][:, None] * far_feat[0][None, :]
        + own_feat[1][:, None] * far_feat[1][None, :]
        + own_feat[2][:, None] * far_feat[2][None, :]
    )
    vert_gap = own_feat[3][:, None] - far_feat[3][None, :]
    kernel = jnp.exp((inner - 1.0) / HORIZ_SQ - vert_gap * vert_gap / (2.0 * VERT_SQ))
    same_type = own_feat[5][:, None] == far_feat[5][None, :]
    height_pair = (own_feat[5][:, None] == 0.0) | (far_feat[5][None, :] == 0.0)
    coupling = jnp.where(same_type, 1.0, jnp.where(height_pair, 0.45, 0.25)).astype(jnp.float32)
    return (own_feat[4][:, None] * far_feat[4][None, :] * coupling * kernel * weight).astype(
        jnp.bfloat16
    )


def build_tile(own_feat, far_feat, weight):
    count = own_feat[0].shape[0]
    stacked = jnp.stack(own_feat).reshape(6, count // 128, 128).transpose(1, 0, 2)
    pieces = lax.map(
        lambda piece: tile_rows(tuple((piece[i] for i in range(6))), far_feat, weight), stacked
    )
    return pieces.reshape(count, count)


def neighbours(field):
    widened = extended(field, (("lon", 1),), 1)
    northern = passed_along(widened, "lat", -1)
    return (widened, northern)


def southern_of(widened):
    return passed_along(widened, "lat", 1)


def contract(field, tile):
    return lax.dot_general(
        field, tile, (((1,), (1,)), ((), ())), preferred_element_type=jnp.float32
    )


def local(innovations, obs_error, where_frac, spread, obs_type):
    bands = lax.axis_size("lat")
    sectors = lax.axis_size("lon")
    my_band = lax.axis_index("lat")
    my_sector = lax.axis_index("lon")
    obs_info = jnp.concatenate(
        [where_frac[0, 0], spread[0, 0][None], obs_type[0, 0][None].astype(jnp.bfloat16)], axis=0
    )[None, None]
    info_wide, info_north = neighbours(obs_info)
    own_feat = features(obs_info[0, 0], my_band, my_sector, bands, sectors)
    error_var = obs_error[0, 0]

    def far_tile(blocks, step_lat, step_lon):
        near_info = blocks[step_lat][0, step_lon + 1]
        far_feat = features(near_info, my_band + step_lat, my_sector + step_lon, bands, sectors)
        return build_tile(own_feat, far_feat, TAPER_STEP ** (abs(step_lat) + abs(step_lon)))

    info_blocks = {0: info_wide, 1: info_north, -1: southern_of(info_wide)}
    offsets = [(a, b) for a in (-1, 0, 1) for b in (-1, 0, 1)]
    tile_list = [far_tile(info_blocks, a, b) for a, b in offsets]
    residual = innovations[0, 0]
    direction = residual
    solution = jnp.zeros_like(residual)
    norm_now = lax.psum(jnp.sum(residual * residual, axis=1), ("lat", "lon"))
    for iteration in range(ITERS):
        field = direction.astype(jnp.bfloat16)[None, None]
        widened, northern = neighbours(field)
        field_blocks = {0: widened, 1: northern, -1: southern_of(widened)}
        result = jnp.zeros(direction.shape, jnp.float32)
        for (apply_a, apply_b), tile in zip(offsets, tile_list):
            result = result + contract(field_blocks[apply_a][0, apply_b + 1], tile)
        image = result + error_var[None, :] * direction
        curve = lax.psum(jnp.sum(direction * image, axis=1), ("lat", "lon"))
        step_len = norm_now / curve
        solution = solution + step_len[:, None] * direction
        residual = residual - step_len[:, None] * image
        norm_next = lax.psum(jnp.sum(residual * residual, axis=1), ("lat", "lon"))
        direction = residual + (norm_next / norm_now)[:, None] * direction
        norm_now = norm_next
    return (solution[None, None], residual[None, None])


def solution(mesh):
    in_specs = (
        P("lat", "lon", None, None),
        P("lat", "lon", None),
        P("lat", "lon", None, None),
        P("lat", "lon", None),
        P("lat", "lon", None),
    )
    out_specs = (P("lat", "lon", None, None), P("lat", "lon", None, None))
    return jax.shard_map(local, mesh=mesh, in_specs=in_specs, out_specs=out_specs, check_vma=False)
```

profile of v0, /device:TPU:1, one launch (start us, length us, event | category | flops | bytes accessed | tf_op | source)
XLA Modules:
  0.0 591.6 jit_solution(4130293158664656240)
XLA Ops:
  0.6 0.7 convert_bitcast_fusion.2
  1.4 0.7 fusion.65
  2.0 4.6 collective-permute-start.3
  6.6 6.1 %collective-permute-start.4 = (bf16[1,1,5,512]{3,2,1,0:T(8,128)(2,1)S(1)}, bf16[1,1,5,512]{3,2,1,0:T(8,128)(2,1)S(1)}, u32[]{:S(2)}, u32[]{:S(2)}) collective-permute-start(bf16[1,1,5,512]{3,2,1,0:T(8,128)(2,1)S(1)} %get-tuple-element.1325), channel_id=1, source_target_pairs={{1,0},{2,1},{3,2},{4,3},{5,4},{6,5},{7,6},{8,7},{9,8},{10,9},{11,1... | collective-permute-start | bytes 15368 | tf_op jit(solution)/shard_map/ppermute | solution.py:26
  12.8 1.9 collective-permute-start
  14.7 7.9 %collective-permute-start.1 = (bf16[1,1,16,512]{3,2,1,0:T(8,128)(2,1)S(1)}, bf16[1,1,16,512]{3,2,1,0:T(8,128)(2,1)S(1)}, u32[]{:S(2)}, u32[]{:S(2)}) collective-permute-start(bf16[1,1,16,512]{3,2,1,0:T(8,128)(2,1)S(1)} %convert_element_type.212), channel_id=1, source_target_pairs={{1,0},{2,1},{3,2},{4,3},{5,4},{6,5},{7,6},{8,7},{9,8},{10,9},{11,1... | collective-permute-start | bytes 49160 | tf_op jit(solution)/shard_map/ppermute | solution.py:26
  23.0 1.4 while.112
  24.6 3.1 collective-permute-start.5
  27.7 1.3 collective-permute-start.7
  29.4 1.4 while.111
  31.0 1.4 while.113
  31.0 0.3 fusion.155
  31.4 0.3 fusion.155
  31.7 0.3 fusion.155
  32.1 0.3 fusion.155
  32.4 4.0 collective-permute-start.2
  36.4 1.3 collective-permute-start.6
  38.4 1.4 while.110
  40.3 1.4 while.109
  40.4 0.3 fusion.151
  40.7 0.3 fusion.151
  41.0 0.3 fusion.151
  41.4 0.3 fusion.151
  41.7 1.4 while.108
  43.5 0.9 broadcast.3776.clone.2
  44.4 3.8 while.114
  44.4 0.9 fusion.156
  45.4 0.9 fusion.156
  46.4 0.9 fusion.156
  47.3 0.9 fusion.156
  48.3 1.4 while.115
  48.4 0.3 fusion.157
  48.7 0.3 fusion.157
  49.0 0.3 fusion.157
  49.4 0.3 fusion.157
  49.7 0.8 copy-done.7
  50.5 1.4 while.116
  51.6 0.3 fusion.158
  52.4 0.5 copy-done.4
  53.8 0.6 copy-done.1
  54.6 0.7 copy-done.12
  55.3 0.4 fusion.32
  55.6 105.1 %all-reduce = (f32[16]{0:T(128)S(1)}, f32[16]{0:T(128)S(1)}) all-reduce(f32[16]{0:T(128)S(1)} %get-tuple-element.1029, f32[16]{0:T(128)S(1)} %get-tuple-element.1028), channel_id=1, replica_groups=mesh['lat'=8,'lon'=64] {'lat','lon'}, use_global_device_ids=true, to_apply=%region_1.2 | all-reduce | flops 32 | bytes 256 | tf_op jit(solution)/shard_map/psum | solution.py:116
  160.9 94.5 %psum.44 = f32[16]{0:T(128)S(1)} all-reduce(f32[16]{0:T(128)S(1)} %multiply_reduce_fusion.3), channel_id=1, replica_groups=mesh['lat'=8,'lon'=64] {'lat','lon'}, use_global_device_ids=true, to_apply=%region_23.24 | all-reduce | flops 16 | bytes 128 | tf_op jit(solution)/shard_map/psum | solution.py:129
  255.4 2.4 collective-permute-start.8
  257.9 2.1 collective-permute-start.9
  260.2 3.0 collective-permute-done.9
  263.2 2.9 collective-permute-start.10
  266.1 1.3 collective-permute-start.11
  268.2 2.8 collective-permute-done.11
  271.7 0.6 copy-done.2
  272.5 0.4 multiply_reduce_fusion.2
  272.9 102.2 %psum.45 = f32[16]{0:T(128)S(1)} all-reduce(f32[16]{0:T(128)S(1)} %get-tuple-element.1330), channel_id=1, replica_groups=mesh['lat'=8,'lon'=64] {'lat','lon'}, use_global_device_ids=true, to_apply=%region_25.26 | all-reduce | flops 16 | bytes 128 | tf_op jit(solution)/shard_map/psum | solution.py:125
  375.3 94.6 %psum.46 = f32[16]{0:T(128)S(1)} all-reduce(f32[16]{0:T(128)S(1)} %get-tuple-element.1196), channel_id=1, replica_groups=mesh['lat'=8,'lon'=64] {'lat','lon'}, use_global_device_ids=true, to_apply=%region_27.28 | all-reduce | flops 16 | bytes 128 | tf_op jit(solution)/shard_map/psum | solution.py:129
  470.0 3.6 collective-permute-start.12
  473.6 1.9 collective-permute-start.13
  475.8 3.2 collective-permute-done.13
  479.0 3.7 collective-permute-start.14
  482.7 1.3 collective-permute-start.15
  484.7 2.8 collective-permute-done.15
  488.2 0.6 copy-done.3
  489.0 0.4 multiply_reduce_fusion
  489.4 101.4 %psum.47 = f32[16]{0:T(128)S(1)} all-reduce(f32[16]{0:T(128)S(1)} %get-tuple-element.1332), channel_id=1, replica_groups=mesh['lat'=8,'lon'=64] {'lat','lon'}, use_global_device_ids=true, to_apply=%region_29.30 | all-reduce | flops 16 | bytes 128 | tf_op jit(solution)/shard_map/psum | solution.py:125
  590.8 0.7 subtract_bitcast_fusion
  (264 shorter events, 14.7 us)
Async XLA Ops:
  0.6 0.7 copy-start.13
  0.6 12.1 %copy-start.11 = (f32[1,1,16,512]{3,2,1,0:T(8,128)S(1)}, f32[1,1,16,512]{3,2,1,0:T(8,128)}, u32[]{:S(2)}) copy-start(f32[1,1,16,512]{3,2,1,0:T(8,128)} %param.23) | copy-start | bytes 98308
  2.0 22.5 %collective-permute-start.3 = (bf16[1,1,5,512]{3,2,1,0:T(8,128)(2,1)S(1)}, bf16[1,1,5,512]{3,2,1,0:T(8,128)(2,1)S(1)}, u32[]{:S(2)}, u32[]{:S(2)}) collective-permute-start(bf16[1,1,5,512]{3,2,1,0:T(8,128)(2,1)S(1)} %get-tuple-element.1325), channel_id=1, source_target_pairs={{0,1},{1,2},{2,3},{3,4},{4,5},{5,6},{6,7},{7,8},{8,9},{9,10},{10,1... | collective-permute-start | bytes 15368 | tf_op jit(solution)/shard_map/ppermute | solution.py:23
  6.6 17.9 %collective-permute-start.4 = (bf16[1,1,5,512]{3,2,1,0:T(8,128)(2,1)S(1)}, bf16[1,1,5,512]{3,2,1,0:T(8,128)(2,1)S(1)}, u32[]{:S(2)}, u32[]{:S(2)}) collective-permute-start(bf16[1,1,5,512]{3,2,1,0:T(8,128)(2,1)S(1)} %get-tuple-element.1325), channel_id=1, source_target_pairs={{1,0},{2,1},{3,2},{4,3},{5,4},{6,5},{7,6},{8,7},{9,8},{10,9},{11,1... | collective-permute-start | bytes 15368 | tf_op jit(solution)/shard_map/ppermute | solution.py:26
  12.8 19.6 %collective-permute-start = (bf16[1,1,16,512]{3,2,1,0:T(8,128)(2,1)S(1)}, bf16[1,1,16,512]{3,2,1,0:T(8,128)(2,1)S(1)}, u32[]{:S(2)}, u32[]{:S(2)}) collective-permute-start(bf16[1,1,16,512]{3,2,1,0:T(8,128)(2,1)S(1)} %convert_element_type.212), channel_id=1, source_target_pairs={{0,1},{1,2},{2,3},{3,4},{4,5},{5,6},{6,7},{7,8},{8,9},{9,10},{10,1... | collective-permute-start | bytes 49160 | tf_op jit(solution)/shard_map/ppermute | solution.py:23
  14.7 17.6 %collective-permute-start.1 = (bf16[1,1,16,512]{3,2,1,0:T(8,128)(2,1)S(1)}, bf16[1,1,16,512]{3,2,1,0:T(8,128)(2,1)S(1)}, u32[]{:S(2)}, u32[]{:S(2)}) collective-permute-start(bf16[1,1,16,512]{3,2,1,0:T(8,128)(2,1)S(1)} %convert_element_type.212), channel_id=1, source_target_pairs={{1,0},{2,1},{3,2},{4,3},{5,4},{6,5},{7,6},{8,7},{9,8},{10,9},{11,1... | collective-permute-start | bytes 49160 | tf_op jit(solution)/shard_map/ppermute | solution.py:26
  24.6 13.3 %collective-permute-start.5 = (bf16[1,3,5,512]{3,2,1,0:T(8,128)(2,1)S(1)}, bf16[1,3,5,512]{3,2,1,0:T(8,128)(2,1)S(1)}, u32[]{:S(2)}, u32[]{:S(2)}) collective-permute-start(bf16[1,3,5,512]{3,2,1,0:T(8,128)(2,1)S(1)} %pad_maximum_fusion.3), channel_id=1, source_target_pairs={{0,64},{64,128},{128,192},{192,256},{256,320},{320,384},{384,448},... | collective-permute-start | bytes 46088 | tf_op jit(solution)/shard_map/ppermute | solution.py:34
  27.7 12.2 %collective-permute-start.7 = (bf16[1,3,5,512]{3,2,1,0:T(8,128)(2,1)S(1)}, bf16[1,3,5,512]{3,2,1,0:T(8,128)(2,1)S(1)}, u32[]{:S(2)}, u32[]{:S(2)}) collective-permute-start(bf16[1,3,5,512]{3,2,1,0:T(8,128)(2,1)S(1)} %pad_maximum_fusion.3), channel_id=1, source_target_pairs={{64,0},{128,64},{192,128},{256,192},{320,256},{384,320},{448,384},... | collective-permute-start | bytes 46088 | tf_op jit(solution)/shard_map/ppermute | solution.py:34
  32.4 19.5 %collective-permute-start.2 = (bf16[1,3,16,512]{3,2,1,0:T(8,128)(2,1)S(1)}, bf16[1,3,16,512]{3,2,1,0:T(8,128)(2,1)S(1)}, u32[]{:S(2)}, u32[]{:S(2)}) collective-permute-start(bf16[1,3,16,512]{3,2,1,0:T(8,128)(2,1)S(1)} %pad_maximum_fusion), channel_id=1, source_target_pairs={{0,64},{64,128},{128,192},{192,256},{256,320},{320,384},{384,448},... | collective-permute-start | bytes 147464 | tf_op jit(solution)/shard_map/ppermute | solution.py:34
  36.4 16.0 %collective-permute-start.6 = (bf16[1,3,16,512]{3,2,1,0:T(8,128)(2,1)S(1)}, bf16[1,3,16,512]{3,2,1,0:T(8,128)(2,1)S(1)}, u32[]{:S(2)}, u32[]{:S(2)}) collective-permute-start(bf16[1,3,16,512]{3,2,1,0:T(8,128)(2,1)S(1)} %pad_maximum_fusion), channel_id=1, source_target_pairs={{64,0},{128,64},{192,128},{256,192},{320,256},{384,320},{448,384},... | collective-permute-start | bytes 147464 | tf_op jit(solution)/shard_map/ppermute | solution.py:34
  43.1 1.3 copy-start
  49.7 0.8 copy-start.7
  51.9 1.0 copy-start.4
  52.2 1.1 copy-start.8
  53.3 1.0 copy-start.1
  54.6 0.7 copy-start.12
  255.4 4.7 collective-permute-start.8
  257.9 5.4 collective-permute-start.9
  263.2 4.4 collective-permute-start.10
  266.1 4.8 collective-permute-start.11
  267.6 3.3 copy-start.5
  267.9 3.3 copy-start.9
  271.2 1.1 copy-start.2
  470.0 5.8 collective-permute-start.12
  473.6 5.4 collective-permute-start.13
  479.0 5.2 collective-permute-start.14
  482.7 4.8 collective-permute-start.15
  484.2 3.3 copy-start.6
  484.4 3.3 copy-start.10
  487.7 1.1 copy-start.3
where the time goes:
time: 593 us; the launch traced here: 592 us
  blocking collectives  498 us (84%)
  starting transfers between devices  49.4 us (8%)
  other arithmetic  17.2 us (3%)
  waiting for transfers between devices  11.8 us (2%)
  matrix products  6.92 us (1%)
    psum x2, blocking collectives, local(): curve = lax.psum(jnp.sum(direction * image, axis=1), ('lat', 'lon'))  204 us
    psum x2, blocking collectives, local(): norm_next = lax.psum(jnp.sum(residual * residual, axis=1), ('lat', 'lon'))  189 us
    psum x1, blocking collectives, local(): norm_now = lax.psum(jnp.sum(residual * residual, axis=1), ('lat', 'lon'))  105 us
    ppermute x8, starting transfers between devices, passed_along(): lax.ppermute(value, axis, [(source, source + steps) for source in range(i...  18.8 us
    ppermute x4, starting transfers between devices, extended(): lax.ppermute(lax.slice_in_dim(block, 0, width, axis=dim), axis, backward)  18 us
    ppermute x4, starting transfers between devices, extended(): lax.ppermute(lax.slice_in_dim(block, block.shape[dim] - width, None, axis...  12.5 us
    dynamic_update_slice x36, other arithmetic, build_tile(): lax.map(lambda piece: tile_rows(tuple((piece[i] for i in range(6))), far_...  12.3 us
  transfers between devices with their start and end apart: 16, of which 4 were waited for; matrix products, arithmetic and copies ran while one was open for 3% of the time, Pallas kernels for 0%

commit v1 on v0

v1 whole, which is shorter than its diff:
```python
import math

import jax
import jax.numpy as jnp
from jax import lax
from jax.sharding import Mesh, PartitionSpec as P

ITERS = 3


LAT_LIMIT = 80.0 * math.pi / 180.0
HORIZ_SQ = 0.05 * 0.05
VERT_SQ = 0.3 * 0.3
TAPER_STEP = 0.45


def features(obs_info, band_at, sector_at, bands, sectors):
    values = obs_info.astype(jnp.float32)
    latitude = (band_at.astype(jnp.float32) + values[0]) * (2.0 * LAT_LIMIT / bands) - LAT_LIMIT
    longitude = (sector_at.astype(jnp.float32) + values[1]) * (2.0 * math.pi / sectors)
    cos_lat = jnp.cos(latitude)
    return (
        cos_lat * jnp.cos(longitude),
        cos_lat * jnp.sin(longitude),
        jnp.sin(latitude),
        values[2],
        values[3],
        values[4],
    )


def tile_rows(own_feat, far_feat, weight):
    inner = (
        own_feat[0][:, None] * far_feat[0][None, :]
        + own_feat[1][:, None] * far_feat[1][None, :]
        + own_feat[2][:, None] * far_feat[2][None, :]
    )
    vert_gap = own_feat[3][:, None] - far_feat[3][None, :]
    kernel = jnp.exp((inner - 1.0) / HORIZ_SQ - vert_gap * vert_gap / (2.0 * VERT_SQ))
    same_type = own_feat[5][:, None] == far_feat[5][None, :]
    height_pair = (own_feat[5][:, None] == 0.0) | (far_feat[5][None, :] == 0.0)
    coupling = jnp.where(same_type, 1.0, jnp.where(height_pair, 0.45, 0.25)).astype(jnp.float32)
    return (own_feat[4][:, None] * far_feat[4][None, :] * coupling * kernel * weight).astype(
        jnp.bfloat16
    )


def build_tile(own_feat, far_feat, weight):
    count = own_feat[0].shape[0]
    stacked = jnp.stack(own_feat).reshape(6, count // 128, 128).transpose(1, 0, 2)
    pieces = lax.map(
        lambda piece: tile_rows(tuple((piece[i] for i in range(6))), far_feat, weight), stacked
    )
    return pieces.reshape(count, count)


LAT = ("z_lo", "x")
LON = ("z_hi", "y", "core")
GROUPS = (("z_lo", "z_hi", "x"), ("y", "core"))


def extent(axes):
    size = 1
    for axis in axes:
        size *= lax.axis_size(axis)
    return size


def swaps(count, first):
    pairs = []
    for low in range(first, count + first - 1, 2):
        high = (low + 1) % count
        pairs += [(low, high), (high, low)]
    return pairs


def widened(block):
    count = extent(LON)
    outer = lax.ppermute(block, LON, swaps(count, 1))
    inner = lax.ppermute(block, LON, swaps(count, 0))
    odd = lax.axis_index(LON) % 2 == 1
    return jnp.stack([jnp.where(odd, inner, outer), block, jnp.where(odd, outer, inner)])


def all_bands(wide):
    count = extent(LAT)
    below = lax.ppermute(wide, LAT, [(i, i + 1) for i in range(count - 1)])
    above = lax.ppermute(wide, LAT, [(i + 1, i) for i in range(count - 1)])
    return below, above


def contract(field, tile):
    return lax.dot_general(
        field, tile, (((1,), (1,)), ((), ())), preferred_element_type=jnp.float32
    )


def global_sum(value):
    for axes in GROUPS:
        count = extent(axes)
        spread_out = jnp.broadcast_to(value, (count,) + value.shape)
        value = jnp.sum(lax.all_to_all(spread_out, axes, 0, 0), axis=0)
    return value


def coefficients(gram):
    def inner(left, right):
        total = 0.0
        for i in range(4):
            for j in range(4):
                if left[i] is not None and right[j] is not None:
                    total = total + left[i] * right[j] * gram[min(i, j), max(i, j)]
        return total

    def axpy(scale, added, start):
        out = []
        for a, s in zip(added, start):
            if a is None:
                out.append(s)
            else:
                out.append(scale * a if s is None else s + scale * a)
        return out

    one = jnp.ones_like(gram[0, 0])
    answer = [None] * 4
    residual = [one, None, None, None]
    direction = residual
    norm_now = gram[0, 0]
    for iteration in range(ITERS):
        image = [None] + direction[:3]
        step_len = norm_now / inner(direction, image)
        answer = axpy(step_len, direction, answer)
        residual = axpy(-step_len, image, residual)
        if iteration < ITERS - 1:
            norm_next = inner(residual, residual)
            direction = axpy(norm_next / norm_now, direction, residual)
            norm_now = norm_next
    return answer[:3], residual


def local(innovations, obs_error, where_frac, spread, obs_type):
    bands = extent(LAT)
    sectors = extent(LON)
    my_band = lax.axis_index(LAT)
    my_sector = lax.axis_index(LON)
    start = innovations[0, 0]
    error_var = obs_error[0, 0]
    message = jnp.concatenate(
        [
            start.astype(jnp.bfloat16),
            where_frac[0, 0],
            spread[0, 0][None],
            obs_type[0, 0][None].astype(jnp.bfloat16),
            jnp.zeros((3, start.shape[1]), jnp.bfloat16),
        ],
        axis=0,
    )
    wide = widened(message)
    below, above = all_bands(wide)
    blocks = {-1: below, 0: wide, 1: above}
    own_feat = features(message[16:21], my_band, my_sector, bands, sectors)
    offsets = [(a, b) for a in (-1, 0, 1) for b in (-1, 0, 1)]

    def far_tile(step_lat, step_lon):
        near_info = blocks[step_lat][step_lon + 1, 16:21]
        far_feat = features(near_info, my_band + step_lat, my_sector + step_lon, bands, sectors)
        return build_tile(own_feat, far_feat, TAPER_STEP ** (abs(step_lat) + abs(step_lon)))

    tiles = [far_tile(a, b) for a, b in offsets]

    def apply(field, near):
        result = error_var[None, :] * field
        for (a, b), tile in zip(offsets, tiles):
            result = result + contract(near[a][b + 1, :16], tile)
        return result

    basis = [start]
    for power in range(3):
        if power > 0:
            wide = widened(basis[-1].astype(jnp.bfloat16))
            below, above = all_bands(wide)
            blocks = {-1: below, 0: wide, 1: above}
        basis.append(apply(basis[-1], blocks))
    pairs = [(i, j) for i in range(4) for j in range(i, 4) if (i, j) != (3, 3)]
    parts = [jnp.sum(basis[i] * basis[j], axis=1) for i, j in pairs]
    parts += [jnp.zeros_like(parts[0])] * (16 - len(parts))
    sums = global_sum(jnp.concatenate(parts).reshape(2, 128)).reshape(16, 16)
    gram = {pair: sums[i] for i, pair in enumerate(pairs)}
    answer, residual = coefficients(gram)
    answer = sum(c[:, None] * v for c, v in zip(answer, basis))
    residual = sum(c[:, None] * v for c, v in zip(residual, basis))
    return (answer[None, None], residual[None, None])


def solution(mesh):
    fine = Mesh(mesh.devices.reshape(2, 4, 4, 8, 2), LAT + LON)
    in_specs = (
        P(LAT, LON, None, None),
        P(LAT, LON, None),
        P(LAT, LON, None, None),
        P(LAT, LON, None),
        P(LAT, LON, None),
    )
    out_specs = (P(LAT, LON, None, None), P(LAT, LON, None, None))
    return jax.shard_map(local, mesh=fine, in_specs=in_specs, out_specs=out_specs, check_vma=False)
```

time: 593 us -> 128 us (0.22)
  blocking collectives: 498 us -> 35.6 us
    psum x5 -> x0, blocking collectives: 498 us -> none  [the longest x2 204 us: local(): curve = lax.psum(jnp.sum(direction * image, axis=1), ('lat', 'lon'))]
    all_to_all x0 -> x2, blocking collectives: none -> 35.6 us  [global_sum(): value = jnp.sum(lax.all_to_all(spread_out, axes, 0, 0), axis=0)]
    ppermute x16 -> x12, starting transfers between devices: 49.4 us -> 44.1 us  [the longest x3 25.7 us: widened(): inner = lax.ppermute(block, LON, swaps(count, 0))]
    ppermute x16 -> x12, waiting for transfers between devices: 11.8 us -> 14.4 us  [the longest x3 8.58 us: widened(): outer = lax.ppermute(block, LON, swaps(count, 1))]
  transfers between devices with their start and end apart: 16 -> 12, of which waited for: 4 -> 5; matrix products, arithmetic and copies ran while one was open for 3% -> 7% of each run, Pallas kernels for 0% -> 0%
where the time goes in v1:
time: 128 us; the launch traced here: 127 us
  starting transfers between devices  44.1 us (34%)
  blocking collectives  35.6 us (28%)
  other arithmetic  17.2 us (13%)
  waiting for transfers between devices  14.4 us (11%)
  matrix products  6.8 us (5%)
  local copies, waits for them, and re-layouts  5.96 us (5%)
  loops' own time  1.68 us (1%)
    all_to_all x2, blocking collectives, global_sum(): value = jnp.sum(lax.all_to_all(spread_out, axes, 0, 0), axis=0)  35.6 us
    ppermute x3, starting transfers between devices, widened(): inner = lax.ppermute(block, LON, swaps(count, 0))  25.7 us
    dynamic_update_slice x36, other arithmetic, build_tile(): lax.map(lambda piece: tile_rows(tuple((piece[i] for i in range(6))), far_...  12.2 us
    ppermute x3, starting transfers between devices, all_bands(): below = lax.ppermute(wide, LAT, [(i, i + 1) for i in range(count - 1)])  8.68 us
    ppermute x3, waiting for transfers between devices, widened(): outer = lax.ppermute(block, LON, swaps(count, 1))  8.58 us
    dot_general x27, matrix products, contract(): lax.dot_general(field, tile, (((1,), (1,)), ((), ())), preferred_element_...  6.8 us
    ppermute x3, waiting for transfers between devices, all_bands(): above = lax.ppermute(wide, LAT, [(i + 1, i) for i in range(count - 1)])  5.85 us
    ppermute x3, starting transfers between devices, widened(): outer = lax.ppermute(block, LON, swaps(count, 1))  5.76 us
  transfers between devices with their start and end apart: 12, of which 5 were waited for; matrix products, arithmetic and copies ran while one was open for 7% of the time, Pallas kernels for 0%

profile of v1, /device:TPU:1, one launch (start us, length us, event | category | flops | bytes accessed | tf_op | source)
XLA Modules:
  0.0 126.9 jit_solution(7445581444220875829)
XLA Ops:
  0.6 0.7 convert_bitcast_fusion.1
  1.3 0.8 bitcast_convert_fusion
  2.1 0.7 copy-done.6
  2.8 8.8 %collective-permute-start = (bf16[24,512]{1,0:T(8,128)(2,1)S(1)}, bf16[24,512]{1,0:T(8,128)(2,1)S(1)}, u32[]{:S(2)}, u32[]{:S(2)}) collective-permute-start(bf16[24,512]{1,0:T(8,128)(2,1)S(1)} %concatenate.13), channel_id=1, source_target_pairs={{0,1},{1,0},{2,3},{3,2},{4,5},{5,4},{6,7},{7,6},{8,9},{9,8},{10,11... | collective-permute-start | bytes 73736 | tf_op jit(solution)/shard_map/ppermute | solution.py:80
  11.6 1.9 %collective-permute-start.1 = (bf16[24,512]{1,0:T(8,128)(2,1)S(1)}, bf16[24,512]{1,0:T(8,128)(2,1)S(1)}, u32[]{:S(2)}, u32[]{:S(2)}) collective-permute-start(bf16[24,512]{1,0:T(8,128)(2,1)S(1)} %concatenate.13), channel_id=1, source_target_pairs={{1,2},{2,1},{3,4},{4,3},{5,6},{6,5},{7,8},{8,7},{9,10},{10,9},{11,... | collective-permute-start | bytes 73736 | tf_op jit(solution)/shard_map/ppermute | solution.py:79
  13.9 2.8 %collective-permute-done.1 = bf16[24,512]{1,0:T(8,128)(2,1)S(1)} collective-permute-done((bf16[24,512]{1,0:T(8,128)(2,1)S(1)}, bf16[24,512]{1,0:T(8,128)(2,1)S(1)}, u32[]{:S(2)}, u32[]{:S(2)}) %collective-permute-start.1) | collective-permute-done | bytes 24608 | tf_op jit(solution)/shard_map/ppermute | solution.py:79
  16.8 1.3 %collective-permute-start.2 = (bf16[3,24,512]{2,1,0:T(8,128)(2,1)S(1)}, bf16[3,24,512]{2,1,0:T(8,128)(2,1)S(1)}, u32[]{:S(2)}, u32[]{:S(2)}) collective-permute-start(bf16[3,24,512]{2,1,0:T(8,128)(2,1)S(1)} %pad_maximum_fusion), channel_id=1, source_target_pairs={{0,64},{64,128},{128,192},{192,256},{256,320},{320,384},{384,448},... | collective-permute-start | bytes 221192 | tf_op jit(solution)/shard_map/ppermute | solution.py:87
  18.1 1.3 %collective-permute-start.3 = (bf16[3,24,512]{2,1,0:T(8,128)(2,1)S(1)}, bf16[3,24,512]{2,1,0:T(8,128)(2,1)S(1)}, u32[]{:S(2)}, u32[]{:S(2)}) collective-permute-start(bf16[3,24,512]{2,1,0:T(8,128)(2,1)S(1)} %pad_maximum_fusion), channel_id=1, source_target_pairs={{64,0},{128,64},{192,128},{256,192},{320,256},{384,320},{448,384},... | collective-permute-start | bytes 221192 | tf_op jit(solution)/shard_map/ppermute | solution.py:88
  19.7 1.4 %while.111 = (s32[]{:T(128)}, bf16[4,128,512]{2,1,0:T(8,128)(2,1)S(1)}, f32[4,6,128]{2,1,0:T(8,128)S(1)}, f32[1,512]{1,0:T(1,128)S(1)}, f32[1,512]{1,0:T(1,128)S...) while((s32[]{:T(128)}, ...), condition=%wide.region_8.9_spmd, body=%wide.region_7.8_spmd.sunk | while | flops 1311362 | bytes 163053 | solution.py:51
  19.7 0.3 fusion.163
  20.1 0.3 fusion.163
  20.4 0.3 fusion.163
  20.8 0.3 fusion.163
  21.4 1.4 %while.112 = (s32[]{:T(128)}, bf16[4,128,512]{2,1,0:T(8,128)(2,1)S(1)}, f32[4,6,128]{2,1,0:T(8,128)S(1)}, f32[1,512]{1,0:T(1,128)S(1)}, f32[1,512]{1,0:T(1,128)S...) while((s32[]{:T(128)}, ...), condition=%wide.region_10.11_spmd, body=%wide.region_9.10_spmd.sunk | while | flops 1245826 | bytes 163053 | solution.py:51
  22.9 1.4 %while.113 = (s32[]{:T(128)}, bf16[4,128,512]{2,1,0:T(8,128)(2,1)S(1)}, f32[4,6,128]{2,1,0:T(8,128)S(1)}, f32[1,512]{1,0:T(1,128)S(1)}, f32[1,512]{1,0:T(1,128)S...) while((s32[]{:T(128)}, ...), condition=%wide.region_12.13_spmd, body=%wide.region_11.12_spmd.sunk | while | flops 1311362 | bytes 163053 | solution.py:51
  25.0 1.4 %while.108 = (s32[]{:T(128)}, bf16[4,128,512]{2,1,0:T(8,128)(2,1)S(1)}, f32[4,6,128]{2,1,0:T(8,128)S(1)}, f32[1,512]{1,0:T(1,128)S(1)}, f32[1,512]{1,0:T(1,128)S...) while((s32[]{:T(128)}, ...), condition=%wide.region_2.3_spmd, body=%wide.region_1.2_spmd.sunk | while | flops 1311362 | bytes 163053 | solution.py:51
  26.9 1.4 %while.109 = (s32[]{:T(128)}, bf16[4,128,512]{2,1,0:T(8,128)(2,1)S(1)}, f32[4,6,128]{2,1,0:T(8,128)S(1)}, f32[1,512]{1,0:T(1,128)S(1)}, f32[1,512]{1,0:T(1,128)S...) while((s32[]{:T(128)}, ...), condition=%wide.region_4.5_spmd, body=%wide.region_3.4_spmd.sunk | while | flops 1311362 | bytes 163053 | solution.py:51
  27.0 0.3 fusion.161
  27.3 0.3 fusion.161
  27.7 0.3 fusion.161
  28.0 0.3 fusion.161
  28.4 1.4 %while.110 = (s32[]{:T(128)}, bf16[4,128,512]{2,1,0:T(8,128)(2,1)S(1)}, f32[4,6,128]{2,1,0:T(8,128)S(1)}, f32[1,512]{1,0:T(1,128)S(1)}, f32[1,512]{1,0:T(1,128)S...) while((s32[]{:T(128)}, ...), condition=%wide.region_6.7_spmd, body=%wide.region_5.6_spmd.sunk | while | flops 1311362 | bytes 163053 | solution.py:51
  28.4 0.3 fusion.162
  28.8 0.3 fusion.162
  29.1 0.3 fusion.162
  29.5 0.3 fusion.162
  30.2 0.9 broadcast.3824.clone.8
  31.0 3.8 %while.114 = (s32[]{:T(128)}, bf16[4,128,512]{2,1,0:T(8,128)(2,1)}, f32[4,6,128]{2,1,0:T(8,128)S(1)}, f32[1,512]{1,0:T(1,128)S(1)}, f32[1,512]{1,0:T(1,128)S(1)}...) while((s32[]{:T(128)}, bf16[4,128,512]{2,1,0:T(8,128)(2,1)}, ...), condition=%wide.region_14.15_spmd, body=%wide.region_13.14_spmd.sunk | while | flops 1311362 | bytes 163177 | solution.py:51
  31.1 0.9 fusion.166
  32.0 0.9 fusion.166
  32.9 0.9 fusion.166
  33.9 0.9 fusion.166
  34.9 1.4 %while.115 = (s32[]{:T(128)}, bf16[4,128,512]{2,1,0:T(8,128)(2,1)S(1)}, f32[4,6,128]{2,1,0:T(8,128)S(1)}, f32[1,512]{1,0:T(1,128)S(1)}, f32[1,512]{1,0:T(1,128)S...) while((s32[]{:T(128)}, ...), condition=%wide.region_16.17_spmd, body=%wide.region_15.16_spmd.sunk | while | flops 1311362 | bytes 163053 | solution.py:51
  34.9 0.3 fusion.167
  35.3 0.3 fusion.167
  35.6 0.3 fusion.167
  36.0 0.3 fusion.167
  36.3 0.8 copy-done.3
  37.1 1.4 %while.116 = (s32[]{:T(128)}, bf16[4,128,512]{2,1,0:T(8,128)(2,1)S(1)}, f32[4,6,128]{2,1,0:T(8,128)S(1)}, f32[1,512]{1,0:T(1,128)S(1)}, f32[1,512]{1,0:T(1,128)S...) while((s32[]{:T(128)}, ...), condition=%wide.region_18.19_spmd, body=%wide.region_17.18_spmd.sunk | while | flops 1311362 | bytes 163053 | solution.py:51
  37.2 0.3 fusion.168
  37.5 0.3 fusion.168
  37.9 0.3 fusion.168
  38.2 0.3 fusion.168
  38.7 0.8 copy-done.1
  39.8 0.5 copy-done.5
  41.2 0.6 copy-done.4
  42.3 0.6 copy-done.2
  43.1 9.2 %collective-permute-start.4 = (bf16[16,512]{1,0:T(8,128)(2,1)S(1)}, bf16[16,512]{1,0:T(8,128)(2,1)S(1)}, u32[]{:S(2)}, u32[]{:S(2)}) collective-permute-start(bf16[16,512]{1,0:T(8,128)(2,1)S(1)} %get-tuple-element.1350), channel_id=1, source_target_pairs={{0,1},{1,0},{2,3},{3,2},{4,5},{5,4},{6,7},{7,6},{8,9},{9,8},{10,11... | collective-permute-start | bytes 49160 | tf_op jit(solution)/shard_map/ppermute | solution.py:80
  52.3 1.9 %collective-permute-start.5 = (bf16[16,512]{1,0:T(8,128)(2,1)S(1)}, bf16[16,512]{1,0:T(8,128)(2,1)S(1)}, u32[]{:S(2)}, u32[]{:S(2)}) collective-permute-start(bf16[16,512]{1,0:T(8,128)(2,1)S(1)} %get-tuple-element.1350), channel_id=1, source_target_pairs={{1,2},{2,1},{3,4},{4,3},{5,6},{6,5},{7,8},{8,7},{9,10},{10,9},{11,... | collective-permute-start | bytes 49160 | tf_op jit(solution)/shard_map/ppermute | solution.py:79
  54.4 2.9 %collective-permute-done.5 = bf16[16,512]{1,0:T(8,128)(2,1)S(1)} collective-permute-done((bf16[16,512]{1,0:T(8,128)(2,1)S(1)}, bf16[16,512]{1,0:T(8,128)(2,1)S(1)}, u32[]{:S(2)}, u32[]{:S(2)}) %collective-permute-start.5) | collective-permute-done | bytes 16416 | tf_op jit(solution)/shard_map/ppermute | solution.py:79
  57.4 4.3 %collective-permute-start.6 = (bf16[3,16,512]{2,1,0:T(8,128)(2,1)S(1)}, bf16[3,16,512]{2,1,0:T(8,128)(2,1)S(1)}, u32[]{:S(2)}, u32[]{:S(2)}) collective-permute-start(bf16[3,16,512]{2,1,0:T(8,128)(2,1)S(1)} %pad_maximum_fusion.1), channel_id=1, source_target_pairs={{0,64},{64,128},{128,192},{192,256},{256,320},{320,384},{384,448},... | collective-permute-start | bytes 147464 | tf_op jit(solution)/shard_map/ppermute | solution.py:87
  61.6 1.3 %collective-permute-start.7 = (bf16[3,16,512]{2,1,0:T(8,128)(2,1)S(1)}, bf16[3,16,512]{2,1,0:T(8,128)(2,1)S(1)}, u32[]{:S(2)}, u32[]{:S(2)}) collective-permute-start(bf16[3,16,512]{2,1,0:T(8,128)(2,1)S(1)} %pad_maximum_fusion.1), channel_id=1, source_target_pairs={{64,0},{128,64},{192,128},{256,192},{320,256},{384,320},{448,384},... | collective-permute-start | bytes 147464 | tf_op jit(solution)/shard_map/ppermute | solution.py:88
  63.9 2.5 %collective-permute-done.7 = bf16[3,16,512]{2,1,0:T(8,128)(2,1)S(1)} collective-permute-done((bf16[3,16,512]{2,1,0:T(8,128)(2,1)S(1)}, bf16[3,16,512]{2,1,0:T(8,128)(2,1)S(1)}, u32[]{:S(2)}, u32[]{:S(2)}) %collective-permute-start.7) | collective-permute-done | bytes 49184 | tf_op jit(solution)/shard_map/ppermute | solution.py:88
  67.2 0.3 fusion.119
  67.5 7.7 %collective-permute-start.8 = (bf16[16,512]{1,0:T(8,128)(2,1)S(1)}, bf16[16,512]{1,0:T(8,128)(2,1)S(1)}, u32[]{:S(2)}, u32[]{:S(2)}) collective-permute-start(bf16[16,512]{1,0:T(8,128)(2,1)S(1)} %get-tuple-element.1352), channel_id=1, source_target_pairs={{0,1},{1,0},{2,3},{3,2},{4,5},{5,4},{6,7},{7,6},{8,9},{9,8},{10,11... | collective-permute-start | bytes 49160 | tf_op jit(solution)/shard_map/ppermute | solution.py:80
  75.2 1.9 %collective-permute-start.9 = (bf16[16,512]{1,0:T(8,128)(2,1)S(1)}, bf16[16,512]{1,0:T(8,128)(2,1)S(1)}, u32[]{:S(2)}, u32[]{:S(2)}) collective-permute-start(bf16[16,512]{1,0:T(8,128)(2,1)S(1)} %get-tuple-element.1352), channel_id=1, source_target_pairs={{1,2},{2,1},{3,4},{4,3},{5,6},{6,5},{7,8},{8,7},{9,10},{10,9},{11,... | collective-permute-start | bytes 49160 | tf_op jit(solution)/shard_map/ppermute | solution.py:79
  77.4 2.9 %collective-permute-done.9 = bf16[16,512]{1,0:T(8,128)(2,1)S(1)} collective-permute-done((bf16[16,512]{1,0:T(8,128)(2,1)S(1)}, bf16[16,512]{1,0:T(8,128)(2,1)S(1)}, u32[]{:S(2)}, u32[]{:S(2)}) %collective-permute-start.9) | collective-permute-done | bytes 16416 | tf_op jit(solution)/shard_map/ppermute | solution.py:79
  80.3 3.1 %collective-permute-start.10 = (bf16[3,16,512]{2,1,0:T(8,128)(2,1)S(1)}, bf16[3,16,512]{2,1,0:T(8,128)(2,1)S(1)}, u32[]{:S(2)}, u32[]{:S(2)}) collective-permute-start(bf16[3,16,512]{2,1,0:T(8,128)(2,1)S(1)} %pad_maximum_fusion.2), channel_id=1, source_target_pairs={{0,64},{64,128},{128,192},{192,256},{256,320},{320,384},{384,448},... | collective-permute-start | bytes 147464 | tf_op jit(solution)/shard_map/ppermute | solution.py:87
  83.4 1.3 %collective-permute-start.11 = (bf16[3,16,512]{2,1,0:T(8,128)(2,1)S(1)}, bf16[3,16,512]{2,1,0:T(8,128)(2,1)S(1)}, u32[]{:S(2)}, u32[]{:S(2)}) collective-permute-start(bf16[3,16,512]{2,1,0:T(8,128)(2,1)S(1)} %pad_maximum_fusion.2), channel_id=1, source_target_pairs={{64,0},{128,64},{192,128},{256,192},{320,256},{384,320},{448,384},... | collective-permute-start | bytes 147464 | tf_op jit(solution)/shard_map/ppermute | solution.py:88
  85.7 3.3 %collective-permute-done.11 = bf16[3,16,512]{2,1,0:T(8,128)(2,1)S(1)} collective-permute-done((bf16[3,16,512]{2,1,0:T(8,128)(2,1)S(1)}, bf16[3,16,512]{2,1,0:T(8,128)(2,1)S(1)}, u32[]{:S(2)}, u32[]{:S(2)}) %collective-permute-start.11) | collective-permute-done | bytes 49184 | tf_op jit(solution)/shard_map/ppermute | solution.py:88
  89.8 0.5 multiply_reduce_fusion
  90.3 19.0 %all_to_all.10 = f32[32,2,128]{2,1,0:T(2,128)S(1)} all-to-all(f32[32,2,128]{2,1,0:T(2,128)S(1)} %broadcast_in_dim.143), channel_id=1, replica_groups=mesh['z_lo'=2,'x'=4,'z_hi'=4,'y'=8,'core'=2] {'z_lo','z_hi','x'}, dimensions={0} | all-to-all | bytes 65536 | tf_op jit(solution)/shard_map/all_to_all | solution.py:102
  109.4 16.6 %all_to_all.11 = f32[16,2,128]{2,1,0:T(2,128)S(1)} all-to-all(f32[16,2,128]{2,1,0:T(2,128)S(1)} %broadcast_in_dim.144), channel_id=1, replica_groups=mesh['z_lo'=2,'x'=4,'z_hi'=4,'y'=8,'core'=2] {'y','core'}, dimensions={0} | all-to-all | bytes 32768 | tf_op jit(solution)/shard_map/all_to_all | solution.py:102
  126.2 0.7 fusion.29
  (250 shorter events, 13.3 us)
Async XLA Ops:
  2.1 0.7 copy-start.6
  2.1 0.7 copy-start.7
  2.8 11.1 %collective-permute-start = (bf16[24,512]{1,0:T(8,128)(2,1)S(1)}, bf16[24,512]{1,0:T(8,128)(2,1)S(1)}, u32[]{:S(2)}, u32[]{:S(2)}) collective-permute-start(bf16[24,512]{1,0:T(8,128)(2,1)S(1)} %concatenate.13), channel_id=1, source_target_pairs={{0,1},{1,0},{2,3},{3,2},{4,5},{5,4},{6,7},{7,6},{8,9},{9,8},{10,11... | collective-permute-start | bytes 73736 | tf_op jit(solution)/shard_map/ppermute | solution.py:80
  11.6 5.1 %collective-permute-start.1 = (bf16[24,512]{1,0:T(8,128)(2,1)S(1)}, bf16[24,512]{1,0:T(8,128)(2,1)S(1)}, u32[]{:S(2)}, u32[]{:S(2)}) collective-permute-start(bf16[24,512]{1,0:T(8,128)(2,1)S(1)} %concatenate.13), channel_id=1, source_target_pairs={{1,2},{2,1},{3,4},{4,3},{5,6},{6,5},{7,8},{8,7},{9,10},{10,9},{11,... | collective-permute-start | bytes 73736 | tf_op jit(solution)/shard_map/ppermute | solution.py:79
  16.8 7.8 %collective-permute-start.2 = (bf16[3,24,512]{2,1,0:T(8,128)(2,1)S(1)}, bf16[3,24,512]{2,1,0:T(8,128)(2,1)S(1)}, u32[]{:S(2)}, u32[]{:S(2)}) collective-permute-start(bf16[3,24,512]{2,1,0:T(8,128)(2,1)S(1)} %pad_maximum_fusion), channel_id=1, source_target_pairs={{0,64},{64,128},{128,192},{192,256},{256,320},{320,384},{384,448},... | collective-permute-start | bytes 221192 | tf_op jit(solution)/shard_map/ppermute | solution.py:87
  18.1 8.4 %collective-permute-start.3 = (bf16[3,24,512]{2,1,0:T(8,128)(2,1)S(1)}, bf16[3,24,512]{2,1,0:T(8,128)(2,1)S(1)}, u32[]{:S(2)}, u32[]{:S(2)}) collective-permute-start(bf16[3,24,512]{2,1,0:T(8,128)(2,1)S(1)} %pad_maximum_fusion), channel_id=1, source_target_pairs={{64,0},{128,64},{192,128},{256,192},{320,256},{384,320},{448,384},... | collective-permute-start | bytes 221192 | tf_op jit(solution)/shard_map/ppermute | solution.py:88
  29.8 1.3 %copy-start = (bf16[4,128,512]{2,1,0:T(8,128)(2,1)}, bf16[4,128,512]{2,1,0:T(8,128)(2,1)S(1)}, u32[]{:S(2)}) copy-start(bf16[4,128,512]{2,1,0:T(8,128)(2,1)S(1)} %get-tuple-element.1021) | copy-start | bytes 1572868
  36.3 0.8 copy-start.3
  38.5 1.0 copy-start.1
  39.5 0.8 copy-start.5
  39.8 0.7 copy-start.8
  40.7 1.1 copy-start.4
  41.8 1.0 copy-start.2
  43.1 11.4 %collective-permute-start.4 = (bf16[16,512]{1,0:T(8,128)(2,1)S(1)}, bf16[16,512]{1,0:T(8,128)(2,1)S(1)}, u32[]{:S(2)}, u32[]{:S(2)}) collective-permute-start(bf16[16,512]{1,0:T(8,128)(2,1)S(1)} %get-tuple-element.1350), channel_id=1, source_target_pairs={{0,1},{1,0},{2,3},{3,2},{4,5},{5,4},{6,7},{7,6},{8,9},{9,8},{10,11... | collective-permute-start | bytes 49160 | tf_op jit(solution)/shard_map/ppermute | solution.py:80
  52.3 5.1 %collective-permute-start.5 = (bf16[16,512]{1,0:T(8,128)(2,1)S(1)}, bf16[16,512]{1,0:T(8,128)(2,1)S(1)}, u32[]{:S(2)}, u32[]{:S(2)}) collective-permute-start(bf16[16,512]{1,0:T(8,128)(2,1)S(1)} %get-tuple-element.1350), channel_id=1, source_target_pairs={{1,2},{2,1},{3,4},{4,3},{5,6},{6,5},{7,8},{8,7},{9,10},{10,9},{11,... | collective-permute-start | bytes 49160 | tf_op jit(solution)/shard_map/ppermute | solution.py:79
  57.4 5.8 %collective-permute-start.6 = (bf16[3,16,512]{2,1,0:T(8,128)(2,1)S(1)}, bf16[3,16,512]{2,1,0:T(8,128)(2,1)S(1)}, u32[]{:S(2)}, u32[]{:S(2)}) collective-permute-start(bf16[3,16,512]{2,1,0:T(8,128)(2,1)S(1)} %pad_maximum_fusion.1), channel_id=1, source_target_pairs={{0,64},{64,128},{128,192},{192,256},{256,320},{320,384},{384,448},... | collective-permute-start | bytes 147464 | tf_op jit(solution)/shard_map/ppermute | solution.py:87
  61.6 4.8 %collective-permute-start.7 = (bf16[3,16,512]{2,1,0:T(8,128)(2,1)S(1)}, bf16[3,16,512]{2,1,0:T(8,128)(2,1)S(1)}, u32[]{:S(2)}, u32[]{:S(2)}) collective-permute-start(bf16[3,16,512]{2,1,0:T(8,128)(2,1)S(1)} %pad_maximum_fusion.1), channel_id=1, source_target_pairs={{64,0},{128,64},{192,128},{256,192},{320,256},{384,320},{448,384},... | collective-permute-start | bytes 147464 | tf_op jit(solution)/shard_map/ppermute | solution.py:88
  67.5 9.9 %collective-permute-start.8 = (bf16[16,512]{1,0:T(8,128)(2,1)S(1)}, bf16[16,512]{1,0:T(8,128)(2,1)S(1)}, u32[]{:S(2)}, u32[]{:S(2)}) collective-permute-start(bf16[16,512]{1,0:T(8,128)(2,1)S(1)} %get-tuple-element.1352), channel_id=1, source_target_pairs={{0,1},{1,0},{2,3},{3,2},{4,5},{5,4},{6,7},{7,6},{8,9},{9,8},{10,11... | collective-permute-start | bytes 49160 | tf_op jit(solution)/shard_map/ppermute | solution.py:80
  75.2 5.1 %collective-permute-start.9 = (bf16[16,512]{1,0:T(8,128)(2,1)S(1)}, bf16[16,512]{1,0:T(8,128)(2,1)S(1)}, u32[]{:S(2)}, u32[]{:S(2)}) collective-permute-start(bf16[16,512]{1,0:T(8,128)(2,1)S(1)} %get-tuple-element.1352), channel_id=1, source_target_pairs={{1,2},{2,1},{3,4},{4,3},{5,6},{6,5},{7,8},{8,7},{9,10},{10,9},{11,... | collective-permute-start | bytes 49160 | tf_op jit(solution)/shard_map/ppermute | solution.py:79
  80.3 4.7 %collective-permute-start.10 = (bf16[3,16,512]{2,1,0:T(8,128)(2,1)S(1)}, bf16[3,16,512]{2,1,0:T(8,128)(2,1)S(1)}, u32[]{:S(2)}, u32[]{:S(2)}) collective-permute-start(bf16[3,16,512]{2,1,0:T(8,128)(2,1)S(1)} %pad_maximum_fusion.2), channel_id=1, source_target_pairs={{0,64},{64,128},{128,192},{192,256},{256,320},{320,384},{384,448},... | collective-permute-start | bytes 147464 | tf_op jit(solution)/shard_map/ppermute | solution.py:87
  83.4 5.6 %collective-permute-start.11 = (bf16[3,16,512]{2,1,0:T(8,128)(2,1)S(1)}, bf16[3,16,512]{2,1,0:T(8,128)(2,1)S(1)}, u32[]{:S(2)}, u32[]{:S(2)}) collective-permute-start(bf16[3,16,512]{2,1,0:T(8,128)(2,1)S(1)} %pad_maximum_fusion.2), channel_id=1, source_target_pairs={{64,0},{128,64},{192,128},{256,192},{320,256},{384,320},{448,384},... | collective-permute-start | bytes 147464 | tf_op jit(solution)/shard_map/ppermute | solution.py:88

commit v2 on v1

v2 whole, which is shorter than its diff:
```python
import functools
import math

import jax
import jax.numpy as jnp
from jax import lax
from jax.experimental import pallas as pl
from jax.experimental.pallas import tpu as pltpu
from jax.sharding import Mesh, PartitionSpec as P

ITERS = 3
BANDS = 8
SECTORS = 64
OBS = 512
RHS = 16

LAT_LIMIT = 80.0 * math.pi / 180.0
HORIZ_SQ = 0.05 * 0.05
VERT_SQ = 0.3 * 0.3
TAPER_STEP = 0.45
LOG2E = 1.0 / math.log(2.0)
HORIZ = LOG2E / HORIZ_SQ
VERT = LOG2E / (2.0 * VERT_SQ)
COUPLING = ((1.0, 0.45, 0.45), (0.45, 1.0, 0.25), (0.45, 0.25, 1.0))

LAT = ("z_lo", "x")
LON = ("z_hi", "y", "core")
GROUPS = (("z_lo", "z_hi", "x"), ("y", "core"))


def extent(axes):
    size = 1
    for axis in axes:
        size *= lax.axis_size(axis)
    return size


def swaps(count, first):
    pairs = []
    for low in range(first, count + first - 1, 2):
        high = (low + 1) % count
        pairs += [(low, high), (high, low)]
    return pairs


def widened(block):
    count = extent(LON)
    inner = lax.ppermute(block, LON, swaps(count, 0))
    outer = lax.ppermute(block, LON, swaps(count, 1))
    odd = lax.axis_index(LON) % 2 == 1
    return jnp.stack([jnp.where(odd, inner, outer), block, jnp.where(odd, outer, inner)])


def all_bands(wide):
    count = extent(LAT)
    below = lax.ppermute(wide, LAT, [(i, i + 1) for i in range(count - 1)])
    above = lax.ppermute(wide, LAT, [(i + 1, i) for i in range(count - 1)])
    return below, above


def rounded(value):
    return value.astype(jnp.bfloat16).astype(jnp.float32)


def pieces(value):
    high = rounded(value)
    mid = rounded(value - high)
    return high, mid, rounded(value - high - mid)


def describe_kernel(place_ref, start_ref, frac_ref, spread_ref, type_ref, message_ref, own_ref, far_rows, own_rows):
    frac = frac_ref[...].astype(jnp.float32)
    latitude = (place_ref[0].astype(jnp.float32) + frac[0:1]) * (2.0 * LAT_LIMIT / BANDS) - LAT_LIMIT
    longitude = (place_ref[1].astype(jnp.float32) + frac[1:2]) * (2.0 * math.pi / SECTORS)
    angles = jnp.concatenate([latitude, longitude], axis=0)
    cosines, sines = jnp.cos(angles), jnp.sin(angles)
    place = (cosines[0:1] * cosines[1:2], cosines[0:1] * sines[1:2], sines[0:1])
    level = frac[2:3]
    sigma = jnp.log(spread_ref[...].astype(jnp.float32)) * LOG2E - VERT * level * level
    kind = type_ref[...]
    one = jnp.ones_like(level)
    table = [[math.log2(k) for k in row] for row in COUPLING]

    def looked_up(column):
        return jnp.where(kind == 0, table[0][column], jnp.where(kind == 1, table[1][column], table[2][column]))

    at_height = looked_up(0)
    far = []
    own = []
    for axis in place:
        far += pieces(axis)
        own += [HORIZ * axis] * 3
    far += [level, jnp.where(kind == 1, one, 0.0), jnp.where(kind == 2, one, 0.0)]
    own += [2.0 * VERT * level, looked_up(1) - at_height, looked_up(2) - at_height]
    far += [*pieces(sigma), one]
    own += [one, one, one, sigma + at_height - HORIZ]
    for row in range(16):
        far_rows[row : row + 1, :] = far[row]
        own_rows[row : row + 1, :] = own[row]
    message_ref[0:16, :] = start_ref[...].astype(jnp.bfloat16)
    message_ref[16:32, :] = far_rows[...].astype(jnp.bfloat16)
    left = own_rows[...]
    for piece in range(3):
        part = left.astype(jnp.bfloat16)
        own_ref[16 * piece : 16 * piece + 16, :] = part
        left = left - part.astype(jnp.float32)


def whole(space=pltpu.VMEM):
    return pl.BlockSpec(memory_space=space)


def describe(place, start, where_frac, spread, obs_type):
    return pl.pallas_call(
        describe_kernel,
        out_shape=(
            jax.ShapeDtypeStruct((32, OBS), jnp.bfloat16),
            jax.ShapeDtypeStruct((48, OBS), jnp.bfloat16),
        ),
        in_specs=[whole(pltpu.SMEM)] + [whole()] * 4,
        out_specs=(whole(), whole()),
        scratch_shapes=[pltpu.VMEM((16, OBS), jnp.float32)] * 2,
        name="describe",
    )(place, start, where_frac, spread, obs_type)


CHUNK = 256


def build_kernel(steps, carried, *refs):
    messages, (own_ref, added_ref), (tile_ref, sum_ref, *sent) = refs[: len(carried)], refs[len(carried) : len(carried) + 2], refs[len(carried) + 2 :]
    own = own_ref[...]
    total = added_ref[...]
    for k, (which, slot, step) in enumerate(steps):
        taper = step * math.log2(TAPER_STEP)
        for low in range(0, OBS, CHUNK):
            far = messages[which][slot, 16:32, low : low + CHUNK]
            far = jnp.concatenate([far, far, far], axis=0)
            power = lax.dot_general(far, own, (((0,), (0,)), ((), ())), preferred_element_type=jnp.float32)
            tile = jnp.exp2(power + taper if step else power).astype(jnp.bfloat16)
            tile_ref[k, low : low + CHUNK, :] = tile
            field = messages[which][slot, 0:16, low : low + CHUNK]
            total = total + jnp.dot(field, tile, preferred_element_type=jnp.float32)
    sum_ref[...] = total
    for ref in sent:
        ref[...] = total.astype(jnp.bfloat16)


def apply_kernel(steps, carried, *refs):
    messages, (tile_ref, added_ref), (sum_ref, *sent) = refs[: len(carried)], refs[len(carried) : len(carried) + 2], refs[len(carried) + 2 :]
    total = added_ref[...]
    for k, (which, slot, _) in enumerate(steps):
        total = total + jnp.dot(messages[which][slot], tile_ref[k], preferred_element_type=jnp.float32)
    sum_ref[...] = total
    for ref in sent:
        ref[...] = total.astype(jnp.bfloat16)


SAME_BAND = ((0, 0, 1), (0, 1, 0), (0, 2, 1))
OTHER_BANDS = ((0, 0, 2), (0, 1, 1), (0, 2, 2), (1, 0, 2), (1, 1, 1), (1, 2, 2))


def cost(steps, built):
    entries = len(steps) * OBS * OBS
    return pl.CostEstimate(
        flops=2 * entries * (RHS + 256 * built),
        bytes_accessed=2 * entries,
        transcendentals=entries * built,
    )


def sums(last):
    shapes = [jax.ShapeDtypeStruct((RHS, OBS), jnp.float32)]
    if last:
        shapes.append(jax.ShapeDtypeStruct((RHS, OBS), jnp.bfloat16))
    return shapes


def build(steps, carried, own, added, last):
    tiles = pltpu.VMEM((len(steps), OBS, OBS), jnp.bfloat16)
    shapes = [tiles] + sums(last)
    return pl.pallas_call(
        functools.partial(build_kernel, steps, carried),
        out_shape=shapes,
        in_specs=[whole()] * (len(carried) + 2),
        out_specs=[whole()] * len(shapes),
        compiler_params=pltpu.CompilerParams(vmem_limit_bytes=24 << 20),
        cost_estimate=cost(steps, 1),
        name="build",
    )(*carried, own, added)


def apply(steps, carried, tiles, added, last):
    shapes = sums(last)
    return pl.pallas_call(
        functools.partial(apply_kernel, steps, carried),
        out_shape=shapes,
        in_specs=[whole()] * (len(carried) + 2),
        out_specs=[whole()] * len(shapes),
        compiler_params=pltpu.CompilerParams(vmem_limit_bytes=24 << 20),
        cost_estimate=cost(steps, 0),
        name="apply",
    )(*carried, tiles, added)


def local(innovations, obs_error, where_frac, spread, obs_type):
    start = innovations[0, 0]
    error_var = obs_error[0, 0][None]
    place = jnp.stack([lax.axis_index(LAT), lax.axis_index(LON)]).astype(jnp.int32)
    message, own = describe(place, start, where_frac[0, 0], spread[0], obs_type[0])
    wide = widened(message)
    below, above = all_bands(wide)
    near_tiles, part = build(SAME_BAND, [wide], own, error_var * start, False)
    far_tiles, field, sent = build(OTHER_BANDS, [below, above], own, part, True)
    basis = [start, field]
    for last in (False, True):
        wide = widened(sent)
        below, above = all_bands(wide)
        part, = apply(SAME_BAND, [wide], near_tiles, error_var * field, False)
        if last:
            field, = apply(OTHER_BANDS, [below, above], far_tiles, part, False)
        else:
            field, sent = apply(OTHER_BANDS, [below, above], far_tiles, part, True)
        basis.append(field)
    pairs = [(i, j) for i in range(4) for j in range(i, 4) if (i, j) != (3, 3)]
    parts = [jnp.sum(basis[i] * basis[j], axis=1) for i, j in pairs]
    parts += [jnp.zeros_like(parts[0])] * (16 - len(parts))
    totals = global_sum(jnp.concatenate(parts).reshape(2, 128)).reshape(16, 16)
    gram = {pair: totals[i] for i, pair in enumerate(pairs)}
    answer, residual = coefficients(gram)
    answer = sum(c[:, None] * v for c, v in zip(answer, basis))
    residual = sum(c[:, None] * v for c, v in zip(residual, basis))
    return (answer[None, None], residual[None, None])


def global_sum(value):
    for axes in GROUPS:
        count = extent(axes)
        spread_out = jnp.broadcast_to(value, (count,) + value.shape)
        value = jnp.sum(lax.all_to_all(spread_out, axes, 0, 0), axis=0)
    return value


def coefficients(gram):
    def inner(left, right):
        total = 0.0
        for i in range(4):
            for j in range(4):
                if left[i] is not None and right[j] is not None:
                    total = total + left[i] * right[j] * gram[min(i, j), max(i, j)]
        return total

    def axpy(scale, added, start):
        out = []
        for a, s in zip(added, start):
            if a is None:
                out.append(s)
            else:
                out.append(scale * a if s is None else s + scale * a)
        return out

    one = jnp.ones_like(gram[0, 0])
    answer = [None] * 4
    residual = [one, None, None, None]
    direction = residual
    norm_now = gram[0, 0]
    for iteration in range(ITERS):
        image = [None] + direction[:3]
        step_len = norm_now / inner(direction, image)
        answer = axpy(step_len, direction, answer)
        residual = axpy(-step_len, image, residual)
        if iteration < ITERS - 1:
            norm_next = inner(residual, residual)
            direction = axpy(norm_next / norm_now, direction, residual)
            norm_now = norm_next
    return answer[:3], residual


def solution(mesh):
    fine = Mesh(mesh.devices.reshape(2, 4, 4, 8, 2), LAT + LON)
    in_specs = (
        P(LAT, LON, None, None),
        P(LAT, LON, None),
        P(LAT, LON, None, None),
        P(LAT, LON, None),
        P(LAT, LON, None),
    )
    out_specs = (P(LAT, LON, None, None), P(LAT, LON, None, None))
    return jax.shard_map(local, mesh=fine, in_specs=in_specs, out_specs=out_specs, check_vma=False)
```

time: 128 us -> 110 us (0.86)
  other arithmetic: 17.2 us -> 3.4 us
  Pallas kernels: 0 us -> 7.21 us
  matrix products: 6.8 us -> 0 us
  local copies, waits for them, and re-layouts: 5.96 us -> 1 us
  waiting for transfers between devices: 14.4 us -> 17.5 us
  loops' own time: 1.68 us -> 0 us
  blocking collectives: 35.6 us -> 34 us
    dynamic_update_slice x36 -> x0, other arithmetic: 12.2 us -> none  [build_tile(): lax.map(lambda piece: tile_rows(tuple((piece[i] for i in range(6))), far_...]
    pallas_call x0 -> x7, Pallas kernels: none -> 7.21 us  [the longest x2 4.03 us: build(): pl.pallas_call(functools.partial(build_kernel, steps, carried), out_shape...]
    dot_general x27 -> x0, matrix products: 6.8 us -> none  [contract(): lax.dot_general(field, tile, (((1,), (1,)), ((), ())), preferred_element_...]
    unnamed x18 -> x6, local copies, waits for them, and re-layouts: 4.09 us -> 0.81 us
    ppermute x3, waiting for transfers between devices: 5.85 us -> 7.77 us  [all_bands(): above = lax.ppermute(wide, LAT, [(i + 1, i) for i in range(count - 1)])]
    another operation x9 -> x0, loops' own time: 1.68 us -> none  [build_tile(): lax.map(lambda piece: tile_rows(tuple((piece[i] for i in range(6))), far_...]
    all_to_all x2, blocking collectives: 35.6 us -> 34 us  [global_sum(): value = jnp.sum(lax.all_to_all(spread_out, axes, 0, 0), axis=0)]
    convert_element_type x7 -> x0, other arithmetic: 1.49 us -> none  [the longest x1 0.76 us: local(): start.astype(jnp.bfloat16)]
  transfers between devices with their start and end apart: 12 -> 12, of which waited for: 5 -> 6; matrix products, arithmetic and copies ran while one was open for 7% -> 1% of each run, Pallas kernels for 0% -> 2%
where the time goes in v2:
time: 110 us; the launch traced here: 109 us
  starting transfers between devices  45.3 us (41%)
  blocking collectives  34 us (31%)
  waiting for transfers between devices  17.5 us (16%)
  Pallas kernels  7.21 us (7%)
  other arithmetic  3.4 us (3%)
    all_to_all x2, blocking collectives, global_sum(): value = jnp.sum(lax.all_to_all(spread_out, axes, 0, 0), axis=0)  34 us
    ppermute x3, starting transfers between devices, widened(): inner = lax.ppermute(block, LON, swaps(count, 0))  27.1 us
    ppermute x3, waiting for transfers between devices, widened(): outer = lax.ppermute(block, LON, swaps(count, 1))  9.73 us
    ppermute x3, starting transfers between devices, all_bands(): below = lax.ppermute(wide, LAT, [(i, i + 1) for i in range(count - 1)])  8.54 us
    ppermute x3, waiting for transfers between devices, all_bands(): above = lax.ppermute(wide, LAT, [(i + 1, i) for i in range(count - 1)])  7.77 us
    ppermute x3, starting transfers between devices, widened(): outer = lax.ppermute(block, LON, swaps(count, 1))  5.76 us
    pallas_call x2, Pallas kernels, build(): pl.pallas_call(functools.partial(build_kernel, steps, carried), out_shape...  4.03 us
    ppermute x3, starting transfers between devices, all_bands(): above = lax.ppermute(wide, LAT, [(i + 1, i) for i in range(count - 1)])  3.88 us
  transfers between devices with their start and end apart: 12, of which 6 were waited for; matrix products, arithmetic and copies ran while one was open for 1% of the time, Pallas kernels for 2%

profile of v2, /device:TPU:1, one launch (start us, length us, event | category | flops | bytes accessed | tf_op | source)
XLA Modules:
  0.0 109.3 jit_solution(8595364853178728609)
XLA Ops:
  0.6 0.0 copy-start.2
  0.7 0.6 pad_add_fusion.place_ref
  1.3 1.6 %describe.1 = (bf16[32,512]{1,0:T(8,128)(2,1)}, bf16[48,512]{1,0:T(8,128)(2,1)}) custom-call(s32[2]{0:T(128)} %pad_add_fusion.place_ref, f32[16,512]{1,0:T(8,128)} %bitcast.136, bf16[3,512]{1,0:T(4,128)(2,1)} %bitcast.142, bf16[1,512]{1,0:T(2,128)(2,1)} %bitcast.143, s32[1,512]{1,0:T(1,128)} %bitcast.144), custom_call_target="tpu_custom_call" | custom-call | tf_op jit(solution)/shard_map/describe/pallas_call | solution.py:114
  2.9 8.8 %collective-permute-start = (bf16[32,512]{1,0:T(8,128)(2,1)}, bf16[32,512]{1,0:T(8,128)(2,1)S(1)}, u32[]{:S(2)}, u32[]{:S(2)}) collective-permute-start(bf16[32,512]{1,0:T(8,128)(2,1)} %get-tuple-element.11), channel_id=1, source_target_pairs={{0,1},{1,0},{2,3},{3,2},{4,5},{5,4},{6,7},{7,6},{8,9},{9,8},{10,11... | collective-permute-start | bytes 98312 | tf_op jit(solution)/shard_map/ppermute | solution.py:48
  11.6 1.9 %collective-permute-start.1 = (bf16[32,512]{1,0:T(8,128)(2,1)}, bf16[32,512]{1,0:T(8,128)(2,1)S(1)}, u32[]{:S(2)}, u32[]{:S(2)}) collective-permute-start(bf16[32,512]{1,0:T(8,128)(2,1)} %get-tuple-element.11), channel_id=1, source_target_pairs={{1,2},{2,1},{3,4},{4,3},{5,6},{6,5},{7,8},{8,7},{9,10},{10,9},{11,... | collective-permute-start | bytes 98312 | tf_op jit(solution)/shard_map/ppermute | solution.py:49
  13.6 0.0 collective-permute-done
  13.6 3.5 %collective-permute-done.1 = bf16[32,512]{1,0:T(8,128)(2,1)S(1)} collective-permute-done((bf16[32,512]{1,0:T(8,128)(2,1)}, bf16[32,512]{1,0:T(8,128)(2,1)S(1)}, u32[]{:S(2)}, u32[]{:S(2)}) %collective-permute-start.1) | collective-permute-done | bytes 32800 | tf_op jit(solution)/shard_map/ppermute | solution.py:49
  17.1 0.8 pad_maximum_fusion.refs_0_
  17.9 1.3 %collective-permute-start.2 = (bf16[3,32,512]{2,1,0:T(8,128)(2,1)S(1)}, bf16[3,32,512]{2,1,0:T(8,128)(2,1)S(1)}, u32[]{:S(2)}, u32[]{:S(2)}) collective-permute-start(bf16[3,32,512]{2,1,0:T(8,128)(2,1)S(1)} %pad_maximum_fusion.refs_0_), channel_id=1, source_target_pairs={{0,64},{64,128},{128,192},{192,256},{256,320},{320,384},{384,448},... | collective-permute-start | bytes 294920 | tf_op jit(solution)/shard_map/ppermute | solution.py:56
  19.2 1.3 %collective-permute-start.3 = (bf16[3,32,512]{2,1,0:T(8,128)(2,1)S(1)}, bf16[3,32,512]{2,1,0:T(8,128)(2,1)S(1)}, u32[]{:S(2)}, u32[]{:S(2)}) collective-permute-start(bf16[3,32,512]{2,1,0:T(8,128)(2,1)S(1)} %pad_maximum_fusion.refs_0_), channel_id=1, source_target_pairs={{64,0},{128,64},{192,128},{256,192},{320,256},{384,320},{448,384},... | collective-permute-start | bytes 294920 | tf_op jit(solution)/shard_map/ppermute | solution.py:57
  20.5 0.8 broadcast_multiply_fusion.2.refs_2_
  21.3 0.0 copy-start
  21.3 0.8 copy-done
  22.1 1.4 %build.2 = (bf16[3,512,512]{2,1,0:T(8,128)(2,1)S(1)}, f32[16,512]{1,0:T(8,128)S(1)}) custom-call(bf16[3,32,512]{2,1,0:T(8,128)(2,1)S(1)} %pad_maximum_fusion.refs_0_, bf16[48,512]{1,0:T(8,128)(2,1)S(1)} %copy-done, f32[16,512]{1,0:T(8,128)S(1)} %broadcast_multiply_fusion.2.refs_2_), custom_call_target="tpu_custom_call" | custom-call | flops 427819008 | bytes 1572864 | tf_op jit(solution)/shard_map/build/pallas_call | solution.py:182
  23.5 0.0 collective-permute-done.2.refs_0_
  23.5 1.1 collective-permute-done.3.refs_1_
  24.5 2.6 %build.3 = (bf16[6,512,512]{2,1,0:T(8,128)(2,1)S(1)}, f32[16,512]{1,0:T(8,128)S(1)}, bf16[16,512]{1,0:T(8,128)(2,1)S(1)}) custom-call(bf16[3,32,512]{2,1,0:T(8,128)(2,1)S(1)} %collective-permute-done.2.refs_0_, bf16[3,32,512]{2,1,0:T(8,128)(2,1)S(1)} %collective-permute-done.3.refs_1_, bf16[48,512]{1,0:T(8,128)(2,1)S(1)} %copy-done, ...), custom_call_target="tpu_custom_call" | custom-call | flops 855638016 | bytes 3145728 | tf_op jit(solution)/shard_map/build/pallas_call | solution.py:182
  27.2 10.4 %collective-permute-start.4 = (bf16[16,512]{1,0:T(8,128)(2,1)S(1)}, bf16[16,512]{1,0:T(8,128)(2,1)S(1)}, u32[]{:S(2)}, u32[]{:S(2)}) collective-permute-start(bf16[16,512]{1,0:T(8,128)(2,1)S(1)} %get-tuple-element.15), channel_id=1, source_target_pairs={{0,1},{1,0},{2,3},{3,2},{4,5},{5,4},{6,7},{7,6},{8,9},{9,8},{10,11... | collective-permute-start | bytes 49160 | tf_op jit(solution)/shard_map/ppermute | solution.py:48
  37.6 1.9 %collective-permute-start.5 = (bf16[16,512]{1,0:T(8,128)(2,1)S(1)}, bf16[16,512]{1,0:T(8,128)(2,1)S(1)}, u32[]{:S(2)}, u32[]{:S(2)}) collective-permute-start(bf16[16,512]{1,0:T(8,128)(2,1)S(1)} %get-tuple-element.15), channel_id=1, source_target_pairs={{1,2},{2,1},{3,4},{4,3},{5,6},{6,5},{7,8},{8,7},{9,10},{10,9},{11,... | collective-permute-start | bytes 49160 | tf_op jit(solution)/shard_map/ppermute | solution.py:49
  39.5 0.0 collective-permute-done.4
  39.5 3.1 %collective-permute-done.5 = bf16[16,512]{1,0:T(8,128)(2,1)S(1)} collective-permute-done((bf16[16,512]{1,0:T(8,128)(2,1)S(1)}, bf16[16,512]{1,0:T(8,128)(2,1)S(1)}, u32[]{:S(2)}, u32[]{:S(2)}) %collective-permute-start.5) | collective-permute-done | bytes 16416 | tf_op jit(solution)/shard_map/ppermute | solution.py:49
  42.7 3.1 %collective-permute-start.6 = (bf16[3,16,512]{2,1,0:T(8,128)(2,1)S(1)}, bf16[3,16,512]{2,1,0:T(8,128)(2,1)S(1)}, u32[]{:S(2)}, u32[]{:S(2)}) collective-permute-start(bf16[3,16,512]{2,1,0:T(8,128)(2,1)S(1)} %pad_maximum_fusion.1.refs_0_), channel_id=1, source_target_pairs={{0,64},{64,128},{128,192},{192,256},{256,320},{320,384},{384,448},... | collective-permute-start | bytes 147464 | tf_op jit(solution)/shard_map/ppermute | solution.py:56
  45.8 1.3 %collective-permute-start.7 = (bf16[3,16,512]{2,1,0:T(8,128)(2,1)S(1)}, bf16[3,16,512]{2,1,0:T(8,128)(2,1)S(1)}, u32[]{:S(2)}, u32[]{:S(2)}) collective-permute-start(bf16[3,16,512]{2,1,0:T(8,128)(2,1)S(1)} %pad_maximum_fusion.1.refs_0_), channel_id=1, source_target_pairs={{64,0},{128,64},{192,128},{256,192},{320,256},{384,320},{448,384},... | collective-permute-start | bytes 147464 | tf_op jit(solution)/shard_map/ppermute | solution.py:57
  47.1 0.0 copy-done.2
  47.1 0.3 apply.4.refs_3_
  47.4 0.0 collective-permute-done.6.refs_0_
  47.4 3.2 %collective-permute-done.7.refs_1_ = bf16[3,16,512]{2,1,0:T(8,128)(2,1)S(1)} collective-permute-done((bf16[3,16,512]{2,1,0:T(8,128)(2,1)S(1)}, bf16[3,16,512]{2,1,0:T(8,128)(2,1)S(1)}, u32[]{:S(2)}, u32[]{:S(2)}) %collective-permute-start.7) | collective-permute-done | bytes 49184 | tf_op jit(solution)/shard_map/ppermute | solution.py:57
  50.6 0.5 apply.5
  51.2 0.0 copy-start.1
  51.2 7.9 %collective-permute-start.8 = (bf16[16,512]{1,0:T(8,128)(2,1)S(1)}, bf16[16,512]{1,0:T(8,128)(2,1)S(1)}, u32[]{:S(2)}, u32[]{:S(2)}) collective-permute-start(bf16[16,512]{1,0:T(8,128)(2,1)S(1)} %get-tuple-element.19), channel_id=1, source_target_pairs={{0,1},{1,0},{2,3},{3,2},{4,5},{5,4},{6,7},{7,6},{8,9},{9,8},{10,11... | collective-permute-start | bytes 49160 | tf_op jit(solution)/shard_map/ppermute | solution.py:48
  59.1 1.9 %collective-permute-start.9 = (bf16[16,512]{1,0:T(8,128)(2,1)S(1)}, bf16[16,512]{1,0:T(8,128)(2,1)S(1)}, u32[]{:S(2)}, u32[]{:S(2)}) collective-permute-start(bf16[16,512]{1,0:T(8,128)(2,1)S(1)} %get-tuple-element.19), channel_id=1, source_target_pairs={{1,2},{2,1},{3,4},{4,3},{5,6},{6,5},{7,8},{8,7},{9,10},{10,9},{11,... | collective-permute-start | bytes 49160 | tf_op jit(solution)/shard_map/ppermute | solution.py:49
  61.0 0.0 collective-permute-done.8
  61.0 3.1 %collective-permute-done.9 = bf16[16,512]{1,0:T(8,128)(2,1)S(1)} collective-permute-done((bf16[16,512]{1,0:T(8,128)(2,1)S(1)}, bf16[16,512]{1,0:T(8,128)(2,1)S(1)}, u32[]{:S(2)}, u32[]{:S(2)}) %collective-permute-start.9) | collective-permute-done | bytes 16416 | tf_op jit(solution)/shard_map/ppermute | solution.py:49
  64.1 4.1 %collective-permute-start.10 = (bf16[3,16,512]{2,1,0:T(8,128)(2,1)S(1)}, bf16[3,16,512]{2,1,0:T(8,128)(2,1)S(1)}, u32[]{:S(2)}, u32[]{:S(2)}) collective-permute-start(bf16[3,16,512]{2,1,0:T(8,128)(2,1)S(1)} %pad_maximum_fusion.2.refs_0_), channel_id=1, source_target_pairs={{0,64},{64,128},{128,192},{192,256},{256,320},{320,384},{384,448},... | collective-permute-start | bytes 147464 | tf_op jit(solution)/shard_map/ppermute | solution.py:56
  68.3 1.3 %collective-permute-start.11 = (bf16[3,16,512]{2,1,0:T(8,128)(2,1)S(1)}, bf16[3,16,512]{2,1,0:T(8,128)(2,1)S(1)}, u32[]{:S(2)}, u32[]{:S(2)}) collective-permute-start(bf16[3,16,512]{2,1,0:T(8,128)(2,1)S(1)} %pad_maximum_fusion.2.refs_0_), channel_id=1, source_target_pairs={{64,0},{128,64},{192,128},{256,192},{320,256},{384,320},{448,384},... | collective-permute-start | bytes 147464 | tf_op jit(solution)/shard_map/ppermute | solution.py:57
  69.6 0.3 apply.6.refs_3_
  69.9 0.0 collective-permute-done.10.refs_0_
  69.9 3.5 %collective-permute-done.11.refs_1_ = bf16[3,16,512]{2,1,0:T(8,128)(2,1)S(1)} collective-permute-done((bf16[3,16,512]{2,1,0:T(8,128)(2,1)S(1)}, bf16[3,16,512]{2,1,0:T(8,128)(2,1)S(1)}, u32[]{:S(2)}, u32[]{:S(2)}) %collective-permute-start.11) | collective-permute-done | bytes 49184 | tf_op jit(solution)/shard_map/ppermute | solution.py:57
  73.4 0.5 apply.7
  73.9 0.0 copy-done.1
  73.9 0.3 multiply_reduce_fusion
  74.2 0.1 concatenate.7
  74.3 17.4 %all_to_all.10 = f32[32,2,128]{2,1,0:T(2,128)S(1)} all-to-all(f32[32,2,128]{2,1,0:T(2,128)S(1)} %broadcast_in_dim.8), channel_id=1, replica_groups=mesh['z_lo'=2,'x'=4,'z_hi'=4,'y'=8,'core'=2] {'z_lo','z_hi','x'}, dimensions={0} | all-to-all | bytes 65536 | tf_op jit(solution)/shard_map/all_to_all | solution.py:240
  91.8 16.6 %all_to_all.11 = f32[16,2,128]{2,1,0:T(2,128)S(1)} all-to-all(f32[16,2,128]{2,1,0:T(2,128)S(1)} %broadcast_in_dim.9), channel_id=1, replica_groups=mesh['z_lo'=2,'x'=4,'z_hi'=4,'y'=8,'core'=2] {'y','core'}, dimensions={0} | all-to-all | bytes 32768 | tf_op jit(solution)/shard_map/all_to_all | solution.py:240
  108.4 0.1 reshape.473
  108.6 0.7 add_bitcast_fusion
  (15 shorter events, 0.2 us)
Async XLA Ops:
  0.6 46.5 %copy-start.2 = (f32[1,1,512]{2,1,0:T(1,128)S(1)}, f32[1,1,512]{2,1,0:T(1,128)}, u32[]{:S(2)}) copy-start(f32[1,1,512]{2,1,0:T(1,128)} %param.6) | copy-start | bytes 6148
  2.9 10.7 %collective-permute-start = (bf16[32,512]{1,0:T(8,128)(2,1)}, bf16[32,512]{1,0:T(8,128)(2,1)S(1)}, u32[]{:S(2)}, u32[]{:S(2)}) collective-permute-start(bf16[32,512]{1,0:T(8,128)(2,1)} %get-tuple-element.11), channel_id=1, source_target_pairs={{0,1},{1,0},{2,3},{3,2},{4,5},{5,4},{6,7},{7,6},{8,9},{9,8},{10,11... | collective-permute-start | bytes 98312 | tf_op jit(solution)/shard_map/ppermute | solution.py:48
  11.6 5.4 %collective-permute-start.1 = (bf16[32,512]{1,0:T(8,128)(2,1)}, bf16[32,512]{1,0:T(8,128)(2,1)S(1)}, u32[]{:S(2)}, u32[]{:S(2)}) collective-permute-start(bf16[32,512]{1,0:T(8,128)(2,1)} %get-tuple-element.11), channel_id=1, source_target_pairs={{1,2},{2,1},{3,4},{4,3},{5,6},{6,5},{7,8},{8,7},{9,10},{10,9},{11,... | collective-permute-start | bytes 98312 | tf_op jit(solution)/shard_map/ppermute | solution.py:49
  17.9 5.6 %collective-permute-start.2 = (bf16[3,32,512]{2,1,0:T(8,128)(2,1)S(1)}, bf16[3,32,512]{2,1,0:T(8,128)(2,1)S(1)}, u32[]{:S(2)}, u32[]{:S(2)}) collective-permute-start(bf16[3,32,512]{2,1,0:T(8,128)(2,1)S(1)} %pad_maximum_fusion.refs_0_), channel_id=1, source_target_pairs={{0,64},{64,128},{128,192},{192,256},{256,320},{320,384},{384,448},... | collective-permute-start | bytes 294920 | tf_op jit(solution)/shard_map/ppermute | solution.py:56
  19.2 5.4 %collective-permute-start.3 = (bf16[3,32,512]{2,1,0:T(8,128)(2,1)S(1)}, bf16[3,32,512]{2,1,0:T(8,128)(2,1)S(1)}, u32[]{:S(2)}, u32[]{:S(2)}) collective-permute-start(bf16[3,32,512]{2,1,0:T(8,128)(2,1)S(1)} %pad_maximum_fusion.refs_0_), channel_id=1, source_target_pairs={{64,0},{128,64},{192,128},{256,192},{320,256},{384,320},{448,384},... | collective-permute-start | bytes 294920 | tf_op jit(solution)/shard_map/ppermute | solution.py:57
  21.3 0.8 copy-start
  27.2 12.4 %collective-permute-start.4 = (bf16[16,512]{1,0:T(8,128)(2,1)S(1)}, bf16[16,512]{1,0:T(8,128)(2,1)S(1)}, u32[]{:S(2)}, u32[]{:S(2)}) collective-permute-start(bf16[16,512]{1,0:T(8,128)(2,1)S(1)} %get-tuple-element.15), channel_id=1, source_target_pairs={{0,1},{1,0},{2,3},{3,2},{4,5},{5,4},{6,7},{7,6},{8,9},{9,8},{10,11... | collective-permute-start | bytes 49160 | tf_op jit(solution)/shard_map/ppermute | solution.py:48
  37.6 5.1 %collective-permute-start.5 = (bf16[16,512]{1,0:T(8,128)(2,1)S(1)}, bf16[16,512]{1,0:T(8,128)(2,1)S(1)}, u32[]{:S(2)}, u32[]{:S(2)}) collective-permute-start(bf16[16,512]{1,0:T(8,128)(2,1)S(1)} %get-tuple-element.15), channel_id=1, source_target_pairs={{1,2},{2,1},{3,4},{4,3},{5,6},{6,5},{7,8},{8,7},{9,10},{10,9},{11,... | collective-permute-start | bytes 49160 | tf_op jit(solution)/shard_map/ppermute | solution.py:49
  42.7 4.8 %collective-permute-start.6 = (bf16[3,16,512]{2,1,0:T(8,128)(2,1)S(1)}, bf16[3,16,512]{2,1,0:T(8,128)(2,1)S(1)}, u32[]{:S(2)}, u32[]{:S(2)}) collective-permute-start(bf16[3,16,512]{2,1,0:T(8,128)(2,1)S(1)} %pad_maximum_fusion.1.refs_0_), channel_id=1, source_target_pairs={{0,64},{64,128},{128,192},{192,256},{256,320},{320,384},{384,448},... | collective-permute-start | bytes 147464 | tf_op jit(solution)/shard_map/ppermute | solution.py:56
  45.8 4.8 %collective-permute-start.7 = (bf16[3,16,512]{2,1,0:T(8,128)(2,1)S(1)}, bf16[3,16,512]{2,1,0:T(8,128)(2,1)S(1)}, u32[]{:S(2)}, u32[]{:S(2)}) collective-permute-start(bf16[3,16,512]{2,1,0:T(8,128)(2,1)S(1)} %pad_maximum_fusion.1.refs_0_), channel_id=1, source_target_pairs={{64,0},{128,64},{192,128},{256,192},{320,256},{384,320},{448,384},... | collective-permute-start | bytes 147464 | tf_op jit(solution)/shard_map/ppermute | solution.py:57
  51.2 22.7 %copy-start.1 = (f32[1,1,16,512]{3,2,1,0:T(8,128)S(1)}, f32[1,1,16,512]{3,2,1,0:T(8,128)}, u32[]{:S(2)}) copy-start(f32[1,1,16,512]{3,2,1,0:T(8,128)} %param.5) | copy-start | bytes 98308
  51.2 9.8 %collective-permute-start.8 = (bf16[16,512]{1,0:T(8,128)(2,1)S(1)}, bf16[16,512]{1,0:T(8,128)(2,1)S(1)}, u32[]{:S(2)}, u32[]{:S(2)}) collective-permute-start(bf16[16,512]{1,0:T(8,128)(2,1)S(1)} %get-tuple-element.19), channel_id=1, source_target_pairs={{0,1},{1,0},{2,3},{3,2},{4,5},{5,4},{6,7},{7,6},{8,9},{9,8},{10,11... | collective-permute-start | bytes 49160 | tf_op jit(solution)/shard_map/ppermute | solution.py:48
  59.1 5.1 %collective-permute-start.9 = (bf16[16,512]{1,0:T(8,128)(2,1)S(1)}, bf16[16,512]{1,0:T(8,128)(2,1)S(1)}, u32[]{:S(2)}, u32[]{:S(2)}) collective-permute-start(bf16[16,512]{1,0:T(8,128)(2,1)S(1)} %get-tuple-element.19), channel_id=1, source_target_pairs={{1,2},{2,1},{3,4},{4,3},{5,6},{6,5},{7,8},{8,7},{9,10},{10,9},{11,... | collective-permute-start | bytes 49160 | tf_op jit(solution)/shard_map/ppermute | solution.py:49
  64.1 5.8 %collective-permute-start.10 = (bf16[3,16,512]{2,1,0:T(8,128)(2,1)S(1)}, bf16[3,16,512]{2,1,0:T(8,128)(2,1)S(1)}, u32[]{:S(2)}, u32[]{:S(2)}) collective-permute-start(bf16[3,16,512]{2,1,0:T(8,128)(2,1)S(1)} %pad_maximum_fusion.2.refs_0_), channel_id=1, source_target_pairs={{0,64},{64,128},{128,192},{192,256},{256,320},{320,384},{384,448},... | collective-permute-start | bytes 147464 | tf_op jit(solution)/shard_map/ppermute | solution.py:56
  68.3 5.1 %collective-permute-start.11 = (bf16[3,16,512]{2,1,0:T(8,128)(2,1)S(1)}, bf16[3,16,512]{2,1,0:T(8,128)(2,1)S(1)}, u32[]{:S(2)}, u32[]{:S(2)}) collective-permute-start(bf16[3,16,512]{2,1,0:T(8,128)(2,1)S(1)} %pad_maximum_fusion.2.refs_0_), channel_id=1, source_target_pairs={{64,0},{128,64},{192,128},{256,192},{320,256},{384,320},{448,384},... | collective-permute-start | bytes 147464 | tf_op jit(solution)/shard_map/ppermute | solution.py:57

commit v3 on v2

--- a/solution.py
+++ b/solution.py
@@ -47,8 +47,7 @@
     count = extent(LON)
     inner = lax.ppermute(block, LON, swaps(count, 0))
     outer = lax.ppermute(block, LON, swaps(count, 1))
-    odd = lax.axis_index(LON) % 2 == 1
-    return jnp.stack([jnp.where(odd, inner, outer), block, jnp.where(odd, outer, inner)])
+    return jnp.stack([outer, block, inner])
 
 
 def all_bands(wide):
@@ -68,7 +67,10 @@
     return high, mid, rounded(value - high - mid)
 
 
-def describe_kernel(place_ref, start_ref, frac_ref, spread_ref, type_ref, message_ref, own_ref, far_rows, own_rows):
+def describe_kernel(
+    place_ref, start_ref, error_ref, frac_ref, spread_ref, type_ref,
+    message_ref, own_ref, error_out_ref, added_ref, far_rows, own_rows,
+):
     frac = frac_ref[...].astype(jnp.float32)
     latitude = (place_ref[0].astype(jnp.float32) + frac[0:1]) * (2.0 * LAT_LIMIT / BANDS) - LAT_LIMIT
     longitude = (place_ref[1].astype(jnp.float32) + frac[1:2]) * (2.0 * math.pi / SECTORS)
@@ -99,6 +101,8 @@
         own_rows[row : row + 1, :] = own[row]
     message_ref[0:16, :] = start_ref[...].astype(jnp.bfloat16)
     message_ref[16:32, :] = far_rows[...].astype(jnp.bfloat16)
+    error_out_ref[...] = error_ref[...]
+    added_ref[...] = error_ref[...] * start_ref[...]
     left = own_rows[...]
     for piece in range(3):
         part = left.astype(jnp.bfloat16)
@@ -110,18 +114,20 @@
     return pl.BlockSpec(memory_space=space)
 
 
-def describe(place, start, where_frac, spread, obs_type):
+def describe(place, start, error_var, where_frac, spread, obs_type):
     return pl.pallas_call(
         describe_kernel,
         out_shape=(
-            jax.ShapeDtypeStruct((32, OBS), jnp.bfloat16),
-            jax.ShapeDtypeStruct((48, OBS), jnp.bfloat16),
+            pltpu.VMEM((32, OBS), jnp.bfloat16),
+            pltpu.VMEM((48, OBS), jnp.bfloat16),
+            pltpu.VMEM((1, OBS), jnp.float32),
+            pltpu.VMEM((RHS, OBS), jnp.float32),
         ),
-        in_specs=[whole(pltpu.SMEM)] + [whole()] * 4,
-        out_specs=(whole(), whole()),
+        in_specs=[whole(pltpu.SMEM)] + [whole()] * 5,
+        out_specs=[whole()] * 4,
         scratch_shapes=[pltpu.VMEM((16, OBS), jnp.float32)] * 2,
         name="describe",
-    )(place, start, where_frac, spread, obs_type)
+    )(place, start, error_var, where_frac, spread, obs_type)
 
 
 CHUNK = 256
@@ -146,9 +152,12 @@
         ref[...] = total.astype(jnp.bfloat16)
 
 
-def apply_kernel(steps, carried, *refs):
-    messages, (tile_ref, added_ref), (sum_ref, *sent) = refs[: len(carried)], refs[len(carried) : len(carried) + 2], refs[len(carried) + 2 :]
-    total = added_ref[...]
+def apply_kernel(steps, carried, scaled, *refs):
+    messages, (tile_ref, *added) = refs[: len(carried)], refs[len(carried) : len(carried) + 2 + scaled]
+    sum_ref, *sent = refs[len(carried) + 2 + scaled :]
+    total = added[0][...]
+    if scaled:
+        total = total * added[1][...]
     for k, (which, slot, _) in enumerate(steps):
         total = total + jnp.dot(messages[which][slot], tile_ref[k], preferred_element_type=jnp.float32)
     sum_ref[...] = total
@@ -170,9 +179,9 @@
 
 
 def sums(last):
-    shapes = [jax.ShapeDtypeStruct((RHS, OBS), jnp.float32)]
+    shapes = [pltpu.VMEM((RHS, OBS), jnp.float32)]
     if last:
-        shapes.append(jax.ShapeDtypeStruct((RHS, OBS), jnp.bfloat16))
+        shapes.append(pltpu.VMEM((RHS, OBS), jnp.bfloat16))
     return shapes
 
 
@@ -192,35 +201,35 @@
 
 def apply(steps, carried, tiles, added, last):
     shapes = sums(last)
+    scaled = len(added) - 1
     return pl.pallas_call(
-        functools.partial(apply_kernel, steps, carried),
+        functools.partial(apply_kernel, steps, carried, scaled),
         out_shape=shapes,
-        in_specs=[whole()] * (len(carried) + 2),
+        in_specs=[whole()] * (len(carried) + 2 + scaled),
         out_specs=[whole()] * len(shapes),
         compiler_params=pltpu.CompilerParams(vmem_limit_bytes=24 << 20),
         cost_estimate=cost(steps, 0),
         name="apply",
-    )(*carried, tiles, added)
+    )(*carried, tiles, *added)
 
 
 def local(innovations, obs_error, where_frac, spread, obs_type):
     start = innovations[0, 0]
-    error_var = obs_error[0, 0][None]
     place = jnp.stack([lax.axis_index(LAT), lax.axis_index(LON)]).astype(jnp.int32)
-    message, own = describe(place, start, where_frac[0, 0], spread[0], obs_type[0])
+    message, own, error_var, added = describe(place, start, obs_error[0], where_frac[0, 0], spread[0], obs_type[0])
     wide = widened(message)
     below, above = all_bands(wide)
-    near_tiles, part = build(SAME_BAND, [wide], own, error_var * start, False)
+    near_tiles, part = build(SAME_BAND, [wide], own, added, False)
     far_tiles, field, sent = build(OTHER_BANDS, [below, above], own, part, True)
     basis = [start, field]
     for last in (False, True):
         wide = widened(sent)
         below, above = all_bands(wide)
-        part, = apply(SAME_BAND, [wide], near_tiles, error_var * field, False)
+        part, = apply(SAME_BAND, [wide], near_tiles, [field, error_var], False)
         if last:
-            field, = apply(OTHER_BANDS, [below, above], far_tiles, part, False)
+            field, = apply(OTHER_BANDS, [below, above], far_tiles, [part], False)
         else:
-            field, sent = apply(OTHER_BANDS, [below, above], far_tiles, part, True)
+            field, sent = apply(OTHER_BANDS, [below, above], far_tiles, [part], True)
         basis.append(field)
     pairs = [(i, j) for i in range(4) for j in range(i, 4) if (i, j) != (3, 3)]
     parts = [jnp.sum(basis[i] * basis[j], axis=1) for i, j in pairs]

time: 110 us -> 102 us (0.927)
  waiting for transfers between devices: 17.5 us -> 11.6 us
  starting transfers between devices: 45.3 us -> 48.6 us
  blocking collectives: 34 us -> 31.8 us
  other arithmetic: 3.4 us -> 1.83 us
    ppermute x3, waiting for transfers between devices: 9.73 us -> 0.01 us  [widened(): outer = lax.ppermute(block, LON, swaps(count, 1))]
    ppermute x3, starting transfers between devices: 5.76 us -> 8.56 us  [widened(): outer = lax.ppermute(block, LON, swaps(count, 1))]
    ppermute x3, waiting for transfers between devices: 0.01 us -> 2.44 us  [widened(): inner = lax.ppermute(block, LON, swaps(count, 0))]
    all_to_all x2, blocking collectives: 34 us -> 31.8 us  [global_sum(): value = jnp.sum(lax.all_to_all(spread_out, axes, 0, 0), axis=0)]
    ppermute x3, starting transfers between devices: 8.54 us -> 10.7 us  [all_bands(): below = lax.ppermute(wide, LAT, [(i, i + 1) for i in range(count - 1)])]
    ppermute x3, starting transfers between devices: 27.1 us -> 25.4 us  [widened(): inner = lax.ppermute(block, LON, swaps(count, 0))]
    ppermute x3, waiting for transfers between devices: 7.77 us -> 9.19 us  [all_bands(): above = lax.ppermute(wide, LAT, [(i + 1, i) for i in range(count - 1)])]
  transfers between devices with their start and end apart: 12 -> 12, of which waited for: 6 -> 6; matrix products, arithmetic and copies ran while one was open for 1% -> 0% of each run, Pallas kernels for 2% -> 2%
where the time goes in v3:
time: 102 us; the launch traced here: 101 us
  starting transfers between devices  48.6 us (48%)
  blocking collectives  31.8 us (31%)
  waiting for transfers between devices  11.6 us (11%)
  Pallas kernels  6.59 us (6%)
  other arithmetic  1.83 us (2%)
    all_to_all x2, blocking collectives, global_sum(): value = jnp.sum(lax.all_to_all(spread_out, axes, 0, 0), axis=0)  31.8 us
    ppermute x3, starting transfers between devices, widened(): inner = lax.ppermute(block, LON, swaps(count, 0))  25.4 us
    ppermute x3, starting transfers between devices, all_bands(): below = lax.ppermute(wide, LAT, [(i, i + 1) for i in range(count - 1)])  10.7 us
    ppermute x3, waiting for transfers between devices, all_bands(): above = lax.ppermute(wide, LAT, [(i + 1, i) for i in range(count - 1)])  9.19 us
    ppermute x3, starting transfers between devices, widened(): outer = lax.ppermute(block, LON, swaps(count, 1))  8.56 us
    pallas_call x2, Pallas kernels, build(): pl.pallas_call(functools.partial(build_kernel, steps, carried), out_shape...  4.03 us
    ppermute x3, starting transfers between devices, all_bands(): above = lax.ppermute(wide, LAT, [(i + 1, i) for i in range(count - 1)])  3.88 us
    ppermute x3, waiting for transfers between devices, widened(): inner = lax.ppermute(block, LON, swaps(count, 0))  2.44 us
  transfers between devices with their start and end apart: 12, of which 6 were waited for; matrix products, arithmetic and copies ran while one was open for 0% of the time, Pallas kernels for 2%

profile of v3, /device:TPU:1, one launch (start us, length us, event | category | flops | bytes accessed | tf_op | source)
XLA Modules:
  0.0 101.5 jit_solution(10999042686307513686)
XLA Ops:
  0.6 0.7 pad_add_fusion.place_ref
  1.3 0.9 describe.1
  2.2 4.6 %collective-permute-start = (bf16[32,512]{1,0:T(8,128)(2,1)S(1)}, bf16[32,512]{1,0:T(8,128)(2,1)S(1)}, u32[]{:S(2)}, u32[]{:S(2)}) collective-permute-start(bf16[32,512]{1,0:T(8,128)(2,1)S(1)} %get-tuple-element.13), channel_id=1, source_target_pairs={{1,2},{2,1},{3,4},{4,3},{5,6},{6,5},{7,8},{8,7},{9,10},{10,9},{11,... | collective-permute-start | bytes 98312 | tf_op jit(solution)/shard_map/ppermute | solution.py:49
  6.8 12.1 %collective-permute-start.1 = (bf16[32,512]{1,0:T(8,128)(2,1)S(1)}, bf16[32,512]{1,0:T(8,128)(2,1)S(1)}, u32[]{:S(2)}, u32[]{:S(2)}) collective-permute-start(bf16[32,512]{1,0:T(8,128)(2,1)S(1)} %get-tuple-element.13), channel_id=1, source_target_pairs={{0,1},{1,0},{2,3},{3,2},{4,5},{5,4},{6,7},{7,6},{8,9},{9,8},{10,11... | collective-permute-start | bytes 98312 | tf_op jit(solution)/shard_map/ppermute | solution.py:48
  18.9 0.0 collective-permute-done
  19.0 0.8 collective-permute-done.1
  19.8 3.1 %collective-permute-start.2 = (bf16[3,32,512]{2,1,0:T(8,128)(2,1)S(1)}, bf16[3,32,512]{2,1,0:T(8,128)(2,1)S(1)}, u32[]{:S(2)}, u32[]{:S(2)}) collective-permute-start(bf16[3,32,512]{2,1,0:T(8,128)(2,1)S(1)} %pad_maximum_fusion.refs_0_), channel_id=1, source_target_pairs={{0,64},{64,128},{128,192},{192,256},{256,320},{320,384},{384,448},... | collective-permute-start | bytes 294920 | tf_op jit(solution)/shard_map/ppermute | solution.py:55
  22.9 1.3 %collective-permute-start.3 = (bf16[3,32,512]{2,1,0:T(8,128)(2,1)S(1)}, bf16[3,32,512]{2,1,0:T(8,128)(2,1)S(1)}, u32[]{:S(2)}, u32[]{:S(2)}) collective-permute-start(bf16[3,32,512]{2,1,0:T(8,128)(2,1)S(1)} %pad_maximum_fusion.refs_0_), channel_id=1, source_target_pairs={{64,0},{128,64},{192,128},{256,192},{320,256},{384,320},{448,384},... | collective-permute-start | bytes 294920 | tf_op jit(solution)/shard_map/ppermute | solution.py:56
  24.2 1.4 %build.2 = (bf16[3,512,512]{2,1,0:T(8,128)(2,1)S(1)}, f32[16,512]{1,0:T(8,128)S(1)}) custom-call(bf16[3,32,512]{2,1,0:T(8,128)(2,1)S(1)} %pad_maximum_fusion.refs_0_, bf16[48,512]{1,0:T(8,128)(2,1)S(1)} %get-tuple-element.14.refs_1_.refs_2_, f32[16,512]{1,0:T(8,128)S(1)} %get-tuple-element.15.refs_2_), custom_call_target="tpu_custom_call" | custom-call | flops 427819008 | bytes 1572864 | tf_op jit(solution)/shard_map/build/pallas_call | solution.py:191
  25.6 0.0 collective-permute-done.2.refs_0_
  25.6 2.7 %collective-permute-done.3.refs_1_ = bf16[3,32,512]{2,1,0:T(8,128)(2,1)S(1)} collective-permute-done((bf16[3,32,512]{2,1,0:T(8,128)(2,1)S(1)}, bf16[3,32,512]{2,1,0:T(8,128)(2,1)S(1)}, u32[]{:S(2)}, u32[]{:S(2)}) %collective-permute-start.3) | collective-permute-done | bytes 98336 | tf_op jit(solution)/shard_map/ppermute | solution.py:56
  28.3 2.6 %build.3 = (bf16[6,512,512]{2,1,0:T(8,128)(2,1)S(1)}, f32[16,512]{1,0:T(8,128)S(1)}, bf16[16,512]{1,0:T(8,128)(2,1)S(1)}) custom-call(bf16[3,32,512]{2,1,0:T(8,128)(2,1)S(1)} %collective-permute-done.2.refs_0_, bf16[3,32,512]{2,1,0:T(8,128)(2,1)S(1)} %collective-permute-done.3.refs_1_, bf16[48,512]{1,0:T(8,128)(2,1)S(1)} %get-tuple-element.14.refs_1_.refs_2_, ...), custom_call_target="tpu_custom_call" | custom-call | flops 855638016 | bytes 3145728 | tf_op jit(solution)/shard_map/build/pallas_call | solution.py:191
  30.9 1.9 %collective-permute-start.4 = (bf16[16,512]{1,0:T(8,128)(2,1)S(1)}, bf16[16,512]{1,0:T(8,128)(2,1)S(1)}, u32[]{:S(2)}, u32[]{:S(2)}) collective-permute-start(bf16[16,512]{1,0:T(8,128)(2,1)S(1)} %get-tuple-element.18), channel_id=1, source_target_pairs={{1,2},{2,1},{3,4},{4,3},{5,6},{6,5},{7,8},{8,7},{9,10},{10,9},{11,... | collective-permute-start | bytes 49160 | tf_op jit(solution)/shard_map/ppermute | solution.py:49
  32.8 6.7 %collective-permute-start.5 = (bf16[16,512]{1,0:T(8,128)(2,1)S(1)}, bf16[16,512]{1,0:T(8,128)(2,1)S(1)}, u32[]{:S(2)}, u32[]{:S(2)}) collective-permute-start(bf16[16,512]{1,0:T(8,128)(2,1)S(1)} %get-tuple-element.18), channel_id=1, source_target_pairs={{0,1},{1,0},{2,3},{3,2},{4,5},{5,4},{6,7},{7,6},{8,9},{9,8},{10,11... | collective-permute-start | bytes 49160 | tf_op jit(solution)/shard_map/ppermute | solution.py:48
  39.5 0.0 collective-permute-done.4
  39.6 0.8 collective-permute-done.5
  40.4 3.1 %collective-permute-start.6 = (bf16[3,16,512]{2,1,0:T(8,128)(2,1)S(1)}, bf16[3,16,512]{2,1,0:T(8,128)(2,1)S(1)}, u32[]{:S(2)}, u32[]{:S(2)}) collective-permute-start(bf16[3,16,512]{2,1,0:T(8,128)(2,1)S(1)} %pad_maximum_fusion.1.refs_0_), channel_id=1, source_target_pairs={{0,64},{64,128},{128,192},{192,256},{256,320},{320,384},{384,448},... | collective-permute-start | bytes 147464 | tf_op jit(solution)/shard_map/ppermute | solution.py:55
  43.5 1.3 %collective-permute-start.7 = (bf16[3,16,512]{2,1,0:T(8,128)(2,1)S(1)}, bf16[3,16,512]{2,1,0:T(8,128)(2,1)S(1)}, u32[]{:S(2)}, u32[]{:S(2)}) collective-permute-start(bf16[3,16,512]{2,1,0:T(8,128)(2,1)S(1)} %pad_maximum_fusion.1.refs_0_), channel_id=1, source_target_pairs={{64,0},{128,64},{192,128},{256,192},{320,256},{384,320},{448,384},... | collective-permute-start | bytes 147464 | tf_op jit(solution)/shard_map/ppermute | solution.py:56
  44.8 0.3 apply.4.refs_3_
  45.1 0.0 collective-permute-done.6.refs_0_
  45.1 3.2 %collective-permute-done.7.refs_1_ = bf16[3,16,512]{2,1,0:T(8,128)(2,1)S(1)} collective-permute-done((bf16[3,16,512]{2,1,0:T(8,128)(2,1)S(1)}, bf16[3,16,512]{2,1,0:T(8,128)(2,1)S(1)}, u32[]{:S(2)}, u32[]{:S(2)}) %collective-permute-start.7) | collective-permute-done | bytes 49184 | tf_op jit(solution)/shard_map/ppermute | solution.py:56
  48.3 0.5 apply.5
  48.8 0.0 copy-start
  48.8 2.1 %collective-permute-start.8 = (bf16[16,512]{1,0:T(8,128)(2,1)S(1)}, bf16[16,512]{1,0:T(8,128)(2,1)S(1)}, u32[]{:S(2)}, u32[]{:S(2)}) collective-permute-start(bf16[16,512]{1,0:T(8,128)(2,1)S(1)} %get-tuple-element.23), channel_id=1, source_target_pairs={{1,2},{2,1},{3,4},{4,3},{5,6},{6,5},{7,8},{8,7},{9,10},{10,9},{11,... | collective-permute-start | bytes 49160 | tf_op jit(solution)/shard_map/ppermute | solution.py:49
  50.9 6.6 %collective-permute-start.9 = (bf16[16,512]{1,0:T(8,128)(2,1)S(1)}, bf16[16,512]{1,0:T(8,128)(2,1)S(1)}, u32[]{:S(2)}, u32[]{:S(2)}) collective-permute-start(bf16[16,512]{1,0:T(8,128)(2,1)S(1)} %get-tuple-element.23), channel_id=1, source_target_pairs={{0,1},{1,0},{2,3},{3,2},{4,5},{5,4},{6,7},{7,6},{8,9},{9,8},{10,11... | collective-permute-start | bytes 49160 | tf_op jit(solution)/shard_map/ppermute | solution.py:48
  57.5 0.0 collective-permute-done.8
  57.5 0.8 collective-permute-done.9
  58.4 4.5 %collective-permute-start.10 = (bf16[3,16,512]{2,1,0:T(8,128)(2,1)S(1)}, bf16[3,16,512]{2,1,0:T(8,128)(2,1)S(1)}, u32[]{:S(2)}, u32[]{:S(2)}) collective-permute-start(bf16[3,16,512]{2,1,0:T(8,128)(2,1)S(1)} %pad_maximum_fusion.2.refs_0_), channel_id=1, source_target_pairs={{0,64},{64,128},{128,192},{192,256},{256,320},{320,384},{384,448},... | collective-permute-start | bytes 147464 | tf_op jit(solution)/shard_map/ppermute | solution.py:55
  62.9 1.3 %collective-permute-start.11 = (bf16[3,16,512]{2,1,0:T(8,128)(2,1)S(1)}, bf16[3,16,512]{2,1,0:T(8,128)(2,1)S(1)}, u32[]{:S(2)}, u32[]{:S(2)}) collective-permute-start(bf16[3,16,512]{2,1,0:T(8,128)(2,1)S(1)} %pad_maximum_fusion.2.refs_0_), channel_id=1, source_target_pairs={{64,0},{128,64},{192,128},{256,192},{320,256},{384,320},{448,384},... | collective-permute-start | bytes 147464 | tf_op jit(solution)/shard_map/ppermute | solution.py:56
  64.2 0.3 apply.6.refs_3_
  64.5 0.0 collective-permute-done.10.refs_0_
  64.5 3.3 %collective-permute-done.11.refs_1_ = bf16[3,16,512]{2,1,0:T(8,128)(2,1)S(1)} collective-permute-done((bf16[3,16,512]{2,1,0:T(8,128)(2,1)S(1)}, bf16[3,16,512]{2,1,0:T(8,128)(2,1)S(1)}, u32[]{:S(2)}, u32[]{:S(2)}) %collective-permute-start.11) | collective-permute-done | bytes 49184 | tf_op jit(solution)/shard_map/ppermute | solution.py:56
  67.8 0.5 apply.7
  68.3 0.0 copy-done
  68.3 0.3 multiply_reduce_fusion
  68.6 0.1 concatenate.7
  68.7 15.4 %all_to_all.10 = f32[32,2,128]{2,1,0:T(2,128)S(1)} all-to-all(f32[32,2,128]{2,1,0:T(2,128)S(1)} %broadcast_in_dim.8), channel_id=1, replica_groups=mesh['z_lo'=2,'x'=4,'z_hi'=4,'y'=8,'core'=2] {'z_lo','z_hi','x'}, dimensions={0} | all-to-all | bytes 65536 | tf_op jit(solution)/shard_map/all_to_all | solution.py:249
  84.1 16.5 %all_to_all.11 = f32[16,2,128]{2,1,0:T(2,128)S(1)} all-to-all(f32[16,2,128]{2,1,0:T(2,128)S(1)} %broadcast_in_dim.9), channel_id=1, replica_groups=mesh['z_lo'=2,'x'=4,'z_hi'=4,'y'=8,'core'=2] {'y','core'}, dimensions={0} | all-to-all | bytes 32768 | tf_op jit(solution)/shard_map/all_to_all | solution.py:249
  100.6 0.1 reshape.472
  100.8 0.7 add_bitcast_fusion
  (11 shorter events, 0.2 us)
Async XLA Ops:
  2.2 16.7 %collective-permute-start = (bf16[32,512]{1,0:T(8,128)(2,1)S(1)}, bf16[32,512]{1,0:T(8,128)(2,1)S(1)}, u32[]{:S(2)}, u32[]{:S(2)}) collective-permute-start(bf16[32,512]{1,0:T(8,128)(2,1)S(1)} %get-tuple-element.13), channel_id=1, source_target_pairs={{1,2},{2,1},{3,4},{4,3},{5,6},{6,5},{7,8},{8,7},{9,10},{10,9},{11,... | collective-permute-start | bytes 98312 | tf_op jit(solution)/shard_map/ppermute | solution.py:49
  6.8 12.9 %collective-permute-start.1 = (bf16[32,512]{1,0:T(8,128)(2,1)S(1)}, bf16[32,512]{1,0:T(8,128)(2,1)S(1)}, u32[]{:S(2)}, u32[]{:S(2)}) collective-permute-start(bf16[32,512]{1,0:T(8,128)(2,1)S(1)} %get-tuple-element.13), channel_id=1, source_target_pairs={{0,1},{1,0},{2,3},{3,2},{4,5},{5,4},{6,7},{7,6},{8,9},{9,8},{10,11... | collective-permute-start | bytes 98312 | tf_op jit(solution)/shard_map/ppermute | solution.py:48
  19.8 5.8 %collective-permute-start.2 = (bf16[3,32,512]{2,1,0:T(8,128)(2,1)S(1)}, bf16[3,32,512]{2,1,0:T(8,128)(2,1)S(1)}, u32[]{:S(2)}, u32[]{:S(2)}) collective-permute-start(bf16[3,32,512]{2,1,0:T(8,128)(2,1)S(1)} %pad_maximum_fusion.refs_0_), channel_id=1, source_target_pairs={{0,64},{64,128},{128,192},{192,256},{256,320},{320,384},{384,448},... | collective-permute-start | bytes 294920 | tf_op jit(solution)/shard_map/ppermute | solution.py:55
  22.9 5.4 %collective-permute-start.3 = (bf16[3,32,512]{2,1,0:T(8,128)(2,1)S(1)}, bf16[3,32,512]{2,1,0:T(8,128)(2,1)S(1)}, u32[]{:S(2)}, u32[]{:S(2)}) collective-permute-start(bf16[3,32,512]{2,1,0:T(8,128)(2,1)S(1)} %pad_maximum_fusion.refs_0_), channel_id=1, source_target_pairs={{64,0},{128,64},{192,128},{256,192},{320,256},{384,320},{448,384},... | collective-permute-start | bytes 294920 | tf_op jit(solution)/shard_map/ppermute | solution.py:56
  30.9 8.6 %collective-permute-start.4 = (bf16[16,512]{1,0:T(8,128)(2,1)S(1)}, bf16[16,512]{1,0:T(8,128)(2,1)S(1)}, u32[]{:S(2)}, u32[]{:S(2)}) collective-permute-start(bf16[16,512]{1,0:T(8,128)(2,1)S(1)} %get-tuple-element.18), channel_id=1, source_target_pairs={{1,2},{2,1},{3,4},{4,3},{5,6},{6,5},{7,8},{8,7},{9,10},{10,9},{11,... | collective-permute-start | bytes 49160 | tf_op jit(solution)/shard_map/ppermute | solution.py:49
  32.8 7.5 %collective-permute-start.5 = (bf16[16,512]{1,0:T(8,128)(2,1)S(1)}, bf16[16,512]{1,0:T(8,128)(2,1)S(1)}, u32[]{:S(2)}, u32[]{:S(2)}) collective-permute-start(bf16[16,512]{1,0:T(8,128)(2,1)S(1)} %get-tuple-element.18), channel_id=1, source_target_pairs={{0,1},{1,0},{2,3},{3,2},{4,5},{5,4},{6,7},{7,6},{8,9},{9,8},{10,11... | collective-permute-start | bytes 49160 | tf_op jit(solution)/shard_map/ppermute | solution.py:48
  40.4 4.7 %collective-permute-start.6 = (bf16[3,16,512]{2,1,0:T(8,128)(2,1)S(1)}, bf16[3,16,512]{2,1,0:T(8,128)(2,1)S(1)}, u32[]{:S(2)}, u32[]{:S(2)}) collective-permute-start(bf16[3,16,512]{2,1,0:T(8,128)(2,1)S(1)} %pad_maximum_fusion.1.refs_0_), channel_id=1, source_target_pairs={{0,64},{64,128},{128,192},{192,256},{256,320},{320,384},{384,448},... | collective-permute-start | bytes 147464 | tf_op jit(solution)/shard_map/ppermute | solution.py:55
  43.5 4.8 %collective-permute-start.7 = (bf16[3,16,512]{2,1,0:T(8,128)(2,1)S(1)}, bf16[3,16,512]{2,1,0:T(8,128)(2,1)S(1)}, u32[]{:S(2)}, u32[]{:S(2)}) collective-permute-start(bf16[3,16,512]{2,1,0:T(8,128)(2,1)S(1)} %pad_maximum_fusion.1.refs_0_), channel_id=1, source_target_pairs={{64,0},{128,64},{192,128},{256,192},{320,256},{384,320},{448,384},... | collective-permute-start | bytes 147464 | tf_op jit(solution)/shard_map/ppermute | solution.py:56
  48.8 19.5 %copy-start = (f32[1,1,16,512]{3,2,1,0:T(8,128)S(1)}, f32[1,1,16,512]{3,2,1,0:T(8,128)}, u32[]{:S(2)}) copy-start(f32[1,1,16,512]{3,2,1,0:T(8,128)} %param.5) | copy-start | bytes 98308
  48.8 8.7 %collective-permute-start.8 = (bf16[16,512]{1,0:T(8,128)(2,1)S(1)}, bf16[16,512]{1,0:T(8,128)(2,1)S(1)}, u32[]{:S(2)}, u32[]{:S(2)}) collective-permute-start(bf16[16,512]{1,0:T(8,128)(2,1)S(1)} %get-tuple-element.23), channel_id=1, source_target_pairs={{1,2},{2,1},{3,4},{4,3},{5,6},{6,5},{7,8},{8,7},{9,10},{10,9},{11,... | collective-permute-start | bytes 49160 | tf_op jit(solution)/shard_map/ppermute | solution.py:49
  50.9 7.5 %collective-permute-start.9 = (bf16[16,512]{1,0:T(8,128)(2,1)S(1)}, bf16[16,512]{1,0:T(8,128)(2,1)S(1)}, u32[]{:S(2)}, u32[]{:S(2)}) collective-permute-start(bf16[16,512]{1,0:T(8,128)(2,1)S(1)} %get-tuple-element.23), channel_id=1, source_target_pairs={{0,1},{1,0},{2,3},{3,2},{4,5},{5,4},{6,7},{7,6},{8,9},{9,8},{10,11... | collective-permute-start | bytes 49160 | tf_op jit(solution)/shard_map/ppermute | solution.py:48
  58.4 6.1 %collective-permute-start.10 = (bf16[3,16,512]{2,1,0:T(8,128)(2,1)S(1)}, bf16[3,16,512]{2,1,0:T(8,128)(2,1)S(1)}, u32[]{:S(2)}, u32[]{:S(2)}) collective-permute-start(bf16[3,16,512]{2,1,0:T(8,128)(2,1)S(1)} %pad_maximum_fusion.2.refs_0_), channel_id=1, source_target_pairs={{0,64},{64,128},{128,192},{192,256},{256,320},{320,384},{384,448},... | collective-permute-start | bytes 147464 | tf_op jit(solution)/shard_map/ppermute | solution.py:55
  62.9 4.9 %collective-permute-start.11 = (bf16[3,16,512]{2,1,0:T(8,128)(2,1)S(1)}, bf16[3,16,512]{2,1,0:T(8,128)(2,1)S(1)}, u32[]{:S(2)}, u32[]{:S(2)}) collective-permute-start(bf16[3,16,512]{2,1,0:T(8,128)(2,1)S(1)} %pad_maximum_fusion.2.refs_0_), channel_id=1, source_target_pairs={{64,0},{128,64},{192,128},{256,192},{320,256},{384,320},{448,384},... | collective-permute-start | bytes 147464 | tf_op jit(solution)/shard_map/ppermute | solution.py:56

commit v4 on v3

--- a/solution.py
+++ b/solution.py
@@ -68,12 +68,12 @@
 
 
 def describe_kernel(
-    place_ref, start_ref, error_ref, frac_ref, spread_ref, type_ref,
+    start_ref, error_ref, frac_ref, spread_ref, type_ref,
     message_ref, own_ref, error_out_ref, added_ref, far_rows, own_rows,
 ):
     frac = frac_ref[...].astype(jnp.float32)
-    latitude = (place_ref[0].astype(jnp.float32) + frac[0:1]) * (2.0 * LAT_LIMIT / BANDS) - LAT_LIMIT
-    longitude = (place_ref[1].astype(jnp.float32) + frac[1:2]) * (2.0 * math.pi / SECTORS)
+    latitude = (lax.axis_index(LAT).astype(jnp.float32) + frac[0:1]) * (2.0 * LAT_LIMIT / BANDS) - LAT_LIMIT
+    longitude = (lax.axis_index(LON).astype(jnp.float32) + frac[1:2]) * (2.0 * math.pi / SECTORS)
     angles = jnp.concatenate([latitude, longitude], axis=0)
     cosines, sines = jnp.cos(angles), jnp.sin(angles)
     place = (cosines[0:1] * cosines[1:2], cosines[0:1] * sines[1:2], sines[0:1])
@@ -103,74 +103,74 @@
     message_ref[16:32, :] = far_rows[...].astype(jnp.bfloat16)
     error_out_ref[...] = error_ref[...]
     added_ref[...] = error_ref[...] * start_ref[...]
-    left = own_rows[...]
-    for piece in range(3):
-        part = left.astype(jnp.bfloat16)
-        own_ref[16 * piece : 16 * piece + 16, :] = part
-        left = left - part.astype(jnp.float32)
+    for step in range(3):
+        if step:
+            own_rows[15:16, :] = own[15] + step * math.log2(TAPER_STEP)
+        left = own_rows[...]
+        for piece in range(3):
+            part = left.astype(jnp.bfloat16)
+            own_ref[step, 16 * piece : 16 * piece + 16, :] = part
+            left = left - part.astype(jnp.float32)
 
 
 def whole(space=pltpu.VMEM):
     return pl.BlockSpec(memory_space=space)
 
 
-def describe(place, start, error_var, where_frac, spread, obs_type):
+def describe(start, error_var, where_frac, spread, obs_type):
     return pl.pallas_call(
         describe_kernel,
         out_shape=(
             pltpu.VMEM((32, OBS), jnp.bfloat16),
-            pltpu.VMEM((48, OBS), jnp.bfloat16),
+            pltpu.VMEM((3, 48, OBS), jnp.bfloat16),
             pltpu.VMEM((1, OBS), jnp.float32),
             pltpu.VMEM((RHS, OBS), jnp.float32),
         ),
-        in_specs=[whole(pltpu.SMEM)] + [whole()] * 5,
+        in_specs=[whole()] * 5,
         out_specs=[whole()] * 4,
         scratch_shapes=[pltpu.VMEM((16, OBS), jnp.float32)] * 2,
         name="describe",
-    )(place, start, error_var, where_frac, spread, obs_type)
+    )(start, error_var, where_frac, spread, obs_type)
 
 
 CHUNK = 256
 
 
-def build_kernel(steps, carried, *refs):
-    messages, (own_ref, added_ref), (tile_ref, sum_ref, *sent) = refs[: len(carried)], refs[len(carried) : len(carried) + 2], refs[len(carried) + 2 :]
-    own = own_ref[...]
+def build_kernel(steps, near_ref, own_ref, added_ref, tile_ref, sum_ref, *sent):
     total = added_ref[...]
-    for k, (which, slot, step) in enumerate(steps):
-        taper = step * math.log2(TAPER_STEP)
+    for slot, step in enumerate(steps):
+        own = own_ref[step]
         for low in range(0, OBS, CHUNK):
-            far = messages[which][slot, 16:32, low : low + CHUNK]
+            far = near_ref[slot, 16:32, low : low + CHUNK]
             far = jnp.concatenate([far, far, far], axis=0)
             power = lax.dot_general(far, own, (((0,), (0,)), ((), ())), preferred_element_type=jnp.float32)
-            tile = jnp.exp2(power + taper if step else power).astype(jnp.bfloat16)
-            tile_ref[k, low : low + CHUNK, :] = tile
-            field = messages[which][slot, 0:16, low : low + CHUNK]
+            tile = jnp.exp2(power).astype(jnp.bfloat16)
+            tile_ref[slot, low : low + CHUNK, :] = tile
+            field = near_ref[slot, 0:16, low : low + CHUNK]
             total = total + jnp.dot(field, tile, preferred_element_type=jnp.float32)
     sum_ref[...] = total
     for ref in sent:
         ref[...] = total.astype(jnp.bfloat16)
 
 
-def apply_kernel(steps, carried, scaled, *refs):
-    messages, (tile_ref, *added) = refs[: len(carried)], refs[len(carried) : len(carried) + 2 + scaled]
-    sum_ref, *sent = refs[len(carried) + 2 + scaled :]
-    total = added[0][...]
+def apply_kernel(scaled, near_ref, tile_ref, *refs):
+    total = refs[0][...]
     if scaled:
-        total = total * added[1][...]
-    for k, (which, slot, _) in enumerate(steps):
-        total = total + jnp.dot(messages[which][slot], tile_ref[k], preferred_element_type=jnp.float32)
+        total = total * refs[1][...]
+    for slot in range(3):
+        total = total + jnp.dot(near_ref[slot], tile_ref[slot], preferred_element_type=jnp.float32)
+    sum_ref, *sent = refs[1 + scaled :]
     sum_ref[...] = total
     for ref in sent:
         ref[...] = total.astype(jnp.bfloat16)
 
 
-SAME_BAND = ((0, 0, 1), (0, 1, 0), (0, 2, 1))
-OTHER_BANDS = ((0, 0, 2), (0, 1, 1), (0, 2, 2), (1, 0, 2), (1, 1, 1), (1, 2, 2))
-
-
-def cost(steps, built):
-    entries = len(steps) * OBS * OBS
+SAME_BAND = (1, 0, 1)
+OTHER_BAND = (2, 1, 2)
+
+
+def cost(built):
+    entries = 3 * OBS * OBS
     return pl.CostEstimate(
         flops=2 * entries * (RHS + 256 * built),
         bytes_accessed=2 * entries,
@@ -185,57 +185,60 @@
     return shapes
 
 
-def build(steps, carried, own, added, last):
-    tiles = pltpu.VMEM((len(steps), OBS, OBS), jnp.bfloat16)
-    shapes = [tiles] + sums(last)
+def build(steps, near, own, added, last=False):
+    shapes = [pltpu.VMEM((3, OBS, OBS), jnp.bfloat16)] + sums(last)
     return pl.pallas_call(
-        functools.partial(build_kernel, steps, carried),
+        functools.partial(build_kernel, steps),
         out_shape=shapes,
-        in_specs=[whole()] * (len(carried) + 2),
+        in_specs=[whole()] * 3,
         out_specs=[whole()] * len(shapes),
-        compiler_params=pltpu.CompilerParams(vmem_limit_bytes=24 << 20),
-        cost_estimate=cost(steps, 1),
+        compiler_params=pltpu.CompilerParams(vmem_limit_bytes=16 << 20),
+        cost_estimate=cost(1),
         name="build",
-    )(*carried, own, added)
-
-
-def apply(steps, carried, tiles, added, last):
+    )(near, own, added)
+
+
+def apply(near, tiles, added, scale=None, last=False):
     shapes = sums(last)
-    scaled = len(added) - 1
+    scales = [] if scale is None else [scale]
     return pl.pallas_call(
-        functools.partial(apply_kernel, steps, carried, scaled),
+        functools.partial(apply_kernel, len(scales)),
         out_shape=shapes,
-        in_specs=[whole()] * (len(carried) + 2 + scaled),
+        in_specs=[whole()] * (3 + len(scales)),
         out_specs=[whole()] * len(shapes),
-        compiler_params=pltpu.CompilerParams(vmem_limit_bytes=24 << 20),
-        cost_estimate=cost(steps, 0),
+        compiler_params=pltpu.CompilerParams(vmem_limit_bytes=16 << 20),
+        cost_estimate=cost(0),
         name="apply",
-    )(*carried, tiles, *added)
+    )(near, tiles, added, *scales)
 
 
 def local(innovations, obs_error, where_frac, spread, obs_type):
     start = innovations[0, 0]
-    place = jnp.stack([lax.axis_index(LAT), lax.axis_index(LON)]).astype(jnp.int32)
-    message, own, error_var, added = describe(place, start, obs_error[0], where_frac[0, 0], spread[0], obs_type[0])
+    message, own, error_var, added = describe(start, obs_error[0], where_frac[0, 0], spread[0], obs_type[0])
     wide = widened(message)
     below, above = all_bands(wide)
-    near_tiles, part = build(SAME_BAND, [wide], own, added, False)
-    far_tiles, field, sent = build(OTHER_BANDS, [below, above], own, part, True)
-    basis = [start, field]
-    for last in (False, True):
-        wide = widened(sent)
-        below, above = all_bands(wide)
-        part, = apply(SAME_BAND, [wide], near_tiles, [field, error_var], False)
-        if last:
-            field, = apply(OTHER_BANDS, [below, above], far_tiles, [part], False)
-        else:
-            field, sent = apply(OTHER_BANDS, [below, above], far_tiles, [part], True)
-        basis.append(field)
-    pairs = [(i, j) for i in range(4) for j in range(i, 4) if (i, j) != (3, 3)]
-    parts = [jnp.sum(basis[i] * basis[j], axis=1) for i, j in pairs]
-    parts += [jnp.zeros_like(parts[0])] * (16 - len(parts))
-    totals = global_sum(jnp.concatenate(parts).reshape(2, 128)).reshape(16, 16)
-    gram = {pair: totals[i] for i, pair in enumerate(pairs)}
+    tiles, part = build(SAME_BAND, wide, own, added)
+    tiles_below, part = build(OTHER_BAND, below, own, part)
+    tiles_above, first, sent = build(OTHER_BAND, above, own, part, True)
+    wide = widened(sent)
+    below, above = all_bands(wide)
+    part, = apply(wide, tiles, first, error_var)
+    part, = apply(below, tiles_below, part)
+    second, sent = apply(above, tiles_above, part, last=True)
+    wide = widened(sent)
+    below, above = all_bands(wide)
+    part, = apply(wide, tiles, second, error_var)
+    lower, = apply(below, tiles_below, part)
+    basis = [start, first, second]
+    products = [start * start, start * first, first * first, start * second, first * second, second * second]
+    products.append(second * (2.0 * lower - part))
+    parts = [jnp.sum(product, axis=1) for product in products]
+    parts.append(jnp.zeros_like(parts[0]))
+    totals = global_sum(jnp.concatenate(parts).reshape(1, 128)).reshape(8, 16)
+    third, = apply(above, tiles_above, lower)
+    basis.append(third)
+    names = {(0, 0): 0, (0, 1): 1, (1, 1): 2, (0, 2): 3, (1, 2): 4, (2, 2): 5, (2, 3): 6, (0, 3): 4, (1, 3): 5}
+    gram = {pair: totals[at] for pair, at in names.items()}
     answer, residual = coefficients(gram)
     answer = sum(c[:, None] * v for c, v in zip(answer, basis))
     residual = sum(c[:, None] * v for c, v in zip(residual, basis))

time: 102 us -> 99.1 us (0.972)
  blocking collectives: 31.8 us -> 15.7 us
  starting transfers between devices: 48.6 us -> 57.3 us
  waiting for transfers between devices: 11.6 us -> 15.6 us
    all_to_all x2 -> x1, blocking collectives: 31.8 us -> 15.7 us  [global_sum(): value = jnp.sum(lax.all_to_all(spread_out, axes, 0, 0), axis=0)]
    all_to_all x0 -> x1, starting transfers between devices: none -> 9.29 us  [global_sum(): value = jnp.sum(lax.all_to_all(spread_out, axes, 0, 0), axis=0)]
    all_to_all x0 -> x1, waiting for transfers between devices: none -> 6.67 us  [global_sum(): value = jnp.sum(lax.all_to_all(spread_out, axes, 0, 0), axis=0)]
    ppermute x3, waiting for transfers between devices: 9.19 us -> 4.17 us  [all_bands(): above = lax.ppermute(wide, LAT, [(i + 1, i) for i in range(count - 1)])]
    ppermute x3, waiting for transfers between devices: 0.01 us -> 3.12 us  [widened(): outer = lax.ppermute(block, LON, swaps(count, 1))]
    ppermute x3, starting transfers between devices: 25.4 us -> 23.5 us  [widened(): inner = lax.ppermute(block, LON, swaps(count, 0))]
    ppermute x3, starting transfers between devices: 8.56 us -> 9.87 us  [widened(): outer = lax.ppermute(block, LON, swaps(count, 1))]
    pallas_call x6 -> x9, Pallas kernels: 5.67 us -> 6.05 us  [the longest x3 4.17 us: build(): pl.pallas_call(functools.partial(build_kernel, steps), out_shape=shapes,...]
  transfers between devices with their start and end apart: 12 -> 13, of which waited for: 6 -> 6; matrix products, arithmetic and copies ran while one was open for 0% -> 1% of each run, Pallas kernels for 2% -> 4%
where the time goes in v4:
time: 99.1 us; the launch traced here: 98.5 us
  starting transfers between devices  57.3 us (58%)
  blocking collectives  15.7 us (16%)
  waiting for transfers between devices  15.6 us (16%)
  Pallas kernels  6.99 us (7%)
  other arithmetic  1.21 us (1%)
    ppermute x3, starting transfers between devices, widened(): inner = lax.ppermute(block, LON, swaps(count, 0))  23.5 us
    all_to_all x1, blocking collectives, global_sum(): value = jnp.sum(lax.all_to_all(spread_out, axes, 0, 0), axis=0)  15.7 us
    ppermute x3, starting transfers between devices, all_bands(): below = lax.ppermute(wide, LAT, [(i, i + 1) for i in range(count - 1)])  10.8 us
    ppermute x3, starting transfers between devices, widened(): outer = lax.ppermute(block, LON, swaps(count, 1))  9.87 us
    all_to_all x1, starting transfers between devices, global_sum(): value = jnp.sum(lax.all_to_all(spread_out, axes, 0, 0), axis=0)  9.29 us
    all_to_all x1, waiting for transfers between devices, global_sum(): value = jnp.sum(lax.all_to_all(spread_out, axes, 0, 0), axis=0)  6.67 us
    ppermute x3, waiting for transfers between devices, all_bands(): above = lax.ppermute(wide, LAT, [(i + 1, i) for i in range(count - 1)])  4.17 us
    pallas_call x3, Pallas kernels, build(): pl.pallas_call(functools.partial(build_kernel, steps), out_shape=shapes,...  4.17 us
  transfers between devices with their start and end apart: 13, of which 6 were waited for; matrix products, arithmetic and copies ran while one was open for 1% of the time, Pallas kernels for 4%

profile of v4, /device:TPU:1, one launch (start us, length us, event | category | flops | bytes accessed | tf_op | source)
XLA Modules:
  0.0 98.5 jit_solution(2541729392350525523)
XLA Ops:
  0.6 0.9 describe.1
  1.6 4.6 %collective-permute-start = (bf16[32,512]{1,0:T(8,128)(2,1)S(1)}, bf16[32,512]{1,0:T(8,128)(2,1)S(1)}, u32[]{:S(2)}, u32[]{:S(2)}) collective-permute-start(bf16[32,512]{1,0:T(8,128)(2,1)S(1)} %get-tuple-element.15), channel_id=1, source_target_pairs={{1,2},{2,1},{3,4},{4,3},{5,6},{6,5},{7,8},{8,7},{9,10},{10,9},{11,... | collective-permute-start | bytes 98312 | tf_op jit(solution)/shard_map/ppermute | solution.py:49
  6.2 12.1 %collective-permute-start.1 = (bf16[32,512]{1,0:T(8,128)(2,1)S(1)}, bf16[32,512]{1,0:T(8,128)(2,1)S(1)}, u32[]{:S(2)}, u32[]{:S(2)}) collective-permute-start(bf16[32,512]{1,0:T(8,128)(2,1)S(1)} %get-tuple-element.15), channel_id=1, source_target_pairs={{0,1},{1,0},{2,3},{3,2},{4,5},{5,4},{6,7},{7,6},{8,9},{9,8},{10,11... | collective-permute-start | bytes 98312 | tf_op jit(solution)/shard_map/ppermute | solution.py:48
  18.3 0.0 collective-permute-done
  18.3 0.8 collective-permute-done.1
  19.1 3.1 %collective-permute-start.3 = (bf16[3,32,512]{2,1,0:T(8,128)(2,1)S(1)}, bf16[3,32,512]{2,1,0:T(8,128)(2,1)S(1)}, u32[]{:S(2)}, u32[]{:S(2)}) collective-permute-start(bf16[3,32,512]{2,1,0:T(8,128)(2,1)S(1)} %pad_maximum_fusion.near_ref), channel_id=1, source_target_pairs={{0,64},{64,128},{128,192},{192,256},{256,320},{320,384},{384,448},... | collective-permute-start | bytes 294920 | tf_op jit(solution)/shard_map/ppermute | solution.py:55
  22.3 1.3 %collective-permute-start.2 = (bf16[3,32,512]{2,1,0:T(8,128)(2,1)S(1)}, bf16[3,32,512]{2,1,0:T(8,128)(2,1)S(1)}, u32[]{:S(2)}, u32[]{:S(2)}) collective-permute-start(bf16[3,32,512]{2,1,0:T(8,128)(2,1)S(1)} %pad_maximum_fusion.near_ref), channel_id=1, source_target_pairs={{64,0},{128,64},{192,128},{256,192},{320,256},{384,320},{448,384},... | collective-permute-start | bytes 294920 | tf_op jit(solution)/shard_map/ppermute | solution.py:56
  23.6 1.4 %build.3 = (bf16[3,512,512]{2,1,0:T(8,128)(2,1)S(1)}, f32[16,512]{1,0:T(8,128)S(1)}) custom-call(bf16[3,32,512]{2,1,0:T(8,128)(2,1)S(1)} %pad_maximum_fusion.near_ref, bf16[3,48,512]{2,1,0:T(8,128)(2,1)S(1)} %get-tuple-element.16.own_ref, f32[16,512]{1,0:T(8,128)S(1)} %get-tuple-element.17.added_ref), custom_call_target="tpu_custom_call" | custom-call | flops 427819008 | bytes 1572864 | tf_op jit(solution)/shard_map/build/pallas_call | solution.py:190
  25.0 0.0 collective-permute-done.3.near_ref
  25.0 1.4 %build.4 = (bf16[3,512,512]{2,1,0:T(8,128)(2,1)S(1)}, f32[16,512]{1,0:T(8,128)S(1)}) custom-call(bf16[3,32,512]{2,1,0:T(8,128)(2,1)S(1)} %collective-permute-done.3.near_ref, bf16[3,48,512]{2,1,0:T(8,128)(2,1)S(1)} %get-tuple-element.16.own_ref, f32[16,512]{1,0:T(8,128)S(1)} %get-tuple-element.18.added_ref), custom_call_target="tpu_custom_call" | custom-call | flops 427819008 | bytes 1572864 | tf_op jit(solution)/shard_map/build/pallas_call | solution.py:190
  26.4 1.3 %collective-permute-done.2.near_ref = bf16[3,32,512]{2,1,0:T(8,128)(2,1)S(1)} collective-permute-done((bf16[3,32,512]{2,1,0:T(8,128)(2,1)S(1)}, bf16[3,32,512]{2,1,0:T(8,128)(2,1)S(1)}, u32[]{:S(2)}, u32[]{:S(2)}) %collective-permute-start.2) | collective-permute-done | bytes 98336 | tf_op jit(solution)/shard_map/ppermute | solution.py:56
  27.6 1.4 %build.5 = (bf16[3,512,512]{2,1,0:T(8,128)(2,1)S(1)}, f32[16,512]{1,0:T(8,128)S(1)}, bf16[16,512]{1,0:T(8,128)(2,1)S(1)}) custom-call(bf16[3,32,512]{2,1,0:T(8,128)(2,1)S(1)} %collective-permute-done.2.near_ref, bf16[3,48,512]{2,1,0:T(8,128)(2,1)S(1)} %get-tuple-element.16.own_ref, f32[16,512]{1,0:T(8,128)S(1)} %get-tuple-element.19.added_ref), custom_call_target="tpu_custom_call" | custom-call | flops 427819008 | bytes 1572864 | tf_op jit(solution)/shard_map/build/pallas_call | solution.py:190
  29.0 3.7 %collective-permute-start.5 = (bf16[16,512]{1,0:T(8,128)(2,1)S(1)}, bf16[16,512]{1,0:T(8,128)(2,1)S(1)}, u32[]{:S(2)}, u32[]{:S(2)}) collective-permute-start(bf16[16,512]{1,0:T(8,128)(2,1)S(1)} %get-tuple-element.21), channel_id=1, source_target_pairs={{0,1},{1,0},{2,3},{3,2},{4,5},{5,4},{6,7},{7,6},{8,9},{9,8},{10,11... | collective-permute-start | bytes 49160 | tf_op jit(solution)/shard_map/ppermute | solution.py:48
  32.7 1.9 %collective-permute-start.4 = (bf16[16,512]{1,0:T(8,128)(2,1)S(1)}, bf16[16,512]{1,0:T(8,128)(2,1)S(1)}, u32[]{:S(2)}, u32[]{:S(2)}) collective-permute-start(bf16[16,512]{1,0:T(8,128)(2,1)S(1)} %get-tuple-element.21), channel_id=1, source_target_pairs={{1,2},{2,1},{3,4},{4,3},{5,6},{6,5},{7,8},{8,7},{9,10},{10,9},{11,... | collective-permute-start | bytes 49160 | tf_op jit(solution)/shard_map/ppermute | solution.py:49
  34.6 0.0 collective-permute-done.5
  34.6 3.1 %collective-permute-done.4 = bf16[16,512]{1,0:T(8,128)(2,1)S(1)} collective-permute-done((bf16[16,512]{1,0:T(8,128)(2,1)S(1)}, bf16[16,512]{1,0:T(8,128)(2,1)S(1)}, u32[]{:S(2)}, u32[]{:S(2)}) %collective-permute-start.4) | collective-permute-done | bytes 16416 | tf_op jit(solution)/shard_map/ppermute | solution.py:49
  37.8 3.1 %collective-permute-start.7 = (bf16[3,16,512]{2,1,0:T(8,128)(2,1)S(1)}, bf16[3,16,512]{2,1,0:T(8,128)(2,1)S(1)}, u32[]{:S(2)}, u32[]{:S(2)}) collective-permute-start(bf16[3,16,512]{2,1,0:T(8,128)(2,1)S(1)} %pad_maximum_fusion.1.near_ref), channel_id=1, source_target_pairs={{0,64},{64,128},{128,192},{192,256},{256,320},{320,384},{384,448},... | collective-permute-start | bytes 147464 | tf_op jit(solution)/shard_map/ppermute | solution.py:55
  40.9 1.3 %collective-permute-start.6 = (bf16[3,16,512]{2,1,0:T(8,128)(2,1)S(1)}, bf16[3,16,512]{2,1,0:T(8,128)(2,1)S(1)}, u32[]{:S(2)}, u32[]{:S(2)}) collective-permute-start(bf16[3,16,512]{2,1,0:T(8,128)(2,1)S(1)} %pad_maximum_fusion.1.near_ref), channel_id=1, source_target_pairs={{64,0},{128,64},{192,128},{256,192},{320,256},{384,320},{448,384},... | collective-permute-start | bytes 147464 | tf_op jit(solution)/shard_map/ppermute | solution.py:56
  42.2 0.3 apply.6.refs_0_
  42.5 0.0 collective-permute-done.7.near_ref
  42.5 0.3 apply.7.refs_0_
  42.8 2.9 %collective-permute-done.6.near_ref = bf16[3,16,512]{2,1,0:T(8,128)(2,1)S(1)} collective-permute-done((bf16[3,16,512]{2,1,0:T(8,128)(2,1)S(1)}, bf16[3,16,512]{2,1,0:T(8,128)(2,1)S(1)}, u32[]{:S(2)}, u32[]{:S(2)}) %collective-permute-start.6) | collective-permute-done | bytes 49184 | tf_op jit(solution)/shard_map/ppermute | solution.py:56
  45.7 0.3 apply.8
  46.1 3.4 %collective-permute-start.8 = (bf16[16,512]{1,0:T(8,128)(2,1)S(1)}, bf16[16,512]{1,0:T(8,128)(2,1)S(1)}, u32[]{:S(2)}, u32[]{:S(2)}) collective-permute-start(bf16[16,512]{1,0:T(8,128)(2,1)S(1)} %get-tuple-element.27), channel_id=1, source_target_pairs={{1,2},{2,1},{3,4},{4,3},{5,6},{6,5},{7,8},{8,7},{9,10},{10,9},{11,... | collective-permute-start | bytes 49160 | tf_op jit(solution)/shard_map/ppermute | solution.py:49
  49.4 7.7 %collective-permute-start.9 = (bf16[16,512]{1,0:T(8,128)(2,1)S(1)}, bf16[16,512]{1,0:T(8,128)(2,1)S(1)}, u32[]{:S(2)}, u32[]{:S(2)}) collective-permute-start(bf16[16,512]{1,0:T(8,128)(2,1)S(1)} %get-tuple-element.27), channel_id=1, source_target_pairs={{0,1},{1,0},{2,3},{3,2},{4,5},{5,4},{6,7},{7,6},{8,9},{9,8},{10,11... | collective-permute-start | bytes 49160 | tf_op jit(solution)/shard_map/ppermute | solution.py:48
  57.1 0.0 collective-permute-done.8
  57.1 0.8 collective-permute-done.9
  57.9 4.6 %collective-permute-start.10 = (bf16[3,16,512]{2,1,0:T(8,128)(2,1)S(1)}, bf16[3,16,512]{2,1,0:T(8,128)(2,1)S(1)}, u32[]{:S(2)}, u32[]{:S(2)}) collective-permute-start(bf16[3,16,512]{2,1,0:T(8,128)(2,1)S(1)} %pad_maximum_fusion.2.near_ref), channel_id=1, source_target_pairs={{0,64},{64,128},{128,192},{192,256},{256,320},{320,384},{384,448},... | collective-permute-start | bytes 147464 | tf_op jit(solution)/shard_map/ppermute | solution.py:55
  62.5 1.3 %collective-permute-start.11 = (bf16[3,16,512]{2,1,0:T(8,128)(2,1)S(1)}, bf16[3,16,512]{2,1,0:T(8,128)(2,1)S(1)}, u32[]{:S(2)}, u32[]{:S(2)}) collective-permute-start(bf16[3,16,512]{2,1,0:T(8,128)(2,1)S(1)} %pad_maximum_fusion.2.near_ref), channel_id=1, source_target_pairs={{64,0},{128,64},{192,128},{256,192},{320,256},{384,320},{448,384},... | collective-permute-start | bytes 147464 | tf_op jit(solution)/shard_map/ppermute | solution.py:56
  63.8 0.0 copy-start
  63.9 0.3 apply.9.refs_0_
  64.2 0.0 collective-permute-done.10.near_ref
  64.2 0.3 apply.10.refs_0_
  64.5 0.1 copy-done
  64.6 0.2 multiply_reduce_fusion
  64.8 0.1 concatenate.3
  64.9 15.7 %all_to_all.10 = f32[32,1,128]{2,1,0:T(1,128)S(1)} all-to-all(f32[32,1,128]{2,1,0:T(1,128)S(1)} %broadcast_in_dim.8), channel_id=1, replica_groups=mesh['z_lo'=2,'x'=4,'z_hi'=4,'y'=8,'core'=2] {'z_lo','z_hi','x'}, dimensions={0} | all-to-all | bytes 32768 | tf_op jit(solution)/shard_map/all_to_all | solution.py:252
  80.6 0.6 broadcast_in_dim.9
  81.2 9.3 %all-to-all-start.1 = ((f32[16,1,128]{2,1,0:T(1,128)}), f32[16,1,128]{2,1,0:T(1,128)S(1)}, u32[]{:S(2)}, u32[]{:S(2)}) async-start(f32[16,1,128]{2,1,0:T(1,128)} %broadcast_in_dim.9), calls=%async_computation.1 | async-start | bytes 16384 | tf_op jit(solution)/shard_map/all_to_all | solution.py:252
  90.5 0.0 collective-permute-done.11.near_ref
  90.5 0.3 apply.11
  90.8 6.7 %all-to-all-done.1 = f32[16,1,128]{2,1,0:T(1,128)S(1)} async-done(((f32[16,1,128]{2,1,0:T(1,128)}), f32[16,1,128]{2,1,0:T(1,128)S(1)}, u32[]{:S(2)}, u32[]{:S(2)}) %all-to-all-start.1) | async-done | bytes 8224 | tf_op jit(solution)/shard_map/all_to_all | solution.py:252
  97.5 0.1 fusion.3
  97.6 0.1 multiply_add_fusion.1
  97.7 0.7 add_bitcast_fusion
  (8 shorter events, 0.1 us)
Async XLA Ops:
  1.6 16.7 %collective-permute-start = (bf16[32,512]{1,0:T(8,128)(2,1)S(1)}, bf16[32,512]{1,0:T(8,128)(2,1)S(1)}, u32[]{:S(2)}, u32[]{:S(2)}) collective-permute-start(bf16[32,512]{1,0:T(8,128)(2,1)S(1)} %get-tuple-element.15), channel_id=1, source_target_pairs={{1,2},{2,1},{3,4},{4,3},{5,6},{6,5},{7,8},{8,7},{9,10},{10,9},{11,... | collective-permute-start | bytes 98312 | tf_op jit(solution)/shard_map/ppermute | solution.py:49
  6.2 12.9 %collective-permute-start.1 = (bf16[32,512]{1,0:T(8,128)(2,1)S(1)}, bf16[32,512]{1,0:T(8,128)(2,1)S(1)}, u32[]{:S(2)}, u32[]{:S(2)}) collective-permute-start(bf16[32,512]{1,0:T(8,128)(2,1)S(1)} %get-tuple-element.15), channel_id=1, source_target_pairs={{0,1},{1,0},{2,3},{3,2},{4,5},{5,4},{6,7},{7,6},{8,9},{9,8},{10,11... | collective-permute-start | bytes 98312 | tf_op jit(solution)/shard_map/ppermute | solution.py:48
  19.1 5.8 %collective-permute-start.3 = (bf16[3,32,512]{2,1,0:T(8,128)(2,1)S(1)}, bf16[3,32,512]{2,1,0:T(8,128)(2,1)S(1)}, u32[]{:S(2)}, u32[]{:S(2)}) collective-permute-start(bf16[3,32,512]{2,1,0:T(8,128)(2,1)S(1)} %pad_maximum_fusion.near_ref), channel_id=1, source_target_pairs={{0,64},{64,128},{128,192},{192,256},{256,320},{320,384},{384,448},... | collective-permute-start | bytes 294920 | tf_op jit(solution)/shard_map/ppermute | solution.py:55
  22.3 5.4 %collective-permute-start.2 = (bf16[3,32,512]{2,1,0:T(8,128)(2,1)S(1)}, bf16[3,32,512]{2,1,0:T(8,128)(2,1)S(1)}, u32[]{:S(2)}, u32[]{:S(2)}) collective-permute-start(bf16[3,32,512]{2,1,0:T(8,128)(2,1)S(1)} %pad_maximum_fusion.near_ref), channel_id=1, source_target_pairs={{64,0},{128,64},{192,128},{256,192},{320,256},{384,320},{448,384},... | collective-permute-start | bytes 294920 | tf_op jit(solution)/shard_map/ppermute | solution.py:56
  29.0 5.6 %collective-permute-start.5 = (bf16[16,512]{1,0:T(8,128)(2,1)S(1)}, bf16[16,512]{1,0:T(8,128)(2,1)S(1)}, u32[]{:S(2)}, u32[]{:S(2)}) collective-permute-start(bf16[16,512]{1,0:T(8,128)(2,1)S(1)} %get-tuple-element.21), channel_id=1, source_target_pairs={{0,1},{1,0},{2,3},{3,2},{4,5},{5,4},{6,7},{7,6},{8,9},{9,8},{10,11... | collective-permute-start | bytes 49160 | tf_op jit(solution)/shard_map/ppermute | solution.py:48
  32.7 5.1 %collective-permute-start.4 = (bf16[16,512]{1,0:T(8,128)(2,1)S(1)}, bf16[16,512]{1,0:T(8,128)(2,1)S(1)}, u32[]{:S(2)}, u32[]{:S(2)}) collective-permute-start(bf16[16,512]{1,0:T(8,128)(2,1)S(1)} %get-tuple-element.21), channel_id=1, source_target_pairs={{1,2},{2,1},{3,4},{4,3},{5,6},{6,5},{7,8},{8,7},{9,10},{10,9},{11,... | collective-permute-start | bytes 49160 | tf_op jit(solution)/shard_map/ppermute | solution.py:49
  37.8 4.7 %collective-permute-start.7 = (bf16[3,16,512]{2,1,0:T(8,128)(2,1)S(1)}, bf16[3,16,512]{2,1,0:T(8,128)(2,1)S(1)}, u32[]{:S(2)}, u32[]{:S(2)}) collective-permute-start(bf16[3,16,512]{2,1,0:T(8,128)(2,1)S(1)} %pad_maximum_fusion.1.near_ref), channel_id=1, source_target_pairs={{0,64},{64,128},{128,192},{192,256},{256,320},{320,384},{384,448},... | collective-permute-start | bytes 147464 | tf_op jit(solution)/shard_map/ppermute | solution.py:55
  40.9 4.8 %collective-permute-start.6 = (bf16[3,16,512]{2,1,0:T(8,128)(2,1)S(1)}, bf16[3,16,512]{2,1,0:T(8,128)(2,1)S(1)}, u32[]{:S(2)}, u32[]{:S(2)}) collective-permute-start(bf16[3,16,512]{2,1,0:T(8,128)(2,1)S(1)} %pad_maximum_fusion.1.near_ref), channel_id=1, source_target_pairs={{64,0},{128,64},{192,128},{256,192},{320,256},{384,320},{448,384},... | collective-permute-start | bytes 147464 | tf_op jit(solution)/shard_map/ppermute | solution.py:56
  46.1 11.1 %collective-permute-start.8 = (bf16[16,512]{1,0:T(8,128)(2,1)S(1)}, bf16[16,512]{1,0:T(8,128)(2,1)S(1)}, u32[]{:S(2)}, u32[]{:S(2)}) collective-permute-start(bf16[16,512]{1,0:T(8,128)(2,1)S(1)} %get-tuple-element.27), channel_id=1, source_target_pairs={{1,2},{2,1},{3,4},{4,3},{5,6},{6,5},{7,8},{8,7},{9,10},{10,9},{11,... | collective-permute-start | bytes 49160 | tf_op jit(solution)/shard_map/ppermute | solution.py:49
  49.4 8.5 %collective-permute-start.9 = (bf16[16,512]{1,0:T(8,128)(2,1)S(1)}, bf16[16,512]{1,0:T(8,128)(2,1)S(1)}, u32[]{:S(2)}, u32[]{:S(2)}) collective-permute-start(bf16[16,512]{1,0:T(8,128)(2,1)S(1)} %get-tuple-element.27), channel_id=1, source_target_pairs={{0,1},{1,0},{2,3},{3,2},{4,5},{5,4},{6,7},{7,6},{8,9},{9,8},{10,11... | collective-permute-start | bytes 49160 | tf_op jit(solution)/shard_map/ppermute | solution.py:48
  57.9 6.2 %collective-permute-start.10 = (bf16[3,16,512]{2,1,0:T(8,128)(2,1)S(1)}, bf16[3,16,512]{2,1,0:T(8,128)(2,1)S(1)}, u32[]{:S(2)}, u32[]{:S(2)}) collective-permute-start(bf16[3,16,512]{2,1,0:T(8,128)(2,1)S(1)} %pad_maximum_fusion.2.near_ref), channel_id=1, source_target_pairs={{0,64},{64,128},{128,192},{192,256},{256,320},{320,384},{384,448},... | collective-permute-start | bytes 147464 | tf_op jit(solution)/shard_map/ppermute | solution.py:55
  62.5 28.0 %collective-permute-start.11 = (bf16[3,16,512]{2,1,0:T(8,128)(2,1)S(1)}, bf16[3,16,512]{2,1,0:T(8,128)(2,1)S(1)}, u32[]{:S(2)}, u32[]{:S(2)}) collective-permute-start(bf16[3,16,512]{2,1,0:T(8,128)(2,1)S(1)} %pad_maximum_fusion.2.near_ref), channel_id=1, source_target_pairs={{64,0},{128,64},{192,128},{256,192},{320,256},{384,320},{448,384},... | collective-permute-start | bytes 147464 | tf_op jit(solution)/shard_map/ppermute | solution.py:56
  63.8 0.8 copy-start
  81.2 16.3 %all-to-all-start.1 = ((f32[16,1,128]{2,1,0:T(1,128)}), f32[16,1,128]{2,1,0:T(1,128)S(1)}, u32[]{:S(2)}, u32[]{:S(2)}) async-start(f32[16,1,128]{2,1,0:T(1,128)} %broadcast_in_dim.9), calls=%async_computation.1 | async-start | bytes 16384 | tf_op jit(solution)/shard_map/all_to_all | solution.py:252

commit v5 on v4

--- a/solution.py
+++ b/solution.py
@@ -35,18 +35,20 @@
     return size
 
 
-def swaps(count, first):
-    pairs = []
-    for low in range(first, count + first - 1, 2):
-        high = (low + 1) % count
-        pairs += [(low, high), (high, low)]
-    return pairs
+def pairs(count, first):
+    return [[low, (low + 1) % count] for low in range(first, count, 2)]
+
+
+def partner(block, axes, first):
+    both = lax.all_gather(block, axes, axis_index_groups=pairs(extent(axes), first))
+    leads = lax.axis_index(axes) % 2 == first
+    return jnp.where(leads, both[1], both[0])
 
 
 def widened(block):
-    count = extent(LON)
-    inner = lax.ppermute(block, LON, swaps(count, 0))
-    outer = lax.ppermute(block, LON, swaps(count, 1))
+    inner = partner(block, LON, 0)
+    inner, block = lax.optimization_barrier((inner, block))
+    outer = partner(block, LON, 1)
     return jnp.stack([outer, block, inner])
 
 
@@ -57,6 +59,16 @@
     return below, above
 
 
+def all_bands_paired(wide):
+    count = extent(LAT)
+    band = lax.axis_index(LAT)
+    inner = lax.ppermute(wide, LAT, [p for a, b in pairs(count, 0) for p in ((a, b), (b, a))])
+    outer = partner(wide, LAT, 1)
+    outer = jnp.where((band == 0) | (band == count - 1), jnp.zeros_like(outer), outer)
+    odd = band % 2 == 1
+    return jnp.where(odd, inner, outer), jnp.where(odd, outer, inner)
+
+
 def rounded(value):
     return value.astype(jnp.bfloat16).astype(jnp.float32)
 
@@ -69,7 +81,7 @@
 
 def describe_kernel(
     start_ref, error_ref, frac_ref, spread_ref, type_ref,
-    message_ref, own_ref, error_out_ref, added_ref, far_rows, own_rows,
+    message_ref, own_ref, error_out_ref, added_ref, kept_ref, far_rows, own_rows,
 ):
     frac = frac_ref[...].astype(jnp.float32)
     latitude = (lax.axis_index(LAT).astype(jnp.float32) + frac[0:1]) * (2.0 * LAT_LIMIT / BANDS) - LAT_LIMIT
@@ -102,6 +114,7 @@
     message_ref[0:16, :] = start_ref[...].astype(jnp.bfloat16)
     message_ref[16:32, :] = far_rows[...].astype(jnp.bfloat16)
     error_out_ref[...] = error_ref[...]
+    kept_ref[...] = start_ref[...]
     added_ref[...] = error_ref[...] * start_ref[...]
     for step in range(3):
         if step:
@@ -125,9 +138,10 @@
             pltpu.VMEM((3, 48, OBS), jnp.bfloat16),
             pltpu.VMEM((1, OBS), jnp.float32),
             pltpu.VMEM((RHS, OBS), jnp.float32),
+            pltpu.VMEM((RHS, OBS), jnp.float32),
         ),
         in_specs=[whole()] * 5,
-        out_specs=[whole()] * 4,
+        out_specs=[whole()] * 5,
         scratch_shapes=[pltpu.VMEM((16, OBS), jnp.float32)] * 2,
         name="describe",
     )(start, error_var, where_frac, spread, obs_type)
@@ -212,47 +226,6 @@
     )(near, tiles, added, *scales)
 
 
-def local(innovations, obs_error, where_frac, spread, obs_type):
-    start = innovations[0, 0]
-    message, own, error_var, added = describe(start, obs_error[0], where_frac[0, 0], spread[0], obs_type[0])
-    wide = widened(message)
-    below, above = all_bands(wide)
-    tiles, part = build(SAME_BAND, wide, own, added)
-    tiles_below, part = build(OTHER_BAND, below, own, part)
-    tiles_above, first, sent = build(OTHER_BAND, above, own, part, True)
-    wide = widened(sent)
-    below, above = all_bands(wide)
-    part, = apply(wide, tiles, first, error_var)
-    part, = apply(below, tiles_below, part)
-    second, sent = apply(above, tiles_above, part, last=True)
-    wide = widened(sent)
-    below, above = all_bands(wide)
-    part, = apply(wide, tiles, second, error_var)
-    lower, = apply(below, tiles_below, part)
-    basis = [start, first, second]
-    products = [start * start, start * first, first * first, start * second, first * second, second * second]
-    products.append(second * (2.0 * lower - part))
-    parts = [jnp.sum(product, axis=1) for product in products]
-    parts.append(jnp.zeros_like(parts[0]))
-    totals = global_sum(jnp.concatenate(parts).reshape(1, 128)).reshape(8, 16)
-    third, = apply(above, tiles_above, lower)
-    basis.append(third)
-    names = {(0, 0): 0, (0, 1): 1, (1, 1): 2, (0, 2): 3, (1, 2): 4, (2, 2): 5, (2, 3): 6, (0, 3): 4, (1, 3): 5}
-    gram = {pair: totals[at] for pair, at in names.items()}
-    answer, residual = coefficients(gram)
-    answer = sum(c[:, None] * v for c, v in zip(answer, basis))
-    residual = sum(c[:, None] * v for c, v in zip(residual, basis))
-    return (answer[None, None], residual[None, None])
-
-
-def global_sum(value):
-    for axes in GROUPS:
-        count = extent(axes)
-        spread_out = jnp.broadcast_to(value, (count,) + value.shape)
-        value = jnp.sum(lax.all_to_all(spread_out, axes, 0, 0), axis=0)
-    return value
-
-
 def coefficients(gram):
     def inner(left, right):
         total = 0.0
@@ -288,6 +261,118 @@
     return answer[:3], residual
 
 
+def lane_sums(products):
+    empty = jnp.zeros((128 - RHS * len(products), OBS), jnp.float32)
+    stacked = jnp.concatenate([*products, empty], axis=0) if len(products) < 8 else jnp.concatenate(products, axis=0)
+    ones = jnp.ones((8, OBS), jnp.bfloat16)
+    total = 0.0
+    for part in pieces(stacked):
+        total = total + lax.dot_general(
+            ones, part.astype(jnp.bfloat16), (((1,), (1,)), ((), ())), preferred_element_type=jnp.float32
+        )
+    return total[0:1]
+
+
+MOMENTS = 6
+
+
+def same_band_kernel(near_ref, tile_ref, second_ref, scale_ref, start_ref, first_ref, sum_ref, row_ref):
+    start, first, second = start_ref[...], first_ref[...], second_ref[...]
+    total = second * scale_ref[...]
+    for slot in range(3):
+        total = total + jnp.dot(near_ref[slot], tile_ref[slot], preferred_element_type=jnp.float32)
+    sum_ref[...] = total
+    row_ref[...] = lane_sums(
+        [start * start, start * first, first * first, start * second, first * second, second * second]
+    )
+
+
+def below_kernel(near_ref, tile_ref, part_ref, second_ref, row_ref, sum_ref, copies_ref):
+    part = part_ref[...]
+    total = part
+    for slot in range(3):
+        total = total + jnp.dot(near_ref[slot], tile_ref[slot], preferred_element_type=jnp.float32)
+    sum_ref[...] = total
+    product = second_ref[...] * (2.0 * total - part)
+    before = [jnp.zeros_like(product)] * MOMENTS
+    row = row_ref[...] + lane_sums([*before, product])
+    copies_ref[...] = jnp.broadcast_to(row[None], copies_ref.shape)
+
+
+def finish_kernel(
+    total_ref, near_ref, tile_ref, lower_ref, start_ref, first_ref, second_ref, answer_ref, residual_ref
+):
+    totals = jnp.broadcast_to(jnp.sum(total_ref[...], axis=0), (RHS, 128))
+    lane = lax.broadcasted_iota(jnp.int32, (RHS, 128), 1)
+    row = lax.broadcasted_iota(jnp.int32, (RHS, 128), 0)
+    moments = [
+        jnp.sum(jnp.where(lane == row + RHS * at, totals, 0.0), axis=1, keepdims=True) for at in range(MOMENTS + 1)
+    ]
+    names = {(0, 0): 0, (0, 1): 1, (1, 1): 2, (0, 2): 3, (1, 2): 4, (2, 2): 5, (2, 3): 6, (0, 3): 4, (1, 3): 5}
+    answer, residual = coefficients({pair: moments[at] for pair, at in names.items()})
+    third = lower_ref[...]
+    for slot in range(3):
+        third = third + jnp.dot(near_ref[slot], tile_ref[slot], preferred_element_type=jnp.float32)
+    basis = (start_ref[...], first_ref[...], second_ref[...], third)
+    answer_ref[0, 0] = sum(c * v for c, v in zip(answer, basis))
+    residual_ref[0, 0] = sum(c * v for c, v in zip(residual, basis))
+
+
+def call(kernel, shapes, operands, name):
+    return pl.pallas_call(
+        kernel,
+        out_shape=shapes,
+        in_specs=[whole()] * len(operands),
+        out_specs=[whole()] * len(shapes),
+        compiler_params=pltpu.CompilerParams(vmem_limit_bytes=16 << 20),
+        cost_estimate=cost(0),
+        name=name,
+    )(*operands)
+
+
+def global_sum(copies):
+    for at, axes in enumerate(GROUPS):
+        if at:
+            copies = jnp.broadcast_to(jnp.sum(copies, axis=0), (extent(axes),) + copies.shape[1:])
+        copies = lax.all_to_all(copies, axes, 0, 0)
+    return copies
+
+
+def local(innovations, obs_error, where_frac, spread, obs_type):
+    message, own, error_var, added, start = describe(
+        innovations[0, 0], obs_error[0], where_frac[0, 0], spread[0], obs_type[0]
+    )
+    wide = widened(message)
+    below, above = all_bands(wide)
+    tiles, part = build(SAME_BAND, wide, own, added)
+    tiles_below, part = build(OTHER_BAND, below, own, part)
+    tiles_above, first, sent = build(OTHER_BAND, above, own, part, True)
+    wide = widened(sent)
+    below, above = all_bands_paired(wide)
+    part, = apply(wide, tiles, first, error_var)
+    part, = apply(below, tiles_below, part)
+    second, sent = apply(above, tiles_above, part, last=True)
+    wide = widened(sent)
+    below, above = all_bands(wide)
+    field = pltpu.VMEM((RHS, OBS), jnp.float32)
+    part, row = call(
+        same_band_kernel,
+        [field, pltpu.VMEM((1, 128), jnp.float32)],
+        [wide, tiles, second, error_var, start, first],
+        "same_band",
+    )
+    copies = pltpu.VMEM((extent(GROUPS[0]), 1, 128), jnp.float32)
+    lower, copies = call(below_kernel, [field, copies], [below, tiles_below, part, second, row], "below")
+    totals = global_sum(copies)
+    whole_field = jax.ShapeDtypeStruct((1, 1, RHS, OBS), jnp.float32)
+    return call(
+        finish_kernel,
+        [whole_field] * 2,
+        [totals, above, tiles_above, lower, start, first, second],
+        "finish",
+    )
+
+
 def solution(mesh):
     fine = Mesh(mesh.devices.reshape(2, 4, 4, 8, 2), LAT + LON)
     in_specs = (

time: 99.1 us -> 99.5 us (level)
  blocking collectives: 15.7 us -> 61.1 us
  starting transfers between devices: 57.3 us -> 18.8 us
  waiting for transfers between devices: 15.6 us -> 8.26 us
  local copies, waits for them, and re-layouts: 0.82 us -> 2.02 us
  other arithmetic: 1.21 us -> 0.14 us
    all_gather x0 -> x7, blocking collectives: none -> 43.4 us  [partner(): lax.all_gather(block, axes, axis_index_groups=pairs(extent(axes), first))]
    ppermute x6 -> x1, starting transfers between devices: 33.3 us -> 3.12 us  [all_bands_paired(): lax.ppermute(wide, LAT, [p for a, b in pairs(count, 0) for p in ((a, b),...]
    ppermute x3 -> x2, starting transfers between devices: 10.8 us -> 3.31 us  [all_bands(): below = lax.ppermute(wide, LAT, [(i, i + 1) for i in range(count - 1)])]
    ppermute x6 -> x1, waiting for transfers between devices: 4.76 us -> 0.01 us  [all_bands_paired(): lax.ppermute(wide, LAT, [p for a, b in pairs(count, 0) for p in ((a, b),...]
    ppermute x3 -> x2, waiting for transfers between devices: 4.17 us -> 1.27 us  [all_bands(): above = lax.ppermute(wide, LAT, [(i + 1, i) for i in range(count - 1)])]
    all_to_all x1, blocking collectives: 15.7 us -> 17.7 us  [global_sum(): copies = lax.all_to_all(copies, axes, 0, 0)]
    pallas_call x0 -> x3, Pallas kernels: none -> 1.86 us  [call(): pl.pallas_call(kernel, out_shape=shapes, in_specs=[whole()] * len(operand...]
    ppermute x3 -> x2, starting transfers between devices: 3.88 us -> 2.58 us  [all_bands(): above = lax.ppermute(wide, LAT, [(i + 1, i) for i in range(count - 1)])]
  transfers between devices with their start and end apart: 13 -> 6, of which waited for: 6 -> 2; matrix products, arithmetic and copies ran while one was open for 1% -> 1% of each run, Pallas kernels for 4% -> 4%
where the time goes in v5:
time: 99.5 us; the launch traced here: 99.1 us
  blocking collectives  61.1 us (61%)
  starting transfers between devices  18.8 us (19%)
  waiting for transfers between devices  8.26 us (8%)
  Pallas kernels  7.91 us (8%)
  local copies, waits for them, and re-layouts  2.02 us (2%)
    all_gather x7, blocking collectives, partner(): lax.all_gather(block, axes, axis_index_groups=pairs(extent(axes), first))  43.4 us
    all_to_all x1, blocking collectives, global_sum(): copies = lax.all_to_all(copies, axes, 0, 0)  17.7 us
    all_to_all x1, starting transfers between devices, global_sum(): copies = lax.all_to_all(copies, axes, 0, 0)  9.83 us
    all_to_all x1, waiting for transfers between devices, global_sum(): copies = lax.all_to_all(copies, axes, 0, 0)  6.98 us
    pallas_call x3, Pallas kernels, build(): pl.pallas_call(functools.partial(build_kernel, steps), out_shape=shapes,...  4.18 us
    ppermute x2, starting transfers between devices, all_bands(): below = lax.ppermute(wide, LAT, [(i, i + 1) for i in range(count - 1)])  3.31 us
    ppermute x1, starting transfers between devices, all_bands_paired(): lax.ppermute(wide, LAT, [p for a, b in pairs(count, 0) for p in ((a, b),...  3.12 us
    ppermute x2, starting transfers between devices, all_bands(): above = lax.ppermute(wide, LAT, [(i + 1, i) for i in range(count - 1)])  2.58 us
  transfers between devices with their start and end apart: 6, of which 2 were waited for; matrix products, arithmetic and copies ran while one was open for 1% of the time, Pallas kernels for 4%

profile of v5, /device:TPU:1, one launch (start us, length us, event | category | flops | bytes accessed | tf_op | source)
XLA Modules:
  0.0 99.1 jit_solution(9898987216085263231)
XLA Ops:
  0.7 0.9 describe.1
  1.6 8.4 %all-gather = bf16[64,512]{1,0:T(8,128)(2,1)S(1)} all-gather(bf16[32,512]{1,0:T(8,128)(2,1)S(1)} %get-tuple-element.27), channel_id=2, replica_groups={{0,1},{2,3},{4,5},{6,7},{8,9},{10,11},{12,13},{14,15},{16,17},{18,19},{..., dimensions={0}, use_global_device_ids=true | all-gather | bytes 98304 | tf_op jit(solution)/shard_map/all_gather | solution.py:43
  10.0 4.0 %all-gather.1 = bf16[64,512]{1,0:T(8,128)(2,1)S(1)} all-gather(bf16[32,512]{1,0:T(8,128)(2,1)S(1)} %get-tuple-element.27), channel_id=3, replica_groups={{1,2},{3,4},{5,6},{7,8},{9,10},{11,12},{13,14},{15,16},{17,18},{19,20},..., dimensions={0}, use_global_device_ids=true | all-gather | bytes 98304 | tf_op jit(solution)/shard_map/all_gather | solution.py:43
  14.0 1.3 %collective-permute-start.1 = (bf16[3,32,512]{2,1,0:T(8,128)(2,1)S(1)}, bf16[3,32,512]{2,1,0:T(8,128)(2,1)S(1)}, u32[]{:S(2)}, u32[]{:S(2)}) collective-permute-start(bf16[3,32,512]{2,1,0:T(8,128)(2,1)S(1)} %pad_maximum_fusion.near_ref), channel_id=1, source_target_pairs={{0,64},{64,128},{128,192},{192,256},{256,320},{320,384},{384,448},... | collective-permute-start | bytes 294920 | tf_op jit(solution)/shard_map/ppermute | solution.py:57
  15.3 1.3 %collective-permute-start = (bf16[3,32,512]{2,1,0:T(8,128)(2,1)S(1)}, bf16[3,32,512]{2,1,0:T(8,128)(2,1)S(1)}, u32[]{:S(2)}, u32[]{:S(2)}) collective-permute-start(bf16[3,32,512]{2,1,0:T(8,128)(2,1)S(1)} %pad_maximum_fusion.near_ref), channel_id=1, source_target_pairs={{64,0},{128,64},{192,128},{256,192},{320,256},{384,320},{448,384},... | collective-permute-start | bytes 294920 | tf_op jit(solution)/shard_map/ppermute | solution.py:58
  16.6 1.4 %build.3 = (bf16[3,512,512]{2,1,0:T(8,128)(2,1)S(1)}, f32[16,512]{1,0:T(8,128)S(1)}) custom-call(bf16[3,32,512]{2,1,0:T(8,128)(2,1)S(1)} %pad_maximum_fusion.near_ref, bf16[3,48,512]{2,1,0:T(8,128)(2,1)S(1)} %get-tuple-element.29.own_ref, f32[16,512]{1,0:T(8,128)S(1)} %get-tuple-element.30.added_ref), custom_call_target="tpu_custom_call" | custom-call | flops 427819008 | bytes 1572864 | tf_op jit(solution)/shard_map/build/pallas_call | solution.py:204
  18.0 0.0 copy-start
  18.0 0.0 collective-permute-done.1.near_ref
  18.0 1.4 %build.4 = (bf16[3,512,512]{2,1,0:T(8,128)(2,1)S(1)}, f32[16,512]{1,0:T(8,128)S(1)}) custom-call(bf16[3,32,512]{2,1,0:T(8,128)(2,1)S(1)} %collective-permute-done.1.near_ref, bf16[3,48,512]{2,1,0:T(8,128)(2,1)S(1)} %get-tuple-element.29.own_ref, f32[16,512]{1,0:T(8,128)S(1)} %get-tuple-element.31.added_ref), custom_call_target="tpu_custom_call" | custom-call | flops 427819008 | bytes 1572864 | tf_op jit(solution)/shard_map/build/pallas_call | solution.py:204
  19.4 1.3 %collective-permute-done.near_ref = bf16[3,32,512]{2,1,0:T(8,128)(2,1)S(1)} collective-permute-done((bf16[3,32,512]{2,1,0:T(8,128)(2,1)S(1)}, bf16[3,32,512]{2,1,0:T(8,128)(2,1)S(1)}, u32[]{:S(2)}, u32[]{:S(2)}) %collective-permute-start) | collective-permute-done | bytes 98336 | tf_op jit(solution)/shard_map/ppermute | solution.py:58
  20.7 1.4 %build.5 = (bf16[3,512,512]{2,1,0:T(8,128)(2,1)S(1)}, f32[16,512]{1,0:T(8,128)S(1)}, bf16[16,512]{1,0:T(8,128)(2,1)S(1)}) custom-call(bf16[3,32,512]{2,1,0:T(8,128)(2,1)S(1)} %collective-permute-done.near_ref, bf16[3,48,512]{2,1,0:T(8,128)(2,1)S(1)} %get-tuple-element.29.own_ref, f32[16,512]{1,0:T(8,128)S(1)} %get-tuple-element.32.added_ref), custom_call_target="tpu_custom_call" | custom-call | flops 427819008 | bytes 1572864 | tf_op jit(solution)/shard_map/build/pallas_call | solution.py:204
  22.1 0.0 copy-done
  22.1 10.0 %all-gather.2 = bf16[32,512]{1,0:T(8,128)(2,1)S(1)} all-gather(bf16[16,512]{1,0:T(8,128)(2,1)S(1)} %get-tuple-element.34), channel_id=4, replica_groups={{0,1},{2,3},{4,5},{6,7},{8,9},{10,11},{12,13},{14,15},{16,17},{18,19},{..., dimensions={0}, use_global_device_ids=true | all-gather | bytes 49152 | tf_op jit(solution)/shard_map/all_gather | solution.py:43
  32.1 3.8 %all-gather.3 = bf16[32,512]{1,0:T(8,128)(2,1)S(1)} all-gather(bf16[16,512]{1,0:T(8,128)(2,1)S(1)} %get-tuple-element.34), channel_id=5, replica_groups={{1,2},{3,4},{5,6},{7,8},{9,10},{11,12},{13,14},{15,16},{17,18},{19,20},..., dimensions={0}, use_global_device_ids=true | all-gather | bytes 49152 | tf_op jit(solution)/shard_map/all_gather | solution.py:43
  35.9 3.1 %collective-permute-start.2 = (bf16[3,16,512]{2,1,0:T(8,128)(2,1)S(1)}, bf16[3,16,512]{2,1,0:T(8,128)(2,1)S(1)}, u32[]{:S(2)}, u32[]{:S(2)}) collective-permute-start(bf16[3,16,512]{2,1,0:T(8,128)(2,1)S(1)} %pad_maximum_fusion.1.near_ref), channel_id=1, source_target_pairs={{0,64},{64,0},{128,192},{192,128},{256,320},{320,256},{384,448},{4... | collective-permute-start | bytes 147464 | tf_op jit(solution)/shard_map/ppermute | solution.py:65
  39.1 0.0 copy-start.1
  39.1 1.4 %copy-done.1 = bf16[3,512,512]{2,1,0:T(8,128)(2,1)S(1)} copy-done((bf16[3,512,512]{2,1,0:T(8,128)(2,1)S(1)}, bf16[3,512,512]{2,1,0:T(8,128)(2,1)}, u32[]{:S(2)}) %copy-start.1) | copy-done | bytes 1572888
  40.5 0.3 apply.3.refs_0_
  40.8 5.7 %all-gather.4 = bf16[6,16,512]{2,1,0:T(8,128)(2,1)S(1)} all-gather(bf16[3,16,512]{2,1,0:T(8,128)(2,1)S(1)} %pad_maximum_fusion.1.near_ref), channel_id=6, replica_groups={{64,128},{192,256},{320,384},{448,0},{65,129},{193,257},{321,385},{449,..., dimensions={0}, use_global_device_ids=true | all-gather | bytes 147456 | tf_op jit(solution)/shard_map/all_gather | solution.py:43
  46.5 0.0 collective-permute-done.2
  46.5 0.0 copy-start.2
  46.5 0.3 apply.4.refs_0_
  46.9 0.3 apply.5
  47.2 7.6 %all-gather.5 = bf16[32,512]{1,0:T(8,128)(2,1)S(1)} all-gather(bf16[16,512]{1,0:T(8,128)(2,1)S(1)} %get-tuple-element.42), channel_id=7, replica_groups={{0,1},{2,3},{4,5},{6,7},{8,9},{10,11},{12,13},{14,15},{16,17},{18,19},{..., dimensions={0}, use_global_device_ids=true | all-gather | bytes 49152 | tf_op jit(solution)/shard_map/all_gather | solution.py:43
  54.8 3.8 %all-gather.6 = bf16[32,512]{1,0:T(8,128)(2,1)S(1)} all-gather(bf16[16,512]{1,0:T(8,128)(2,1)S(1)} %get-tuple-element.42), channel_id=8, replica_groups={{1,2},{3,4},{5,6},{7,8},{9,10},{11,12},{13,14},{15,16},{17,18},{19,20},..., dimensions={0}, use_global_device_ids=true | all-gather | bytes 49152 | tf_op jit(solution)/shard_map/all_gather | solution.py:43
  58.7 2.0 %collective-permute-start.3 = (bf16[3,16,512]{2,1,0:T(8,128)(2,1)S(1)}, bf16[3,16,512]{2,1,0:T(8,128)(2,1)S(1)}, u32[]{:S(2)}, u32[]{:S(2)}) collective-permute-start(bf16[3,16,512]{2,1,0:T(8,128)(2,1)S(1)} %pad_maximum_fusion.2.near_ref), channel_id=1, source_target_pairs={{0,64},{64,128},{128,192},{192,256},{256,320},{320,384},{384,448},... | collective-permute-start | bytes 147464 | tf_op jit(solution)/shard_map/ppermute | solution.py:57
  60.7 1.3 %collective-permute-start.4 = (bf16[3,16,512]{2,1,0:T(8,128)(2,1)S(1)}, bf16[3,16,512]{2,1,0:T(8,128)(2,1)S(1)}, u32[]{:S(2)}, u32[]{:S(2)}) collective-permute-start(bf16[3,16,512]{2,1,0:T(8,128)(2,1)S(1)} %pad_maximum_fusion.2.near_ref), channel_id=1, source_target_pairs={{64,0},{128,64},{192,128},{256,192},{320,256},{384,320},{448,384},... | collective-permute-start | bytes 147464 | tf_op jit(solution)/shard_map/ppermute | solution.py:58
  62.0 0.0 copy-done.2
  62.0 0.4 same_band.1
  62.4 0.0 collective-permute-done.3.near_ref
  62.4 0.5 below.1
  63.0 17.7 %all_to_all.10 = f32[32,1,128]{2,1,0:T(1,128)S(1)} all-to-all(f32[32,1,128]{2,1,0:T(1,128)S(1)} %get-tuple-element.48), channel_id=1, replica_groups=mesh['z_lo'=2,'x'=4,'z_hi'=4,'y'=8,'core'=2] {'z_lo','z_hi','x'}, dimensions={0} | all-to-all | bytes 32768 | tf_op jit(solution)/shard_map/all_to_all | solution.py:337
  80.7 0.1 reduce_sum.9
  80.7 0.6 broadcast_in_dim.7
  81.3 9.8 %all-to-all-start.1 = ((f32[16,1,128]{2,1,0:T(1,128)}), f32[16,1,128]{2,1,0:T(1,128)S(1)}, u32[]{:S(2)}, u32[]{:S(2)}) async-start(f32[16,1,128]{2,1,0:T(1,128)} %broadcast_in_dim.7), calls=%async_computation.1 | async-start | bytes 16384 | tf_op jit(solution)/shard_map/all_to_all | solution.py:337
  91.2 0.0 collective-permute-done.4.near_ref
  91.2 7.0 %all-to-all-done.1.total_ref = f32[16,1,128]{2,1,0:T(1,128)S(1)} async-done(((f32[16,1,128]{2,1,0:T(1,128)}), f32[16,1,128]{2,1,0:T(1,128)S(1)}, u32[]{:S(2)}, u32[]{:S(2)}) %all-to-all-start.1) | async-done | bytes 8224 | tf_op jit(solution)/shard_map/all_to_all | solution.py:337
  98.1 0.9 finish.1
  (10 shorter events, 0.1 us)
Async XLA Ops:
  14.0 4.0 %collective-permute-start.1 = (bf16[3,32,512]{2,1,0:T(8,128)(2,1)S(1)}, bf16[3,32,512]{2,1,0:T(8,128)(2,1)S(1)}, u32[]{:S(2)}, u32[]{:S(2)}) collective-permute-start(bf16[3,32,512]{2,1,0:T(8,128)(2,1)S(1)} %pad_maximum_fusion.near_ref), channel_id=1, source_target_pairs={{0,64},{64,128},{128,192},{192,256},{256,320},{320,384},{384,448},... | collective-permute-start | bytes 294920 | tf_op jit(solution)/shard_map/ppermute | solution.py:57
  15.3 5.4 %collective-permute-start = (bf16[3,32,512]{2,1,0:T(8,128)(2,1)S(1)}, bf16[3,32,512]{2,1,0:T(8,128)(2,1)S(1)}, u32[]{:S(2)}, u32[]{:S(2)}) collective-permute-start(bf16[3,32,512]{2,1,0:T(8,128)(2,1)S(1)} %pad_maximum_fusion.near_ref), channel_id=1, source_target_pairs={{64,0},{128,64},{192,128},{256,192},{320,256},{384,320},{448,384},... | collective-permute-start | bytes 294920 | tf_op jit(solution)/shard_map/ppermute | solution.py:58
  18.0 4.1 %copy-start = (bf16[3,512,512]{2,1,0:T(8,128)(2,1)}, bf16[3,512,512]{2,1,0:T(8,128)(2,1)S(1)}, u32[]{:S(2)}) copy-start(bf16[3,512,512]{2,1,0:T(8,128)(2,1)S(1)} %get-tuple-element.38.tile_ref) | copy-start | bytes 4718596
  35.9 10.6 %collective-permute-start.2 = (bf16[3,16,512]{2,1,0:T(8,128)(2,1)S(1)}, bf16[3,16,512]{2,1,0:T(8,128)(2,1)S(1)}, u32[]{:S(2)}, u32[]{:S(2)}) collective-permute-start(bf16[3,16,512]{2,1,0:T(8,128)(2,1)S(1)} %pad_maximum_fusion.1.near_ref), channel_id=1, source_target_pairs={{0,64},{64,0},{128,192},{192,128},{256,320},{320,256},{384,448},{4... | collective-permute-start | bytes 147464 | tf_op jit(solution)/shard_map/ppermute | solution.py:65
  39.1 1.4 %copy-start.1 = (bf16[3,512,512]{2,1,0:T(8,128)(2,1)S(1)}, bf16[3,512,512]{2,1,0:T(8,128)(2,1)}, u32[]{:S(2)}) copy-start(bf16[3,512,512]{2,1,0:T(8,128)(2,1)} %copy-done) | copy-start | bytes 4718596
  46.5 15.5 %copy-start.2 = (bf16[3,512,512]{2,1,0:T(8,128)(2,1)S(1)}, bf16[3,512,512]{2,1,0:T(8,128)(2,1)}, u32[]{:S(2)}) copy-start(bf16[3,512,512]{2,1,0:T(8,128)(2,1)} %copy-done) | copy-start | bytes 4718596
  58.7 3.7 %collective-permute-start.3 = (bf16[3,16,512]{2,1,0:T(8,128)(2,1)S(1)}, bf16[3,16,512]{2,1,0:T(8,128)(2,1)S(1)}, u32[]{:S(2)}, u32[]{:S(2)}) collective-permute-start(bf16[3,16,512]{2,1,0:T(8,128)(2,1)S(1)} %pad_maximum_fusion.2.near_ref), channel_id=1, source_target_pairs={{0,64},{64,128},{128,192},{192,256},{256,320},{320,384},{384,448},... | collective-permute-start | bytes 147464 | tf_op jit(solution)/shard_map/ppermute | solution.py:57
  60.7 30.5 %collective-permute-start.4 = (bf16[3,16,512]{2,1,0:T(8,128)(2,1)S(1)}, bf16[3,16,512]{2,1,0:T(8,128)(2,1)S(1)}, u32[]{:S(2)}, u32[]{:S(2)}) collective-permute-start(bf16[3,16,512]{2,1,0:T(8,128)(2,1)S(1)} %pad_maximum_fusion.2.near_ref), channel_id=1, source_target_pairs={{64,0},{128,64},{192,128},{256,192},{320,256},{384,320},{448,384},... | collective-permute-start | bytes 147464 | tf_op jit(solution)/shard_map/ppermute | solution.py:58
  81.3 16.8 %all-to-all-start.1 = ((f32[16,1,128]{2,1,0:T(1,128)}), f32[16,1,128]{2,1,0:T(1,128)S(1)}, u32[]{:S(2)}, u32[]{:S(2)}) async-start(f32[16,1,128]{2,1,0:T(1,128)} %broadcast_in_dim.7), calls=%async_computation.1 | async-start | bytes 16384 | tf_op jit(solution)/shard_map/all_to_all | solution.py:337

commit v6 on v5

--- a/solution.py
+++ b/solution.py
@@ -61,12 +61,8 @@
 
 def all_bands_paired(wide):
     count = extent(LAT)
-    band = lax.axis_index(LAT)
-    inner = lax.ppermute(wide, LAT, [p for a, b in pairs(count, 0) for p in ((a, b), (b, a))])
-    outer = partner(wide, LAT, 1)
-    outer = jnp.where((band == 0) | (band == count - 1), jnp.zeros_like(outer), outer)
-    odd = band % 2 == 1
-    return jnp.where(odd, inner, outer), jnp.where(odd, outer, inner)
+    swap = lax.ppermute(wide, LAT, [p for a, b in pairs(count, 0) for p in ((a, b), (b, a))])
+    return swap, lax.all_gather(wide, LAT, axis_index_groups=pairs(count, 1))
 
 
 def rounded(value):
@@ -147,32 +143,27 @@
     )(start, error_var, where_frac, spread, obs_type)
 
 
-CHUNK = 256
-
-
 def build_kernel(steps, near_ref, own_ref, added_ref, tile_ref, sum_ref, *sent):
-    total = added_ref[...]
     for slot, step in enumerate(steps):
-        own = own_ref[step]
-        for low in range(0, OBS, CHUNK):
-            far = near_ref[slot, 16:32, low : low + CHUNK]
-            far = jnp.concatenate([far, far, far], axis=0)
-            power = lax.dot_general(far, own, (((0,), (0,)), ((), ())), preferred_element_type=jnp.float32)
-            tile = jnp.exp2(power).astype(jnp.bfloat16)
-            tile_ref[slot, low : low + CHUNK, :] = tile
-            field = near_ref[slot, 0:16, low : low + CHUNK]
-            total = total + jnp.dot(field, tile, preferred_element_type=jnp.float32)
+        far = near_ref[slot, 16:32, :]
+        far = jnp.concatenate([far, far, far], axis=0)
+        power = lax.dot_general(far, own_ref[step], (((0,), (0,)), ((), ())), preferred_element_type=jnp.float32)
+        tile_ref[slot] = jnp.exp2(power).astype(jnp.bfloat16)
+    total = added_ref[...] + products(lambda slot: near_ref[slot, 0:16, :], tile_ref)
     sum_ref[...] = total
     for ref in sent:
         ref[...] = total.astype(jnp.bfloat16)
+
+
+def products(field_of, tile_ref):
+    return sum(jnp.dot(field_of(slot), tile_ref[slot], preferred_element_type=jnp.float32) for slot in range(3))
 
 
 def apply_kernel(scaled, near_ref, tile_ref, *refs):
     total = refs[0][...]
     if scaled:
         total = total * refs[1][...]
-    for slot in range(3):
-        total = total + jnp.dot(near_ref[slot], tile_ref[slot], preferred_element_type=jnp.float32)
+    total = total + products(lambda slot: near_ref[slot], tile_ref)
     sum_ref, *sent = refs[1 + scaled :]
     sum_ref[...] = total
     for ref in sent:
@@ -278,10 +269,7 @@
 
 def same_band_kernel(near_ref, tile_ref, second_ref, scale_ref, start_ref, first_ref, sum_ref, row_ref):
     start, first, second = start_ref[...], first_ref[...], second_ref[...]
-    total = second * scale_ref[...]
-    for slot in range(3):
-        total = total + jnp.dot(near_ref[slot], tile_ref[slot], preferred_element_type=jnp.float32)
-    sum_ref[...] = total
+    sum_ref[...] = second * scale_ref[...] + products(lambda slot: near_ref[slot], tile_ref)
     row_ref[...] = lane_sums(
         [start * start, start * first, first * first, start * second, first * second, second * second]
     )
@@ -289,9 +277,7 @@
 
 def below_kernel(near_ref, tile_ref, part_ref, second_ref, row_ref, sum_ref, copies_ref):
     part = part_ref[...]
-    total = part
-    for slot in range(3):
-        total = total + jnp.dot(near_ref[slot], tile_ref[slot], preferred_element_type=jnp.float32)
+    total = part + products(lambda slot: near_ref[slot], tile_ref)
     sum_ref[...] = total
     product = second_ref[...] * (2.0 * total - part)
     before = [jnp.zeros_like(product)] * MOMENTS
@@ -299,9 +285,31 @@
     copies_ref[...] = jnp.broadcast_to(row[None], copies_ref.shape)
 
 
-def finish_kernel(
-    total_ref, near_ref, tile_ref, lower_ref, start_ref, first_ref, second_ref, answer_ref, residual_ref
-):
+def paired_kernel(swap_ref, both_ref, below_ref, above_ref, part_ref, sum_ref, sent_ref):
+    band = lax.axis_index(LAT)
+    inside = jnp.where((band == 0) | (band == BANDS - 1), 0.0, 1.0)
+
+    def add(swap_tiles, both_tiles, position):
+        total = part_ref[...] + products(lambda slot: swap_ref[slot], swap_tiles)
+        total = total + inside * products(lambda slot: both_ref[position, slot], both_tiles)
+        sum_ref[...] = total
+        sent_ref[...] = total.astype(jnp.bfloat16)
+
+    @pl.when(band % 2 == 1)
+    def _():
+        add(below_ref, above_ref, 1)
+
+    @pl.when(band % 2 == 0)
+    def _():
+        add(above_ref, below_ref, 0)
+
+
+def above_kernel(near_ref, total_ref, tile_ref, lower_ref, third_ref, copies_ref):
+    third_ref[...] = lower_ref[...] + products(lambda slot: near_ref[slot], tile_ref)
+    copies_ref[...] = jnp.broadcast_to(jnp.sum(total_ref[...], axis=0)[None], copies_ref.shape)
+
+
+def finish_kernel(total_ref, start_ref, first_ref, second_ref, third_ref, answer_ref, residual_ref):
     totals = jnp.broadcast_to(jnp.sum(total_ref[...], axis=0), (RHS, 128))
     lane = lax.broadcasted_iota(jnp.int32, (RHS, 128), 1)
     row = lax.broadcasted_iota(jnp.int32, (RHS, 128), 0)
@@ -310,10 +318,7 @@
     ]
     names = {(0, 0): 0, (0, 1): 1, (1, 1): 2, (0, 2): 3, (1, 2): 4, (2, 2): 5, (2, 3): 6, (0, 3): 4, (1, 3): 5}
     answer, residual = coefficients({pair: moments[at] for pair, at in names.items()})
-    third = lower_ref[...]
-    for slot in range(3):
-        third = third + jnp.dot(near_ref[slot], tile_ref[slot], preferred_element_type=jnp.float32)
-    basis = (start_ref[...], first_ref[...], second_ref[...], third)
+    basis = (start_ref[...], first_ref[...], second_ref[...], third_ref[...])
     answer_ref[0, 0] = sum(c * v for c, v in zip(answer, basis))
     residual_ref[0, 0] = sum(c * v for c, v in zip(residual, basis))
 
@@ -330,14 +335,6 @@
     )(*operands)
 
 
-def global_sum(copies):
-    for at, axes in enumerate(GROUPS):
-        if at:
-            copies = jnp.broadcast_to(jnp.sum(copies, axis=0), (extent(axes),) + copies.shape[1:])
-        copies = lax.all_to_all(copies, axes, 0, 0)
-    return copies
-
-
 def local(innovations, obs_error, where_frac, spread, obs_type):
     message, own, error_var, added, start = describe(
         innovations[0, 0], obs_error[0], where_frac[0, 0], spread[0], obs_type[0]
@@ -348,29 +345,30 @@
     tiles_below, part = build(OTHER_BAND, below, own, part)
     tiles_above, first, sent = build(OTHER_BAND, above, own, part, True)
     wide = widened(sent)
-    below, above = all_bands_paired(wide)
+    swap, both = all_bands_paired(wide)
     part, = apply(wide, tiles, first, error_var)
-    part, = apply(below, tiles_below, part)
-    second, sent = apply(above, tiles_above, part, last=True)
+    field = pltpu.VMEM((RHS, OBS), jnp.float32)
+    second, sent = call(
+        paired_kernel,
+        [field, pltpu.VMEM((RHS, OBS), jnp.bfloat16)],
+        [swap, both, tiles_below, tiles_above, part],
+        "paired",
+    )
     wide = widened(sent)
     below, above = all_bands(wide)
-    field = pltpu.VMEM((RHS, OBS), jnp.float32)
     part, row = call(
         same_band_kernel,
         [field, pltpu.VMEM((1, 128), jnp.float32)],
         [wide, tiles, second, error_var, start, first],
         "same_band",
     )
-    copies = pltpu.VMEM((extent(GROUPS[0]), 1, 128), jnp.float32)
-    lower, copies = call(below_kernel, [field, copies], [below, tiles_below, part, second, row], "below")
-    totals = global_sum(copies)
+    copies = [pltpu.VMEM((extent(axes), 1, 128), jnp.float32) for axes in GROUPS]
+    lower, partial = call(below_kernel, [field, copies[0]], [below, tiles_below, part, second, row], "below")
+    partial = lax.all_to_all(partial, GROUPS[0], 0, 0)
+    third, partial = call(above_kernel, [field, copies[1]], [above, partial, tiles_above, lower], "above")
+    totals = lax.all_to_all(partial, GROUPS[1], 0, 0)
     whole_field = jax.ShapeDtypeStruct((1, 1, RHS, OBS), jnp.float32)
-    return call(
-        finish_kernel,
-        [whole_field] * 2,
-        [totals, above, tiles_above, lower, start, first, second],
-        "finish",
-    )
+    return call(finish_kernel, [whole_field] * 2, [totals, start, first, second, third], "finish")
 
 
 def solution(mesh):

time: 99.5 us -> 96.6 us (0.971)
  waiting for transfers between devices: 8.26 us -> 11 us
  local copies, waits for them, and re-layouts: 2.02 us -> 0 us
  blocking collectives: 61.1 us -> 59.4 us
  Pallas kernels: 7.91 us -> 6.75 us
    all_gather x7 -> x6, blocking collectives: 43.4 us -> 37.7 us  [partner(): lax.all_gather(block, axes, axis_index_groups=pairs(extent(axes), first))]
    all_gather x0 -> x1, blocking collectives: none -> 5.73 us  [all_bands_paired(): return (swap, lax.all_gather(wide, LAT, axis_index_groups=pairs(count, 1)))]
    pallas_call x3, Pallas kernels: 4.18 us -> 2.35 us  [build(): pl.pallas_call(functools.partial(build_kernel, steps), out_shape=shapes,...]
    all_to_all x1, blocking collectives: 17.7 us -> 16 us  [local(): totals = lax.all_to_all(partial, GROUPS[1], 0, 0)]
    all_to_all x1, waiting for transfers between devices: 6.98 us -> 8.5 us  [local(): partial = lax.all_to_all(partial, GROUPS[0], 0, 0)]
    unnamed x6 -> x0, local copies, waits for them, and re-layouts: 1.41 us -> none
    pallas_call x3 -> x5, Pallas kernels: 1.86 us -> 3.16 us  [call(): pl.pallas_call(kernel, out_shape=shapes, in_specs=[whole()] * len(operand...]
    ppermute x2, waiting for transfers between devices: 1.27 us -> 2.49 us  [all_bands(): above = lax.ppermute(wide, LAT, [(i + 1, i) for i in range(count - 1)])]
  transfers between devices with their start and end apart: 6 -> 6, of which waited for: 2 -> 2; matrix products, arithmetic and copies ran while one was open for 1% -> 0% of each run, Pallas kernels for 4% -> 4%
where the time goes in v6:
time: 96.6 us; the launch traced here: 96.2 us
  blocking collectives  59.4 us (61%)
  starting transfers between devices  18.2 us (19%)
  waiting for transfers between devices  11 us (11%)
  Pallas kernels  6.75 us (7%)
    all_gather x6, blocking collectives, partner(): lax.all_gather(block, axes, axis_index_groups=pairs(extent(axes), first))  37.7 us
    all_to_all x1, blocking collectives, local(): totals = lax.all_to_all(partial, GROUPS[1], 0, 0)  16 us
    all_to_all x1, starting transfers between devices, local(): partial = lax.all_to_all(partial, GROUPS[0], 0, 0)  9.23 us
    all_to_all x1, waiting for transfers between devices, local(): partial = lax.all_to_all(partial, GROUPS[0], 0, 0)  8.5 us
    all_gather x1, blocking collectives, all_bands_paired(): return (swap, lax.all_gather(wide, LAT, axis_index_groups=pairs(count, 1)))  5.73 us
    ppermute x2, starting transfers between devices, all_bands(): below = lax.ppermute(wide, LAT, [(i, i + 1) for i in range(count - 1)])  3.3 us
    pallas_call x5, Pallas kernels, call(): pl.pallas_call(kernel, out_shape=shapes, in_specs=[whole()] * len(operand...  3.16 us
    ppermute x1, starting transfers between devices, all_bands_paired(): lax.ppermute(wide, LAT, [p for a, b in pairs(count, 0) for p in ((a, b),...  3.12 us
  transfers between devices with their start and end apart: 6, of which 2 were waited for; matrix products, arithmetic and copies ran while one was open for 0% of the time, Pallas kernels for 4%

profile of v6, /device:TPU:1, one launch (start us, length us, event | category | flops | bytes accessed | tf_op | source)
XLA Modules:
  0.0 96.2 jit_solution(6973248252334001818)
XLA Ops:
  0.6 0.9 describe.1
  1.6 8.4 %all-gather = bf16[64,512]{1,0:T(8,128)(2,1)S(1)} all-gather(bf16[32,512]{1,0:T(8,128)(2,1)S(1)} %get-tuple-element.29), channel_id=2, replica_groups={{0,1},{2,3},{4,5},{6,7},{8,9},{10,11},{12,13},{14,15},{16,17},{18,19},{..., dimensions={0}, use_global_device_ids=true | all-gather | bytes 98304 | tf_op jit(solution)/shard_map/all_gather | solution.py:43
  10.0 4.0 %all-gather.1 = bf16[64,512]{1,0:T(8,128)(2,1)S(1)} all-gather(bf16[32,512]{1,0:T(8,128)(2,1)S(1)} %get-tuple-element.29), channel_id=3, replica_groups={{1,2},{3,4},{5,6},{7,8},{9,10},{11,12},{13,14},{15,16},{17,18},{19,20},..., dimensions={0}, use_global_device_ids=true | all-gather | bytes 98304 | tf_op jit(solution)/shard_map/all_gather | solution.py:43
  14.0 1.3 %collective-permute-start.1 = (bf16[3,32,512]{2,1,0:T(8,128)(2,1)S(1)}, bf16[3,32,512]{2,1,0:T(8,128)(2,1)S(1)}, u32[]{:S(2)}, u32[]{:S(2)}) collective-permute-start(bf16[3,32,512]{2,1,0:T(8,128)(2,1)S(1)} %pad_maximum_fusion.near_ref), channel_id=1, source_target_pairs={{0,64},{64,128},{128,192},{192,256},{256,320},{320,384},{384,448},... | collective-permute-start | bytes 294920 | tf_op jit(solution)/shard_map/ppermute | solution.py:57
  15.3 1.3 %collective-permute-start = (bf16[3,32,512]{2,1,0:T(8,128)(2,1)S(1)}, bf16[3,32,512]{2,1,0:T(8,128)(2,1)S(1)}, u32[]{:S(2)}, u32[]{:S(2)}) collective-permute-start(bf16[3,32,512]{2,1,0:T(8,128)(2,1)S(1)} %pad_maximum_fusion.near_ref), channel_id=1, source_target_pairs={{64,0},{128,64},{192,128},{256,192},{320,256},{384,320},{448,384},... | collective-permute-start | bytes 294920 | tf_op jit(solution)/shard_map/ppermute | solution.py:58
  16.6 0.8 build.3
  17.4 0.0 collective-permute-done.1.near_ref
  17.4 0.8 build.4
  18.2 2.5 %collective-permute-done.near_ref = bf16[3,32,512]{2,1,0:T(8,128)(2,1)S(1)} collective-permute-done((bf16[3,32,512]{2,1,0:T(8,128)(2,1)S(1)}, bf16[3,32,512]{2,1,0:T(8,128)(2,1)S(1)}, u32[]{:S(2)}, u32[]{:S(2)}) %collective-permute-start) | collective-permute-done | bytes 98336 | tf_op jit(solution)/shard_map/ppermute | solution.py:58
  20.7 0.8 build.5
  21.5 10.0 %all-gather.2 = bf16[32,512]{1,0:T(8,128)(2,1)S(1)} all-gather(bf16[16,512]{1,0:T(8,128)(2,1)S(1)} %get-tuple-element.36), channel_id=4, replica_groups={{0,1},{2,3},{4,5},{6,7},{8,9},{10,11},{12,13},{14,15},{16,17},{18,19},{..., dimensions={0}, use_global_device_ids=true | all-gather | bytes 49152 | tf_op jit(solution)/shard_map/all_gather | solution.py:43
  31.5 3.8 %all-gather.3 = bf16[32,512]{1,0:T(8,128)(2,1)S(1)} all-gather(bf16[16,512]{1,0:T(8,128)(2,1)S(1)} %get-tuple-element.36), channel_id=5, replica_groups={{1,2},{3,4},{5,6},{7,8},{9,10},{11,12},{13,14},{15,16},{17,18},{19,20},..., dimensions={0}, use_global_device_ids=true | all-gather | bytes 49152 | tf_op jit(solution)/shard_map/all_gather | solution.py:43
  35.3 3.1 %collective-permute-start.2 = (bf16[3,16,512]{2,1,0:T(8,128)(2,1)S(1)}, bf16[3,16,512]{2,1,0:T(8,128)(2,1)S(1)}, u32[]{:S(2)}, u32[]{:S(2)}) collective-permute-start(bf16[3,16,512]{2,1,0:T(8,128)(2,1)S(1)} %pad_maximum_fusion.1.near_ref), channel_id=1, source_target_pairs={{0,64},{64,0},{128,192},{192,128},{256,320},{320,256},{384,448},{4... | collective-permute-start | bytes 147464 | tf_op jit(solution)/shard_map/ppermute | solution.py:64
  38.4 0.3 apply.1.part_ref
  38.7 5.7 %all-gather.4 = bf16[6,16,512]{2,1,0:T(8,128)(2,1)S(1)} all-gather(bf16[3,16,512]{2,1,0:T(8,128)(2,1)S(1)} %pad_maximum_fusion.1.near_ref), channel_id=6, replica_groups={{64,128},{192,256},{320,384},{448,0},{65,129},{193,257},{321,385},{449,..., dimensions={0}, use_global_device_ids=true | all-gather | bytes 147456 | tf_op jit(solution)/shard_map/all_gather | solution.py:65
  44.5 0.0 collective-permute-done.2.swap_ref
  44.5 0.5 paired.1
  45.0 7.6 %all-gather.5 = bf16[32,512]{1,0:T(8,128)(2,1)S(1)} all-gather(bf16[16,512]{1,0:T(8,128)(2,1)S(1)} %get-tuple-element.44), channel_id=7, replica_groups={{0,1},{2,3},{4,5},{6,7},{8,9},{10,11},{12,13},{14,15},{16,17},{18,19},{..., dimensions={0}, use_global_device_ids=true | all-gather | bytes 49152 | tf_op jit(solution)/shard_map/all_gather | solution.py:43
  52.6 3.8 %all-gather.6 = bf16[32,512]{1,0:T(8,128)(2,1)S(1)} all-gather(bf16[16,512]{1,0:T(8,128)(2,1)S(1)} %get-tuple-element.44), channel_id=8, replica_groups={{1,2},{3,4},{5,6},{7,8},{9,10},{11,12},{13,14},{15,16},{17,18},{19,20},..., dimensions={0}, use_global_device_ids=true | all-gather | bytes 49152 | tf_op jit(solution)/shard_map/all_gather | solution.py:43
  56.5 2.0 %collective-permute-start.4 = (bf16[3,16,512]{2,1,0:T(8,128)(2,1)S(1)}, bf16[3,16,512]{2,1,0:T(8,128)(2,1)S(1)}, u32[]{:S(2)}, u32[]{:S(2)}) collective-permute-start(bf16[3,16,512]{2,1,0:T(8,128)(2,1)S(1)} %pad_maximum_fusion.2.near_ref), channel_id=1, source_target_pairs={{0,64},{64,128},{128,192},{192,256},{256,320},{320,384},{384,448},... | collective-permute-start | bytes 147464 | tf_op jit(solution)/shard_map/ppermute | solution.py:57
  58.5 1.3 %collective-permute-start.3 = (bf16[3,16,512]{2,1,0:T(8,128)(2,1)S(1)}, bf16[3,16,512]{2,1,0:T(8,128)(2,1)S(1)}, u32[]{:S(2)}, u32[]{:S(2)}) collective-permute-start(bf16[3,16,512]{2,1,0:T(8,128)(2,1)S(1)} %pad_maximum_fusion.2.near_ref), channel_id=1, source_target_pairs={{64,0},{128,64},{192,128},{256,192},{320,256},{384,320},{448,384},... | collective-permute-start | bytes 147464 | tf_op jit(solution)/shard_map/ppermute | solution.py:58
  59.8 0.4 same_band.1
  60.2 0.0 collective-permute-done.4.near_ref
  60.2 1.2 %below.1 = (f32[16,512]{1,0:T(8,128)S(1)}, f32[32,1,128]{2,1,0:T(1,128)}) custom-call(bf16[3,16,512]{2,1,0:T(8,128)(2,1)S(1)} %collective-permute-done.4.near_ref, bf16[3,512,512]{2,1,0:T(8,128)(2,1)S(1)} %get-tuple-element.38.below_ref.tile_ref, f32[16,512]{1,0:T(8,128)S(1)} %get-tuple-element.48.part_ref, f32[16,512]{1,0:T(8,128)S(1)} %get-tuple-element.46.second_ref, ...), custom_call_target="tpu_custom_call" | custom-call | flops 25165824 | bytes 1572864 | tf_op jit(solution)/shard_map/below/pallas_call | solution.py:327
  61.4 9.2 %all-to-all-start = ((f32[32,1,128]{2,1,0:T(1,128)}), f32[32,1,128]{2,1,0:T(1,128)S(1)}, u32[]{:S(2)}, u32[]{:S(2)}) async-start(f32[32,1,128]{2,1,0:T(1,128)} %get-tuple-element.50), calls=%async_computation | async-start | bytes 32768 | tf_op jit(solution)/shard_map/all_to_all | solution.py:367
  70.6 0.0 collective-permute-done.3.near_ref
  70.6 8.5 %all-to-all-done.total_ref = f32[32,1,128]{2,1,0:T(1,128)S(1)} async-done(((f32[32,1,128]{2,1,0:T(1,128)}), f32[32,1,128]{2,1,0:T(1,128)S(1)}, u32[]{:S(2)}, u32[]{:S(2)}) %all-to-all-start) | async-done | bytes 16416 | tf_op jit(solution)/shard_map/all_to_all | solution.py:367
  79.1 0.3 above.1
  79.4 16.0 %all_to_all.10.total_ref = f32[16,1,128]{2,1,0:T(1,128)S(1)} all-to-all(f32[16,1,128]{2,1,0:T(1,128)S(1)} %get-tuple-element.52), channel_id=1, replica_groups=mesh['z_lo'=2,'x'=4,'z_hi'=4,'y'=8,'core'=2] {'y','core'}, dimensions={0} | all-to-all | bytes 16384 | tf_op jit(solution)/shard_map/all_to_all | solution.py:369
  95.4 0.8 finish.1
  (9 shorter events, 0.1 us)
Async XLA Ops:
  14.0 3.4 %collective-permute-start.1 = (bf16[3,32,512]{2,1,0:T(8,128)(2,1)S(1)}, bf16[3,32,512]{2,1,0:T(8,128)(2,1)S(1)}, u32[]{:S(2)}, u32[]{:S(2)}) collective-permute-start(bf16[3,32,512]{2,1,0:T(8,128)(2,1)S(1)} %pad_maximum_fusion.near_ref), channel_id=1, source_target_pairs={{0,64},{64,128},{128,192},{192,256},{256,320},{320,384},{384,448},... | collective-permute-start | bytes 294920 | tf_op jit(solution)/shard_map/ppermute | solution.py:57
  15.3 5.4 %collective-permute-start = (bf16[3,32,512]{2,1,0:T(8,128)(2,1)S(1)}, bf16[3,32,512]{2,1,0:T(8,128)(2,1)S(1)}, u32[]{:S(2)}, u32[]{:S(2)}) collective-permute-start(bf16[3,32,512]{2,1,0:T(8,128)(2,1)S(1)} %pad_maximum_fusion.near_ref), channel_id=1, source_target_pairs={{64,0},{128,64},{192,128},{256,192},{320,256},{384,320},{448,384},... | collective-permute-start | bytes 294920 | tf_op jit(solution)/shard_map/ppermute | solution.py:58
  35.3 9.2 %collective-permute-start.2 = (bf16[3,16,512]{2,1,0:T(8,128)(2,1)S(1)}, bf16[3,16,512]{2,1,0:T(8,128)(2,1)S(1)}, u32[]{:S(2)}, u32[]{:S(2)}) collective-permute-start(bf16[3,16,512]{2,1,0:T(8,128)(2,1)S(1)} %pad_maximum_fusion.1.near_ref), channel_id=1, source_target_pairs={{0,64},{64,0},{128,192},{192,128},{256,320},{320,256},{384,448},{4... | collective-permute-start | bytes 147464 | tf_op jit(solution)/shard_map/ppermute | solution.py:64
  56.5 3.7 %collective-permute-start.4 = (bf16[3,16,512]{2,1,0:T(8,128)(2,1)S(1)}, bf16[3,16,512]{2,1,0:T(8,128)(2,1)S(1)}, u32[]{:S(2)}, u32[]{:S(2)}) collective-permute-start(bf16[3,16,512]{2,1,0:T(8,128)(2,1)S(1)} %pad_maximum_fusion.2.near_ref), channel_id=1, source_target_pairs={{0,64},{64,128},{128,192},{192,256},{256,320},{320,384},{384,448},... | collective-permute-start | bytes 147464 | tf_op jit(solution)/shard_map/ppermute | solution.py:57
  58.5 12.1 %collective-permute-start.3 = (bf16[3,16,512]{2,1,0:T(8,128)(2,1)S(1)}, bf16[3,16,512]{2,1,0:T(8,128)(2,1)S(1)}, u32[]{:S(2)}, u32[]{:S(2)}) collective-permute-start(bf16[3,16,512]{2,1,0:T(8,128)(2,1)S(1)} %pad_maximum_fusion.2.near_ref), channel_id=1, source_target_pairs={{64,0},{128,64},{192,128},{256,192},{320,256},{384,320},{448,384},... | collective-permute-start | bytes 147464 | tf_op jit(solution)/shard_map/ppermute | solution.py:58
  61.4 17.7 %all-to-all-start = ((f32[32,1,128]{2,1,0:T(1,128)}), f32[32,1,128]{2,1,0:T(1,128)S(1)}, u32[]{:S(2)}, u32[]{:S(2)}) async-start(f32[32,1,128]{2,1,0:T(1,128)} %get-tuple-element.50), calls=%async_computation | async-start | bytes 32768 | tf_op jit(solution)/shard_map/all_to_all | solution.py:367

commit v7 on v6

--- a/solution.py
+++ b/solution.py
@@ -275,25 +275,13 @@
     )
 
 
-def below_kernel(near_ref, tile_ref, part_ref, second_ref, row_ref, sum_ref, copies_ref):
-    part = part_ref[...]
-    total = part + products(lambda slot: near_ref[slot], tile_ref)
-    sum_ref[...] = total
-    product = second_ref[...] * (2.0 * total - part)
-    before = [jnp.zeros_like(product)] * MOMENTS
-    row = row_ref[...] + lane_sums([*before, product])
-    copies_ref[...] = jnp.broadcast_to(row[None], copies_ref.shape)
-
-
-def paired_kernel(swap_ref, both_ref, below_ref, above_ref, part_ref, sum_ref, sent_ref):
+def other_bands(swap_ref, both_ref, below_ref, above_ref, done):
     band = lax.axis_index(LAT)
     inside = jnp.where((band == 0) | (band == BANDS - 1), 0.0, 1.0)
 
     def add(swap_tiles, both_tiles, position):
-        total = part_ref[...] + products(lambda slot: swap_ref[slot], swap_tiles)
-        total = total + inside * products(lambda slot: both_ref[position, slot], both_tiles)
-        sum_ref[...] = total
-        sent_ref[...] = total.astype(jnp.bfloat16)
+        total = products(lambda slot: swap_ref[slot], swap_tiles)
+        done(total + inside * products(lambda slot: both_ref[position, slot], both_tiles))
 
     @pl.when(band % 2 == 1)
     def _():
@@ -304,8 +292,27 @@
         add(above_ref, below_ref, 0)
 
 
-def above_kernel(near_ref, total_ref, tile_ref, lower_ref, third_ref, copies_ref):
-    third_ref[...] = lower_ref[...] + products(lambda slot: near_ref[slot], tile_ref)
+def second_kernel(swap_ref, both_ref, below_ref, above_ref, part_ref, sum_ref, sent_ref):
+    def done(others):
+        total = part_ref[...] + others
+        sum_ref[...] = total
+        sent_ref[...] = total.astype(jnp.bfloat16)
+
+    other_bands(swap_ref, both_ref, below_ref, above_ref, done)
+
+
+def third_kernel(swap_ref, both_ref, below_ref, above_ref, part_ref, second_ref, row_ref, sum_ref, copies_ref):
+    def done(others):
+        total = part_ref[...] + others
+        sum_ref[...] = total
+        before = [jnp.zeros_like(total)] * MOMENTS
+        row = row_ref[...] + lane_sums([*before, second_ref[...] * total])
+        copies_ref[...] = jnp.broadcast_to(row[None], copies_ref.shape)
+
+    other_bands(swap_ref, both_ref, below_ref, above_ref, done)
+
+
+def between_kernel(total_ref, copies_ref):
     copies_ref[...] = jnp.broadcast_to(jnp.sum(total_ref[...], axis=0)[None], copies_ref.shape)
 
 
@@ -349,13 +356,13 @@
     part, = apply(wide, tiles, first, error_var)
     field = pltpu.VMEM((RHS, OBS), jnp.float32)
     second, sent = call(
-        paired_kernel,
+        second_kernel,
         [field, pltpu.VMEM((RHS, OBS), jnp.bfloat16)],
         [swap, both, tiles_below, tiles_above, part],
-        "paired",
+        "second",
     )
     wide = widened(sent)
-    below, above = all_bands(wide)
+    swap, both = all_bands_paired(wide)
     part, row = call(
         same_band_kernel,
         [field, pltpu.VMEM((1, 128), jnp.float32)],
@@ -363,9 +370,14 @@
         "same_band",
     )
     copies = [pltpu.VMEM((extent(axes), 1, 128), jnp.float32) for axes in GROUPS]
-    lower, partial = call(below_kernel, [field, copies[0]], [below, tiles_below, part, second, row], "below")
+    third, partial = call(
+        third_kernel,
+        [field, copies[0]],
+        [swap, both, tiles_below, tiles_above, part, second, row],
+        "third",
+    )
     partial = lax.all_to_all(partial, GROUPS[0], 0, 0)
-    third, partial = call(above_kernel, [field, copies[1]], [above, partial, tiles_above, lower], "above")
+    partial, = call(between_kernel, [copies[1]], [partial], "between")
     totals = lax.all_to_all(partial, GROUPS[1], 0, 0)
     whole_field = jax.ShapeDtypeStruct((1, 1, RHS, OBS), jnp.float32)
     return call(finish_kernel, [whole_field] * 2, [totals, start, first, second, third], "finish")

time: 96.6 us -> 98.8 us (1.023)
  blocking collectives: 59.4 us -> 81.3 us
  starting transfers between devices: 18.2 us -> 7.71 us
  waiting for transfers between devices: 11 us -> 2.5 us
    all_to_all x0 -> x1, blocking collectives: none -> 15.6 us  [local(): partial = lax.all_to_all(partial, GROUPS[0], 0, 0)]
    all_to_all x1 -> x0, starting transfers between devices: 9.23 us -> none  [local(): partial = lax.all_to_all(partial, GROUPS[0], 0, 0)]
    all_to_all x1 -> x0, waiting for transfers between devices: 8.5 us -> none  [local(): partial = lax.all_to_all(partial, GROUPS[0], 0, 0)]
    all_gather x1 -> x2, blocking collectives: 5.73 us -> 11.5 us  [all_bands_paired(): return (swap, lax.all_gather(wide, LAT, axis_index_groups=pairs(count, 1)))]
    ppermute x1 -> x2, starting transfers between devices: 3.12 us -> 5.13 us  [all_bands_paired(): lax.ppermute(wide, LAT, [p for a, b in pairs(count, 0) for p in ((a, b),...]
    ppermute x2 -> x1, starting transfers between devices: 3.3 us -> 1.3 us  [all_bands(): below = lax.ppermute(wide, LAT, [(i, i + 1) for i in range(count - 1)])]
    ppermute x2 -> x1, starting transfers between devices: 2.58 us -> 1.29 us  [all_bands(): above = lax.ppermute(wide, LAT, [(i + 1, i) for i in range(count - 1)])]
    ppermute x2 -> x1, waiting for transfers between devices: 2.49 us -> 2.49 us  [all_bands(): above = lax.ppermute(wide, LAT, [(i + 1, i) for i in range(count - 1)])]
  transfers between devices with their start and end apart: 6 -> 4, of which waited for: 2 -> 1; matrix products, arithmetic and copies ran while one was open for 0% -> 0% of each run, Pallas kernels for 4% -> 2%
where the time goes in v7:
time: 98.8 us; the launch traced here: 98.4 us
  blocking collectives  81.3 us (82%)
  starting transfers between devices  7.71 us (8%)
  Pallas kernels  6.05 us (6%)
  waiting for transfers between devices  2.5 us (3%)
    all_gather x6, blocking collectives, partner(): lax.all_gather(block, axes, axis_index_groups=pairs(extent(axes), first))  37.7 us
    all_to_all x1, blocking collectives, local(): totals = lax.all_to_all(partial, GROUPS[1], 0, 0)  16.6 us
    all_to_all x1, blocking collectives, local(): partial = lax.all_to_all(partial, GROUPS[0], 0, 0)  15.6 us
    all_gather x2, blocking collectives, all_bands_paired(): return (swap, lax.all_gather(wide, LAT, axis_index_groups=pairs(count, 1)))  11.5 us
    ppermute x2, starting transfers between devices, all_bands_paired(): lax.ppermute(wide, LAT, [p for a, b in pairs(count, 0) for p in ((a, b),...  5.13 us
    ppermute x1, waiting for transfers between devices, all_bands(): above = lax.ppermute(wide, LAT, [(i + 1, i) for i in range(count - 1)])  2.49 us
    pallas_call x5, Pallas kernels, call(): pl.pallas_call(kernel, out_shape=shapes, in_specs=[whole()] * len(operand...  2.47 us
    pallas_call x3, Pallas kernels, build(): pl.pallas_call(functools.partial(build_kernel, steps), out_shape=shapes,...  2.34 us
  transfers between devices with their start and end apart: 4, of which 1 were waited for; matrix products, arithmetic and copies ran while one was open for 0% of the time, Pallas kernels for 2%

profile of v7, /device:TPU:1, one launch (start us, length us, event | category | flops | bytes accessed | tf_op | source)
XLA Modules:
  0.0 98.4 jit_solution(10255615741833350129)
XLA Ops:
  0.6 0.9 describe.1
  1.6 8.4 %all-gather = bf16[64,512]{1,0:T(8,128)(2,1)S(1)} all-gather(bf16[32,512]{1,0:T(8,128)(2,1)S(1)} %get-tuple-element.27), channel_id=2, replica_groups={{0,1},{2,3},{4,5},{6,7},{8,9},{10,11},{12,13},{14,15},{16,17},{18,19},{..., dimensions={0}, use_global_device_ids=true | all-gather | bytes 98304 | tf_op jit(solution)/shard_map/all_gather | solution.py:43
  10.0 4.0 %all-gather.1 = bf16[64,512]{1,0:T(8,128)(2,1)S(1)} all-gather(bf16[32,512]{1,0:T(8,128)(2,1)S(1)} %get-tuple-element.27), channel_id=3, replica_groups={{1,2},{3,4},{5,6},{7,8},{9,10},{11,12},{13,14},{15,16},{17,18},{19,20},..., dimensions={0}, use_global_device_ids=true | all-gather | bytes 98304 | tf_op jit(solution)/shard_map/all_gather | solution.py:43
  14.0 1.3 %collective-permute-start.1 = (bf16[3,32,512]{2,1,0:T(8,128)(2,1)S(1)}, bf16[3,32,512]{2,1,0:T(8,128)(2,1)S(1)}, u32[]{:S(2)}, u32[]{:S(2)}) collective-permute-start(bf16[3,32,512]{2,1,0:T(8,128)(2,1)S(1)} %pad_maximum_fusion.near_ref), channel_id=1, source_target_pairs={{0,64},{64,128},{128,192},{192,256},{256,320},{320,384},{384,448},... | collective-permute-start | bytes 294920 | tf_op jit(solution)/shard_map/ppermute | solution.py:57
  15.3 1.3 %collective-permute-start = (bf16[3,32,512]{2,1,0:T(8,128)(2,1)S(1)}, bf16[3,32,512]{2,1,0:T(8,128)(2,1)S(1)}, u32[]{:S(2)}, u32[]{:S(2)}) collective-permute-start(bf16[3,32,512]{2,1,0:T(8,128)(2,1)S(1)} %pad_maximum_fusion.near_ref), channel_id=1, source_target_pairs={{64,0},{128,64},{192,128},{256,192},{320,256},{384,320},{448,384},... | collective-permute-start | bytes 294920 | tf_op jit(solution)/shard_map/ppermute | solution.py:58
  16.6 0.8 build.3
  17.4 0.0 collective-permute-done.1.near_ref
  17.4 0.8 build.4
  18.2 2.5 %collective-permute-done.near_ref = bf16[3,32,512]{2,1,0:T(8,128)(2,1)S(1)} collective-permute-done((bf16[3,32,512]{2,1,0:T(8,128)(2,1)S(1)}, bf16[3,32,512]{2,1,0:T(8,128)(2,1)S(1)}, u32[]{:S(2)}, u32[]{:S(2)}) %collective-permute-start) | collective-permute-done | bytes 98336 | tf_op jit(solution)/shard_map/ppermute | solution.py:58
  20.7 0.8 build.5
  21.5 10.0 %all-gather.2 = bf16[32,512]{1,0:T(8,128)(2,1)S(1)} all-gather(bf16[16,512]{1,0:T(8,128)(2,1)S(1)} %get-tuple-element.34), channel_id=4, replica_groups={{0,1},{2,3},{4,5},{6,7},{8,9},{10,11},{12,13},{14,15},{16,17},{18,19},{..., dimensions={0}, use_global_device_ids=true | all-gather | bytes 49152 | tf_op jit(solution)/shard_map/all_gather | solution.py:43
  31.5 3.8 %all-gather.3 = bf16[32,512]{1,0:T(8,128)(2,1)S(1)} all-gather(bf16[16,512]{1,0:T(8,128)(2,1)S(1)} %get-tuple-element.34), channel_id=5, replica_groups={{1,2},{3,4},{5,6},{7,8},{9,10},{11,12},{13,14},{15,16},{17,18},{19,20},..., dimensions={0}, use_global_device_ids=true | all-gather | bytes 49152 | tf_op jit(solution)/shard_map/all_gather | solution.py:43
  35.3 3.1 %collective-permute-start.2 = (bf16[3,16,512]{2,1,0:T(8,128)(2,1)S(1)}, bf16[3,16,512]{2,1,0:T(8,128)(2,1)S(1)}, u32[]{:S(2)}, u32[]{:S(2)}) collective-permute-start(bf16[3,16,512]{2,1,0:T(8,128)(2,1)S(1)} %pad_maximum_fusion.1.near_ref), channel_id=1, source_target_pairs={{0,64},{64,0},{128,192},{192,128},{256,320},{320,256},{384,448},{4... | collective-permute-start | bytes 147464 | tf_op jit(solution)/shard_map/ppermute | solution.py:64
  38.4 0.3 apply.1.part_ref
  38.7 5.7 %all-gather.4 = bf16[6,16,512]{2,1,0:T(8,128)(2,1)S(1)} all-gather(bf16[3,16,512]{2,1,0:T(8,128)(2,1)S(1)} %pad_maximum_fusion.1.near_ref), channel_id=6, replica_groups={{64,128},{192,256},{320,384},{448,0},{65,129},{193,257},{321,385},{449,..., dimensions={0}, use_global_device_ids=true | all-gather | bytes 147456 | tf_op jit(solution)/shard_map/all_gather | solution.py:65
  44.5 0.0 collective-permute-done.2.swap_ref
  44.5 0.5 second.1
  45.0 7.6 %all-gather.5 = bf16[32,512]{1,0:T(8,128)(2,1)S(1)} all-gather(bf16[16,512]{1,0:T(8,128)(2,1)S(1)} %get-tuple-element.42), channel_id=7, replica_groups={{0,1},{2,3},{4,5},{6,7},{8,9},{10,11},{12,13},{14,15},{16,17},{18,19},{..., dimensions={0}, use_global_device_ids=true | all-gather | bytes 49152 | tf_op jit(solution)/shard_map/all_gather | solution.py:43
  52.6 3.8 %all-gather.6 = bf16[32,512]{1,0:T(8,128)(2,1)S(1)} all-gather(bf16[16,512]{1,0:T(8,128)(2,1)S(1)} %get-tuple-element.42), channel_id=8, replica_groups={{1,2},{3,4},{5,6},{7,8},{9,10},{11,12},{13,14},{15,16},{17,18},{19,20},..., dimensions={0}, use_global_device_ids=true | all-gather | bytes 49152 | tf_op jit(solution)/shard_map/all_gather | solution.py:43
  56.5 2.0 %collective-permute-start.3 = (bf16[3,16,512]{2,1,0:T(8,128)(2,1)S(1)}, bf16[3,16,512]{2,1,0:T(8,128)(2,1)S(1)}, u32[]{:S(2)}, u32[]{:S(2)}) collective-permute-start(bf16[3,16,512]{2,1,0:T(8,128)(2,1)S(1)} %pad_maximum_fusion.2.near_ref), channel_id=1, source_target_pairs={{0,64},{64,0},{128,192},{192,128},{256,320},{320,256},{384,448},{4... | collective-permute-start | bytes 147464 | tf_op jit(solution)/shard_map/ppermute | solution.py:64
  58.5 0.4 same_band.1
  58.9 5.7 %all-gather.7 = bf16[6,16,512]{2,1,0:T(8,128)(2,1)S(1)} all-gather(bf16[3,16,512]{2,1,0:T(8,128)(2,1)S(1)} %pad_maximum_fusion.2.near_ref), channel_id=9, replica_groups={{64,128},{192,256},{320,384},{448,0},{65,129},{193,257},{321,385},{449,..., dimensions={0}, use_global_device_ids=true | all-gather | bytes 147456 | tf_op jit(solution)/shard_map/all_gather | solution.py:65
  64.6 0.0 collective-permute-done.3.swap_ref
  64.6 0.7 third.1
  65.4 15.6 %all_to_all.10.total_ref = f32[32,1,128]{2,1,0:T(1,128)S(1)} all-to-all(f32[32,1,128]{2,1,0:T(1,128)S(1)} %get-tuple-element.48), channel_id=1, replica_groups=mesh['z_lo'=2,'x'=4,'z_hi'=4,'y'=8,'core'=2] {'z_lo','z_hi','x'}, dimensions={0} | all-to-all | bytes 32768 | tf_op jit(solution)/shard_map/all_to_all | solution.py:379
  81.0 16.6 %all_to_all.11.total_ref = f32[16,1,128]{2,1,0:T(1,128)S(1)} all-to-all(f32[16,1,128]{2,1,0:T(1,128)S(1)} %between.1), channel_id=1, replica_groups=mesh['z_lo'=2,'x'=4,'z_hi'=4,'y'=8,'core'=2] {'y','core'}, dimensions={0} | all-to-all | bytes 16384 | tf_op jit(solution)/shard_map/all_to_all | solution.py:381
  97.6 0.8 finish.1
  (10 shorter events, 0.1 us)
Async XLA Ops:
  14.0 3.4 %collective-permute-start.1 = (bf16[3,32,512]{2,1,0:T(8,128)(2,1)S(1)}, bf16[3,32,512]{2,1,0:T(8,128)(2,1)S(1)}, u32[]{:S(2)}, u32[]{:S(2)}) collective-permute-start(bf16[3,32,512]{2,1,0:T(8,128)(2,1)S(1)} %pad_maximum_fusion.near_ref), channel_id=1, source_target_pairs={{0,64},{64,128},{128,192},{192,256},{256,320},{320,384},{384,448},... | collective-permute-start | bytes 294920 | tf_op jit(solution)/shard_map/ppermute | solution.py:57
  15.3 5.4 %collective-permute-start = (bf16[3,32,512]{2,1,0:T(8,128)(2,1)S(1)}, bf16[3,32,512]{2,1,0:T(8,128)(2,1)S(1)}, u32[]{:S(2)}, u32[]{:S(2)}) collective-permute-start(bf16[3,32,512]{2,1,0:T(8,128)(2,1)S(1)} %pad_maximum_fusion.near_ref), channel_id=1, source_target_pairs={{64,0},{128,64},{192,128},{256,192},{320,256},{384,320},{448,384},... | collective-permute-start | bytes 294920 | tf_op jit(solution)/shard_map/ppermute | solution.py:58
  35.3 9.2 %collective-permute-start.2 = (bf16[3,16,512]{2,1,0:T(8,128)(2,1)S(1)}, bf16[3,16,512]{2,1,0:T(8,128)(2,1)S(1)}, u32[]{:S(2)}, u32[]{:S(2)}) collective-permute-start(bf16[3,16,512]{2,1,0:T(8,128)(2,1)S(1)} %pad_maximum_fusion.1.near_ref), channel_id=1, source_target_pairs={{0,64},{64,0},{128,192},{192,128},{256,320},{320,256},{384,448},{4... | collective-permute-start | bytes 147464 | tf_op jit(solution)/shard_map/ppermute | solution.py:64
  56.5 8.2 %collective-permute-start.3 = (bf16[3,16,512]{2,1,0:T(8,128)(2,1)S(1)}, bf16[3,16,512]{2,1,0:T(8,128)(2,1)S(1)}, u32[]{:S(2)}, u32[]{:S(2)}) collective-permute-start(bf16[3,16,512]{2,1,0:T(8,128)(2,1)S(1)} %pad_maximum_fusion.2.near_ref), channel_id=1, source_target_pairs={{0,64},{64,0},{128,192},{192,128},{256,320},{320,256},{384,448},{4... | collective-permute-start | bytes 147464 | tf_op jit(solution)/shard_map/ppermute | solution.py:64

commit v8 on v6

--- a/solution.py
+++ b/solution.py
@@ -75,9 +75,40 @@
     return high, mid, rounded(value - high - mid)
 
 
+def own_side(place, level, kinds, offset):
+    one = jnp.ones_like(level)
+
+    def looked_up(column):
+        logs = [math.log2(row[column]) for row in COUPLING]
+        return logs[0] + kinds[0] * (logs[1] - logs[0]) + kinds[1] * (logs[2] - logs[0])
+
+    at_height = looked_up(0)
+    rows = [HORIZ * axis for axis in place for _ in range(3)]
+    rows += [2.0 * VERT * level, looked_up(1) - at_height, looked_up(2) - at_height]
+    return rows + [one, one, offset + at_height - HORIZ, jnp.zeros_like(level)]
+
+
+def far_side(place, level, kinds, offset, error):
+    rows = [piece for axis in place for piece in pieces(axis)]
+    return rows + [level, *kinds, *pieces(offset)[:2], jnp.ones_like(level), error]
+
+
+def write_own(own_ref, rows_ref, rows):
+    for row in range(16):
+        rows_ref[row : row + 1, :] = rows[row]
+    for step in range(3):
+        if step:
+            rows_ref[14:15, :] = rows[14] + step * math.log2(TAPER_STEP)
+        left = rows_ref[...]
+        for piece in range(3):
+            part = left.astype(jnp.bfloat16)
+            own_ref[step, 16 * piece : 16 * piece + 16, :] = part
+            left = left - part.astype(jnp.float32)
+
+
 def describe_kernel(
     start_ref, error_ref, frac_ref, spread_ref, type_ref,
-    message_ref, own_ref, error_out_ref, added_ref, kept_ref, far_rows, own_rows,
+    message_ref, own_ref, error_out_ref, added_ref, kept_ref, rows_ref,
 ):
     frac = frac_ref[...].astype(jnp.float32)
     latitude = (lax.axis_index(LAT).astype(jnp.float32) + frac[0:1]) * (2.0 * LAT_LIMIT / BANDS) - LAT_LIMIT
@@ -86,40 +117,17 @@
     cosines, sines = jnp.cos(angles), jnp.sin(angles)
     place = (cosines[0:1] * cosines[1:2], cosines[0:1] * sines[1:2], sines[0:1])
     level = frac[2:3]
-    sigma = jnp.log(spread_ref[...].astype(jnp.float32)) * LOG2E - VERT * level * level
-    kind = type_ref[...]
-    one = jnp.ones_like(level)
-    table = [[math.log2(k) for k in row] for row in COUPLING]
-
-    def looked_up(column):
-        return jnp.where(kind == 0, table[0][column], jnp.where(kind == 1, table[1][column], table[2][column]))
-
-    at_height = looked_up(0)
-    far = []
-    own = []
-    for axis in place:
-        far += pieces(axis)
-        own += [HORIZ * axis] * 3
-    far += [level, jnp.where(kind == 1, one, 0.0), jnp.where(kind == 2, one, 0.0)]
-    own += [2.0 * VERT * level, looked_up(1) - at_height, looked_up(2) - at_height]
-    far += [*pieces(sigma), one]
-    own += [one, one, one, sigma + at_height - HORIZ]
+    offset = jnp.log(spread_ref[...].astype(jnp.float32)) * LOG2E - VERT * level * level
+    kinds = [jnp.where(type_ref[...] == kind, jnp.ones_like(level), 0.0) for kind in (1, 2)]
+    far = far_side(place, level, kinds, offset, error_ref[...])
     for row in range(16):
-        far_rows[row : row + 1, :] = far[row]
-        own_rows[row : row + 1, :] = own[row]
+        rows_ref[row : row + 1, :] = far[row]
     message_ref[0:16, :] = start_ref[...].astype(jnp.bfloat16)
-    message_ref[16:32, :] = far_rows[...].astype(jnp.bfloat16)
+    message_ref[16:32, :] = rows_ref[...].astype(jnp.bfloat16)
     error_out_ref[...] = error_ref[...]
     kept_ref[...] = start_ref[...]
     added_ref[...] = error_ref[...] * start_ref[...]
-    for step in range(3):
-        if step:
-            own_rows[15:16, :] = own[15] + step * math.log2(TAPER_STEP)
-        left = own_rows[...]
-        for piece in range(3):
-            part = left.astype(jnp.bfloat16)
-            own_ref[step, 16 * piece : 16 * piece + 16, :] = part
-            left = left - part.astype(jnp.float32)
+    write_own(own_ref, rows_ref, own_side(place, level, kinds, offset))
 
 
 def whole(space=pltpu.VMEM):
@@ -138,21 +146,46 @@
         ),
         in_specs=[whole()] * 5,
         out_specs=[whole()] * 5,
-        scratch_shapes=[pltpu.VMEM((16, OBS), jnp.float32)] * 2,
+        scratch_shapes=[pltpu.VMEM((16, OBS), jnp.float32)],
         name="describe",
     )(start, error_var, where_frac, spread, obs_type)
 
 
-def build_kernel(steps, near_ref, own_ref, added_ref, tile_ref, sum_ref, *sent):
-    for slot, step in enumerate(steps):
-        far = near_ref[slot, 16:32, :]
+OWN = (1, 2, 3)
+OUTER = (0, 1, 2)
+
+
+def part_of(columns, steps, near_ref, own_ref, tile_ref):
+    for slot, (column, step) in enumerate(zip(columns, steps)):
+        far = near_ref[column, 16:32, :]
         far = jnp.concatenate([far, far, far], axis=0)
         power = lax.dot_general(far, own_ref[step], (((0,), (0,)), ((), ())), preferred_element_type=jnp.float32)
         tile_ref[slot] = jnp.exp2(power).astype(jnp.bfloat16)
-    total = added_ref[...] + products(lambda slot: near_ref[slot, 0:16, :], tile_ref)
+    return products(lambda slot: near_ref[columns[slot], 0:16, :], tile_ref)
+
+
+def build_same_kernel(near_ref, own_ref, added_ref, tile_ref, sum_ref, outer_own_ref, outer_sum_ref, rows_ref, scratch_ref):
+    rows = near_ref[1, 16:32, :].astype(jnp.float32)
+    row = [rows[at : at + 1] for at in range(16)]
+    place = [row[3 * axis] + row[3 * axis + 1] + row[3 * axis + 2] for axis in range(3)]
+    write_own(outer_own_ref, rows_ref, own_side(place, row[9], row[10:12], row[12] + row[13]))
+    sum_ref[...] = added_ref[...] + part_of(OWN, SAME_BAND, near_ref, own_ref, tile_ref)
+    outer_added = row[15] * near_ref[1, 0:16, :].astype(jnp.float32)
+    outer_sum_ref[...] = outer_added + part_of(OUTER, SAME_BAND, near_ref, outer_own_ref, scratch_ref)
+
+
+def build_other_kernel(
+    near_ref, own_ref, added_ref, outer_own_ref, outer_added_ref, tile_ref, sum_ref, *more
+):
+    *outer_refs, scratch_ref = more
+    total = added_ref[...] + part_of(OWN, OTHER_BAND, near_ref, own_ref, tile_ref)
+    outer = outer_added_ref[...] + part_of(OUTER, OTHER_BAND, near_ref, outer_own_ref, scratch_ref)
     sum_ref[...] = total
-    for ref in sent:
-        ref[...] = total.astype(jnp.bfloat16)
+    if len(outer_refs) == 1:
+        outer_refs[0][...] = outer
+    else:
+        for ref, value in zip(outer_refs, (total, outer)):
+            ref[...] = value.astype(jnp.bfloat16)
 
 
 def products(field_of, tile_ref):
@@ -190,17 +223,23 @@
     return shapes
 
 
-def build(steps, near, own, added, last=False):
-    shapes = [pltpu.VMEM((3, OBS, OBS), jnp.bfloat16)] + sums(last)
+FIELD = pltpu.VMEM((RHS, OBS), jnp.float32)
+SENT = pltpu.VMEM((RHS, OBS), jnp.bfloat16)
+TILES = pltpu.VMEM((3, OBS, OBS), jnp.bfloat16)
+OWN_SIDE = pltpu.VMEM((3, 48, OBS), jnp.bfloat16)
+
+
+def build(kernel, shapes, operands, scratch):
     return pl.pallas_call(
-        functools.partial(build_kernel, steps),
+        kernel,
         out_shape=shapes,
-        in_specs=[whole()] * 3,
+        in_specs=[whole()] * len(operands),
         out_specs=[whole()] * len(shapes),
+        scratch_shapes=scratch,
         compiler_params=pltpu.CompilerParams(vmem_limit_bytes=16 << 20),
-        cost_estimate=cost(1),
+        cost_estimate=cost(2),
         name="build",
-    )(near, own, added)
+    )(*operands)
 
 
 def apply(near, tiles, added, scale=None, last=False):
@@ -339,12 +378,23 @@
     message, own, error_var, added, start = describe(
         innovations[0, 0], obs_error[0], where_frac[0, 0], spread[0], obs_type[0]
     )
-    wide = widened(message)
+    inner = partner(message, LON, 0)
+    outer = partner(jnp.stack([message, inner]), LON, 1)
+    wide = jnp.stack([outer[1], outer[0], message, inner])
     below, above = all_bands(wide)
-    tiles, part = build(SAME_BAND, wide, own, added)
-    tiles_below, part = build(OTHER_BAND, below, own, part)
-    tiles_above, first, sent = build(OTHER_BAND, above, own, part, True)
-    wide = widened(sent)
+    tiles, part, outer_own, outer = build(
+        build_same_kernel,
+        [TILES, FIELD, OWN_SIDE, FIELD],
+        [wide, own, added],
+        [pltpu.VMEM((16, OBS), jnp.float32), TILES],
+    )
+    tiles_below, part, outer = build(
+        build_other_kernel, [TILES, FIELD, FIELD], [below, own, part, outer_own, outer], [TILES]
+    )
+    tiles_above, first, sent, outer_sent = build(
+        build_other_kernel, [TILES, FIELD, SENT, SENT], [above, own, part, outer_own, outer], [TILES]
+    )
+    wide = jnp.stack([outer_sent, sent, partner(sent, LON, 0)])
     swap, both = all_bands_paired(wide)
     part, = apply(wide, tiles, first, error_var)
     field = pltpu.VMEM((RHS, OBS), jnp.float32)

time: 96.6 us -> 90.3 us (0.935)
  blocking collectives: 59.4 us -> 51.9 us
  Pallas kernels: 6.75 us -> 8.61 us
    all_gather x6 -> x5, blocking collectives: 37.7 us -> 30.2 us  [partner(): lax.all_gather(block, axes, axis_index_groups=pairs(extent(axes), first))]
    pallas_call x3, Pallas kernels: 2.35 us -> 4.2 us  [build(): pl.pallas_call(kernel, out_shape=shapes, in_specs=[whole()] * len(operand...]
  transfers between devices with their start and end apart: 6 -> 6, of which waited for: 2 -> 2; matrix products, arithmetic and copies ran while one was open for 0% -> 0% of each run, Pallas kernels for 4% -> 5%
where the time goes in v8:
time: 90.3 us; the launch traced here: 89.9 us
  blocking collectives  51.9 us (57%)
  starting transfers between devices  18.4 us (20%)
  waiting for transfers between devices  10.1 us (11%)
  Pallas kernels  8.61 us (10%)
    all_gather x5, blocking collectives, partner(): lax.all_gather(block, axes, axis_index_groups=pairs(extent(axes), first))  30.2 us
    all_to_all x1, blocking collectives, local(): totals = lax.all_to_all(partial, GROUPS[1], 0, 0)  16 us
    all_to_all x1, starting transfers between devices, local(): partial = lax.all_to_all(partial, GROUPS[0], 0, 0)  9.23 us
    all_to_all x1, waiting for transfers between devices, local(): partial = lax.all_to_all(partial, GROUPS[0], 0, 0)  8.5 us
    all_gather x1, blocking collectives, all_bands_paired(): return (swap, lax.all_gather(wide, LAT, axis_index_groups=pairs(count, 1)))  5.73 us
    pallas_call x3, Pallas kernels, build(): pl.pallas_call(kernel, out_shape=shapes, in_specs=[whole()] * len(operand...  4.2 us
    ppermute x2, starting transfers between devices, all_bands(): below = lax.ppermute(wide, LAT, [(i, i + 1) for i in range(count - 1)])  3.46 us
    pallas_call x5, Pallas kernels, call(): pl.pallas_call(kernel, out_shape=shapes, in_specs=[whole()] * len(operand...  3.16 us
  transfers between devices with their start and end apart: 6, of which 2 were waited for; matrix products, arithmetic and copies ran while one was open for 0% of the time, Pallas kernels for 5%

profile of v8, /device:TPU:1, one launch (start us, length us, event | category | flops | bytes accessed | tf_op | source)
XLA Modules:
  0.0 89.9 jit_solution(17913522857562813143)
XLA Ops:
  0.6 0.9 %describe.1 = (bf16[32,512]{1,0:T(8,128)(2,1)S(1)}, bf16[3,48,512]{2,1,0:T(8,128)(2,1)S(1)}, f32[1,512]{1,0:T(1,128)S(1)}, f32[16,512]{1,0:T(8,128)S(1)}, f32[16,512]{1,0:T(8,128)S(1)}) custom-call(f32[16,512]{1,0:T(8,128)} %bitcast.30, f32[1,512]{1,0:T(1,128)} %bitcast.32, bf16[3,512]{1,0:T(4,128)(2,1)} %bitcast.31, bf16[1,512]{1,0:T(2,128)(2,1)} %bitcast.33, ...), custom_call_target="tpu_custom_call" | custom-call | tf_op jit(solution)/shard_map/describe/pallas_call | solution.py:138
  1.6 8.4 %all-gather = bf16[64,512]{1,0:T(8,128)(2,1)S(1)} all-gather(bf16[32,512]{1,0:T(8,128)(2,1)S(1)} %get-tuple-element.28), channel_id=2, replica_groups={{0,1},{2,3},{4,5},{6,7},{8,9},{10,11},{12,13},{14,15},{16,17},{18,19},{..., dimensions={0}, use_global_device_ids=true | all-gather | bytes 98304 | tf_op jit(solution)/shard_map/all_gather | solution.py:43
  10.0 4.4 %all-gather.1 = bf16[4,32,512]{2,1,0:T(8,128)(2,1)S(1)} all-gather(bf16[2,32,512]{2,1,0:T(8,128)(2,1)S(1)} %pad_maximum_fusion.1), channel_id=3, replica_groups={{1,2},{3,4},{5,6},{7,8},{9,10},{11,12},{13,14},{15,16},{17,18},{19,20},..., dimensions={0}, use_global_device_ids=true | all-gather | bytes 196608 | tf_op jit(solution)/shard_map/all_gather | solution.py:43
  14.4 1.3 %collective-permute-start.1 = (bf16[4,32,512]{2,1,0:T(8,128)(2,1)S(1)}, bf16[4,32,512]{2,1,0:T(8,128)(2,1)S(1)}, u32[]{:S(2)}, u32[]{:S(2)}) collective-permute-start(bf16[4,32,512]{2,1,0:T(8,128)(2,1)S(1)} %pad_maximum_fusion.near_ref), channel_id=1, source_target_pairs={{0,64},{64,128},{128,192},{192,256},{256,320},{320,384},{384,448},... | collective-permute-start | bytes 393224 | tf_op jit(solution)/shard_map/ppermute | solution.py:57
  15.7 1.3 %collective-permute-start = (bf16[4,32,512]{2,1,0:T(8,128)(2,1)S(1)}, bf16[4,32,512]{2,1,0:T(8,128)(2,1)S(1)}, u32[]{:S(2)}, u32[]{:S(2)}) collective-permute-start(bf16[4,32,512]{2,1,0:T(8,128)(2,1)S(1)} %pad_maximum_fusion.near_ref), channel_id=1, source_target_pairs={{64,0},{128,64},{192,128},{256,192},{320,256},{384,320},{448,384},... | collective-permute-start | bytes 393224 | tf_op jit(solution)/shard_map/ppermute | solution.py:58
  17.0 1.4 %build.3 = (bf16[3,512,512]{2,1,0:T(8,128)(2,1)S(1)}, f32[16,512]{1,0:T(8,128)S(1)}, bf16[3,48,512]{2,1,0:T(8,128)(2,1)S(1)}, f32[16,512]{1,0:T(8,128)S(1)}) custom-call(bf16[4,32,512]{2,1,0:T(8,128)(2,1)S(1)} %pad_maximum_fusion.near_ref, bf16[3,48,512]{2,1,0:T(8,128)(2,1)S(1)} %get-tuple-element.29.own_ref, f32[16,512]{1,0:T(8,128)S(1)} %get-tuple-element.30.added_ref), custom_call_target="tpu_custom_call" | custom-call | flops 830472192 | bytes 1572864 | tf_op jit(solution)/shard_map/build/pallas_call | solution.py:233
  18.4 0.0 collective-permute-done.1.near_ref
  18.4 1.4 %build.4 = (bf16[3,512,512]{2,1,0:T(8,128)(2,1)S(1)}, f32[16,512]{1,0:T(8,128)S(1)}, f32[16,512]{1,0:T(8,128)S(1)}) custom-call(bf16[4,32,512]{2,1,0:T(8,128)(2,1)S(1)} %collective-permute-done.1.near_ref, bf16[3,48,512]{2,1,0:T(8,128)(2,1)S(1)} %get-tuple-element.29.own_ref, f32[16,512]{1,0:T(8,128)S(1)} %get-tuple-element.31.added_ref, ...), custom_call_target="tpu_custom_call" | custom-call | flops 830472192 | bytes 1572864 | tf_op jit(solution)/shard_map/build/pallas_call | solution.py:233
  19.8 1.6 %collective-permute-done.near_ref = bf16[4,32,512]{2,1,0:T(8,128)(2,1)S(1)} collective-permute-done((bf16[4,32,512]{2,1,0:T(8,128)(2,1)S(1)}, bf16[4,32,512]{2,1,0:T(8,128)(2,1)S(1)}, u32[]{:S(2)}, u32[]{:S(2)}) %collective-permute-start) | collective-permute-done | bytes 131104 | tf_op jit(solution)/shard_map/ppermute | solution.py:58
  21.4 1.4 %build.5 = (bf16[3,512,512]{2,1,0:T(8,128)(2,1)S(1)}, f32[16,512]{1,0:T(8,128)S(1)}, bf16[16,512]{1,0:T(8,128)(2,1)S(1)}, bf16[16,512]{1,0:T(8,128)(2,1)S(1)}) custom-call(bf16[4,32,512]{2,1,0:T(8,128)(2,1)S(1)} %collective-permute-done.near_ref, bf16[3,48,512]{2,1,0:T(8,128)(2,1)S(1)} %get-tuple-element.29.own_ref, ...), custom_call_target="tpu_custom_call" | custom-call | flops 830472192 | bytes 1572864 | tf_op jit(solution)/shard_map/build/pallas_call | solution.py:233
  22.8 10.3 %all-gather.2 = bf16[32,512]{1,0:T(8,128)(2,1)S(1)} all-gather(bf16[16,512]{1,0:T(8,128)(2,1)S(1)} %get-tuple-element.37), channel_id=4, replica_groups={{0,1},{2,3},{4,5},{6,7},{8,9},{10,11},{12,13},{14,15},{16,17},{18,19},{..., dimensions={0}, use_global_device_ids=true | all-gather | bytes 49152 | tf_op jit(solution)/shard_map/all_gather | solution.py:43
  33.2 3.1 %collective-permute-start.2 = (bf16[3,16,512]{2,1,0:T(8,128)(2,1)S(1)}, bf16[3,16,512]{2,1,0:T(8,128)(2,1)S(1)}, u32[]{:S(2)}, u32[]{:S(2)}) collective-permute-start(bf16[3,16,512]{2,1,0:T(8,128)(2,1)S(1)} %pad_maximum_fusion.2.near_ref), channel_id=1, source_target_pairs={{0,64},{64,0},{128,192},{192,128},{256,320},{320,256},{384,448},{4... | collective-permute-start | bytes 147464 | tf_op jit(solution)/shard_map/ppermute | solution.py:64
  36.3 0.3 apply.1.part_ref
  36.6 5.7 %all-gather.3 = bf16[6,16,512]{2,1,0:T(8,128)(2,1)S(1)} all-gather(bf16[3,16,512]{2,1,0:T(8,128)(2,1)S(1)} %pad_maximum_fusion.2.near_ref), channel_id=5, replica_groups={{64,128},{192,256},{320,384},{448,0},{65,129},{193,257},{321,385},{449,..., dimensions={0}, use_global_device_ids=true | all-gather | bytes 147456 | tf_op jit(solution)/shard_map/all_gather | solution.py:65
  42.4 0.0 collective-permute-done.2.swap_ref
  42.4 0.5 paired.1
  42.9 3.3 %all-gather.4 = bf16[32,512]{1,0:T(8,128)(2,1)S(1)} all-gather(bf16[16,512]{1,0:T(8,128)(2,1)S(1)} %get-tuple-element.44), channel_id=6, replica_groups={{0,1},{2,3},{4,5},{6,7},{8,9},{10,11},{12,13},{14,15},{16,17},{18,19},{..., dimensions={0}, use_global_device_ids=true | all-gather | bytes 49152 | tf_op jit(solution)/shard_map/all_gather | solution.py:43
  46.1 3.8 %all-gather.5 = bf16[32,512]{1,0:T(8,128)(2,1)S(1)} all-gather(bf16[16,512]{1,0:T(8,128)(2,1)S(1)} %get-tuple-element.44), channel_id=7, replica_groups={{1,2},{3,4},{5,6},{7,8},{9,10},{11,12},{13,14},{15,16},{17,18},{19,20},..., dimensions={0}, use_global_device_ids=true | all-gather | bytes 49152 | tf_op jit(solution)/shard_map/all_gather | solution.py:43
  50.0 2.2 %collective-permute-start.4 = (bf16[3,16,512]{2,1,0:T(8,128)(2,1)S(1)}, bf16[3,16,512]{2,1,0:T(8,128)(2,1)S(1)}, u32[]{:S(2)}, u32[]{:S(2)}) collective-permute-start(bf16[3,16,512]{2,1,0:T(8,128)(2,1)S(1)} %pad_maximum_fusion.3.near_ref), channel_id=1, source_target_pairs={{0,64},{64,128},{128,192},{192,256},{256,320},{320,384},{384,448},... | collective-permute-start | bytes 147464 | tf_op jit(solution)/shard_map/ppermute | solution.py:57
  52.2 1.3 %collective-permute-start.3 = (bf16[3,16,512]{2,1,0:T(8,128)(2,1)S(1)}, bf16[3,16,512]{2,1,0:T(8,128)(2,1)S(1)}, u32[]{:S(2)}, u32[]{:S(2)}) collective-permute-start(bf16[3,16,512]{2,1,0:T(8,128)(2,1)S(1)} %pad_maximum_fusion.3.near_ref), channel_id=1, source_target_pairs={{64,0},{128,64},{192,128},{256,192},{320,256},{384,320},{448,384},... | collective-permute-start | bytes 147464 | tf_op jit(solution)/shard_map/ppermute | solution.py:58
  53.5 0.4 same_band.1
  53.9 0.0 collective-permute-done.4.near_ref
  53.9 1.2 %below.1 = (f32[16,512]{1,0:T(8,128)S(1)}, f32[32,1,128]{2,1,0:T(1,128)}) custom-call(bf16[3,16,512]{2,1,0:T(8,128)(2,1)S(1)} %collective-permute-done.4.near_ref, bf16[3,512,512]{2,1,0:T(8,128)(2,1)S(1)} %get-tuple-element.38.below_ref.tile_ref, f32[16,512]{1,0:T(8,128)S(1)} %get-tuple-element.48.part_ref, f32[16,512]{1,0:T(8,128)S(1)} %get-tuple-element.46.second_ref, ...), custom_call_target="tpu_custom_call" | custom-call | flops 25165824 | bytes 1572864 | tf_op jit(solution)/shard_map/below/pallas_call | solution.py:366
  55.0 9.2 %all-to-all-start = ((f32[32,1,128]{2,1,0:T(1,128)}), f32[32,1,128]{2,1,0:T(1,128)S(1)}, u32[]{:S(2)}, u32[]{:S(2)}) async-start(f32[32,1,128]{2,1,0:T(1,128)} %get-tuple-element.50), calls=%async_computation | async-start | bytes 32768 | tf_op jit(solution)/shard_map/all_to_all | solution.py:417
  64.3 0.0 collective-permute-done.3.near_ref
  64.3 8.5 %all-to-all-done.total_ref = f32[32,1,128]{2,1,0:T(1,128)S(1)} async-done(((f32[32,1,128]{2,1,0:T(1,128)}), f32[32,1,128]{2,1,0:T(1,128)S(1)}, u32[]{:S(2)}, u32[]{:S(2)}) %all-to-all-start) | async-done | bytes 16416 | tf_op jit(solution)/shard_map/all_to_all | solution.py:417
  72.8 0.3 above.1
  73.1 16.0 %all_to_all.10.total_ref = f32[16,1,128]{2,1,0:T(1,128)S(1)} all-to-all(f32[16,1,128]{2,1,0:T(1,128)S(1)} %get-tuple-element.52), channel_id=1, replica_groups=mesh['z_lo'=2,'x'=4,'z_hi'=4,'y'=8,'core'=2] {'y','core'}, dimensions={0} | all-to-all | bytes 16384 | tf_op jit(solution)/shard_map/all_to_all | solution.py:419
  89.1 0.8 finish.1
  (10 shorter events, 0.1 us)
Async XLA Ops:
  14.4 4.0 %collective-permute-start.1 = (bf16[4,32,512]{2,1,0:T(8,128)(2,1)S(1)}, bf16[4,32,512]{2,1,0:T(8,128)(2,1)S(1)}, u32[]{:S(2)}, u32[]{:S(2)}) collective-permute-start(bf16[4,32,512]{2,1,0:T(8,128)(2,1)S(1)} %pad_maximum_fusion.near_ref), channel_id=1, source_target_pairs={{0,64},{64,128},{128,192},{192,256},{256,320},{320,384},{384,448},... | collective-permute-start | bytes 393224 | tf_op jit(solution)/shard_map/ppermute | solution.py:57
  15.7 5.7 %collective-permute-start = (bf16[4,32,512]{2,1,0:T(8,128)(2,1)S(1)}, bf16[4,32,512]{2,1,0:T(8,128)(2,1)S(1)}, u32[]{:S(2)}, u32[]{:S(2)}) collective-permute-start(bf16[4,32,512]{2,1,0:T(8,128)(2,1)S(1)} %pad_maximum_fusion.near_ref), channel_id=1, source_target_pairs={{64,0},{128,64},{192,128},{256,192},{320,256},{384,320},{448,384},... | collective-permute-start | bytes 393224 | tf_op jit(solution)/shard_map/ppermute | solution.py:58
  33.2 9.2 %collective-permute-start.2 = (bf16[3,16,512]{2,1,0:T(8,128)(2,1)S(1)}, bf16[3,16,512]{2,1,0:T(8,128)(2,1)S(1)}, u32[]{:S(2)}, u32[]{:S(2)}) collective-permute-start(bf16[3,16,512]{2,1,0:T(8,128)(2,1)S(1)} %pad_maximum_fusion.2.near_ref), channel_id=1, source_target_pairs={{0,64},{64,0},{128,192},{192,128},{256,320},{320,256},{384,448},{4... | collective-permute-start | bytes 147464 | tf_op jit(solution)/shard_map/ppermute | solution.py:64
  50.0 3.9 %collective-permute-start.4 = (bf16[3,16,512]{2,1,0:T(8,128)(2,1)S(1)}, bf16[3,16,512]{2,1,0:T(8,128)(2,1)S(1)}, u32[]{:S(2)}, u32[]{:S(2)}) collective-permute-start(bf16[3,16,512]{2,1,0:T(8,128)(2,1)S(1)} %pad_maximum_fusion.3.near_ref), channel_id=1, source_target_pairs={{0,64},{64,128},{128,192},{192,256},{256,320},{320,384},{384,448},... | collective-permute-start | bytes 147464 | tf_op jit(solution)/shard_map/ppermute | solution.py:57
  52.2 12.1 %collective-permute-start.3 = (bf16[3,16,512]{2,1,0:T(8,128)(2,1)S(1)}, bf16[3,16,512]{2,1,0:T(8,128)(2,1)S(1)}, u32[]{:S(2)}, u32[]{:S(2)}) collective-permute-start(bf16[3,16,512]{2,1,0:T(8,128)(2,1)S(1)} %pad_maximum_fusion.3.near_ref), channel_id=1, source_target_pairs={{64,0},{128,64},{192,128},{256,192},{320,256},{384,320},{448,384},... | collective-permute-start | bytes 147464 | tf_op jit(solution)/shard_map/ppermute | solution.py:58
  55.0 17.7 %all-to-all-start = ((f32[32,1,128]{2,1,0:T(1,128)}), f32[32,1,128]{2,1,0:T(1,128)S(1)}, u32[]{:S(2)}, u32[]{:S(2)}) async-start(f32[32,1,128]{2,1,0:T(1,128)} %get-tuple-element.50), calls=%async_computation | async-start | bytes 32768 | tf_op jit(solution)/shard_map/all_to_all | solution.py:417

commit v9 on v8

--- a/solution.py
+++ b/solution.py
@@ -343,8 +343,7 @@
         add(above_ref, below_ref, 0)
 
 
-def above_kernel(near_ref, total_ref, tile_ref, lower_ref, third_ref, copies_ref):
-    third_ref[...] = lower_ref[...] + products(lambda slot: near_ref[slot], tile_ref)
+def between_kernel(total_ref, copies_ref):
     copies_ref[...] = jnp.broadcast_to(jnp.sum(total_ref[...], axis=0)[None], copies_ref.shape)
 
 
@@ -415,7 +414,8 @@
     copies = [pltpu.VMEM((extent(axes), 1, 128), jnp.float32) for axes in GROUPS]
     lower, partial = call(below_kernel, [field, copies[0]], [below, tiles_below, part, second, row], "below")
     partial = lax.all_to_all(partial, GROUPS[0], 0, 0)
-    third, partial = call(above_kernel, [field, copies[1]], [above, partial, tiles_above, lower], "above")
+    third, = apply(above, tiles_above, lower)
+    partial, = call(between_kernel, [copies[1]], [partial], "between")
     totals = lax.all_to_all(partial, GROUPS[1], 0, 0)
     whole_field = jax.ShapeDtypeStruct((1, 1, RHS, OBS), jnp.float32)
     return call(finish_kernel, [whole_field] * 2, [totals, start, first, second, third], "finish")

time: 90.3 us -> 90.7 us (level)
  waiting for transfers between devices: 10.1 us -> 8.29 us
  blocking collectives: 51.9 us -> 53.5 us
    all_to_all x1, waiting for transfers between devices: 8.5 us -> 6.67 us  [local(): totals = lax.all_to_all(partial, GROUPS[1], 0, 0)]
    all_to_all x1, blocking collectives: 16 us -> 17.6 us  [local(): partial = lax.all_to_all(partial, GROUPS[0], 0, 0)]
  transfers between devices with their start and end apart: 6 -> 6, of which waited for: 2 -> 2; matrix products, arithmetic and copies ran while one was open for 0% -> 0% of each run, Pallas kernels for 5% -> 6%
where the time goes in v9:
time: 90.7 us; the launch traced here: 90.3 us
  blocking collectives  53.5 us (59%)
  starting transfers between devices  19 us (21%)
  Pallas kernels  8.63 us (10%)
  waiting for transfers between devices  8.29 us (9%)
    all_gather x5, blocking collectives, partner(): lax.all_gather(block, axes, axis_index_groups=pairs(extent(axes), first))  30.2 us
    all_to_all x1, blocking collectives, local(): partial = lax.all_to_all(partial, GROUPS[0], 0, 0)  17.6 us
    all_to_all x1, starting transfers between devices, local(): totals = lax.all_to_all(partial, GROUPS[1], 0, 0)  9.81 us
    all_to_all x1, waiting for transfers between devices, local(): totals = lax.all_to_all(partial, GROUPS[1], 0, 0)  6.67 us
    all_gather x1, blocking collectives, all_bands_paired(): return (swap, lax.all_gather(wide, LAT, axis_index_groups=pairs(count, 1)))  5.73 us
    pallas_call x3, Pallas kernels, build(): pl.pallas_call(kernel, out_shape=shapes, in_specs=[whole()] * len(operand...  4.2 us
    ppermute x2, starting transfers between devices, all_bands(): below = lax.ppermute(wide, LAT, [(i, i + 1) for i in range(count - 1)])  3.46 us
    ppermute x1, starting transfers between devices, all_bands_paired(): lax.ppermute(wide, LAT, [p for a, b in pairs(count, 0) for p in ((a, b),...  3.12 us
  transfers between devices with their start and end apart: 6, of which 2 were waited for; matrix products, arithmetic and copies ran while one was open for 0% of the time, Pallas kernels for 6%

profile of v9, /device:TPU:1, one launch (start us, length us, event | category | flops | bytes accessed | tf_op | source)
XLA Modules:
  0.0 90.3 jit_solution(7803699731933654882)
XLA Ops:
  0.6 0.9 %describe.1 = (bf16[32,512]{1,0:T(8,128)(2,1)S(1)}, bf16[3,48,512]{2,1,0:T(8,128)(2,1)S(1)}, f32[1,512]{1,0:T(1,128)S(1)}, f32[16,512]{1,0:T(8,128)S(1)}, f32[16,512]{1,0:T(8,128)S(1)}) custom-call(f32[16,512]{1,0:T(8,128)} %bitcast.30, f32[1,512]{1,0:T(1,128)} %bitcast.32, bf16[3,512]{1,0:T(4,128)(2,1)} %bitcast.31, bf16[1,512]{1,0:T(2,128)(2,1)} %bitcast.33, ...), custom_call_target="tpu_custom_call" | custom-call | tf_op jit(solution)/shard_map/describe/pallas_call | solution.py:138
  1.6 8.4 %all-gather = bf16[64,512]{1,0:T(8,128)(2,1)S(1)} all-gather(bf16[32,512]{1,0:T(8,128)(2,1)S(1)} %get-tuple-element.26), channel_id=2, replica_groups={{0,1},{2,3},{4,5},{6,7},{8,9},{10,11},{12,13},{14,15},{16,17},{18,19},{..., dimensions={0}, use_global_device_ids=true | all-gather | bytes 98304 | tf_op jit(solution)/shard_map/all_gather | solution.py:43
  10.0 4.4 %all-gather.1 = bf16[4,32,512]{2,1,0:T(8,128)(2,1)S(1)} all-gather(bf16[2,32,512]{2,1,0:T(8,128)(2,1)S(1)} %pad_maximum_fusion.1), channel_id=3, replica_groups={{1,2},{3,4},{5,6},{7,8},{9,10},{11,12},{13,14},{15,16},{17,18},{19,20},..., dimensions={0}, use_global_device_ids=true | all-gather | bytes 196608 | tf_op jit(solution)/shard_map/all_gather | solution.py:43
  14.4 1.3 %collective-permute-start.1 = (bf16[4,32,512]{2,1,0:T(8,128)(2,1)S(1)}, bf16[4,32,512]{2,1,0:T(8,128)(2,1)S(1)}, u32[]{:S(2)}, u32[]{:S(2)}) collective-permute-start(bf16[4,32,512]{2,1,0:T(8,128)(2,1)S(1)} %pad_maximum_fusion.near_ref), channel_id=1, source_target_pairs={{0,64},{64,128},{128,192},{192,256},{256,320},{320,384},{384,448},... | collective-permute-start | bytes 393224 | tf_op jit(solution)/shard_map/ppermute | solution.py:57
  15.7 1.3 %collective-permute-start = (bf16[4,32,512]{2,1,0:T(8,128)(2,1)S(1)}, bf16[4,32,512]{2,1,0:T(8,128)(2,1)S(1)}, u32[]{:S(2)}, u32[]{:S(2)}) collective-permute-start(bf16[4,32,512]{2,1,0:T(8,128)(2,1)S(1)} %pad_maximum_fusion.near_ref), channel_id=1, source_target_pairs={{64,0},{128,64},{192,128},{256,192},{320,256},{384,320},{448,384},... | collective-permute-start | bytes 393224 | tf_op jit(solution)/shard_map/ppermute | solution.py:58
  17.0 1.4 %build.3 = (bf16[3,512,512]{2,1,0:T(8,128)(2,1)S(1)}, f32[16,512]{1,0:T(8,128)S(1)}, bf16[3,48,512]{2,1,0:T(8,128)(2,1)S(1)}, f32[16,512]{1,0:T(8,128)S(1)}) custom-call(bf16[4,32,512]{2,1,0:T(8,128)(2,1)S(1)} %pad_maximum_fusion.near_ref, bf16[3,48,512]{2,1,0:T(8,128)(2,1)S(1)} %get-tuple-element.27.own_ref, f32[16,512]{1,0:T(8,128)S(1)} %get-tuple-element.28.added_ref), custom_call_target="tpu_custom_call" | custom-call | flops 830472192 | bytes 1572864 | tf_op jit(solution)/shard_map/build/pallas_call | solution.py:233
  18.4 0.0 collective-permute-done.1.near_ref
  18.4 1.4 %build.4 = (bf16[3,512,512]{2,1,0:T(8,128)(2,1)S(1)}, f32[16,512]{1,0:T(8,128)S(1)}, f32[16,512]{1,0:T(8,128)S(1)}) custom-call(bf16[4,32,512]{2,1,0:T(8,128)(2,1)S(1)} %collective-permute-done.1.near_ref, bf16[3,48,512]{2,1,0:T(8,128)(2,1)S(1)} %get-tuple-element.27.own_ref, f32[16,512]{1,0:T(8,128)S(1)} %get-tuple-element.29.added_ref, ...), custom_call_target="tpu_custom_call" | custom-call | flops 830472192 | bytes 1572864 | tf_op jit(solution)/shard_map/build/pallas_call | solution.py:233
  19.8 1.6 %collective-permute-done.near_ref = bf16[4,32,512]{2,1,0:T(8,128)(2,1)S(1)} collective-permute-done((bf16[4,32,512]{2,1,0:T(8,128)(2,1)S(1)}, bf16[4,32,512]{2,1,0:T(8,128)(2,1)S(1)}, u32[]{:S(2)}, u32[]{:S(2)}) %collective-permute-start) | collective-permute-done | bytes 131104 | tf_op jit(solution)/shard_map/ppermute | solution.py:58
  21.4 1.4 %build.5 = (bf16[3,512,512]{2,1,0:T(8,128)(2,1)S(1)}, f32[16,512]{1,0:T(8,128)S(1)}, bf16[16,512]{1,0:T(8,128)(2,1)S(1)}, bf16[16,512]{1,0:T(8,128)(2,1)S(1)}) custom-call(bf16[4,32,512]{2,1,0:T(8,128)(2,1)S(1)} %collective-permute-done.near_ref, bf16[3,48,512]{2,1,0:T(8,128)(2,1)S(1)} %get-tuple-element.27.own_ref, ...), custom_call_target="tpu_custom_call" | custom-call | flops 830472192 | bytes 1572864 | tf_op jit(solution)/shard_map/build/pallas_call | solution.py:233
  22.8 10.3 %all-gather.2 = bf16[32,512]{1,0:T(8,128)(2,1)S(1)} all-gather(bf16[16,512]{1,0:T(8,128)(2,1)S(1)} %get-tuple-element.35), channel_id=4, replica_groups={{0,1},{2,3},{4,5},{6,7},{8,9},{10,11},{12,13},{14,15},{16,17},{18,19},{..., dimensions={0}, use_global_device_ids=true | all-gather | bytes 49152 | tf_op jit(solution)/shard_map/all_gather | solution.py:43
  33.2 3.1 %collective-permute-start.2 = (bf16[3,16,512]{2,1,0:T(8,128)(2,1)S(1)}, bf16[3,16,512]{2,1,0:T(8,128)(2,1)S(1)}, u32[]{:S(2)}, u32[]{:S(2)}) collective-permute-start(bf16[3,16,512]{2,1,0:T(8,128)(2,1)S(1)} %pad_maximum_fusion.2.near_ref), channel_id=1, source_target_pairs={{0,64},{64,0},{128,192},{192,128},{256,320},{320,256},{384,448},{4... | collective-permute-start | bytes 147464 | tf_op jit(solution)/shard_map/ppermute | solution.py:64
  36.3 0.3 apply.2.part_ref
  36.6 5.7 %all-gather.3 = bf16[6,16,512]{2,1,0:T(8,128)(2,1)S(1)} all-gather(bf16[3,16,512]{2,1,0:T(8,128)(2,1)S(1)} %pad_maximum_fusion.2.near_ref), channel_id=5, replica_groups={{64,128},{192,256},{320,384},{448,0},{65,129},{193,257},{321,385},{449,..., dimensions={0}, use_global_device_ids=true | all-gather | bytes 147456 | tf_op jit(solution)/shard_map/all_gather | solution.py:65
  42.4 0.0 collective-permute-done.2.swap_ref
  42.4 0.5 paired.1
  42.9 3.3 %all-gather.4 = bf16[32,512]{1,0:T(8,128)(2,1)S(1)} all-gather(bf16[16,512]{1,0:T(8,128)(2,1)S(1)} %get-tuple-element.42), channel_id=6, replica_groups={{0,1},{2,3},{4,5},{6,7},{8,9},{10,11},{12,13},{14,15},{16,17},{18,19},{..., dimensions={0}, use_global_device_ids=true | all-gather | bytes 49152 | tf_op jit(solution)/shard_map/all_gather | solution.py:43
  46.1 3.8 %all-gather.5 = bf16[32,512]{1,0:T(8,128)(2,1)S(1)} all-gather(bf16[16,512]{1,0:T(8,128)(2,1)S(1)} %get-tuple-element.42), channel_id=7, replica_groups={{1,2},{3,4},{5,6},{7,8},{9,10},{11,12},{13,14},{15,16},{17,18},{19,20},..., dimensions={0}, use_global_device_ids=true | all-gather | bytes 49152 | tf_op jit(solution)/shard_map/all_gather | solution.py:43
  50.0 2.2 %collective-permute-start.3 = (bf16[3,16,512]{2,1,0:T(8,128)(2,1)S(1)}, bf16[3,16,512]{2,1,0:T(8,128)(2,1)S(1)}, u32[]{:S(2)}, u32[]{:S(2)}) collective-permute-start(bf16[3,16,512]{2,1,0:T(8,128)(2,1)S(1)} %pad_maximum_fusion.3.near_ref), channel_id=1, source_target_pairs={{0,64},{64,128},{128,192},{192,256},{256,320},{320,384},{384,448},... | collective-permute-start | bytes 147464 | tf_op jit(solution)/shard_map/ppermute | solution.py:57
  52.2 1.3 %collective-permute-start.4 = (bf16[3,16,512]{2,1,0:T(8,128)(2,1)S(1)}, bf16[3,16,512]{2,1,0:T(8,128)(2,1)S(1)}, u32[]{:S(2)}, u32[]{:S(2)}) collective-permute-start(bf16[3,16,512]{2,1,0:T(8,128)(2,1)S(1)} %pad_maximum_fusion.3.near_ref), channel_id=1, source_target_pairs={{64,0},{128,64},{192,128},{256,192},{320,256},{384,320},{448,384},... | collective-permute-start | bytes 147464 | tf_op jit(solution)/shard_map/ppermute | solution.py:58
  53.5 0.4 same_band.1
  53.9 0.0 collective-permute-done.3.near_ref
  53.9 0.5 below.1
  54.4 17.6 %all_to_all.10.total_ref = f32[32,1,128]{2,1,0:T(1,128)S(1)} all-to-all(f32[32,1,128]{2,1,0:T(1,128)S(1)} %get-tuple-element.48), channel_id=1, replica_groups=mesh['z_lo'=2,'x'=4,'z_hi'=4,'y'=8,'core'=2] {'z_lo','z_hi','x'}, dimensions={0} | all-to-all | bytes 32768 | tf_op jit(solution)/shard_map/all_to_all | solution.py:416
  72.0 0.6 between.1
  72.7 9.8 %all-to-all-start.1 = ((f32[16,1,128]{2,1,0:T(1,128)}), f32[16,1,128]{2,1,0:T(1,128)S(1)}, u32[]{:S(2)}, u32[]{:S(2)}) async-start(f32[16,1,128]{2,1,0:T(1,128)} %between.1), calls=%async_computation.1 | async-start | bytes 16384 | tf_op jit(solution)/shard_map/all_to_all | solution.py:419
  82.5 0.0 collective-permute-done.4.near_ref
  82.5 0.3 apply.3.third_ref
  82.8 6.7 %all-to-all-done.1.total_ref = f32[16,1,128]{2,1,0:T(1,128)S(1)} async-done(((f32[16,1,128]{2,1,0:T(1,128)}), f32[16,1,128]{2,1,0:T(1,128)S(1)}, u32[]{:S(2)}, u32[]{:S(2)}) %all-to-all-start.1) | async-done | bytes 8224 | tf_op jit(solution)/shard_map/all_to_all | solution.py:419
  89.5 0.8 finish.1
  (10 shorter events, 0.1 us)
Async XLA Ops:
  14.4 4.0 %collective-permute-start.1 = (bf16[4,32,512]{2,1,0:T(8,128)(2,1)S(1)}, bf16[4,32,512]{2,1,0:T(8,128)(2,1)S(1)}, u32[]{:S(2)}, u32[]{:S(2)}) collective-permute-start(bf16[4,32,512]{2,1,0:T(8,128)(2,1)S(1)} %pad_maximum_fusion.near_ref), channel_id=1, source_target_pairs={{0,64},{64,128},{128,192},{192,256},{256,320},{320,384},{384,448},... | collective-permute-start | bytes 393224 | tf_op jit(solution)/shard_map/ppermute | solution.py:57
  15.7 5.7 %collective-permute-start = (bf16[4,32,512]{2,1,0:T(8,128)(2,1)S(1)}, bf16[4,32,512]{2,1,0:T(8,128)(2,1)S(1)}, u32[]{:S(2)}, u32[]{:S(2)}) collective-permute-start(bf16[4,32,512]{2,1,0:T(8,128)(2,1)S(1)} %pad_maximum_fusion.near_ref), channel_id=1, source_target_pairs={{64,0},{128,64},{192,128},{256,192},{320,256},{384,320},{448,384},... | collective-permute-start | bytes 393224 | tf_op jit(solution)/shard_map/ppermute | solution.py:58
  33.2 9.2 %collective-permute-start.2 = (bf16[3,16,512]{2,1,0:T(8,128)(2,1)S(1)}, bf16[3,16,512]{2,1,0:T(8,128)(2,1)S(1)}, u32[]{:S(2)}, u32[]{:S(2)}) collective-permute-start(bf16[3,16,512]{2,1,0:T(8,128)(2,1)S(1)} %pad_maximum_fusion.2.near_ref), channel_id=1, source_target_pairs={{0,64},{64,0},{128,192},{192,128},{256,320},{320,256},{384,448},{4... | collective-permute-start | bytes 147464 | tf_op jit(solution)/shard_map/ppermute | solution.py:64
  50.0 3.9 %collective-permute-start.3 = (bf16[3,16,512]{2,1,0:T(8,128)(2,1)S(1)}, bf16[3,16,512]{2,1,0:T(8,128)(2,1)S(1)}, u32[]{:S(2)}, u32[]{:S(2)}) collective-permute-start(bf16[3,16,512]{2,1,0:T(8,128)(2,1)S(1)} %pad_maximum_fusion.3.near_ref), channel_id=1, source_target_pairs={{0,64},{64,128},{128,192},{192,256},{256,320},{320,384},{384,448},... | collective-permute-start | bytes 147464 | tf_op jit(solution)/shard_map/ppermute | solution.py:57
  52.2 30.3 %collective-permute-start.4 = (bf16[3,16,512]{2,1,0:T(8,128)(2,1)S(1)}, bf16[3,16,512]{2,1,0:T(8,128)(2,1)S(1)}, u32[]{:S(2)}, u32[]{:S(2)}) collective-permute-start(bf16[3,16,512]{2,1,0:T(8,128)(2,1)S(1)} %pad_maximum_fusion.3.near_ref), channel_id=1, source_target_pairs={{64,0},{128,64},{192,128},{256,192},{320,256},{384,320},{448,384},... | collective-permute-start | bytes 147464 | tf_op jit(solution)/shard_map/ppermute | solution.py:58
  72.7 16.8 %all-to-all-start.1 = ((f32[16,1,128]{2,1,0:T(1,128)}), f32[16,1,128]{2,1,0:T(1,128)S(1)}, u32[]{:S(2)}, u32[]{:S(2)}) async-start(f32[16,1,128]{2,1,0:T(1,128)} %between.1), calls=%async_computation.1 | async-start | bytes 16384 | tf_op jit(solution)/shard_map/all_to_all | solution.py:419

commit v10 on v8

--- a/solution.py
+++ b/solution.py
@@ -185,22 +185,22 @@
         outer_refs[0][...] = outer
     else:
         for ref, value in zip(outer_refs, (total, outer)):
-            ref[...] = value.astype(jnp.bfloat16)
+            send(ref, value)
 
 
 def products(field_of, tile_ref):
-    return sum(jnp.dot(field_of(slot), tile_ref[slot], preferred_element_type=jnp.float32) for slot in range(3))
-
-
-def apply_kernel(scaled, near_ref, tile_ref, *refs):
-    total = refs[0][...]
-    if scaled:
-        total = total * refs[1][...]
-    total = total + products(lambda slot: near_ref[slot], tile_ref)
-    sum_ref, *sent = refs[1 + scaled :]
-    sum_ref[...] = total
-    for ref in sent:
-        ref[...] = total.astype(jnp.bfloat16)
+    total = sum(jnp.dot(field_of(slot), tile_ref[slot], preferred_element_type=jnp.float32) for slot in range(3))
+    return total if total.shape[0] == RHS else total[:RHS] + total[RHS:]
+
+
+def send(ref, value):
+    high = value.astype(jnp.bfloat16)
+    ref[0:RHS, :] = high
+    ref[RHS : 2 * RHS, :] = (value - high.astype(jnp.float32)).astype(jnp.bfloat16)
+
+
+def apply_kernel(near_ref, tile_ref, added_ref, scale_ref, sum_ref):
+    sum_ref[...] = added_ref[...] * scale_ref[...] + products(lambda slot: near_ref[slot], tile_ref)
 
 
 SAME_BAND = (1, 0, 1)
@@ -216,15 +216,8 @@
     )
 
 
-def sums(last):
-    shapes = [pltpu.VMEM((RHS, OBS), jnp.float32)]
-    if last:
-        shapes.append(pltpu.VMEM((RHS, OBS), jnp.bfloat16))
-    return shapes
-
-
 FIELD = pltpu.VMEM((RHS, OBS), jnp.float32)
-SENT = pltpu.VMEM((RHS, OBS), jnp.bfloat16)
+SENT = pltpu.VMEM((2 * RHS, OBS), jnp.bfloat16)
 TILES = pltpu.VMEM((3, OBS, OBS), jnp.bfloat16)
 OWN_SIDE = pltpu.VMEM((3, 48, OBS), jnp.bfloat16)
 
@@ -240,20 +233,6 @@
         cost_estimate=cost(2),
         name="build",
     )(*operands)
-
-
-def apply(near, tiles, added, scale=None, last=False):
-    shapes = sums(last)
-    scales = [] if scale is None else [scale]
-    return pl.pallas_call(
-        functools.partial(apply_kernel, len(scales)),
-        out_shape=shapes,
-        in_specs=[whole()] * (3 + len(scales)),
-        out_specs=[whole()] * len(shapes),
-        compiler_params=pltpu.CompilerParams(vmem_limit_bytes=16 << 20),
-        cost_estimate=cost(0),
-        name="apply",
-    )(near, tiles, added, *scales)
 
 
 def coefficients(gram):
@@ -332,7 +311,7 @@
         total = part_ref[...] + products(lambda slot: swap_ref[slot], swap_tiles)
         total = total + inside * products(lambda slot: both_ref[position, slot], both_tiles)
         sum_ref[...] = total
-        sent_ref[...] = total.astype(jnp.bfloat16)
+        send(sent_ref, total)
 
     @pl.when(band % 2 == 1)
     def _():
@@ -396,11 +375,11 @@
     )
     wide = jnp.stack([outer_sent, sent, partner(sent, LON, 0)])
     swap, both = all_bands_paired(wide)
-    part, = apply(wide, tiles, first, error_var)
-    field = pltpu.VMEM((RHS, OBS), jnp.float32)
+    part, = call(apply_kernel, [FIELD], [wide, tiles, first, error_var], "apply")
+    field = FIELD
     second, sent = call(
         paired_kernel,
-        [field, pltpu.VMEM((RHS, OBS), jnp.bfloat16)],
+        [field, SENT],
         [swap, both, tiles_below, tiles_above, part],
         "paired",
     )

time: 90.3 us -> 91.7 us (1.016)
  blocking collectives: 51.9 us -> 52.9 us
    pallas_call x5 -> x6, Pallas kernels: 3.16 us -> 3.68 us  [call(): pl.pallas_call(kernel, out_shape=shapes, in_specs=[whole()] * len(operand...]
where the time goes in v10:
time: 91.7 us; the launch traced here: 91.3 us
  blocking collectives  52.9 us (58%)
  starting transfers between devices  18.6 us (20%)
  waiting for transfers between devices  10.1 us (11%)
  Pallas kernels  8.83 us (10%)
    all_gather x5, blocking collectives, partner(): lax.all_gather(block, axes, axis_index_groups=pairs(extent(axes), first))  30.4 us
    all_to_all x1, blocking collectives, local(): totals = lax.all_to_all(partial, GROUPS[1], 0, 0)  16.2 us
    all_to_all x1, starting transfers between devices, local(): partial = lax.all_to_all(partial, GROUPS[0], 0, 0)  9.22 us
    all_to_all x1, waiting for transfers between devices, local(): partial = lax.all_to_all(partial, GROUPS[0], 0, 0)  8.5 us
    all_gather x1, blocking collectives, all_bands_paired(): return (swap, lax.all_gather(wide, LAT, axis_index_groups=pairs(count, 1)))  6.26 us
    pallas_call x3, Pallas kernels, build(): pl.pallas_call(kernel, out_shape=shapes, in_specs=[whole()] * len(operand...  4.2 us
    ppermute x2, starting transfers between devices, all_bands(): below = lax.ppermute(wide, LAT, [(i, i + 1) for i in range(count - 1)])  3.71 us
    pallas_call x6, Pallas kernels, call(): pl.pallas_call(kernel, out_shape=shapes, in_specs=[whole()] * len(operand...  3.68 us
  transfers between devices with their start and end apart: 6, of which 2 were waited for; matrix products, arithmetic and copies ran while one was open for 0% of the time, Pallas kernels for 5%

profile of v10, /device:TPU:1, one launch (start us, length us, event | category | flops | bytes accessed | tf_op | source)
XLA Modules:
  0.0 91.3 jit_solution(11990386450933450982)
XLA Ops:
  0.6 0.9 %describe.1 = (bf16[32,512]{1,0:T(8,128)(2,1)S(1)}, bf16[3,48,512]{2,1,0:T(8,128)(2,1)S(1)}, f32[1,512]{1,0:T(1,128)S(1)}, f32[16,512]{1,0:T(8,128)S(1)}, f32[16,512]{1,0:T(8,128)S(1)}) custom-call(f32[16,512]{1,0:T(8,128)} %bitcast.30, f32[1,512]{1,0:T(1,128)} %bitcast.32, bf16[3,512]{1,0:T(4,128)(2,1)} %bitcast.31, bf16[1,512]{1,0:T(2,128)(2,1)} %bitcast.33, ...), custom_call_target="tpu_custom_call" | custom-call | tf_op jit(solution)/shard_map/describe/pallas_call | solution.py:138
  1.6 8.4 %all-gather = bf16[64,512]{1,0:T(8,128)(2,1)S(1)} all-gather(bf16[32,512]{1,0:T(8,128)(2,1)S(1)} %get-tuple-element.28), channel_id=2, replica_groups={{0,1},{2,3},{4,5},{6,7},{8,9},{10,11},{12,13},{14,15},{16,17},{18,19},{..., dimensions={0}, use_global_device_ids=true | all-gather | bytes 98304 | tf_op jit(solution)/shard_map/all_gather | solution.py:43
  10.0 4.4 %all-gather.1 = bf16[4,32,512]{2,1,0:T(8,128)(2,1)S(1)} all-gather(bf16[2,32,512]{2,1,0:T(8,128)(2,1)S(1)} %pad_maximum_fusion.3), channel_id=3, replica_groups={{1,2},{3,4},{5,6},{7,8},{9,10},{11,12},{13,14},{15,16},{17,18},{19,20},..., dimensions={0}, use_global_device_ids=true | all-gather | bytes 196608 | tf_op jit(solution)/shard_map/all_gather | solution.py:43
  14.4 1.3 %collective-permute-start.1 = (bf16[4,32,512]{2,1,0:T(8,128)(2,1)S(1)}, bf16[4,32,512]{2,1,0:T(8,128)(2,1)S(1)}, u32[]{:S(2)}, u32[]{:S(2)}) collective-permute-start(bf16[4,32,512]{2,1,0:T(8,128)(2,1)S(1)} %pad_maximum_fusion.near_ref), channel_id=1, source_target_pairs={{0,64},{64,128},{128,192},{192,256},{256,320},{320,384},{384,448},... | collective-permute-start | bytes 393224 | tf_op jit(solution)/shard_map/ppermute | solution.py:57
  15.7 1.3 %collective-permute-start = (bf16[4,32,512]{2,1,0:T(8,128)(2,1)S(1)}, bf16[4,32,512]{2,1,0:T(8,128)(2,1)S(1)}, u32[]{:S(2)}, u32[]{:S(2)}) collective-permute-start(bf16[4,32,512]{2,1,0:T(8,128)(2,1)S(1)} %pad_maximum_fusion.near_ref), channel_id=1, source_target_pairs={{64,0},{128,64},{192,128},{256,192},{320,256},{384,320},{448,384},... | collective-permute-start | bytes 393224 | tf_op jit(solution)/shard_map/ppermute | solution.py:58
  17.0 1.4 %build.3 = (bf16[3,512,512]{2,1,0:T(8,128)(2,1)S(1)}, f32[16,512]{1,0:T(8,128)S(1)}, bf16[3,48,512]{2,1,0:T(8,128)(2,1)S(1)}, f32[16,512]{1,0:T(8,128)S(1)}) custom-call(bf16[4,32,512]{2,1,0:T(8,128)(2,1)S(1)} %pad_maximum_fusion.near_ref, bf16[3,48,512]{2,1,0:T(8,128)(2,1)S(1)} %get-tuple-element.29.own_ref, f32[16,512]{1,0:T(8,128)S(1)} %get-tuple-element.30.added_ref), custom_call_target="tpu_custom_call" | custom-call | flops 830472192 | bytes 1572864 | tf_op jit(solution)/shard_map/build/pallas_call | solution.py:226
  18.4 0.0 collective-permute-done.1.near_ref
  18.4 1.4 %build.4 = (bf16[3,512,512]{2,1,0:T(8,128)(2,1)S(1)}, f32[16,512]{1,0:T(8,128)S(1)}, f32[16,512]{1,0:T(8,128)S(1)}) custom-call(bf16[4,32,512]{2,1,0:T(8,128)(2,1)S(1)} %collective-permute-done.1.near_ref, bf16[3,48,512]{2,1,0:T(8,128)(2,1)S(1)} %get-tuple-element.29.own_ref, f32[16,512]{1,0:T(8,128)S(1)} %get-tuple-element.31.added_ref, ...), custom_call_target="tpu_custom_call" | custom-call | flops 830472192 | bytes 1572864 | tf_op jit(solution)/shard_map/build/pallas_call | solution.py:226
  19.8 1.6 %collective-permute-done.near_ref = bf16[4,32,512]{2,1,0:T(8,128)(2,1)S(1)} collective-permute-done((bf16[4,32,512]{2,1,0:T(8,128)(2,1)S(1)}, bf16[4,32,512]{2,1,0:T(8,128)(2,1)S(1)}, u32[]{:S(2)}, u32[]{:S(2)}) %collective-permute-start) | collective-permute-done | bytes 131104 | tf_op jit(solution)/shard_map/ppermute | solution.py:58
  21.4 1.4 %build.5 = (bf16[3,512,512]{2,1,0:T(8,128)(2,1)S(1)}, f32[16,512]{1,0:T(8,128)S(1)}, bf16[32,512]{1,0:T(8,128)(2,1)S(1)}, bf16[32,512]{1,0:T(8,128)(2,1)S(1)}) custom-call(bf16[4,32,512]{2,1,0:T(8,128)(2,1)S(1)} %collective-permute-done.near_ref, bf16[3,48,512]{2,1,0:T(8,128)(2,1)S(1)} %get-tuple-element.29.own_ref, ...), custom_call_target="tpu_custom_call" | custom-call | flops 830472192 | bytes 1572864 | tf_op jit(solution)/shard_map/build/pallas_call | solution.py:226
  22.8 10.4 %all-gather.2 = bf16[64,512]{1,0:T(8,128)(2,1)S(1)} all-gather(bf16[32,512]{1,0:T(8,128)(2,1)S(1)} %get-tuple-element.37), channel_id=4, replica_groups={{0,1},{2,3},{4,5},{6,7},{8,9},{10,11},{12,13},{14,15},{16,17},{18,19},{..., dimensions={0}, use_global_device_ids=true | all-gather | bytes 98304 | tf_op jit(solution)/shard_map/all_gather | solution.py:43
  33.2 3.1 %collective-permute-start.2 = (bf16[3,32,512]{2,1,0:T(8,128)(2,1)S(1)}, bf16[3,32,512]{2,1,0:T(8,128)(2,1)S(1)}, u32[]{:S(2)}, u32[]{:S(2)}) collective-permute-start(bf16[3,32,512]{2,1,0:T(8,128)(2,1)S(1)} %pad_maximum_fusion.1.near_ref), channel_id=1, source_target_pairs={{0,64},{64,0},{128,192},{192,128},{256,320},{320,256},{384,448},{4... | collective-permute-start | bytes 294920 | tf_op jit(solution)/shard_map/ppermute | solution.py:64
  36.3 0.3 apply.1.part_ref
  36.7 6.3 %all-gather.3 = bf16[6,32,512]{2,1,0:T(8,128)(2,1)S(1)} all-gather(bf16[3,32,512]{2,1,0:T(8,128)(2,1)S(1)} %pad_maximum_fusion.1.near_ref), channel_id=5, replica_groups={{64,128},{192,256},{320,384},{448,0},{65,129},{193,257},{321,385},{449,..., dimensions={0}, use_global_device_ids=true | all-gather | bytes 294912 | tf_op jit(solution)/shard_map/all_gather | solution.py:65
  43.0 0.0 collective-permute-done.2.swap_ref
  43.0 0.6 paired.1
  43.6 3.3 %all-gather.4 = bf16[64,512]{1,0:T(8,128)(2,1)S(1)} all-gather(bf16[32,512]{1,0:T(8,128)(2,1)S(1)} %get-tuple-element.44), channel_id=6, replica_groups={{0,1},{2,3},{4,5},{6,7},{8,9},{10,11},{12,13},{14,15},{16,17},{18,19},{..., dimensions={0}, use_global_device_ids=true | all-gather | bytes 98304 | tf_op jit(solution)/shard_map/all_gather | solution.py:43
  46.9 4.0 %all-gather.5 = bf16[64,512]{1,0:T(8,128)(2,1)S(1)} all-gather(bf16[32,512]{1,0:T(8,128)(2,1)S(1)} %get-tuple-element.44), channel_id=7, replica_groups={{1,2},{3,4},{5,6},{7,8},{9,10},{11,12},{13,14},{15,16},{17,18},{19,20},..., dimensions={0}, use_global_device_ids=true | all-gather | bytes 98304 | tf_op jit(solution)/shard_map/all_gather | solution.py:43
  50.9 2.4 %collective-permute-start.4 = (bf16[3,32,512]{2,1,0:T(8,128)(2,1)S(1)}, bf16[3,32,512]{2,1,0:T(8,128)(2,1)S(1)}, u32[]{:S(2)}, u32[]{:S(2)}) collective-permute-start(bf16[3,32,512]{2,1,0:T(8,128)(2,1)S(1)} %pad_maximum_fusion.2.near_ref), channel_id=1, source_target_pairs={{0,64},{64,128},{128,192},{192,256},{256,320},{320,384},{384,448},... | collective-permute-start | bytes 294920 | tf_op jit(solution)/shard_map/ppermute | solution.py:57
  53.3 1.3 %collective-permute-start.3 = (bf16[3,32,512]{2,1,0:T(8,128)(2,1)S(1)}, bf16[3,32,512]{2,1,0:T(8,128)(2,1)S(1)}, u32[]{:S(2)}, u32[]{:S(2)}) collective-permute-start(bf16[3,32,512]{2,1,0:T(8,128)(2,1)S(1)} %pad_maximum_fusion.2.near_ref), channel_id=1, source_target_pairs={{64,0},{128,64},{192,128},{256,192},{320,256},{384,320},{448,384},... | collective-permute-start | bytes 294920 | tf_op jit(solution)/shard_map/ppermute | solution.py:58
  54.6 0.4 same_band.1
  55.0 0.0 collective-permute-done.4.near_ref
  55.0 1.2 %below.1 = (f32[16,512]{1,0:T(8,128)S(1)}, f32[32,1,128]{2,1,0:T(1,128)}) custom-call(bf16[3,32,512]{2,1,0:T(8,128)(2,1)S(1)} %collective-permute-done.4.near_ref, bf16[3,512,512]{2,1,0:T(8,128)(2,1)S(1)} %get-tuple-element.38.below_ref.tile_ref, f32[16,512]{1,0:T(8,128)S(1)} %get-tuple-element.48.part_ref, f32[16,512]{1,0:T(8,128)S(1)} %get-tuple-element.46.second_ref, ...), custom_call_target="tpu_custom_call" | custom-call | flops 25165824 | bytes 1572864 | tf_op jit(solution)/shard_map/below/pallas_call | solution.py:345
  56.2 9.2 %all-to-all-start = ((f32[32,1,128]{2,1,0:T(1,128)}), f32[32,1,128]{2,1,0:T(1,128)S(1)}, u32[]{:S(2)}, u32[]{:S(2)}) async-start(f32[32,1,128]{2,1,0:T(1,128)} %get-tuple-element.50), calls=%async_computation | async-start | bytes 32768 | tf_op jit(solution)/shard_map/all_to_all | solution.py:396
  65.5 0.0 collective-permute-done.3.near_ref
  65.5 8.5 %all-to-all-done.total_ref = f32[32,1,128]{2,1,0:T(1,128)S(1)} async-done(((f32[32,1,128]{2,1,0:T(1,128)}), f32[32,1,128]{2,1,0:T(1,128)S(1)}, u32[]{:S(2)}, u32[]{:S(2)}) %all-to-all-start) | async-done | bytes 16416 | tf_op jit(solution)/shard_map/all_to_all | solution.py:396
  74.0 0.3 above.1
  74.3 16.2 %all_to_all.10.total_ref = f32[16,1,128]{2,1,0:T(1,128)S(1)} all-to-all(f32[16,1,128]{2,1,0:T(1,128)S(1)} %get-tuple-element.52), channel_id=1, replica_groups=mesh['z_lo'=2,'x'=4,'z_hi'=4,'y'=8,'core'=2] {'y','core'}, dimensions={0} | all-to-all | bytes 16384 | tf_op jit(solution)/shard_map/all_to_all | solution.py:398
  90.5 0.8 finish.1
  (10 shorter events, 0.1 us)
Async XLA Ops:
  14.4 4.0 %collective-permute-start.1 = (bf16[4,32,512]{2,1,0:T(8,128)(2,1)S(1)}, bf16[4,32,512]{2,1,0:T(8,128)(2,1)S(1)}, u32[]{:S(2)}, u32[]{:S(2)}) collective-permute-start(bf16[4,32,512]{2,1,0:T(8,128)(2,1)S(1)} %pad_maximum_fusion.near_ref), channel_id=1, source_target_pairs={{0,64},{64,128},{128,192},{192,256},{256,320},{320,384},{384,448},... | collective-permute-start | bytes 393224 | tf_op jit(solution)/shard_map/ppermute | solution.py:57
  15.7 5.7 %collective-permute-start = (bf16[4,32,512]{2,1,0:T(8,128)(2,1)S(1)}, bf16[4,32,512]{2,1,0:T(8,128)(2,1)S(1)}, u32[]{:S(2)}, u32[]{:S(2)}) collective-permute-start(bf16[4,32,512]{2,1,0:T(8,128)(2,1)S(1)} %pad_maximum_fusion.near_ref), channel_id=1, source_target_pairs={{64,0},{128,64},{192,128},{256,192},{320,256},{384,320},{448,384},... | collective-permute-start | bytes 393224 | tf_op jit(solution)/shard_map/ppermute | solution.py:58
  33.2 9.7 %collective-permute-start.2 = (bf16[3,32,512]{2,1,0:T(8,128)(2,1)S(1)}, bf16[3,32,512]{2,1,0:T(8,128)(2,1)S(1)}, u32[]{:S(2)}, u32[]{:S(2)}) collective-permute-start(bf16[3,32,512]{2,1,0:T(8,128)(2,1)S(1)} %pad_maximum_fusion.1.near_ref), channel_id=1, source_target_pairs={{0,64},{64,0},{128,192},{192,128},{256,320},{320,256},{384,448},{4... | collective-permute-start | bytes 294920 | tf_op jit(solution)/shard_map/ppermute | solution.py:64
  50.9 4.1 %collective-permute-start.4 = (bf16[3,32,512]{2,1,0:T(8,128)(2,1)S(1)}, bf16[3,32,512]{2,1,0:T(8,128)(2,1)S(1)}, u32[]{:S(2)}, u32[]{:S(2)}) collective-permute-start(bf16[3,32,512]{2,1,0:T(8,128)(2,1)S(1)} %pad_maximum_fusion.2.near_ref), channel_id=1, source_target_pairs={{0,64},{64,128},{128,192},{192,256},{256,320},{320,384},{384,448},... | collective-permute-start | bytes 294920 | tf_op jit(solution)/shard_map/ppermute | solution.py:57
  53.3 12.2 %collective-permute-start.3 = (bf16[3,32,512]{2,1,0:T(8,128)(2,1)S(1)}, bf16[3,32,512]{2,1,0:T(8,128)(2,1)S(1)}, u32[]{:S(2)}, u32[]{:S(2)}) collective-permute-start(bf16[3,32,512]{2,1,0:T(8,128)(2,1)S(1)} %pad_maximum_fusion.2.near_ref), channel_id=1, source_target_pairs={{64,0},{128,64},{192,128},{256,192},{320,256},{384,320},{448,384},... | collective-permute-start | bytes 294920 | tf_op jit(solution)/shard_map/ppermute | solution.py:58
  56.2 17.7 %all-to-all-start = ((f32[32,1,128]{2,1,0:T(1,128)}), f32[32,1,128]{2,1,0:T(1,128)S(1)}, u32[]{:S(2)}, u32[]{:S(2)}) async-start(f32[32,1,128]{2,1,0:T(1,128)} %get-tuple-element.50), calls=%async_computation | async-start | bytes 32768 | tf_op jit(solution)/shard_map/all_to_all | solution.py:396

commit v11 on v10

--- a/solution.py
+++ b/solution.py
@@ -57,12 +57,6 @@
     below = lax.ppermute(wide, LAT, [(i, i + 1) for i in range(count - 1)])
     above = lax.ppermute(wide, LAT, [(i + 1, i) for i in range(count - 1)])
     return below, above
-
-
-def all_bands_paired(wide):
-    count = extent(LAT)
-    swap = lax.ppermute(wide, LAT, [p for a, b in pairs(count, 0) for p in ((a, b), (b, a))])
-    return swap, lax.all_gather(wide, LAT, axis_index_groups=pairs(count, 1))
 
 
 def rounded(value):
@@ -199,8 +193,10 @@
     ref[RHS : 2 * RHS, :] = (value - high.astype(jnp.float32)).astype(jnp.bfloat16)
 
 
-def apply_kernel(near_ref, tile_ref, added_ref, scale_ref, sum_ref):
-    sum_ref[...] = added_ref[...] * scale_ref[...] + products(lambda slot: near_ref[slot], tile_ref)
+def apply_kernel(near_ref, tile_ref, added_ref, *refs):
+    *scale, sum_ref = refs
+    added = added_ref[...] * scale[0][...] if scale else added_ref[...]
+    sum_ref[...] = added + products(lambda slot: near_ref[slot], tile_ref)
 
 
 SAME_BAND = (1, 0, 1)
@@ -303,23 +299,10 @@
     copies_ref[...] = jnp.broadcast_to(row[None], copies_ref.shape)
 
 
-def paired_kernel(swap_ref, both_ref, below_ref, above_ref, part_ref, sum_ref, sent_ref):
-    band = lax.axis_index(LAT)
-    inside = jnp.where((band == 0) | (band == BANDS - 1), 0.0, 1.0)
-
-    def add(swap_tiles, both_tiles, position):
-        total = part_ref[...] + products(lambda slot: swap_ref[slot], swap_tiles)
-        total = total + inside * products(lambda slot: both_ref[position, slot], both_tiles)
-        sum_ref[...] = total
-        send(sent_ref, total)
-
-    @pl.when(band % 2 == 1)
-    def _():
-        add(below_ref, above_ref, 1)
-
-    @pl.when(band % 2 == 0)
-    def _():
-        add(above_ref, below_ref, 0)
+def second_kernel(near_ref, tile_ref, part_ref, sum_ref, sent_ref):
+    total = part_ref[...] + products(lambda slot: near_ref[slot], tile_ref)
+    sum_ref[...] = total
+    send(sent_ref, total)
 
 
 def above_kernel(near_ref, total_ref, tile_ref, lower_ref, third_ref, copies_ref):
@@ -374,15 +357,11 @@
         build_other_kernel, [TILES, FIELD, SENT, SENT], [above, own, part, outer_own, outer], [TILES]
     )
     wide = jnp.stack([outer_sent, sent, partner(sent, LON, 0)])
-    swap, both = all_bands_paired(wide)
-    part, = call(apply_kernel, [FIELD], [wide, tiles, first, error_var], "apply")
+    below, above = all_bands(wide)
     field = FIELD
-    second, sent = call(
-        paired_kernel,
-        [field, SENT],
-        [swap, both, tiles_below, tiles_above, part],
-        "paired",
-    )
+    part, = call(apply_kernel, [field], [wide, tiles, first, error_var], "apply")
+    part, = call(apply_kernel, [field], [below, tiles_below, part], "apply")
+    second, sent = call(second_kernel, [field, SENT], [above, tiles_above, part], "second")
     wide = widened(sent)
     below, above = all_bands(wide)
     part, row = call(

time: 91.7 us -> 92.4 us (level)
  blocking collectives: 52.9 us -> 46.6 us
  waiting for transfers between devices: 10.1 us -> 13.5 us
  starting transfers between devices: 18.6 us -> 22 us
    all_gather x1 -> x0, blocking collectives: 6.26 us -> none  [all_bands_paired(): return (swap, lax.all_gather(wide, LAT, axis_index_groups=pairs(count, 1)))]
    ppermute x2 -> x3, starting transfers between devices: 3.71 us -> 8.97 us  [all_bands(): below = lax.ppermute(wide, LAT, [(i, i + 1) for i in range(count - 1)])]
    ppermute x2 -> x3, waiting for transfers between devices: 1.61 us -> 4.81 us  [all_bands(): above = lax.ppermute(wide, LAT, [(i + 1, i) for i in range(count - 1)])]
    ppermute x1 -> x0, starting transfers between devices: 3.12 us -> none  [all_bands_paired(): lax.ppermute(wide, LAT, [p for a, b in pairs(count, 0) for p in ((a, b),...]
    ppermute x2 -> x3, starting transfers between devices: 2.58 us -> 3.88 us  [all_bands(): above = lax.ppermute(wide, LAT, [(i + 1, i) for i in range(count - 1)])]
    pallas_call x6 -> x7, Pallas kernels: 3.68 us -> 3.78 us  [call(): pl.pallas_call(kernel, out_shape=shapes, in_specs=[whole()] * len(operand...]
  transfers between devices with their start and end apart: 6 -> 7, of which waited for: 2 -> 4; matrix products, arithmetic and copies ran while one was open for 0% -> 0% of each run, Pallas kernels for 5% -> 6%
where the time goes in v11:
time: 92.4 us; the launch traced here: 91.9 us
  blocking collectives  46.6 us (50%)
  starting transfers between devices  22 us (24%)
  waiting for transfers between devices  13.5 us (15%)
  Pallas kernels  8.92 us (10%)
    all_gather x5, blocking collectives, partner(): lax.all_gather(block, axes, axis_index_groups=pairs(extent(axes), first))  30.4 us
    all_to_all x1, blocking collectives, local(): totals = lax.all_to_all(partial, GROUPS[1], 0, 0)  16.2 us
    all_to_all x1, starting transfers between devices, local(): partial = lax.all_to_all(partial, GROUPS[0], 0, 0)  9.19 us
    ppermute x3, starting transfers between devices, all_bands(): below = lax.ppermute(wide, LAT, [(i, i + 1) for i in range(count - 1)])  8.97 us
    all_to_all x1, waiting for transfers between devices, local(): partial = lax.all_to_all(partial, GROUPS[0], 0, 0)  8.5 us
    ppermute x3, waiting for transfers between devices, all_bands(): above = lax.ppermute(wide, LAT, [(i + 1, i) for i in range(count - 1)])  4.81 us
    pallas_call x3, Pallas kernels, build(): pl.pallas_call(kernel, out_shape=shapes, in_specs=[whole()] * len(operand...  4.2 us
    ppermute x3, starting transfers between devices, all_bands(): above = lax.ppermute(wide, LAT, [(i + 1, i) for i in range(count - 1)])  3.88 us
  transfers between devices with their start and end apart: 7, of which 4 were waited for; matrix products, arithmetic and copies ran while one was open for 0% of the time, Pallas kernels for 6%

profile of v11, /device:TPU:1, one launch (start us, length us, event | category | flops | bytes accessed | tf_op | source)
XLA Modules:
  0.0 91.9 jit_solution(4876321935979682027)
XLA Ops:
  0.6 0.9 %describe.1 = (bf16[32,512]{1,0:T(8,128)(2,1)S(1)}, bf16[3,48,512]{2,1,0:T(8,128)(2,1)S(1)}, f32[1,512]{1,0:T(1,128)S(1)}, f32[16,512]{1,0:T(8,128)S(1)}, f32[16,512]{1,0:T(8,128)S(1)}) custom-call(f32[16,512]{1,0:T(8,128)} %bitcast.28, f32[1,512]{1,0:T(1,128)} %bitcast.30, bf16[3,512]{1,0:T(4,128)(2,1)} %bitcast.29, bf16[1,512]{1,0:T(2,128)(2,1)} %bitcast.31, ...), custom_call_target="tpu_custom_call" | custom-call | tf_op jit(solution)/shard_map/describe/pallas_call | solution.py:132
  1.6 8.4 %all-gather = bf16[64,512]{1,0:T(8,128)(2,1)S(1)} all-gather(bf16[32,512]{1,0:T(8,128)(2,1)S(1)} %get-tuple-element.28), channel_id=2, replica_groups={{0,1},{2,3},{4,5},{6,7},{8,9},{10,11},{12,13},{14,15},{16,17},{18,19},{..., dimensions={0}, use_global_device_ids=true | all-gather | bytes 98304 | tf_op jit(solution)/shard_map/all_gather | solution.py:43
  10.0 4.4 %all-gather.1 = bf16[4,32,512]{2,1,0:T(8,128)(2,1)S(1)} all-gather(bf16[2,32,512]{2,1,0:T(8,128)(2,1)S(1)} %pad_maximum_fusion.3), channel_id=3, replica_groups={{1,2},{3,4},{5,6},{7,8},{9,10},{11,12},{13,14},{15,16},{17,18},{19,20},..., dimensions={0}, use_global_device_ids=true | all-gather | bytes 196608 | tf_op jit(solution)/shard_map/all_gather | solution.py:43
  14.4 1.3 %collective-permute-start.1 = (bf16[4,32,512]{2,1,0:T(8,128)(2,1)S(1)}, bf16[4,32,512]{2,1,0:T(8,128)(2,1)S(1)}, u32[]{:S(2)}, u32[]{:S(2)}) collective-permute-start(bf16[4,32,512]{2,1,0:T(8,128)(2,1)S(1)} %pad_maximum_fusion.near_ref), channel_id=1, source_target_pairs={{0,64},{64,128},{128,192},{192,256},{256,320},{320,384},{384,448},... | collective-permute-start | bytes 393224 | tf_op jit(solution)/shard_map/ppermute | solution.py:57
  15.7 1.3 %collective-permute-start = (bf16[4,32,512]{2,1,0:T(8,128)(2,1)S(1)}, bf16[4,32,512]{2,1,0:T(8,128)(2,1)S(1)}, u32[]{:S(2)}, u32[]{:S(2)}) collective-permute-start(bf16[4,32,512]{2,1,0:T(8,128)(2,1)S(1)} %pad_maximum_fusion.near_ref), channel_id=1, source_target_pairs={{64,0},{128,64},{192,128},{256,192},{320,256},{384,320},{448,384},... | collective-permute-start | bytes 393224 | tf_op jit(solution)/shard_map/ppermute | solution.py:58
  17.0 1.4 %build.3 = (bf16[3,512,512]{2,1,0:T(8,128)(2,1)S(1)}, f32[16,512]{1,0:T(8,128)S(1)}, bf16[3,48,512]{2,1,0:T(8,128)(2,1)S(1)}, f32[16,512]{1,0:T(8,128)S(1)}) custom-call(bf16[4,32,512]{2,1,0:T(8,128)(2,1)S(1)} %pad_maximum_fusion.near_ref, bf16[3,48,512]{2,1,0:T(8,128)(2,1)S(1)} %get-tuple-element.29.own_ref, f32[16,512]{1,0:T(8,128)S(1)} %get-tuple-element.30.added_ref), custom_call_target="tpu_custom_call" | custom-call | flops 830472192 | bytes 1572864 | tf_op jit(solution)/shard_map/build/pallas_call | solution.py:222
  18.4 0.0 collective-permute-done.1.near_ref
  18.4 1.4 %build.4 = (bf16[3,512,512]{2,1,0:T(8,128)(2,1)S(1)}, f32[16,512]{1,0:T(8,128)S(1)}, f32[16,512]{1,0:T(8,128)S(1)}) custom-call(bf16[4,32,512]{2,1,0:T(8,128)(2,1)S(1)} %collective-permute-done.1.near_ref, bf16[3,48,512]{2,1,0:T(8,128)(2,1)S(1)} %get-tuple-element.29.own_ref, f32[16,512]{1,0:T(8,128)S(1)} %get-tuple-element.31.added_ref, ...), custom_call_target="tpu_custom_call" | custom-call | flops 830472192 | bytes 1572864 | tf_op jit(solution)/shard_map/build/pallas_call | solution.py:222
  19.8 1.6 %collective-permute-done.near_ref = bf16[4,32,512]{2,1,0:T(8,128)(2,1)S(1)} collective-permute-done((bf16[4,32,512]{2,1,0:T(8,128)(2,1)S(1)}, bf16[4,32,512]{2,1,0:T(8,128)(2,1)S(1)}, u32[]{:S(2)}, u32[]{:S(2)}) %collective-permute-start) | collective-permute-done | bytes 131104 | tf_op jit(solution)/shard_map/ppermute | solution.py:58
  21.4 1.4 %build.5 = (bf16[3,512,512]{2,1,0:T(8,128)(2,1)S(1)}, f32[16,512]{1,0:T(8,128)S(1)}, bf16[32,512]{1,0:T(8,128)(2,1)S(1)}, bf16[32,512]{1,0:T(8,128)(2,1)S(1)}) custom-call(bf16[4,32,512]{2,1,0:T(8,128)(2,1)S(1)} %collective-permute-done.near_ref, bf16[3,48,512]{2,1,0:T(8,128)(2,1)S(1)} %get-tuple-element.29.own_ref, ...), custom_call_target="tpu_custom_call" | custom-call | flops 830472192 | bytes 1572864 | tf_op jit(solution)/shard_map/build/pallas_call | solution.py:222
  22.8 10.4 %all-gather.2 = bf16[64,512]{1,0:T(8,128)(2,1)S(1)} all-gather(bf16[32,512]{1,0:T(8,128)(2,1)S(1)} %get-tuple-element.37), channel_id=4, replica_groups={{0,1},{2,3},{4,5},{6,7},{8,9},{10,11},{12,13},{14,15},{16,17},{18,19},{..., dimensions={0}, use_global_device_ids=true | all-gather | bytes 98304 | tf_op jit(solution)/shard_map/all_gather | solution.py:43
  33.2 3.1 %collective-permute-start.3 = (bf16[3,32,512]{2,1,0:T(8,128)(2,1)S(1)}, bf16[3,32,512]{2,1,0:T(8,128)(2,1)S(1)}, u32[]{:S(2)}, u32[]{:S(2)}) collective-permute-start(bf16[3,32,512]{2,1,0:T(8,128)(2,1)S(1)} %pad_maximum_fusion.1.near_ref), channel_id=1, source_target_pairs={{0,64},{64,128},{128,192},{192,256},{256,320},{320,384},{384,448},... | collective-permute-start | bytes 294920 | tf_op jit(solution)/shard_map/ppermute | solution.py:57
  36.3 1.3 %collective-permute-start.2 = (bf16[3,32,512]{2,1,0:T(8,128)(2,1)S(1)}, bf16[3,32,512]{2,1,0:T(8,128)(2,1)S(1)}, u32[]{:S(2)}, u32[]{:S(2)}) collective-permute-start(bf16[3,32,512]{2,1,0:T(8,128)(2,1)S(1)} %pad_maximum_fusion.1.near_ref), channel_id=1, source_target_pairs={{64,0},{128,64},{192,128},{256,192},{320,256},{384,320},{448,384},... | collective-permute-start | bytes 294920 | tf_op jit(solution)/shard_map/ppermute | solution.py:58
  37.6 0.3 apply.2.added_ref
  38.0 0.2 collective-permute-done.3.near_ref
  38.2 0.3 apply.3.part_ref
  38.5 3.2 %collective-permute-done.2.near_ref = bf16[3,32,512]{2,1,0:T(8,128)(2,1)S(1)} collective-permute-done((bf16[3,32,512]{2,1,0:T(8,128)(2,1)S(1)}, bf16[3,32,512]{2,1,0:T(8,128)(2,1)S(1)}, u32[]{:S(2)}, u32[]{:S(2)}) %collective-permute-start.2) | collective-permute-done | bytes 98336 | tf_op jit(solution)/shard_map/ppermute | solution.py:58
  41.7 0.3 second.1
  42.1 3.3 %all-gather.3 = bf16[64,512]{1,0:T(8,128)(2,1)S(1)} all-gather(bf16[32,512]{1,0:T(8,128)(2,1)S(1)} %get-tuple-element.44), channel_id=5, replica_groups={{0,1},{2,3},{4,5},{6,7},{8,9},{10,11},{12,13},{14,15},{16,17},{18,19},{..., dimensions={0}, use_global_device_ids=true | all-gather | bytes 98304 | tf_op jit(solution)/shard_map/all_gather | solution.py:43
  45.4 4.0 %all-gather.4 = bf16[64,512]{1,0:T(8,128)(2,1)S(1)} all-gather(bf16[32,512]{1,0:T(8,128)(2,1)S(1)} %get-tuple-element.44), channel_id=6, replica_groups={{1,2},{3,4},{5,6},{7,8},{9,10},{11,12},{13,14},{15,16},{17,18},{19,20},..., dimensions={0}, use_global_device_ids=true | all-gather | bytes 98304 | tf_op jit(solution)/shard_map/all_gather | solution.py:43
  49.4 4.6 %collective-permute-start.5 = (bf16[3,32,512]{2,1,0:T(8,128)(2,1)S(1)}, bf16[3,32,512]{2,1,0:T(8,128)(2,1)S(1)}, u32[]{:S(2)}, u32[]{:S(2)}) collective-permute-start(bf16[3,32,512]{2,1,0:T(8,128)(2,1)S(1)} %pad_maximum_fusion.2.near_ref), channel_id=1, source_target_pairs={{0,64},{64,128},{128,192},{192,256},{256,320},{320,384},{384,448},... | collective-permute-start | bytes 294920 | tf_op jit(solution)/shard_map/ppermute | solution.py:57
  53.9 1.3 %collective-permute-start.4 = (bf16[3,32,512]{2,1,0:T(8,128)(2,1)S(1)}, bf16[3,32,512]{2,1,0:T(8,128)(2,1)S(1)}, u32[]{:S(2)}, u32[]{:S(2)}) collective-permute-start(bf16[3,32,512]{2,1,0:T(8,128)(2,1)S(1)} %pad_maximum_fusion.2.near_ref), channel_id=1, source_target_pairs={{64,0},{128,64},{192,128},{256,192},{320,256},{384,320},{448,384},... | collective-permute-start | bytes 294920 | tf_op jit(solution)/shard_map/ppermute | solution.py:58
  55.2 0.4 same_band.1
  55.7 0.0 collective-permute-done.5.near_ref
  55.7 1.2 %below.1 = (f32[16,512]{1,0:T(8,128)S(1)}, f32[32,1,128]{2,1,0:T(1,128)}) custom-call(bf16[3,32,512]{2,1,0:T(8,128)(2,1)S(1)} %collective-permute-done.5.near_ref, bf16[3,512,512]{2,1,0:T(8,128)(2,1)S(1)} %get-tuple-element.39.tile_ref, f32[16,512]{1,0:T(8,128)S(1)} %get-tuple-element.48.part_ref, f32[16,512]{1,0:T(8,128)S(1)} %get-tuple-element.46.second_ref, ...), custom_call_target="tpu_custom_call" | custom-call | flops 25165824 | bytes 1572864 | tf_op jit(solution)/shard_map/below/pallas_call | solution.py:328
  56.9 9.2 %all-to-all-start = ((f32[32,1,128]{2,1,0:T(1,128)}), f32[32,1,128]{2,1,0:T(1,128)S(1)}, u32[]{:S(2)}, u32[]{:S(2)}) async-start(f32[32,1,128]{2,1,0:T(1,128)} %get-tuple-element.50), calls=%async_computation | async-start | bytes 32768 | tf_op jit(solution)/shard_map/all_to_all | solution.py:375
  66.1 0.0 collective-permute-done.4.near_ref
  66.1 8.5 %all-to-all-done.total_ref = f32[32,1,128]{2,1,0:T(1,128)S(1)} async-done(((f32[32,1,128]{2,1,0:T(1,128)}), f32[32,1,128]{2,1,0:T(1,128)S(1)}, u32[]{:S(2)}, u32[]{:S(2)}) %all-to-all-start) | async-done | bytes 16416 | tf_op jit(solution)/shard_map/all_to_all | solution.py:375
  74.6 0.3 above.1
  74.9 16.2 %all_to_all.10.total_ref = f32[16,1,128]{2,1,0:T(1,128)S(1)} all-to-all(f32[16,1,128]{2,1,0:T(1,128)S(1)} %get-tuple-element.52), channel_id=1, replica_groups=mesh['z_lo'=2,'x'=4,'z_hi'=4,'y'=8,'core'=2] {'y','core'}, dimensions={0} | all-to-all | bytes 16384 | tf_op jit(solution)/shard_map/all_to_all | solution.py:377
  91.1 0.8 finish.1
  (10 shorter events, 0.1 us)
Async XLA Ops:
  14.4 4.0 %collective-permute-start.1 = (bf16[4,32,512]{2,1,0:T(8,128)(2,1)S(1)}, bf16[4,32,512]{2,1,0:T(8,128)(2,1)S(1)}, u32[]{:S(2)}, u32[]{:S(2)}) collective-permute-start(bf16[4,32,512]{2,1,0:T(8,128)(2,1)S(1)} %pad_maximum_fusion.near_ref), channel_id=1, source_target_pairs={{0,64},{64,128},{128,192},{192,256},{256,320},{320,384},{384,448},... | collective-permute-start | bytes 393224 | tf_op jit(solution)/shard_map/ppermute | solution.py:57
  15.7 5.7 %collective-permute-start = (bf16[4,32,512]{2,1,0:T(8,128)(2,1)S(1)}, bf16[4,32,512]{2,1,0:T(8,128)(2,1)S(1)}, u32[]{:S(2)}, u32[]{:S(2)}) collective-permute-start(bf16[4,32,512]{2,1,0:T(8,128)(2,1)S(1)} %pad_maximum_fusion.near_ref), channel_id=1, source_target_pairs={{64,0},{128,64},{192,128},{256,192},{320,256},{384,320},{448,384},... | collective-permute-start | bytes 393224 | tf_op jit(solution)/shard_map/ppermute | solution.py:58
  33.2 4.9 %collective-permute-start.3 = (bf16[3,32,512]{2,1,0:T(8,128)(2,1)S(1)}, bf16[3,32,512]{2,1,0:T(8,128)(2,1)S(1)}, u32[]{:S(2)}, u32[]{:S(2)}) collective-permute-start(bf16[3,32,512]{2,1,0:T(8,128)(2,1)S(1)} %pad_maximum_fusion.1.near_ref), channel_id=1, source_target_pairs={{0,64},{64,128},{128,192},{192,256},{256,320},{320,384},{384,448},... | collective-permute-start | bytes 294920 | tf_op jit(solution)/shard_map/ppermute | solution.py:57
  36.3 5.4 %collective-permute-start.2 = (bf16[3,32,512]{2,1,0:T(8,128)(2,1)S(1)}, bf16[3,32,512]{2,1,0:T(8,128)(2,1)S(1)}, u32[]{:S(2)}, u32[]{:S(2)}) collective-permute-start(bf16[3,32,512]{2,1,0:T(8,128)(2,1)S(1)} %pad_maximum_fusion.1.near_ref), channel_id=1, source_target_pairs={{64,0},{128,64},{192,128},{256,192},{320,256},{384,320},{448,384},... | collective-permute-start | bytes 294920 | tf_op jit(solution)/shard_map/ppermute | solution.py:58
  49.4 6.3 %collective-permute-start.5 = (bf16[3,32,512]{2,1,0:T(8,128)(2,1)S(1)}, bf16[3,32,512]{2,1,0:T(8,128)(2,1)S(1)}, u32[]{:S(2)}, u32[]{:S(2)}) collective-permute-start(bf16[3,32,512]{2,1,0:T(8,128)(2,1)S(1)} %pad_maximum_fusion.2.near_ref), channel_id=1, source_target_pairs={{0,64},{64,128},{128,192},{192,256},{256,320},{320,384},{384,448},... | collective-permute-start | bytes 294920 | tf_op jit(solution)/shard_map/ppermute | solution.py:57
  53.9 12.1 %collective-permute-start.4 = (bf16[3,32,512]{2,1,0:T(8,128)(2,1)S(1)}, bf16[3,32,512]{2,1,0:T(8,128)(2,1)S(1)}, u32[]{:S(2)}, u32[]{:S(2)}) collective-permute-start(bf16[3,32,512]{2,1,0:T(8,128)(2,1)S(1)} %pad_maximum_fusion.2.near_ref), channel_id=1, source_target_pairs={{64,0},{128,64},{192,128},{256,192},{320,256},{384,320},{448,384},... | collective-permute-start | bytes 294920 | tf_op jit(solution)/shard_map/ppermute | solution.py:58
  56.9 17.7 %all-to-all-start = ((f32[32,1,128]{2,1,0:T(1,128)}), f32[32,1,128]{2,1,0:T(1,128)S(1)}, u32[]{:S(2)}, u32[]{:S(2)}) async-start(f32[32,1,128]{2,1,0:T(1,128)} %get-tuple-element.50), calls=%async_computation | async-start | bytes 32768 | tf_op jit(solution)/shard_map/all_to_all | solution.py:375

commit v12 on v10

--- a/solution.py
+++ b/solution.py
@@ -61,8 +61,8 @@
 
 def all_bands_paired(wide):
     count = extent(LAT)
-    swap = lax.ppermute(wide, LAT, [p for a, b in pairs(count, 0) for p in ((a, b), (b, a))])
-    return swap, lax.all_gather(wide, LAT, axis_index_groups=pairs(count, 1))
+    swap = lax.ppermute(wide, LAT, [p for a, b in pairs(count - 1, 1) for p in ((a, b), (b, a))])
+    return swap, lax.all_gather(wide, LAT, axis_index_groups=pairs(count, 0))
 
 
 def rounded(value):
@@ -304,22 +304,21 @@
 
 
 def paired_kernel(swap_ref, both_ref, below_ref, above_ref, part_ref, sum_ref, sent_ref):
-    band = lax.axis_index(LAT)
-    inside = jnp.where((band == 0) | (band == BANDS - 1), 0.0, 1.0)
+    odd = lax.axis_index(LAT) % 2
 
     def add(swap_tiles, both_tiles, position):
         total = part_ref[...] + products(lambda slot: swap_ref[slot], swap_tiles)
-        total = total + inside * products(lambda slot: both_ref[position, slot], both_tiles)
+        total = total + products(lambda slot: both_ref[position, slot], both_tiles)
         sum_ref[...] = total
         send(sent_ref, total)
 
-    @pl.when(band % 2 == 1)
+    @pl.when(odd == 1)
+    def _():
+        add(above_ref, below_ref, 0)
+
+    @pl.when(odd == 0)
     def _():
         add(below_ref, above_ref, 1)
-
-    @pl.when(band % 2 == 0)
-    def _():
-        add(above_ref, below_ref, 0)
 
 
 def above_kernel(near_ref, total_ref, tile_ref, lower_ref, third_ref, copies_ref):

time: 91.7 us -> 92 us (level)
    ppermute x1, starting transfers between devices: 3.12 us -> 0.67 us  [all_bands_paired(): lax.ppermute(wide, LAT, [p for a, b in pairs(count - 1, 1) for p in ((a,...]
    all_to_all x1, starting transfers between devices: 9.22 us -> 11.2 us  [local(): partial = lax.all_to_all(partial, GROUPS[0], 0, 0)]
    ppermute x2, starting transfers between devices: 3.71 us -> 4.73 us  [all_bands(): below = lax.ppermute(wide, LAT, [(i, i + 1) for i in range(count - 1)])]
where the time goes in v12:
time: 92 us; the launch traced here: 91.6 us
  blocking collectives  52.6 us (57%)
  starting transfers between devices  19.2 us (21%)
  waiting for transfers between devices  10.1 us (11%)
  Pallas kernels  8.83 us (10%)
    all_gather x5, blocking collectives, partner(): lax.all_gather(block, axes, axis_index_groups=pairs(extent(axes), first))  29.8 us
    all_to_all x1, blocking collectives, local(): totals = lax.all_to_all(partial, GROUPS[1], 0, 0)  16.2 us
    all_to_all x1, starting transfers between devices, local(): partial = lax.all_to_all(partial, GROUPS[0], 0, 0)  11.2 us
    all_to_all x1, waiting for transfers between devices, local(): partial = lax.all_to_all(partial, GROUPS[0], 0, 0)  8.5 us
    all_gather x1, blocking collectives, all_bands_paired(): return (swap, lax.all_gather(wide, LAT, axis_index_groups=pairs(count, 0)))  6.61 us
    ppermute x2, starting transfers between devices, all_bands(): below = lax.ppermute(wide, LAT, [(i, i + 1) for i in range(count - 1)])  4.73 us
    pallas_call x3, Pallas kernels, build(): pl.pallas_call(kernel, out_shape=shapes, in_specs=[whole()] * len(operand...  4.2 us
    pallas_call x6, Pallas kernels, call(): pl.pallas_call(kernel, out_shape=shapes, in_specs=[whole()] * len(operand...  3.68 us
  transfers between devices with their start and end apart: 6, of which 2 were waited for; matrix products, arithmetic and copies ran while one was open for 0% of the time, Pallas kernels for 5%

profile of v12, /device:TPU:1, one launch (start us, length us, event | category | flops | bytes accessed | tf_op | source)
XLA Modules:
  0.0 91.6 jit_solution(14389301501724794010)
XLA Ops:
  0.6 0.9 %describe.1 = (bf16[32,512]{1,0:T(8,128)(2,1)S(1)}, bf16[3,48,512]{2,1,0:T(8,128)(2,1)S(1)}, f32[1,512]{1,0:T(1,128)S(1)}, f32[16,512]{1,0:T(8,128)S(1)}, f32[16,512]{1,0:T(8,128)S(1)}) custom-call(f32[16,512]{1,0:T(8,128)} %bitcast.30, f32[1,512]{1,0:T(1,128)} %bitcast.32, bf16[3,512]{1,0:T(4,128)(2,1)} %bitcast.31, bf16[1,512]{1,0:T(2,128)(2,1)} %bitcast.33, ...), custom_call_target="tpu_custom_call" | custom-call | tf_op jit(solution)/shard_map/describe/pallas_call | solution.py:138
  1.6 8.4 %all-gather = bf16[64,512]{1,0:T(8,128)(2,1)S(1)} all-gather(bf16[32,512]{1,0:T(8,128)(2,1)S(1)} %get-tuple-element.28), channel_id=2, replica_groups={{0,1},{2,3},{4,5},{6,7},{8,9},{10,11},{12,13},{14,15},{16,17},{18,19},{..., dimensions={0}, use_global_device_ids=true | all-gather | bytes 98304 | tf_op jit(solution)/shard_map/all_gather | solution.py:43
  10.0 4.4 %all-gather.1 = bf16[4,32,512]{2,1,0:T(8,128)(2,1)S(1)} all-gather(bf16[2,32,512]{2,1,0:T(8,128)(2,1)S(1)} %pad_maximum_fusion.3), channel_id=3, replica_groups={{1,2},{3,4},{5,6},{7,8},{9,10},{11,12},{13,14},{15,16},{17,18},{19,20},..., dimensions={0}, use_global_device_ids=true | all-gather | bytes 196608 | tf_op jit(solution)/shard_map/all_gather | solution.py:43
  14.4 1.3 %collective-permute-start.1 = (bf16[4,32,512]{2,1,0:T(8,128)(2,1)S(1)}, bf16[4,32,512]{2,1,0:T(8,128)(2,1)S(1)}, u32[]{:S(2)}, u32[]{:S(2)}) collective-permute-start(bf16[4,32,512]{2,1,0:T(8,128)(2,1)S(1)} %pad_maximum_fusion.near_ref), channel_id=1, source_target_pairs={{0,64},{64,128},{128,192},{192,256},{256,320},{320,384},{384,448},... | collective-permute-start | bytes 393224 | tf_op jit(solution)/shard_map/ppermute | solution.py:57
  15.7 1.3 %collective-permute-start = (bf16[4,32,512]{2,1,0:T(8,128)(2,1)S(1)}, bf16[4,32,512]{2,1,0:T(8,128)(2,1)S(1)}, u32[]{:S(2)}, u32[]{:S(2)}) collective-permute-start(bf16[4,32,512]{2,1,0:T(8,128)(2,1)S(1)} %pad_maximum_fusion.near_ref), channel_id=1, source_target_pairs={{64,0},{128,64},{192,128},{256,192},{320,256},{384,320},{448,384},... | collective-permute-start | bytes 393224 | tf_op jit(solution)/shard_map/ppermute | solution.py:58
  17.0 1.4 %build.3 = (bf16[3,512,512]{2,1,0:T(8,128)(2,1)S(1)}, f32[16,512]{1,0:T(8,128)S(1)}, bf16[3,48,512]{2,1,0:T(8,128)(2,1)S(1)}, f32[16,512]{1,0:T(8,128)S(1)}) custom-call(bf16[4,32,512]{2,1,0:T(8,128)(2,1)S(1)} %pad_maximum_fusion.near_ref, bf16[3,48,512]{2,1,0:T(8,128)(2,1)S(1)} %get-tuple-element.29.own_ref, f32[16,512]{1,0:T(8,128)S(1)} %get-tuple-element.30.added_ref), custom_call_target="tpu_custom_call" | custom-call | flops 830472192 | bytes 1572864 | tf_op jit(solution)/shard_map/build/pallas_call | solution.py:226
  18.4 0.0 collective-permute-done.1.near_ref
  18.4 1.4 %build.4 = (bf16[3,512,512]{2,1,0:T(8,128)(2,1)S(1)}, f32[16,512]{1,0:T(8,128)S(1)}, f32[16,512]{1,0:T(8,128)S(1)}) custom-call(bf16[4,32,512]{2,1,0:T(8,128)(2,1)S(1)} %collective-permute-done.1.near_ref, bf16[3,48,512]{2,1,0:T(8,128)(2,1)S(1)} %get-tuple-element.29.own_ref, f32[16,512]{1,0:T(8,128)S(1)} %get-tuple-element.31.added_ref, ...), custom_call_target="tpu_custom_call" | custom-call | flops 830472192 | bytes 1572864 | tf_op jit(solution)/shard_map/build/pallas_call | solution.py:226
  19.8 1.6 %collective-permute-done.near_ref = bf16[4,32,512]{2,1,0:T(8,128)(2,1)S(1)} collective-permute-done((bf16[4,32,512]{2,1,0:T(8,128)(2,1)S(1)}, bf16[4,32,512]{2,1,0:T(8,128)(2,1)S(1)}, u32[]{:S(2)}, u32[]{:S(2)}) %collective-permute-start) | collective-permute-done | bytes 131104 | tf_op jit(solution)/shard_map/ppermute | solution.py:58
  21.4 1.4 %build.5 = (bf16[3,512,512]{2,1,0:T(8,128)(2,1)S(1)}, f32[16,512]{1,0:T(8,128)S(1)}, bf16[32,512]{1,0:T(8,128)(2,1)S(1)}, bf16[32,512]{1,0:T(8,128)(2,1)S(1)}) custom-call(bf16[4,32,512]{2,1,0:T(8,128)(2,1)S(1)} %collective-permute-done.near_ref, bf16[3,48,512]{2,1,0:T(8,128)(2,1)S(1)} %get-tuple-element.29.own_ref, ...), custom_call_target="tpu_custom_call" | custom-call | flops 830472192 | bytes 1572864 | tf_op jit(solution)/shard_map/build/pallas_call | solution.py:226
  22.8 10.4 %all-gather.2 = bf16[64,512]{1,0:T(8,128)(2,1)S(1)} all-gather(bf16[32,512]{1,0:T(8,128)(2,1)S(1)} %get-tuple-element.37), channel_id=4, replica_groups={{0,1},{2,3},{4,5},{6,7},{8,9},{10,11},{12,13},{14,15},{16,17},{18,19},{..., dimensions={0}, use_global_device_ids=true | all-gather | bytes 98304 | tf_op jit(solution)/shard_map/all_gather | solution.py:43
  33.2 0.7 collective-permute-start.2
  33.9 0.3 apply.1.part_ref
  34.2 6.6 %all-gather.3 = bf16[6,32,512]{2,1,0:T(8,128)(2,1)S(1)} all-gather(bf16[3,32,512]{2,1,0:T(8,128)(2,1)S(1)} %pad_maximum_fusion.1.near_ref), channel_id=5, replica_groups={{0,64},{128,192},{256,320},{384,448},{1,65},{129,193},{257,321},{385,44..., dimensions={0}, use_global_device_ids=true | all-gather | bytes 294912 | tf_op jit(solution)/shard_map/all_gather | solution.py:65
  40.9 0.0 collective-permute-done.2.swap_ref
  40.9 0.6 paired.1
  41.4 2.7 %all-gather.4 = bf16[64,512]{1,0:T(8,128)(2,1)S(1)} all-gather(bf16[32,512]{1,0:T(8,128)(2,1)S(1)} %get-tuple-element.44), channel_id=6, replica_groups={{0,1},{2,3},{4,5},{6,7},{8,9},{10,11},{12,13},{14,15},{16,17},{18,19},{..., dimensions={0}, use_global_device_ids=true | all-gather | bytes 98304 | tf_op jit(solution)/shard_map/all_gather | solution.py:43
  44.1 4.0 %all-gather.5 = bf16[64,512]{1,0:T(8,128)(2,1)S(1)} all-gather(bf16[32,512]{1,0:T(8,128)(2,1)S(1)} %get-tuple-element.44), channel_id=7, replica_groups={{1,2},{3,4},{5,6},{7,8},{9,10},{11,12},{13,14},{15,16},{17,18},{19,20},..., dimensions={0}, use_global_device_ids=true | all-gather | bytes 98304 | tf_op jit(solution)/shard_map/all_gather | solution.py:43
  48.2 3.4 %collective-permute-start.4 = (bf16[3,32,512]{2,1,0:T(8,128)(2,1)S(1)}, bf16[3,32,512]{2,1,0:T(8,128)(2,1)S(1)}, u32[]{:S(2)}, u32[]{:S(2)}) collective-permute-start(bf16[3,32,512]{2,1,0:T(8,128)(2,1)S(1)} %pad_maximum_fusion.2.near_ref), channel_id=1, source_target_pairs={{0,64},{64,128},{128,192},{192,256},{256,320},{320,384},{384,448},... | collective-permute-start | bytes 294920 | tf_op jit(solution)/shard_map/ppermute | solution.py:57
  51.6 1.3 %collective-permute-start.3 = (bf16[3,32,512]{2,1,0:T(8,128)(2,1)S(1)}, bf16[3,32,512]{2,1,0:T(8,128)(2,1)S(1)}, u32[]{:S(2)}, u32[]{:S(2)}) collective-permute-start(bf16[3,32,512]{2,1,0:T(8,128)(2,1)S(1)} %pad_maximum_fusion.2.near_ref), channel_id=1, source_target_pairs={{64,0},{128,64},{192,128},{256,192},{320,256},{384,320},{448,384},... | collective-permute-start | bytes 294920 | tf_op jit(solution)/shard_map/ppermute | solution.py:58
  52.9 0.4 same_band.1
  53.3 0.0 collective-permute-done.4.near_ref
  53.3 1.2 %below.1 = (f32[16,512]{1,0:T(8,128)S(1)}, f32[32,1,128]{2,1,0:T(1,128)}) custom-call(bf16[3,32,512]{2,1,0:T(8,128)(2,1)S(1)} %collective-permute-done.4.near_ref, bf16[3,512,512]{2,1,0:T(8,128)(2,1)S(1)} %get-tuple-element.38.below_ref.tile_ref, f32[16,512]{1,0:T(8,128)S(1)} %get-tuple-element.48.part_ref, f32[16,512]{1,0:T(8,128)S(1)} %get-tuple-element.46.second_ref, ...), custom_call_target="tpu_custom_call" | custom-call | flops 25165824 | bytes 1572864 | tf_op jit(solution)/shard_map/below/pallas_call | solution.py:344
  54.5 11.2 %all-to-all-start = ((f32[32,1,128]{2,1,0:T(1,128)}), f32[32,1,128]{2,1,0:T(1,128)S(1)}, u32[]{:S(2)}, u32[]{:S(2)}) async-start(f32[32,1,128]{2,1,0:T(1,128)} %get-tuple-element.50), calls=%async_computation | async-start | bytes 32768 | tf_op jit(solution)/shard_map/all_to_all | solution.py:395
  65.8 0.0 collective-permute-done.3.near_ref
  65.8 8.5 %all-to-all-done.total_ref = f32[32,1,128]{2,1,0:T(1,128)S(1)} async-done(((f32[32,1,128]{2,1,0:T(1,128)}), f32[32,1,128]{2,1,0:T(1,128)S(1)}, u32[]{:S(2)}, u32[]{:S(2)}) %all-to-all-start) | async-done | bytes 16416 | tf_op jit(solution)/shard_map/all_to_all | solution.py:395
  74.3 0.3 above.1
  74.6 16.2 %all_to_all.10.total_ref = f32[16,1,128]{2,1,0:T(1,128)S(1)} all-to-all(f32[16,1,128]{2,1,0:T(1,128)S(1)} %get-tuple-element.52), channel_id=1, replica_groups=mesh['z_lo'=2,'x'=4,'z_hi'=4,'y'=8,'core'=2] {'y','core'}, dimensions={0} | all-to-all | bytes 16384 | tf_op jit(solution)/shard_map/all_to_all | solution.py:397
  90.8 0.8 finish.1
  (10 shorter events, 0.1 us)
Async XLA Ops:
  14.4 4.0 %collective-permute-start.1 = (bf16[4,32,512]{2,1,0:T(8,128)(2,1)S(1)}, bf16[4,32,512]{2,1,0:T(8,128)(2,1)S(1)}, u32[]{:S(2)}, u32[]{:S(2)}) collective-permute-start(bf16[4,32,512]{2,1,0:T(8,128)(2,1)S(1)} %pad_maximum_fusion.near_ref), channel_id=1, source_target_pairs={{0,64},{64,128},{128,192},{192,256},{256,320},{320,384},{384,448},... | collective-permute-start | bytes 393224 | tf_op jit(solution)/shard_map/ppermute | solution.py:57
  15.7 5.7 %collective-permute-start = (bf16[4,32,512]{2,1,0:T(8,128)(2,1)S(1)}, bf16[4,32,512]{2,1,0:T(8,128)(2,1)S(1)}, u32[]{:S(2)}, u32[]{:S(2)}) collective-permute-start(bf16[4,32,512]{2,1,0:T(8,128)(2,1)S(1)} %pad_maximum_fusion.near_ref), channel_id=1, source_target_pairs={{64,0},{128,64},{192,128},{256,192},{320,256},{384,320},{448,384},... | collective-permute-start | bytes 393224 | tf_op jit(solution)/shard_map/ppermute | solution.py:58
  33.2 7.6 %collective-permute-start.2 = (bf16[3,32,512]{2,1,0:T(8,128)(2,1)S(1)}, bf16[3,32,512]{2,1,0:T(8,128)(2,1)S(1)}, u32[]{:S(2)}, u32[]{:S(2)}) collective-permute-start(bf16[3,32,512]{2,1,0:T(8,128)(2,1)S(1)} %pad_maximum_fusion.1.near_ref), channel_id=1, source_target_pairs={{64,128},{128,64},{192,256},{256,192},{320,384},{384,320},{65,129}... | collective-permute-start | bytes 294920 | tf_op jit(solution)/shard_map/ppermute | solution.py:64
  48.2 5.1 %collective-permute-start.4 = (bf16[3,32,512]{2,1,0:T(8,128)(2,1)S(1)}, bf16[3,32,512]{2,1,0:T(8,128)(2,1)S(1)}, u32[]{:S(2)}, u32[]{:S(2)}) collective-permute-start(bf16[3,32,512]{2,1,0:T(8,128)(2,1)S(1)} %pad_maximum_fusion.2.near_ref), channel_id=1, source_target_pairs={{0,64},{64,128},{128,192},{192,256},{256,320},{320,384},{384,448},... | collective-permute-start | bytes 294920 | tf_op jit(solution)/shard_map/ppermute | solution.py:57
  51.6 14.2 %collective-permute-start.3 = (bf16[3,32,512]{2,1,0:T(8,128)(2,1)S(1)}, bf16[3,32,512]{2,1,0:T(8,128)(2,1)S(1)}, u32[]{:S(2)}, u32[]{:S(2)}) collective-permute-start(bf16[3,32,512]{2,1,0:T(8,128)(2,1)S(1)} %pad_maximum_fusion.2.near_ref), channel_id=1, source_target_pairs={{64,0},{128,64},{192,128},{256,192},{320,256},{384,320},{448,384},... | collective-permute-start | bytes 294920 | tf_op jit(solution)/shard_map/ppermute | solution.py:58
  54.5 19.7 %all-to-all-start = ((f32[32,1,128]{2,1,0:T(1,128)}), f32[32,1,128]{2,1,0:T(1,128)S(1)}, u32[]{:S(2)}, u32[]{:S(2)}) async-start(f32[32,1,128]{2,1,0:T(1,128)} %get-tuple-element.50), calls=%async_computation | async-start | bytes 32768 | tf_op jit(solution)/shard_map/all_to_all | solution.py:395

commit v13 on v10

--- a/solution.py
+++ b/solution.py
@@ -374,7 +374,7 @@
         build_other_kernel, [TILES, FIELD, SENT, SENT], [above, own, part, outer_own, outer], [TILES]
     )
     wide = jnp.stack([outer_sent, sent, partner(sent, LON, 0)])
-    swap, both = all_bands_paired(wide)
+    swap, both = all_bands_paired(wide[:, :RHS])
     part, = call(apply_kernel, [FIELD], [wide, tiles, first, error_var], "apply")
     field = FIELD
     second, sent = call(

time: 91.7 us -> 90.9 us (level)
  no operation moved by 1% of the time
where the time goes in v13:
time: 90.9 us; the launch traced here: 90.5 us
  blocking collectives  52.3 us (58%)
  starting transfers between devices  18.4 us (20%)
  waiting for transfers between devices  10.1 us (11%)
  Pallas kernels  8.75 us (10%)
    all_gather x5, blocking collectives, partner(): lax.all_gather(block, axes, axis_index_groups=pairs(extent(axes), first))  30.4 us
    all_to_all x1, blocking collectives, local(): totals = lax.all_to_all(partial, GROUPS[1], 0, 0)  16.2 us
    all_to_all x1, starting transfers between devices, local(): partial = lax.all_to_all(partial, GROUPS[0], 0, 0)  9.22 us
    all_to_all x1, waiting for transfers between devices, local(): partial = lax.all_to_all(partial, GROUPS[0], 0, 0)  8.5 us
    all_gather x1, blocking collectives, all_bands_paired(): return (swap, lax.all_gather(wide, LAT, axis_index_groups=pairs(count, 1)))  5.73 us
    pallas_call x3, Pallas kernels, build(): pl.pallas_call(kernel, out_shape=shapes, in_specs=[whole()] * len(operand...  4.2 us
    pallas_call x6, Pallas kernels, call(): pl.pallas_call(kernel, out_shape=shapes, in_specs=[whole()] * len(operand...  3.6 us
    ppermute x2, starting transfers between devices, all_bands(): below = lax.ppermute(wide, LAT, [(i, i + 1) for i in range(count - 1)])  3.47 us
  transfers between devices with their start and end apart: 6, of which 2 were waited for; matrix products, arithmetic and copies ran while one was open for 0% of the time, Pallas kernels for 5%

profile of v13, /device:TPU:1, one launch (start us, length us, event | category | flops | bytes accessed | tf_op | source)
XLA Modules:
  0.0 90.5 jit_solution(15944373026597168569)
XLA Ops:
  0.6 0.9 %describe.1 = (bf16[32,512]{1,0:T(8,128)(2,1)S(1)}, bf16[3,48,512]{2,1,0:T(8,128)(2,1)S(1)}, f32[1,512]{1,0:T(1,128)S(1)}, f32[16,512]{1,0:T(8,128)S(1)}, f32[16,512]{1,0:T(8,128)S(1)}) custom-call(f32[16,512]{1,0:T(8,128)} %bitcast.30, f32[1,512]{1,0:T(1,128)} %bitcast.32, bf16[3,512]{1,0:T(4,128)(2,1)} %bitcast.31, bf16[1,512]{1,0:T(2,128)(2,1)} %bitcast.33, ...), custom_call_target="tpu_custom_call" | custom-call | tf_op jit(solution)/shard_map/describe/pallas_call | solution.py:138
  1.6 8.4 %all-gather = bf16[64,512]{1,0:T(8,128)(2,1)S(1)} all-gather(bf16[32,512]{1,0:T(8,128)(2,1)S(1)} %get-tuple-element.28), channel_id=2, replica_groups={{0,1},{2,3},{4,5},{6,7},{8,9},{10,11},{12,13},{14,15},{16,17},{18,19},{..., dimensions={0}, use_global_device_ids=true | all-gather | bytes 98304 | tf_op jit(solution)/shard_map/all_gather | solution.py:43
  10.0 4.4 %all-gather.1 = bf16[4,32,512]{2,1,0:T(8,128)(2,1)S(1)} all-gather(bf16[2,32,512]{2,1,0:T(8,128)(2,1)S(1)} %pad_maximum_fusion.3), channel_id=3, replica_groups={{1,2},{3,4},{5,6},{7,8},{9,10},{11,12},{13,14},{15,16},{17,18},{19,20},..., dimensions={0}, use_global_device_ids=true | all-gather | bytes 196608 | tf_op jit(solution)/shard_map/all_gather | solution.py:43
  14.4 1.3 %collective-permute-start.1 = (bf16[4,32,512]{2,1,0:T(8,128)(2,1)S(1)}, bf16[4,32,512]{2,1,0:T(8,128)(2,1)S(1)}, u32[]{:S(2)}, u32[]{:S(2)}) collective-permute-start(bf16[4,32,512]{2,1,0:T(8,128)(2,1)S(1)} %pad_maximum_fusion.near_ref), channel_id=1, source_target_pairs={{0,64},{64,128},{128,192},{192,256},{256,320},{320,384},{384,448},... | collective-permute-start | bytes 393224 | tf_op jit(solution)/shard_map/ppermute | solution.py:57
  15.7 1.3 %collective-permute-start = (bf16[4,32,512]{2,1,0:T(8,128)(2,1)S(1)}, bf16[4,32,512]{2,1,0:T(8,128)(2,1)S(1)}, u32[]{:S(2)}, u32[]{:S(2)}) collective-permute-start(bf16[4,32,512]{2,1,0:T(8,128)(2,1)S(1)} %pad_maximum_fusion.near_ref), channel_id=1, source_target_pairs={{64,0},{128,64},{192,128},{256,192},{320,256},{384,320},{448,384},... | collective-permute-start | bytes 393224 | tf_op jit(solution)/shard_map/ppermute | solution.py:58
  17.0 1.4 %build.3 = (bf16[3,512,512]{2,1,0:T(8,128)(2,1)S(1)}, f32[16,512]{1,0:T(8,128)S(1)}, bf16[3,48,512]{2,1,0:T(8,128)(2,1)S(1)}, f32[16,512]{1,0:T(8,128)S(1)}) custom-call(bf16[4,32,512]{2,1,0:T(8,128)(2,1)S(1)} %pad_maximum_fusion.near_ref, bf16[3,48,512]{2,1,0:T(8,128)(2,1)S(1)} %get-tuple-element.29.own_ref, f32[16,512]{1,0:T(8,128)S(1)} %get-tuple-element.30.added_ref), custom_call_target="tpu_custom_call" | custom-call | flops 830472192 | bytes 1572864 | tf_op jit(solution)/shard_map/build/pallas_call | solution.py:226
  18.4 0.0 collective-permute-done.1.near_ref
  18.4 1.4 %build.4 = (bf16[3,512,512]{2,1,0:T(8,128)(2,1)S(1)}, f32[16,512]{1,0:T(8,128)S(1)}, f32[16,512]{1,0:T(8,128)S(1)}) custom-call(bf16[4,32,512]{2,1,0:T(8,128)(2,1)S(1)} %collective-permute-done.1.near_ref, bf16[3,48,512]{2,1,0:T(8,128)(2,1)S(1)} %get-tuple-element.29.own_ref, f32[16,512]{1,0:T(8,128)S(1)} %get-tuple-element.31.added_ref, ...), custom_call_target="tpu_custom_call" | custom-call | flops 830472192 | bytes 1572864 | tf_op jit(solution)/shard_map/build/pallas_call | solution.py:226
  19.8 1.6 %collective-permute-done.near_ref = bf16[4,32,512]{2,1,0:T(8,128)(2,1)S(1)} collective-permute-done((bf16[4,32,512]{2,1,0:T(8,128)(2,1)S(1)}, bf16[4,32,512]{2,1,0:T(8,128)(2,1)S(1)}, u32[]{:S(2)}, u32[]{:S(2)}) %collective-permute-start) | collective-permute-done | bytes 131104 | tf_op jit(solution)/shard_map/ppermute | solution.py:58
  21.4 1.4 %build.5 = (bf16[3,512,512]{2,1,0:T(8,128)(2,1)S(1)}, f32[16,512]{1,0:T(8,128)S(1)}, bf16[32,512]{1,0:T(8,128)(2,1)S(1)}, bf16[32,512]{1,0:T(8,128)(2,1)S(1)}) custom-call(bf16[4,32,512]{2,1,0:T(8,128)(2,1)S(1)} %collective-permute-done.near_ref, bf16[3,48,512]{2,1,0:T(8,128)(2,1)S(1)} %get-tuple-element.29.own_ref, ...), custom_call_target="tpu_custom_call" | custom-call | flops 830472192 | bytes 1572864 | tf_op jit(solution)/shard_map/build/pallas_call | solution.py:226
  22.8 10.4 %all-gather.2 = bf16[64,512]{1,0:T(8,128)(2,1)S(1)} all-gather(bf16[32,512]{1,0:T(8,128)(2,1)S(1)} %get-tuple-element.37), channel_id=4, replica_groups={{0,1},{2,3},{4,5},{6,7},{8,9},{10,11},{12,13},{14,15},{16,17},{18,19},{..., dimensions={0}, use_global_device_ids=true | all-gather | bytes 98304 | tf_op jit(solution)/shard_map/all_gather | solution.py:43
  33.2 3.1 %collective-permute-start.2 = (bf16[3,16,512]{2,1,0:T(8,128)(2,1)S(1)}, bf16[3,16,512]{2,1,0:T(8,128)(2,1)S(1)}, u32[]{:S(2)}, u32[]{:S(2)}) collective-permute-start(bf16[3,16,512]{2,1,0:T(8,128)(2,1)S(1)} %slice.78), channel_id=1, source_target_pairs={{0,64},{64,0},{128,192},{192,128},{256,320},{320,256},{384,448},{4... | collective-permute-start | bytes 147464 | tf_op jit(solution)/shard_map/ppermute | solution.py:64
  36.4 0.3 apply.1.part_ref
  36.7 5.7 %all-gather.3 = bf16[6,16,512]{2,1,0:T(8,128)(2,1)S(1)} all-gather(bf16[3,16,512]{2,1,0:T(8,128)(2,1)S(1)} %slice.78), channel_id=5, replica_groups={{64,128},{192,256},{320,384},{448,0},{65,129},{193,257},{321,385},{449,..., dimensions={0}, use_global_device_ids=true | all-gather | bytes 147456 | tf_op jit(solution)/shard_map/all_gather | solution.py:65
  42.4 0.0 collective-permute-done.2.swap_ref
  42.4 0.5 paired.1
  43.0 3.3 %all-gather.4 = bf16[64,512]{1,0:T(8,128)(2,1)S(1)} all-gather(bf16[32,512]{1,0:T(8,128)(2,1)S(1)} %get-tuple-element.44), channel_id=6, replica_groups={{0,1},{2,3},{4,5},{6,7},{8,9},{10,11},{12,13},{14,15},{16,17},{18,19},{..., dimensions={0}, use_global_device_ids=true | all-gather | bytes 98304 | tf_op jit(solution)/shard_map/all_gather | solution.py:43
  46.3 4.0 %all-gather.5 = bf16[64,512]{1,0:T(8,128)(2,1)S(1)} all-gather(bf16[32,512]{1,0:T(8,128)(2,1)S(1)} %get-tuple-element.44), channel_id=7, replica_groups={{1,2},{3,4},{5,6},{7,8},{9,10},{11,12},{13,14},{15,16},{17,18},{19,20},..., dimensions={0}, use_global_device_ids=true | all-gather | bytes 98304 | tf_op jit(solution)/shard_map/all_gather | solution.py:43
  50.3 2.2 %collective-permute-start.4 = (bf16[3,32,512]{2,1,0:T(8,128)(2,1)S(1)}, bf16[3,32,512]{2,1,0:T(8,128)(2,1)S(1)}, u32[]{:S(2)}, u32[]{:S(2)}) collective-permute-start(bf16[3,32,512]{2,1,0:T(8,128)(2,1)S(1)} %pad_maximum_fusion.2.near_ref), channel_id=1, source_target_pairs={{0,64},{64,128},{128,192},{192,256},{256,320},{320,384},{384,448},... | collective-permute-start | bytes 294920 | tf_op jit(solution)/shard_map/ppermute | solution.py:57
  52.5 1.3 %collective-permute-start.3 = (bf16[3,32,512]{2,1,0:T(8,128)(2,1)S(1)}, bf16[3,32,512]{2,1,0:T(8,128)(2,1)S(1)}, u32[]{:S(2)}, u32[]{:S(2)}) collective-permute-start(bf16[3,32,512]{2,1,0:T(8,128)(2,1)S(1)} %pad_maximum_fusion.2.near_ref), channel_id=1, source_target_pairs={{64,0},{128,64},{192,128},{256,192},{320,256},{384,320},{448,384},... | collective-permute-start | bytes 294920 | tf_op jit(solution)/shard_map/ppermute | solution.py:58
  53.8 0.4 same_band.1
  54.2 0.0 collective-permute-done.4.near_ref
  54.2 1.2 %below.1 = (f32[16,512]{1,0:T(8,128)S(1)}, f32[32,1,128]{2,1,0:T(1,128)}) custom-call(bf16[3,32,512]{2,1,0:T(8,128)(2,1)S(1)} %collective-permute-done.4.near_ref, bf16[3,512,512]{2,1,0:T(8,128)(2,1)S(1)} %get-tuple-element.38.below_ref.tile_ref, f32[16,512]{1,0:T(8,128)S(1)} %get-tuple-element.48.part_ref, f32[16,512]{1,0:T(8,128)S(1)} %get-tuple-element.46.second_ref, ...), custom_call_target="tpu_custom_call" | custom-call | flops 25165824 | bytes 1572864 | tf_op jit(solution)/shard_map/below/pallas_call | solution.py:345
  55.4 9.2 %all-to-all-start = ((f32[32,1,128]{2,1,0:T(1,128)}), f32[32,1,128]{2,1,0:T(1,128)S(1)}, u32[]{:S(2)}, u32[]{:S(2)}) async-start(f32[32,1,128]{2,1,0:T(1,128)} %get-tuple-element.50), calls=%async_computation | async-start | bytes 32768 | tf_op jit(solution)/shard_map/all_to_all | solution.py:396
  64.6 0.0 collective-permute-done.3.near_ref
  64.6 8.5 %all-to-all-done.total_ref = f32[32,1,128]{2,1,0:T(1,128)S(1)} async-done(((f32[32,1,128]{2,1,0:T(1,128)}), f32[32,1,128]{2,1,0:T(1,128)S(1)}, u32[]{:S(2)}, u32[]{:S(2)}) %all-to-all-start) | async-done | bytes 16416 | tf_op jit(solution)/shard_map/all_to_all | solution.py:396
  73.1 0.3 above.1
  73.5 16.2 %all_to_all.10.total_ref = f32[16,1,128]{2,1,0:T(1,128)S(1)} all-to-all(f32[16,1,128]{2,1,0:T(1,128)S(1)} %get-tuple-element.52), channel_id=1, replica_groups=mesh['z_lo'=2,'x'=4,'z_hi'=4,'y'=8,'core'=2] {'y','core'}, dimensions={0} | all-to-all | bytes 16384 | tf_op jit(solution)/shard_map/all_to_all | solution.py:398
  89.7 0.8 finish.1
  (11 shorter events, 0.1 us)
Async XLA Ops:
  14.4 4.0 %collective-permute-start.1 = (bf16[4,32,512]{2,1,0:T(8,128)(2,1)S(1)}, bf16[4,32,512]{2,1,0:T(8,128)(2,1)S(1)}, u32[]{:S(2)}, u32[]{:S(2)}) collective-permute-start(bf16[4,32,512]{2,1,0:T(8,128)(2,1)S(1)} %pad_maximum_fusion.near_ref), channel_id=1, source_target_pairs={{0,64},{64,128},{128,192},{192,256},{256,320},{320,384},{384,448},... | collective-permute-start | bytes 393224 | tf_op jit(solution)/shard_map/ppermute | solution.py:57
  15.7 5.7 %collective-permute-start = (bf16[4,32,512]{2,1,0:T(8,128)(2,1)S(1)}, bf16[4,32,512]{2,1,0:T(8,128)(2,1)S(1)}, u32[]{:S(2)}, u32[]{:S(2)}) collective-permute-start(bf16[4,32,512]{2,1,0:T(8,128)(2,1)S(1)} %pad_maximum_fusion.near_ref), channel_id=1, source_target_pairs={{64,0},{128,64},{192,128},{256,192},{320,256},{384,320},{448,384},... | collective-permute-start | bytes 393224 | tf_op jit(solution)/shard_map/ppermute | solution.py:58
  33.2 9.2 %collective-permute-start.2 = (bf16[3,16,512]{2,1,0:T(8,128)(2,1)S(1)}, bf16[3,16,512]{2,1,0:T(8,128)(2,1)S(1)}, u32[]{:S(2)}, u32[]{:S(2)}) collective-permute-start(bf16[3,16,512]{2,1,0:T(8,128)(2,1)S(1)} %slice.78), channel_id=1, source_target_pairs={{0,64},{64,0},{128,192},{192,128},{256,320},{320,256},{384,448},{4... | collective-permute-start | bytes 147464 | tf_op jit(solution)/shard_map/ppermute | solution.py:64
  50.3 3.9 %collective-permute-start.4 = (bf16[3,32,512]{2,1,0:T(8,128)(2,1)S(1)}, bf16[3,32,512]{2,1,0:T(8,128)(2,1)S(1)}, u32[]{:S(2)}, u32[]{:S(2)}) collective-permute-start(bf16[3,32,512]{2,1,0:T(8,128)(2,1)S(1)} %pad_maximum_fusion.2.near_ref), channel_id=1, source_target_pairs={{0,64},{64,128},{128,192},{192,256},{256,320},{320,384},{384,448},... | collective-permute-start | bytes 294920 | tf_op jit(solution)/shard_map/ppermute | solution.py:57
  52.5 12.2 %collective-permute-start.3 = (bf16[3,32,512]{2,1,0:T(8,128)(2,1)S(1)}, bf16[3,32,512]{2,1,0:T(8,128)(2,1)S(1)}, u32[]{:S(2)}, u32[]{:S(2)}) collective-permute-start(bf16[3,32,512]{2,1,0:T(8,128)(2,1)S(1)} %pad_maximum_fusion.2.near_ref), channel_id=1, source_target_pairs={{64,0},{128,64},{192,128},{256,192},{320,256},{384,320},{448,384},... | collective-permute-start | bytes 294920 | tf_op jit(solution)/shard_map/ppermute | solution.py:58
  55.4 17.7 %all-to-all-start = ((f32[32,1,128]{2,1,0:T(1,128)}), f32[32,1,128]{2,1,0:T(1,128)S(1)}, u32[]{:S(2)}, u32[]{:S(2)}) async-start(f32[32,1,128]{2,1,0:T(1,128)} %get-tuple-element.50), calls=%async_computation | async-start | bytes 32768 | tf_op jit(solution)/shard_map/all_to_all | solution.py:396

commit v14 on v13

--- a/solution.py
+++ b/solution.py
@@ -384,7 +384,7 @@
         "paired",
     )
     wide = widened(sent)
-    below, above = all_bands(wide)
+    below, above = all_bands(wide[:, :RHS])
     part, row = call(
         same_band_kernel,
         [field, pltpu.VMEM((1, 128), jnp.float32)],

time: 90.9 us -> 90.6 us (level)
  no operation moved by 1% of the time
where the time goes in v14:
time: 90.6 us; the launch traced here: 90.2 us
  blocking collectives  52.1 us (58%)
  starting transfers between devices  18.4 us (20%)
  waiting for transfers between devices  10.1 us (11%)
  Pallas kernels  8.68 us (10%)
    all_gather x5, blocking collectives, partner(): lax.all_gather(block, axes, axis_index_groups=pairs(extent(axes), first))  30.4 us
    all_to_all x1, blocking collectives, local(): totals = lax.all_to_all(partial, GROUPS[1], 0, 0)  16 us
    all_to_all x1, starting transfers between devices, local(): partial = lax.all_to_all(partial, GROUPS[0], 0, 0)  9.23 us
    all_to_all x1, waiting for transfers between devices, local(): partial = lax.all_to_all(partial, GROUPS[0], 0, 0)  8.5 us
    all_gather x1, blocking collectives, all_bands_paired(): return (swap, lax.all_gather(wide, LAT, axis_index_groups=pairs(count, 1)))  5.73 us
    pallas_call x3, Pallas kernels, build(): pl.pallas_call(kernel, out_shape=shapes, in_specs=[whole()] * len(operand...  4.2 us
    pallas_call x6, Pallas kernels, call(): pl.pallas_call(kernel, out_shape=shapes, in_specs=[whole()] * len(operand...  3.53 us
    ppermute x2, starting transfers between devices, all_bands(): below = lax.ppermute(wide, LAT, [(i, i + 1) for i in range(count - 1)])  3.46 us
  transfers between devices with their start and end apart: 6, of which 2 were waited for; matrix products, arithmetic and copies ran while one was open for 0% of the time, Pallas kernels for 5%

profile of v14, /device:TPU:1, one launch (start us, length us, event | category | flops | bytes accessed | tf_op | source)
XLA Modules:
  0.0 90.2 jit_solution(10282144903292260542)
XLA Ops:
  0.6 0.9 %describe.1 = (bf16[32,512]{1,0:T(8,128)(2,1)S(1)}, bf16[3,48,512]{2,1,0:T(8,128)(2,1)S(1)}, f32[1,512]{1,0:T(1,128)S(1)}, f32[16,512]{1,0:T(8,128)S(1)}, f32[16,512]{1,0:T(8,128)S(1)}) custom-call(f32[16,512]{1,0:T(8,128)} %bitcast.30, f32[1,512]{1,0:T(1,128)} %bitcast.32, bf16[3,512]{1,0:T(4,128)(2,1)} %bitcast.31, bf16[1,512]{1,0:T(2,128)(2,1)} %bitcast.33, ...), custom_call_target="tpu_custom_call" | custom-call | tf_op jit(solution)/shard_map/describe/pallas_call | solution.py:138
  1.6 8.4 %all-gather = bf16[64,512]{1,0:T(8,128)(2,1)S(1)} all-gather(bf16[32,512]{1,0:T(8,128)(2,1)S(1)} %get-tuple-element.28), channel_id=2, replica_groups={{0,1},{2,3},{4,5},{6,7},{8,9},{10,11},{12,13},{14,15},{16,17},{18,19},{..., dimensions={0}, use_global_device_ids=true | all-gather | bytes 98304 | tf_op jit(solution)/shard_map/all_gather | solution.py:43
  10.0 4.4 %all-gather.1 = bf16[4,32,512]{2,1,0:T(8,128)(2,1)S(1)} all-gather(bf16[2,32,512]{2,1,0:T(8,128)(2,1)S(1)} %pad_maximum_fusion.3), channel_id=3, replica_groups={{1,2},{3,4},{5,6},{7,8},{9,10},{11,12},{13,14},{15,16},{17,18},{19,20},..., dimensions={0}, use_global_device_ids=true | all-gather | bytes 196608 | tf_op jit(solution)/shard_map/all_gather | solution.py:43
  14.4 1.3 %collective-permute-start.1 = (bf16[4,32,512]{2,1,0:T(8,128)(2,1)S(1)}, bf16[4,32,512]{2,1,0:T(8,128)(2,1)S(1)}, u32[]{:S(2)}, u32[]{:S(2)}) collective-permute-start(bf16[4,32,512]{2,1,0:T(8,128)(2,1)S(1)} %pad_maximum_fusion.near_ref), channel_id=1, source_target_pairs={{0,64},{64,128},{128,192},{192,256},{256,320},{320,384},{384,448},... | collective-permute-start | bytes 393224 | tf_op jit(solution)/shard_map/ppermute | solution.py:57
  15.7 1.3 %collective-permute-start = (bf16[4,32,512]{2,1,0:T(8,128)(2,1)S(1)}, bf16[4,32,512]{2,1,0:T(8,128)(2,1)S(1)}, u32[]{:S(2)}, u32[]{:S(2)}) collective-permute-start(bf16[4,32,512]{2,1,0:T(8,128)(2,1)S(1)} %pad_maximum_fusion.near_ref), channel_id=1, source_target_pairs={{64,0},{128,64},{192,128},{256,192},{320,256},{384,320},{448,384},... | collective-permute-start | bytes 393224 | tf_op jit(solution)/shard_map/ppermute | solution.py:58
  17.0 1.4 %build.3 = (bf16[3,512,512]{2,1,0:T(8,128)(2,1)S(1)}, f32[16,512]{1,0:T(8,128)S(1)}, bf16[3,48,512]{2,1,0:T(8,128)(2,1)S(1)}, f32[16,512]{1,0:T(8,128)S(1)}) custom-call(bf16[4,32,512]{2,1,0:T(8,128)(2,1)S(1)} %pad_maximum_fusion.near_ref, bf16[3,48,512]{2,1,0:T(8,128)(2,1)S(1)} %get-tuple-element.29.own_ref, f32[16,512]{1,0:T(8,128)S(1)} %get-tuple-element.30.added_ref), custom_call_target="tpu_custom_call" | custom-call | flops 830472192 | bytes 1572864 | tf_op jit(solution)/shard_map/build/pallas_call | solution.py:226
  18.4 0.0 collective-permute-done.1.near_ref
  18.4 1.4 %build.4 = (bf16[3,512,512]{2,1,0:T(8,128)(2,1)S(1)}, f32[16,512]{1,0:T(8,128)S(1)}, f32[16,512]{1,0:T(8,128)S(1)}) custom-call(bf16[4,32,512]{2,1,0:T(8,128)(2,1)S(1)} %collective-permute-done.1.near_ref, bf16[3,48,512]{2,1,0:T(8,128)(2,1)S(1)} %get-tuple-element.29.own_ref, f32[16,512]{1,0:T(8,128)S(1)} %get-tuple-element.31.added_ref, ...), custom_call_target="tpu_custom_call" | custom-call | flops 830472192 | bytes 1572864 | tf_op jit(solution)/shard_map/build/pallas_call | solution.py:226
  19.8 1.6 %collective-permute-done.near_ref = bf16[4,32,512]{2,1,0:T(8,128)(2,1)S(1)} collective-permute-done((bf16[4,32,512]{2,1,0:T(8,128)(2,1)S(1)}, bf16[4,32,512]{2,1,0:T(8,128)(2,1)S(1)}, u32[]{:S(2)}, u32[]{:S(2)}) %collective-permute-start) | collective-permute-done | bytes 131104 | tf_op jit(solution)/shard_map/ppermute | solution.py:58
  21.4 1.4 %build.5 = (bf16[3,512,512]{2,1,0:T(8,128)(2,1)S(1)}, f32[16,512]{1,0:T(8,128)S(1)}, bf16[32,512]{1,0:T(8,128)(2,1)S(1)}, bf16[32,512]{1,0:T(8,128)(2,1)S(1)}) custom-call(bf16[4,32,512]{2,1,0:T(8,128)(2,1)S(1)} %collective-permute-done.near_ref, bf16[3,48,512]{2,1,0:T(8,128)(2,1)S(1)} %get-tuple-element.29.own_ref, ...), custom_call_target="tpu_custom_call" | custom-call | flops 830472192 | bytes 1572864 | tf_op jit(solution)/shard_map/build/pallas_call | solution.py:226
  22.8 10.4 %all-gather.2 = bf16[64,512]{1,0:T(8,128)(2,1)S(1)} all-gather(bf16[32,512]{1,0:T(8,128)(2,1)S(1)} %get-tuple-element.37), channel_id=4, replica_groups={{0,1},{2,3},{4,5},{6,7},{8,9},{10,11},{12,13},{14,15},{16,17},{18,19},{..., dimensions={0}, use_global_device_ids=true | all-gather | bytes 98304 | tf_op jit(solution)/shard_map/all_gather | solution.py:43
  33.2 3.1 %collective-permute-start.2 = (bf16[3,16,512]{2,1,0:T(8,128)(2,1)S(1)}, bf16[3,16,512]{2,1,0:T(8,128)(2,1)S(1)}, u32[]{:S(2)}, u32[]{:S(2)}) collective-permute-start(bf16[3,16,512]{2,1,0:T(8,128)(2,1)S(1)} %slice.82), channel_id=1, source_target_pairs={{0,64},{64,0},{128,192},{192,128},{256,320},{320,256},{384,448},{4... | collective-permute-start | bytes 147464 | tf_op jit(solution)/shard_map/ppermute | solution.py:64
  36.4 0.3 apply.1.part_ref
  36.7 5.7 %all-gather.3 = bf16[6,16,512]{2,1,0:T(8,128)(2,1)S(1)} all-gather(bf16[3,16,512]{2,1,0:T(8,128)(2,1)S(1)} %slice.82), channel_id=5, replica_groups={{64,128},{192,256},{320,384},{448,0},{65,129},{193,257},{321,385},{449,..., dimensions={0}, use_global_device_ids=true | all-gather | bytes 147456 | tf_op jit(solution)/shard_map/all_gather | solution.py:65
  42.4 0.0 collective-permute-done.2.swap_ref
  42.4 0.5 paired.1
  43.0 3.3 %all-gather.4 = bf16[64,512]{1,0:T(8,128)(2,1)S(1)} all-gather(bf16[32,512]{1,0:T(8,128)(2,1)S(1)} %get-tuple-element.44), channel_id=6, replica_groups={{0,1},{2,3},{4,5},{6,7},{8,9},{10,11},{12,13},{14,15},{16,17},{18,19},{..., dimensions={0}, use_global_device_ids=true | all-gather | bytes 98304 | tf_op jit(solution)/shard_map/all_gather | solution.py:43
  46.3 4.0 %all-gather.5 = bf16[64,512]{1,0:T(8,128)(2,1)S(1)} all-gather(bf16[32,512]{1,0:T(8,128)(2,1)S(1)} %get-tuple-element.44), channel_id=7, replica_groups={{1,2},{3,4},{5,6},{7,8},{9,10},{11,12},{13,14},{15,16},{17,18},{19,20},..., dimensions={0}, use_global_device_ids=true | all-gather | bytes 98304 | tf_op jit(solution)/shard_map/all_gather | solution.py:43
  50.3 2.2 %collective-permute-start.4 = (bf16[3,16,512]{2,1,0:T(8,128)(2,1)S(1)}, bf16[3,16,512]{2,1,0:T(8,128)(2,1)S(1)}, u32[]{:S(2)}, u32[]{:S(2)}) collective-permute-start(bf16[3,16,512]{2,1,0:T(8,128)(2,1)S(1)} %slice.87), channel_id=1, source_target_pairs={{0,64},{64,128},{128,192},{192,256},{256,320},{320,384},{384,448},... | collective-permute-start | bytes 147464 | tf_op jit(solution)/shard_map/ppermute | solution.py:57
  52.5 1.3 %collective-permute-start.3 = (bf16[3,16,512]{2,1,0:T(8,128)(2,1)S(1)}, bf16[3,16,512]{2,1,0:T(8,128)(2,1)S(1)}, u32[]{:S(2)}, u32[]{:S(2)}) collective-permute-start(bf16[3,16,512]{2,1,0:T(8,128)(2,1)S(1)} %slice.87), channel_id=1, source_target_pairs={{64,0},{128,64},{192,128},{256,192},{320,256},{384,320},{448,384},... | collective-permute-start | bytes 147464 | tf_op jit(solution)/shard_map/ppermute | solution.py:58
  53.8 0.4 same_band.1
  54.2 0.0 collective-permute-done.4.near_ref
  54.2 1.2 %below.1 = (f32[16,512]{1,0:T(8,128)S(1)}, f32[32,1,128]{2,1,0:T(1,128)}) custom-call(bf16[3,16,512]{2,1,0:T(8,128)(2,1)S(1)} %collective-permute-done.4.near_ref, bf16[3,512,512]{2,1,0:T(8,128)(2,1)S(1)} %get-tuple-element.38.below_ref.tile_ref, f32[16,512]{1,0:T(8,128)S(1)} %get-tuple-element.48.part_ref, f32[16,512]{1,0:T(8,128)S(1)} %get-tuple-element.46.second_ref, ...), custom_call_target="tpu_custom_call" | custom-call | flops 25165824 | bytes 1572864 | tf_op jit(solution)/shard_map/below/pallas_call | solution.py:345
  55.4 9.2 %all-to-all-start = ((f32[32,1,128]{2,1,0:T(1,128)}), f32[32,1,128]{2,1,0:T(1,128)S(1)}, u32[]{:S(2)}, u32[]{:S(2)}) async-start(f32[32,1,128]{2,1,0:T(1,128)} %get-tuple-element.50), calls=%async_computation | async-start | bytes 32768 | tf_op jit(solution)/shard_map/all_to_all | solution.py:396
  64.6 0.0 collective-permute-done.3.near_ref
  64.6 8.5 %all-to-all-done.total_ref = f32[32,1,128]{2,1,0:T(1,128)S(1)} async-done(((f32[32,1,128]{2,1,0:T(1,128)}), f32[32,1,128]{2,1,0:T(1,128)S(1)}, u32[]{:S(2)}, u32[]{:S(2)}) %all-to-all-start) | async-done | bytes 16416 | tf_op jit(solution)/shard_map/all_to_all | solution.py:396
  73.1 0.3 above.1
  73.4 16.0 %all_to_all.10.total_ref = f32[16,1,128]{2,1,0:T(1,128)S(1)} all-to-all(f32[16,1,128]{2,1,0:T(1,128)S(1)} %get-tuple-element.52), channel_id=1, replica_groups=mesh['z_lo'=2,'x'=4,'z_hi'=4,'y'=8,'core'=2] {'y','core'}, dimensions={0} | all-to-all | bytes 16384 | tf_op jit(solution)/shard_map/all_to_all | solution.py:398
  89.4 0.8 finish.1
  (12 shorter events, 0.1 us)
Async XLA Ops:
  14.4 4.0 %collective-permute-start.1 = (bf16[4,32,512]{2,1,0:T(8,128)(2,1)S(1)}, bf16[4,32,512]{2,1,0:T(8,128)(2,1)S(1)}, u32[]{:S(2)}, u32[]{:S(2)}) collective-permute-start(bf16[4,32,512]{2,1,0:T(8,128)(2,1)S(1)} %pad_maximum_fusion.near_ref), channel_id=1, source_target_pairs={{0,64},{64,128},{128,192},{192,256},{256,320},{320,384},{384,448},... | collective-permute-start | bytes 393224 | tf_op jit(solution)/shard_map/ppermute | solution.py:57
  15.7 5.7 %collective-permute-start = (bf16[4,32,512]{2,1,0:T(8,128)(2,1)S(1)}, bf16[4,32,512]{2,1,0:T(8,128)(2,1)S(1)}, u32[]{:S(2)}, u32[]{:S(2)}) collective-permute-start(bf16[4,32,512]{2,1,0:T(8,128)(2,1)S(1)} %pad_maximum_fusion.near_ref), channel_id=1, source_target_pairs={{64,0},{128,64},{192,128},{256,192},{320,256},{384,320},{448,384},... | collective-permute-start | bytes 393224 | tf_op jit(solution)/shard_map/ppermute | solution.py:58
  33.2 9.2 %collective-permute-start.2 = (bf16[3,16,512]{2,1,0:T(8,128)(2,1)S(1)}, bf16[3,16,512]{2,1,0:T(8,128)(2,1)S(1)}, u32[]{:S(2)}, u32[]{:S(2)}) collective-permute-start(bf16[3,16,512]{2,1,0:T(8,128)(2,1)S(1)} %slice.82), channel_id=1, source_target_pairs={{0,64},{64,0},{128,192},{192,128},{256,320},{320,256},{384,448},{4... | collective-permute-start | bytes 147464 | tf_op jit(solution)/shard_map/ppermute | solution.py:64
  50.3 3.9 %collective-permute-start.4 = (bf16[3,16,512]{2,1,0:T(8,128)(2,1)S(1)}, bf16[3,16,512]{2,1,0:T(8,128)(2,1)S(1)}, u32[]{:S(2)}, u32[]{:S(2)}) collective-permute-start(bf16[3,16,512]{2,1,0:T(8,128)(2,1)S(1)} %slice.87), channel_id=1, source_target_pairs={{0,64},{64,128},{128,192},{192,256},{256,320},{320,384},{384,448},... | collective-permute-start | bytes 147464 | tf_op jit(solution)/shard_map/ppermute | solution.py:57
  52.5 12.1 %collective-permute-start.3 = (bf16[3,16,512]{2,1,0:T(8,128)(2,1)S(1)}, bf16[3,16,512]{2,1,0:T(8,128)(2,1)S(1)}, u32[]{:S(2)}, u32[]{:S(2)}) collective-permute-start(bf16[3,16,512]{2,1,0:T(8,128)(2,1)S(1)} %slice.87), channel_id=1, source_target_pairs={{64,0},{128,64},{192,128},{256,192},{320,256},{384,320},{448,384},... | collective-permute-start | bytes 147464 | tf_op jit(solution)/shard_map/ppermute | solution.py:58
  55.4 17.7 %all-to-all-start = ((f32[32,1,128]{2,1,0:T(1,128)}), f32[32,1,128]{2,1,0:T(1,128)S(1)}, u32[]{:S(2)}, u32[]{:S(2)}) async-start(f32[32,1,128]{2,1,0:T(1,128)} %get-tuple-element.50), calls=%async_computation | async-start | bytes 32768 | tf_op jit(solution)/shard_map/all_to_all | solution.py:396

commit v15 on v14

--- a/solution.py
+++ b/solution.py
@@ -25,7 +25,7 @@
 
 LAT = ("z_lo", "x")
 LON = ("z_hi", "y", "core")
-GROUPS = (("z_lo", "z_hi", "x"), ("y", "core"))
+GROUPS = (("y", "core"), ("z_lo", "z_hi", "x"))
 
 
 def extent(axes):

time: 90.6 us -> 89.9 us (level)
  blocking collectives: 52.1 us -> 54 us
  waiting for transfers between devices: 10.1 us -> 8.59 us
  starting transfers between devices: 18.4 us -> 17.3 us
    all_to_all x1, blocking collectives: 16 us -> 17.9 us  [local(): totals = lax.all_to_all(partial, GROUPS[1], 0, 0)]
    all_to_all x1, waiting for transfers between devices: 8.5 us -> 6.98 us  [local(): partial = lax.all_to_all(partial, GROUPS[0], 0, 0)]
    all_to_all x1, starting transfers between devices: 9.23 us -> 8.11 us  [local(): partial = lax.all_to_all(partial, GROUPS[0], 0, 0)]
where the time goes in v15:
time: 89.9 us; the launch traced here: 89.5 us
  blocking collectives  54 us (60%)
  starting transfers between devices  17.3 us (19%)
  Pallas kernels  8.69 us (10%)
  waiting for transfers between devices  8.59 us (10%)
    all_gather x5, blocking collectives, partner(): lax.all_gather(block, axes, axis_index_groups=pairs(extent(axes), first))  30.4 us
    all_to_all x1, blocking collectives, local(): totals = lax.all_to_all(partial, GROUPS[1], 0, 0)  17.9 us
    all_to_all x1, starting transfers between devices, local(): partial = lax.all_to_all(partial, GROUPS[0], 0, 0)  8.11 us
    all_to_all x1, waiting for transfers between devices, local(): partial = lax.all_to_all(partial, GROUPS[0], 0, 0)  6.98 us
    all_gather x1, blocking collectives, all_bands_paired(): return (swap, lax.all_gather(wide, LAT, axis_index_groups=pairs(count, 1)))  5.73 us
    pallas_call x3, Pallas kernels, build(): pl.pallas_call(kernel, out_shape=shapes, in_specs=[whole()] * len(operand...  4.2 us
    pallas_call x6, Pallas kernels, call(): pl.pallas_call(kernel, out_shape=shapes, in_specs=[whole()] * len(operand...  3.55 us
    ppermute x2, starting transfers between devices, all_bands(): below = lax.ppermute(wide, LAT, [(i, i + 1) for i in range(count - 1)])  3.46 us
  transfers between devices with their start and end apart: 6, of which 2 were waited for; matrix products, arithmetic and copies ran while one was open for 0% of the time, Pallas kernels for 5%

profile of v15, /device:TPU:1, one launch (start us, length us, event | category | flops | bytes accessed | tf_op | source)
XLA Modules:
  0.0 89.5 jit_solution(1613008774465328367)
XLA Ops:
  0.6 0.9 %describe.1 = (bf16[32,512]{1,0:T(8,128)(2,1)S(1)}, bf16[3,48,512]{2,1,0:T(8,128)(2,1)S(1)}, f32[1,512]{1,0:T(1,128)S(1)}, f32[16,512]{1,0:T(8,128)S(1)}, f32[16,512]{1,0:T(8,128)S(1)}) custom-call(f32[16,512]{1,0:T(8,128)} %bitcast.30, f32[1,512]{1,0:T(1,128)} %bitcast.32, bf16[3,512]{1,0:T(4,128)(2,1)} %bitcast.31, bf16[1,512]{1,0:T(2,128)(2,1)} %bitcast.33, ...), custom_call_target="tpu_custom_call" | custom-call | tf_op jit(solution)/shard_map/describe/pallas_call | solution.py:138
  1.6 8.4 %all-gather = bf16[64,512]{1,0:T(8,128)(2,1)S(1)} all-gather(bf16[32,512]{1,0:T(8,128)(2,1)S(1)} %get-tuple-element.28), channel_id=2, replica_groups={{0,1},{2,3},{4,5},{6,7},{8,9},{10,11},{12,13},{14,15},{16,17},{18,19},{..., dimensions={0}, use_global_device_ids=true | all-gather | bytes 98304 | tf_op jit(solution)/shard_map/all_gather | solution.py:43
  10.0 4.4 %all-gather.1 = bf16[4,32,512]{2,1,0:T(8,128)(2,1)S(1)} all-gather(bf16[2,32,512]{2,1,0:T(8,128)(2,1)S(1)} %pad_maximum_fusion.3), channel_id=3, replica_groups={{1,2},{3,4},{5,6},{7,8},{9,10},{11,12},{13,14},{15,16},{17,18},{19,20},..., dimensions={0}, use_global_device_ids=true | all-gather | bytes 196608 | tf_op jit(solution)/shard_map/all_gather | solution.py:43
  14.4 1.3 %collective-permute-start.1 = (bf16[4,32,512]{2,1,0:T(8,128)(2,1)S(1)}, bf16[4,32,512]{2,1,0:T(8,128)(2,1)S(1)}, u32[]{:S(2)}, u32[]{:S(2)}) collective-permute-start(bf16[4,32,512]{2,1,0:T(8,128)(2,1)S(1)} %pad_maximum_fusion.near_ref), channel_id=1, source_target_pairs={{0,64},{64,128},{128,192},{192,256},{256,320},{320,384},{384,448},... | collective-permute-start | bytes 393224 | tf_op jit(solution)/shard_map/ppermute | solution.py:57
  15.7 1.3 %collective-permute-start = (bf16[4,32,512]{2,1,0:T(8,128)(2,1)S(1)}, bf16[4,32,512]{2,1,0:T(8,128)(2,1)S(1)}, u32[]{:S(2)}, u32[]{:S(2)}) collective-permute-start(bf16[4,32,512]{2,1,0:T(8,128)(2,1)S(1)} %pad_maximum_fusion.near_ref), channel_id=1, source_target_pairs={{64,0},{128,64},{192,128},{256,192},{320,256},{384,320},{448,384},... | collective-permute-start | bytes 393224 | tf_op jit(solution)/shard_map/ppermute | solution.py:58
  17.0 1.4 %build.3 = (bf16[3,512,512]{2,1,0:T(8,128)(2,1)S(1)}, f32[16,512]{1,0:T(8,128)S(1)}, bf16[3,48,512]{2,1,0:T(8,128)(2,1)S(1)}, f32[16,512]{1,0:T(8,128)S(1)}) custom-call(bf16[4,32,512]{2,1,0:T(8,128)(2,1)S(1)} %pad_maximum_fusion.near_ref, bf16[3,48,512]{2,1,0:T(8,128)(2,1)S(1)} %get-tuple-element.29.own_ref, f32[16,512]{1,0:T(8,128)S(1)} %get-tuple-element.30.added_ref), custom_call_target="tpu_custom_call" | custom-call | flops 830472192 | bytes 1572864 | tf_op jit(solution)/shard_map/build/pallas_call | solution.py:226
  18.4 0.0 collective-permute-done.1.near_ref
  18.4 1.4 %build.4 = (bf16[3,512,512]{2,1,0:T(8,128)(2,1)S(1)}, f32[16,512]{1,0:T(8,128)S(1)}, f32[16,512]{1,0:T(8,128)S(1)}) custom-call(bf16[4,32,512]{2,1,0:T(8,128)(2,1)S(1)} %collective-permute-done.1.near_ref, bf16[3,48,512]{2,1,0:T(8,128)(2,1)S(1)} %get-tuple-element.29.own_ref, f32[16,512]{1,0:T(8,128)S(1)} %get-tuple-element.31.added_ref, ...), custom_call_target="tpu_custom_call" | custom-call | flops 830472192 | bytes 1572864 | tf_op jit(solution)/shard_map/build/pallas_call | solution.py:226
  19.8 1.6 %collective-permute-done.near_ref = bf16[4,32,512]{2,1,0:T(8,128)(2,1)S(1)} collective-permute-done((bf16[4,32,512]{2,1,0:T(8,128)(2,1)S(1)}, bf16[4,32,512]{2,1,0:T(8,128)(2,1)S(1)}, u32[]{:S(2)}, u32[]{:S(2)}) %collective-permute-start) | collective-permute-done | bytes 131104 | tf_op jit(solution)/shard_map/ppermute | solution.py:58
  21.4 1.4 %build.5 = (bf16[3,512,512]{2,1,0:T(8,128)(2,1)S(1)}, f32[16,512]{1,0:T(8,128)S(1)}, bf16[32,512]{1,0:T(8,128)(2,1)S(1)}, bf16[32,512]{1,0:T(8,128)(2,1)S(1)}) custom-call(bf16[4,32,512]{2,1,0:T(8,128)(2,1)S(1)} %collective-permute-done.near_ref, bf16[3,48,512]{2,1,0:T(8,128)(2,1)S(1)} %get-tuple-element.29.own_ref, ...), custom_call_target="tpu_custom_call" | custom-call | flops 830472192 | bytes 1572864 | tf_op jit(solution)/shard_map/build/pallas_call | solution.py:226
  22.8 10.4 %all-gather.2 = bf16[64,512]{1,0:T(8,128)(2,1)S(1)} all-gather(bf16[32,512]{1,0:T(8,128)(2,1)S(1)} %get-tuple-element.37), channel_id=4, replica_groups={{0,1},{2,3},{4,5},{6,7},{8,9},{10,11},{12,13},{14,15},{16,17},{18,19},{..., dimensions={0}, use_global_device_ids=true | all-gather | bytes 98304 | tf_op jit(solution)/shard_map/all_gather | solution.py:43
  33.2 3.1 %collective-permute-start.2 = (bf16[3,16,512]{2,1,0:T(8,128)(2,1)S(1)}, bf16[3,16,512]{2,1,0:T(8,128)(2,1)S(1)}, u32[]{:S(2)}, u32[]{:S(2)}) collective-permute-start(bf16[3,16,512]{2,1,0:T(8,128)(2,1)S(1)} %slice.82), channel_id=1, source_target_pairs={{0,64},{64,0},{128,192},{192,128},{256,320},{320,256},{384,448},{4... | collective-permute-start | bytes 147464 | tf_op jit(solution)/shard_map/ppermute | solution.py:64
  36.4 0.3 apply.1.part_ref
  36.7 5.7 %all-gather.3 = bf16[6,16,512]{2,1,0:T(8,128)(2,1)S(1)} all-gather(bf16[3,16,512]{2,1,0:T(8,128)(2,1)S(1)} %slice.82), channel_id=5, replica_groups={{64,128},{192,256},{320,384},{448,0},{65,129},{193,257},{321,385},{449,..., dimensions={0}, use_global_device_ids=true | all-gather | bytes 147456 | tf_op jit(solution)/shard_map/all_gather | solution.py:65
  42.4 0.0 collective-permute-done.2.swap_ref
  42.4 0.5 paired.1
  43.0 3.3 %all-gather.4 = bf16[64,512]{1,0:T(8,128)(2,1)S(1)} all-gather(bf16[32,512]{1,0:T(8,128)(2,1)S(1)} %get-tuple-element.44), channel_id=6, replica_groups={{0,1},{2,3},{4,5},{6,7},{8,9},{10,11},{12,13},{14,15},{16,17},{18,19},{..., dimensions={0}, use_global_device_ids=true | all-gather | bytes 98304 | tf_op jit(solution)/shard_map/all_gather | solution.py:43
  46.3 4.0 %all-gather.5 = bf16[64,512]{1,0:T(8,128)(2,1)S(1)} all-gather(bf16[32,512]{1,0:T(8,128)(2,1)S(1)} %get-tuple-element.44), channel_id=7, replica_groups={{1,2},{3,4},{5,6},{7,8},{9,10},{11,12},{13,14},{15,16},{17,18},{19,20},..., dimensions={0}, use_global_device_ids=true | all-gather | bytes 98304 | tf_op jit(solution)/shard_map/all_gather | solution.py:43
  50.3 2.2 %collective-permute-start.4 = (bf16[3,16,512]{2,1,0:T(8,128)(2,1)S(1)}, bf16[3,16,512]{2,1,0:T(8,128)(2,1)S(1)}, u32[]{:S(2)}, u32[]{:S(2)}) collective-permute-start(bf16[3,16,512]{2,1,0:T(8,128)(2,1)S(1)} %slice.87), channel_id=1, source_target_pairs={{0,64},{64,128},{128,192},{192,256},{256,320},{320,384},{384,448},... | collective-permute-start | bytes 147464 | tf_op jit(solution)/shard_map/ppermute | solution.py:57
  52.5 1.3 %collective-permute-start.3 = (bf16[3,16,512]{2,1,0:T(8,128)(2,1)S(1)}, bf16[3,16,512]{2,1,0:T(8,128)(2,1)S(1)}, u32[]{:S(2)}, u32[]{:S(2)}) collective-permute-start(bf16[3,16,512]{2,1,0:T(8,128)(2,1)S(1)} %slice.87), channel_id=1, source_target_pairs={{64,0},{128,64},{192,128},{256,192},{320,256},{384,320},{448,384},... | collective-permute-start | bytes 147464 | tf_op jit(solution)/shard_map/ppermute | solution.py:58
  53.8 0.4 same_band.1
  54.2 0.0 collective-permute-done.4.near_ref
  54.2 1.1 %below.1 = (f32[16,512]{1,0:T(8,128)S(1)}, f32[16,1,128]{2,1,0:T(1,128)}) custom-call(bf16[3,16,512]{2,1,0:T(8,128)(2,1)S(1)} %collective-permute-done.4.near_ref, bf16[3,512,512]{2,1,0:T(8,128)(2,1)S(1)} %get-tuple-element.38.below_ref.tile_ref, f32[16,512]{1,0:T(8,128)S(1)} %get-tuple-element.48.part_ref, f32[16,512]{1,0:T(8,128)S(1)} %get-tuple-element.46.second_ref, ...), custom_call_target="tpu_custom_call" | custom-call | flops 25165824 | bytes 1572864 | tf_op jit(solution)/shard_map/below/pallas_call | solution.py:345
  55.4 8.1 %all-to-all-start = ((f32[16,1,128]{2,1,0:T(1,128)}), f32[16,1,128]{2,1,0:T(1,128)S(1)}, u32[]{:S(2)}, u32[]{:S(2)}) async-start(f32[16,1,128]{2,1,0:T(1,128)} %get-tuple-element.50), calls=%async_computation | async-start | bytes 16384 | tf_op jit(solution)/shard_map/all_to_all | solution.py:396
  63.5 0.0 collective-permute-done.3.near_ref
  63.5 7.0 %all-to-all-done.total_ref = f32[16,1,128]{2,1,0:T(1,128)S(1)} async-done(((f32[16,1,128]{2,1,0:T(1,128)}), f32[16,1,128]{2,1,0:T(1,128)S(1)}, u32[]{:S(2)}, u32[]{:S(2)}) %all-to-all-start) | async-done | bytes 8224 | tf_op jit(solution)/shard_map/all_to_all | solution.py:396
  70.5 0.3 above.1
  70.8 17.9 %all_to_all.10.total_ref = f32[32,1,128]{2,1,0:T(1,128)S(1)} all-to-all(f32[32,1,128]{2,1,0:T(1,128)S(1)} %get-tuple-element.52), channel_id=1, replica_groups=mesh['z_lo'=2,'x'=4,'z_hi'=4,'y'=8,'core'=2] {'z_lo','z_hi','x'}, dimensions={0} | all-to-all | bytes 32768 | tf_op jit(solution)/shard_map/all_to_all | solution.py:398
  88.7 0.8 finish.1
  (12 shorter events, 0.1 us)
Async XLA Ops:
  14.4 4.0 %collective-permute-start.1 = (bf16[4,32,512]{2,1,0:T(8,128)(2,1)S(1)}, bf16[4,32,512]{2,1,0:T(8,128)(2,1)S(1)}, u32[]{:S(2)}, u32[]{:S(2)}) collective-permute-start(bf16[4,32,512]{2,1,0:T(8,128)(2,1)S(1)} %pad_maximum_fusion.near_ref), channel_id=1, source_target_pairs={{0,64},{64,128},{128,192},{192,256},{256,320},{320,384},{384,448},... | collective-permute-start | bytes 393224 | tf_op jit(solution)/shard_map/ppermute | solution.py:57
  15.7 5.7 %collective-permute-start = (bf16[4,32,512]{2,1,0:T(8,128)(2,1)S(1)}, bf16[4,32,512]{2,1,0:T(8,128)(2,1)S(1)}, u32[]{:S(2)}, u32[]{:S(2)}) collective-permute-start(bf16[4,32,512]{2,1,0:T(8,128)(2,1)S(1)} %pad_maximum_fusion.near_ref), channel_id=1, source_target_pairs={{64,0},{128,64},{192,128},{256,192},{320,256},{384,320},{448,384},... | collective-permute-start | bytes 393224 | tf_op jit(solution)/shard_map/ppermute | solution.py:58
  33.2 9.2 %collective-permute-start.2 = (bf16[3,16,512]{2,1,0:T(8,128)(2,1)S(1)}, bf16[3,16,512]{2,1,0:T(8,128)(2,1)S(1)}, u32[]{:S(2)}, u32[]{:S(2)}) collective-permute-start(bf16[3,16,512]{2,1,0:T(8,128)(2,1)S(1)} %slice.82), channel_id=1, source_target_pairs={{0,64},{64,0},{128,192},{192,128},{256,320},{320,256},{384,448},{4... | collective-permute-start | bytes 147464 | tf_op jit(solution)/shard_map/ppermute | solution.py:64
  50.3 3.9 %collective-permute-start.4 = (bf16[3,16,512]{2,1,0:T(8,128)(2,1)S(1)}, bf16[3,16,512]{2,1,0:T(8,128)(2,1)S(1)}, u32[]{:S(2)}, u32[]{:S(2)}) collective-permute-start(bf16[3,16,512]{2,1,0:T(8,128)(2,1)S(1)} %slice.87), channel_id=1, source_target_pairs={{0,64},{64,128},{128,192},{192,256},{256,320},{320,384},{384,448},... | collective-permute-start | bytes 147464 | tf_op jit(solution)/shard_map/ppermute | solution.py:57
  52.5 11.0 %collective-permute-start.3 = (bf16[3,16,512]{2,1,0:T(8,128)(2,1)S(1)}, bf16[3,16,512]{2,1,0:T(8,128)(2,1)S(1)}, u32[]{:S(2)}, u32[]{:S(2)}) collective-permute-start(bf16[3,16,512]{2,1,0:T(8,128)(2,1)S(1)} %slice.87), channel_id=1, source_target_pairs={{64,0},{128,64},{192,128},{256,192},{320,256},{384,320},{448,384},... | collective-permute-start | bytes 147464 | tf_op jit(solution)/shard_map/ppermute | solution.py:58
  55.4 15.1 %all-to-all-start = ((f32[16,1,128]{2,1,0:T(1,128)}), f32[16,1,128]{2,1,0:T(1,128)S(1)}, u32[]{:S(2)}, u32[]{:S(2)}) async-start(f32[16,1,128]{2,1,0:T(1,128)} %get-tuple-element.50), calls=%async_computation | async-start | bytes 16384 | tf_op jit(solution)/shard_map/all_to_all | solution.py:396

commit v16 on v15

--- a/solution.py
+++ b/solution.py
@@ -108,7 +108,7 @@
 
 def describe_kernel(
     start_ref, error_ref, frac_ref, spread_ref, type_ref,
-    message_ref, own_ref, error_out_ref, added_ref, kept_ref, rows_ref,
+    message_ref, error_out_ref, added_ref, kept_ref, rows_ref,
 ):
     frac = frac_ref[...].astype(jnp.float32)
     latitude = (lax.axis_index(LAT).astype(jnp.float32) + frac[0:1]) * (2.0 * LAT_LIMIT / BANDS) - LAT_LIMIT
@@ -127,7 +127,6 @@
     error_out_ref[...] = error_ref[...]
     kept_ref[...] = start_ref[...]
     added_ref[...] = error_ref[...] * start_ref[...]
-    write_own(own_ref, rows_ref, own_side(place, level, kinds, offset))
 
 
 def whole(space=pltpu.VMEM):
@@ -139,13 +138,12 @@
         describe_kernel,
         out_shape=(
             pltpu.VMEM((32, OBS), jnp.bfloat16),
-            pltpu.VMEM((3, 48, OBS), jnp.bfloat16),
             pltpu.VMEM((1, OBS), jnp.float32),
             pltpu.VMEM((RHS, OBS), jnp.float32),
             pltpu.VMEM((RHS, OBS), jnp.float32),
         ),
         in_specs=[whole()] * 5,
-        out_specs=[whole()] * 5,
+        out_specs=[whole()] * 4,
         scratch_shapes=[pltpu.VMEM((16, OBS), jnp.float32)],
         name="describe",
     )(start, error_var, where_frac, spread, obs_type)
@@ -164,11 +162,14 @@
     return products(lambda slot: near_ref[columns[slot], 0:16, :], tile_ref)
 
 
-def build_same_kernel(near_ref, own_ref, added_ref, tile_ref, sum_ref, outer_own_ref, outer_sum_ref, rows_ref, scratch_ref):
-    rows = near_ref[1, 16:32, :].astype(jnp.float32)
-    row = [rows[at : at + 1] for at in range(16)]
-    place = [row[3 * axis] + row[3 * axis + 1] + row[3 * axis + 2] for axis in range(3)]
-    write_own(outer_own_ref, rows_ref, own_side(place, row[9], row[10:12], row[12] + row[13]))
+def build_same_kernel(
+    near_ref, added_ref, tile_ref, sum_ref, own_ref, outer_own_ref, outer_sum_ref, rows_ref, scratch_ref
+):
+    for column, side_ref in ((2, own_ref), (1, outer_own_ref)):
+        rows = near_ref[column, 16:32, :].astype(jnp.float32)
+        row = [rows[at : at + 1] for at in range(16)]
+        place = [row[3 * axis] + row[3 * axis + 1] + row[3 * axis + 2] for axis in range(3)]
+        write_own(side_ref, rows_ref, own_side(place, row[9], row[10:12], row[12] + row[13]))
     sum_ref[...] = added_ref[...] + part_of(OWN, SAME_BAND, near_ref, own_ref, tile_ref)
     outer_added = row[15] * near_ref[1, 0:16, :].astype(jnp.float32)
     outer_sum_ref[...] = outer_added + part_of(OUTER, SAME_BAND, near_ref, outer_own_ref, scratch_ref)
@@ -354,17 +355,17 @@
 
 
 def local(innovations, obs_error, where_frac, spread, obs_type):
-    message, own, error_var, added, start = describe(
+    message, error_var, added, start = describe(
         innovations[0, 0], obs_error[0], where_frac[0, 0], spread[0], obs_type[0]
     )
     inner = partner(message, LON, 0)
     outer = partner(jnp.stack([message, inner]), LON, 1)
     wide = jnp.stack([outer[1], outer[0], message, inner])
     below, above = all_bands(wide)
-    tiles, part, outer_own, outer = build(
+    tiles, part, own, outer_own, outer = build(
         build_same_kernel,
-        [TILES, FIELD, OWN_SIDE, FIELD],
-        [wide, own, added],
+        [TILES, FIELD, OWN_SIDE, OWN_SIDE, FIELD],
+        [wide, added],
         [pltpu.VMEM((16, OBS), jnp.float32), TILES],
     )
     tiles_below, part, outer = build(

time: 89.9 us -> 89.8 us (level)
  no operation moved by 1% of the time
where the time goes in v16:
time: 89.8 us; the launch traced here: 89.4 us
  blocking collectives  54 us (60%)
  starting transfers between devices  17.3 us (19%)
  Pallas kernels  8.64 us (10%)
  waiting for transfers between devices  8.6 us (10%)
    all_gather x5, blocking collectives, partner(): lax.all_gather(block, axes, axis_index_groups=pairs(extent(axes), first))  30.4 us
    all_to_all x1, blocking collectives, local(): totals = lax.all_to_all(partial, GROUPS[1], 0, 0)  17.9 us
    all_to_all x1, starting transfers between devices, local(): partial = lax.all_to_all(partial, GROUPS[0], 0, 0)  8.11 us
    all_to_all x1, waiting for transfers between devices, local(): partial = lax.all_to_all(partial, GROUPS[0], 0, 0)  6.98 us
    all_gather x1, blocking collectives, all_bands_paired(): return (swap, lax.all_gather(wide, LAT, axis_index_groups=pairs(count, 1)))  5.73 us
    pallas_call x3, Pallas kernels, build(): pl.pallas_call(kernel, out_shape=shapes, in_specs=[whole()] * len(operand...  4.19 us
    pallas_call x6, Pallas kernels, call(): pl.pallas_call(kernel, out_shape=shapes, in_specs=[whole()] * len(operand...  3.55 us
    ppermute x2, starting transfers between devices, all_bands(): below = lax.ppermute(wide, LAT, [(i, i + 1) for i in range(count - 1)])  3.46 us
  transfers between devices with their start and end apart: 6, of which 2 were waited for; matrix products, arithmetic and copies ran while one was open for 0% of the time, Pallas kernels for 5%

profile of v16, /device:TPU:1, one launch (start us, length us, event | category | flops | bytes accessed | tf_op | source)
XLA Modules:
  0.0 89.4 jit_solution(1034417144529738429)
XLA Ops:
  0.6 0.9 %describe.1 = (bf16[32,512]{1,0:T(8,128)(2,1)S(1)}, f32[1,512]{1,0:T(1,128)S(1)}, f32[16,512]{1,0:T(8,128)S(1)}, f32[16,512]{1,0:T(8,128)S(1)}) custom-call(f32[16,512]{1,0:T(8,128)} %bitcast.30, f32[1,512]{1,0:T(1,128)} %bitcast.32, bf16[3,512]{1,0:T(4,128)(2,1)} %bitcast.31, bf16[1,512]{1,0:T(2,128)(2,1)} %bitcast.33, s32[1,512]{1,0:T(1,128)} %bitcast.34), custom_call_target="tpu_custom_call" | custom-call | tf_op jit(solution)/shard_map/describe/pallas_call | solution.py:137
  1.6 8.4 %all-gather = bf16[64,512]{1,0:T(8,128)(2,1)S(1)} all-gather(bf16[32,512]{1,0:T(8,128)(2,1)S(1)} %get-tuple-element.28), channel_id=2, replica_groups={{0,1},{2,3},{4,5},{6,7},{8,9},{10,11},{12,13},{14,15},{16,17},{18,19},{..., dimensions={0}, use_global_device_ids=true | all-gather | bytes 98304 | tf_op jit(solution)/shard_map/all_gather | solution.py:43
  10.0 4.4 %all-gather.1 = bf16[4,32,512]{2,1,0:T(8,128)(2,1)S(1)} all-gather(bf16[2,32,512]{2,1,0:T(8,128)(2,1)S(1)} %pad_maximum_fusion.3), channel_id=3, replica_groups={{1,2},{3,4},{5,6},{7,8},{9,10},{11,12},{13,14},{15,16},{17,18},{19,20},..., dimensions={0}, use_global_device_ids=true | all-gather | bytes 196608 | tf_op jit(solution)/shard_map/all_gather | solution.py:43
  14.4 1.3 %collective-permute-start.1 = (bf16[4,32,512]{2,1,0:T(8,128)(2,1)S(1)}, bf16[4,32,512]{2,1,0:T(8,128)(2,1)S(1)}, u32[]{:S(2)}, u32[]{:S(2)}) collective-permute-start(bf16[4,32,512]{2,1,0:T(8,128)(2,1)S(1)} %pad_maximum_fusion.near_ref), channel_id=1, source_target_pairs={{0,64},{64,128},{128,192},{192,256},{256,320},{320,384},{384,448},... | collective-permute-start | bytes 393224 | tf_op jit(solution)/shard_map/ppermute | solution.py:57
  15.7 1.3 %collective-permute-start = (bf16[4,32,512]{2,1,0:T(8,128)(2,1)S(1)}, bf16[4,32,512]{2,1,0:T(8,128)(2,1)S(1)}, u32[]{:S(2)}, u32[]{:S(2)}) collective-permute-start(bf16[4,32,512]{2,1,0:T(8,128)(2,1)S(1)} %pad_maximum_fusion.near_ref), channel_id=1, source_target_pairs={{64,0},{128,64},{192,128},{256,192},{320,256},{384,320},{448,384},... | collective-permute-start | bytes 393224 | tf_op jit(solution)/shard_map/ppermute | solution.py:58
  17.0 1.4 %build.3 = (bf16[3,512,512]{2,1,0:T(8,128)(2,1)S(1)}, f32[16,512]{1,0:T(8,128)S(1)}, bf16[3,48,512]{2,1,0:T(8,128)(2,1)S(1)}, bf16[3,48,512]{2,1,0:T(8,128)(2,1)S(1)}, f32[16,512]{1,0:T(8,128)S(1)}) custom-call(bf16[4,32,512]{2,1,0:T(8,128)(2,1)S(1)} %pad_maximum_fusion.near_ref, f32[16,512]{1,0:T(8,128)S(1)} %get-tuple-element.29.added_ref), custom_call_target="tpu_custom_call" | custom-call | flops 830472192 | bytes 1572864 | tf_op jit(solution)/shard_map/build/pallas_call | solution.py:227
  18.4 0.0 collective-permute-done.1.near_ref
  18.4 1.4 %build.4 = (bf16[3,512,512]{2,1,0:T(8,128)(2,1)S(1)}, f32[16,512]{1,0:T(8,128)S(1)}, f32[16,512]{1,0:T(8,128)S(1)}) custom-call(bf16[4,32,512]{2,1,0:T(8,128)(2,1)S(1)} %collective-permute-done.1.near_ref, bf16[3,48,512]{2,1,0:T(8,128)(2,1)S(1)} %get-tuple-element.30.own_ref, f32[16,512]{1,0:T(8,128)S(1)} %get-tuple-element.31.added_ref, ...), custom_call_target="tpu_custom_call" | custom-call | flops 830472192 | bytes 1572864 | tf_op jit(solution)/shard_map/build/pallas_call | solution.py:227
  19.8 1.6 %collective-permute-done.near_ref = bf16[4,32,512]{2,1,0:T(8,128)(2,1)S(1)} collective-permute-done((bf16[4,32,512]{2,1,0:T(8,128)(2,1)S(1)}, bf16[4,32,512]{2,1,0:T(8,128)(2,1)S(1)}, u32[]{:S(2)}, u32[]{:S(2)}) %collective-permute-start) | collective-permute-done | bytes 131104 | tf_op jit(solution)/shard_map/ppermute | solution.py:58
  21.4 1.4 %build.5 = (bf16[3,512,512]{2,1,0:T(8,128)(2,1)S(1)}, f32[16,512]{1,0:T(8,128)S(1)}, bf16[32,512]{1,0:T(8,128)(2,1)S(1)}, bf16[32,512]{1,0:T(8,128)(2,1)S(1)}) custom-call(bf16[4,32,512]{2,1,0:T(8,128)(2,1)S(1)} %collective-permute-done.near_ref, bf16[3,48,512]{2,1,0:T(8,128)(2,1)S(1)} %get-tuple-element.30.own_ref, ...), custom_call_target="tpu_custom_call" | custom-call | flops 830472192 | bytes 1572864 | tf_op jit(solution)/shard_map/build/pallas_call | solution.py:227
  22.8 10.4 %all-gather.2 = bf16[64,512]{1,0:T(8,128)(2,1)S(1)} all-gather(bf16[32,512]{1,0:T(8,128)(2,1)S(1)} %get-tuple-element.37), channel_id=4, replica_groups={{0,1},{2,3},{4,5},{6,7},{8,9},{10,11},{12,13},{14,15},{16,17},{18,19},{..., dimensions={0}, use_global_device_ids=true | all-gather | bytes 98304 | tf_op jit(solution)/shard_map/all_gather | solution.py:43
  33.2 3.1 %collective-permute-start.2 = (bf16[3,16,512]{2,1,0:T(8,128)(2,1)S(1)}, bf16[3,16,512]{2,1,0:T(8,128)(2,1)S(1)}, u32[]{:S(2)}, u32[]{:S(2)}) collective-permute-start(bf16[3,16,512]{2,1,0:T(8,128)(2,1)S(1)} %slice.82), channel_id=1, source_target_pairs={{0,64},{64,0},{128,192},{192,128},{256,320},{320,256},{384,448},{4... | collective-permute-start | bytes 147464 | tf_op jit(solution)/shard_map/ppermute | solution.py:64
  36.3 0.3 apply.1.part_ref
  36.7 5.7 %all-gather.3 = bf16[6,16,512]{2,1,0:T(8,128)(2,1)S(1)} all-gather(bf16[3,16,512]{2,1,0:T(8,128)(2,1)S(1)} %slice.82), channel_id=5, replica_groups={{64,128},{192,256},{320,384},{448,0},{65,129},{193,257},{321,385},{449,..., dimensions={0}, use_global_device_ids=true | all-gather | bytes 147456 | tf_op jit(solution)/shard_map/all_gather | solution.py:65
  42.4 0.0 collective-permute-done.2.swap_ref
  42.4 0.5 paired.1
  42.9 3.3 %all-gather.4 = bf16[64,512]{1,0:T(8,128)(2,1)S(1)} all-gather(bf16[32,512]{1,0:T(8,128)(2,1)S(1)} %get-tuple-element.44), channel_id=6, replica_groups={{0,1},{2,3},{4,5},{6,7},{8,9},{10,11},{12,13},{14,15},{16,17},{18,19},{..., dimensions={0}, use_global_device_ids=true | all-gather | bytes 98304 | tf_op jit(solution)/shard_map/all_gather | solution.py:43
  46.2 4.0 %all-gather.5 = bf16[64,512]{1,0:T(8,128)(2,1)S(1)} all-gather(bf16[32,512]{1,0:T(8,128)(2,1)S(1)} %get-tuple-element.44), channel_id=7, replica_groups={{1,2},{3,4},{5,6},{7,8},{9,10},{11,12},{13,14},{15,16},{17,18},{19,20},..., dimensions={0}, use_global_device_ids=true | all-gather | bytes 98304 | tf_op jit(solution)/shard_map/all_gather | solution.py:43
  50.3 2.2 %collective-permute-start.4 = (bf16[3,16,512]{2,1,0:T(8,128)(2,1)S(1)}, bf16[3,16,512]{2,1,0:T(8,128)(2,1)S(1)}, u32[]{:S(2)}, u32[]{:S(2)}) collective-permute-start(bf16[3,16,512]{2,1,0:T(8,128)(2,1)S(1)} %slice.87), channel_id=1, source_target_pairs={{0,64},{64,128},{128,192},{192,256},{256,320},{320,384},{384,448},... | collective-permute-start | bytes 147464 | tf_op jit(solution)/shard_map/ppermute | solution.py:57
  52.4 1.3 %collective-permute-start.3 = (bf16[3,16,512]{2,1,0:T(8,128)(2,1)S(1)}, bf16[3,16,512]{2,1,0:T(8,128)(2,1)S(1)}, u32[]{:S(2)}, u32[]{:S(2)}) collective-permute-start(bf16[3,16,512]{2,1,0:T(8,128)(2,1)S(1)} %slice.87), channel_id=1, source_target_pairs={{64,0},{128,64},{192,128},{256,192},{320,256},{384,320},{448,384},... | collective-permute-start | bytes 147464 | tf_op jit(solution)/shard_map/ppermute | solution.py:58
  53.7 0.4 same_band.1
  54.1 0.0 collective-permute-done.4.near_ref
  54.2 1.1 %below.1 = (f32[16,512]{1,0:T(8,128)S(1)}, f32[16,1,128]{2,1,0:T(1,128)}) custom-call(bf16[3,16,512]{2,1,0:T(8,128)(2,1)S(1)} %collective-permute-done.4.near_ref, bf16[3,512,512]{2,1,0:T(8,128)(2,1)S(1)} %get-tuple-element.38.below_ref.tile_ref, f32[16,512]{1,0:T(8,128)S(1)} %get-tuple-element.48.part_ref, f32[16,512]{1,0:T(8,128)S(1)} %get-tuple-element.46.second_ref, ...), custom_call_target="tpu_custom_call" | custom-call | flops 25165824 | bytes 1572864 | tf_op jit(solution)/shard_map/below/pallas_call | solution.py:346
  55.3 8.1 %all-to-all-start = ((f32[16,1,128]{2,1,0:T(1,128)}), f32[16,1,128]{2,1,0:T(1,128)S(1)}, u32[]{:S(2)}, u32[]{:S(2)}) async-start(f32[16,1,128]{2,1,0:T(1,128)} %get-tuple-element.50), calls=%async_computation | async-start | bytes 16384 | tf_op jit(solution)/shard_map/all_to_all | solution.py:397
  63.4 0.0 collective-permute-done.3.near_ref
  63.4 7.0 %all-to-all-done.total_ref = f32[16,1,128]{2,1,0:T(1,128)S(1)} async-done(((f32[16,1,128]{2,1,0:T(1,128)}), f32[16,1,128]{2,1,0:T(1,128)S(1)}, u32[]{:S(2)}, u32[]{:S(2)}) %all-to-all-start) | async-done | bytes 8224 | tf_op jit(solution)/shard_map/all_to_all | solution.py:397
  70.4 0.3 above.1
  70.7 17.9 %all_to_all.10.total_ref = f32[32,1,128]{2,1,0:T(1,128)S(1)} all-to-all(f32[32,1,128]{2,1,0:T(1,128)S(1)} %get-tuple-element.52), channel_id=1, replica_groups=mesh['z_lo'=2,'x'=4,'z_hi'=4,'y'=8,'core'=2] {'z_lo','z_hi','x'}, dimensions={0} | all-to-all | bytes 32768 | tf_op jit(solution)/shard_map/all_to_all | solution.py:399
  88.6 0.8 finish.1
  (12 shorter events, 0.1 us)
Async XLA Ops:
  14.4 4.0 %collective-permute-start.1 = (bf16[4,32,512]{2,1,0:T(8,128)(2,1)S(1)}, bf16[4,32,512]{2,1,0:T(8,128)(2,1)S(1)}, u32[]{:S(2)}, u32[]{:S(2)}) collective-permute-start(bf16[4,32,512]{2,1,0:T(8,128)(2,1)S(1)} %pad_maximum_fusion.near_ref), channel_id=1, source_target_pairs={{0,64},{64,128},{128,192},{192,256},{256,320},{320,384},{384,448},... | collective-permute-start | bytes 393224 | tf_op jit(solution)/shard_map/ppermute | solution.py:57
  15.7 5.7 %collective-permute-start = (bf16[4,32,512]{2,1,0:T(8,128)(2,1)S(1)}, bf16[4,32,512]{2,1,0:T(8,128)(2,1)S(1)}, u32[]{:S(2)}, u32[]{:S(2)}) collective-permute-start(bf16[4,32,512]{2,1,0:T(8,128)(2,1)S(1)} %pad_maximum_fusion.near_ref), channel_id=1, source_target_pairs={{64,0},{128,64},{192,128},{256,192},{320,256},{384,320},{448,384},... | collective-permute-start | bytes 393224 | tf_op jit(solution)/shard_map/ppermute | solution.py:58
  33.2 9.2 %collective-permute-start.2 = (bf16[3,16,512]{2,1,0:T(8,128)(2,1)S(1)}, bf16[3,16,512]{2,1,0:T(8,128)(2,1)S(1)}, u32[]{:S(2)}, u32[]{:S(2)}) collective-permute-start(bf16[3,16,512]{2,1,0:T(8,128)(2,1)S(1)} %slice.82), channel_id=1, source_target_pairs={{0,64},{64,0},{128,192},{192,128},{256,320},{320,256},{384,448},{4... | collective-permute-start | bytes 147464 | tf_op jit(solution)/shard_map/ppermute | solution.py:64
  50.3 3.9 %collective-permute-start.4 = (bf16[3,16,512]{2,1,0:T(8,128)(2,1)S(1)}, bf16[3,16,512]{2,1,0:T(8,128)(2,1)S(1)}, u32[]{:S(2)}, u32[]{:S(2)}) collective-permute-start(bf16[3,16,512]{2,1,0:T(8,128)(2,1)S(1)} %slice.87), channel_id=1, source_target_pairs={{0,64},{64,128},{128,192},{192,256},{256,320},{320,384},{384,448},... | collective-permute-start | bytes 147464 | tf_op jit(solution)/shard_map/ppermute | solution.py:57
  52.4 11.0 %collective-permute-start.3 = (bf16[3,16,512]{2,1,0:T(8,128)(2,1)S(1)}, bf16[3,16,512]{2,1,0:T(8,128)(2,1)S(1)}, u32[]{:S(2)}, u32[]{:S(2)}) collective-permute-start(bf16[3,16,512]{2,1,0:T(8,128)(2,1)S(1)} %slice.87), channel_id=1, source_target_pairs={{64,0},{128,64},{192,128},{256,192},{320,256},{384,320},{448,384},... | collective-permute-start | bytes 147464 | tf_op jit(solution)/shard_map/ppermute | solution.py:58
  55.3 15.1 %all-to-all-start = ((f32[16,1,128]{2,1,0:T(1,128)}), f32[16,1,128]{2,1,0:T(1,128)S(1)}, u32[]{:S(2)}, u32[]{:S(2)}) async-start(f32[16,1,128]{2,1,0:T(1,128)} %get-tuple-element.50), calls=%async_computation | async-start | bytes 16384 | tf_op jit(solution)/shard_map/all_to_all | solution.py:397
